TPU v7x, 128 devices: a whole 4x4x4 slice. The times are simulated.
128 devices in a mesh: row: 8 (over z, core), col: 16 (over y, x).
Axes of the slice: x: 4, y: 4, z: 4, core: 2. Of those that a mesh axis runs over, the one named last changes fastest.
Arguments:
- amplitudes: float32 [1024, 16384], P('col', 'row'), may hold values from -6 to 6
- integrals: float32 [16384, 32768], P('row', 'col'), may hold values from -0.046875 to 0.046875
- integral_mask: int32 [128, 256], P('row', 'col'), may hold values 0 or 1
- denominators: float32 [1024, 32768], P('row', 'col'), may hold values from 0.25 to 2
- cycle_tiles: float32 [32768, 512], P('col'), may hold values from -0.25 to 0.25
- cycle_mask: int32 [256, 4], P('col'), may hold values 0 or 1
- destination: int32 [1024, 256], P('row', 'col'), may hold values from 0 to 262143, as said below
Outputs:
- update: float32 [1024, 32768], P('row', 'col')
- cycle_term: float32 [1024, 32768], P('row', 'col')
Inputs may be any that keep to these rules, and one draw needn't show every extreme that they name: destination is a permutation of the units. Numbering a unit (r, t) as r * 256 + t and cutting the units into blocks of 128 rows by 16 tiles, every block sends exactly 16 of its units to every block.
All inputs are finite; a program needn't handle non-finite values. No bound on the sum of `integral_mask` or of `cycle_mask` on one device may be relied on, other than what follows from the above.
Results may differ from a plain program's by a relative error of at most 0.0003.
Values sent between devices are 32-bit elements; how exact they have to be, the bound alone decides.
No kernel may reach another device: no remote copies, remote signals or barrier semaphores. Data moves between devices by JAX's collectives and lax.ppermute only.
A program may use at most 128 MiB of HBM per device.

v0:
```python
import jax
import jax.numpy as jnp
from jax import lax
from jax.sharding import PartitionSpec as P

TILE = 128
RB = 512
VT = 256


def targets(dest_map, local_rows, local_tiles, ncol):
    flat = dest_map.reshape(-1)
    out_row = flat // VT
    out_tile = flat % VT
    owner = out_row // local_rows * ncol + out_tile // local_tiles
    place = out_row % local_rows * local_tiles + out_tile % local_tiles
    return (owner, place)


def deliver(units, owner, place, nrow, ncol):
    ndev = nrow * ncol
    order = jnp.argsort(owner, stable=True)
    per_peer = units.shape[0] // ndev
    sending = units[order].reshape(ndev, per_peer, TILE)
    places = place[order].astype(jnp.float32).reshape(ndev, per_peer)
    got, got_place = (
        lax.all_to_all(sending, ("row", "col"), split_axis=0, concat_axis=0, tiled=True),
        lax.all_to_all(places, ("row", "col"), split_axis=0, concat_axis=0, tiled=True),
    )
    return (got.reshape(-1, TILE), got_place.reshape(-1).astype(jnp.int32))


def body(amplitudes, integrals, integral_mask, denominators, cycle_tiles, cycle_mask, destination):
    nrow = lax.axis_size("row")
    ncol = lax.axis_size("col")
    cd_rows, cols = integrals.shape
    local_rows, local_tiles = destination.shape
    mask_f = integral_mask.astype(jnp.float32)
    masked = (
        integrals.reshape(cd_rows // TILE, TILE, cols // TILE, TILE) * mask_f[:, None, :, None]
    ).reshape(cd_rows, cols)
    partial_value = jnp.dot(
        lax.all_gather(amplitudes, "col", axis=0, tiled=True),
        masked,
        precision=lax.Precision.HIGHEST,
        preferred_element_type=jnp.float32,
    )
    empty = jnp.zeros((local_rows * local_tiles, TILE), jnp.float32)
    summed = lax.psum_scatter(partial_value, "row", scatter_dimension=0, tiled=True)
    owner, place = targets(destination, local_rows, local_tiles, ncol)
    got, got_place = deliver(summed.reshape(-1, TILE), owner, place, nrow, ncol)
    moved = empty.at[got_place].set(got)
    update = moved.reshape(local_rows, cols) / denominators
    cycle_f = cycle_mask.astype(jnp.float32)
    cycle = (
        cycle_tiles.reshape(cols // TILE, TILE, RB // TILE, TILE) * cycle_f[:, None, :, None]
    ).reshape(cols // RB, RB, RB)
    cycle_term = jnp.einsum(
        "okr,krs->oks",
        update.reshape(local_rows, cols // RB, RB),
        cycle,
        precision=lax.Precision.HIGHEST,
        preferred_element_type=jnp.float32,
    ).reshape(local_rows, cols)
    return (update, cycle_term)


def solution(mesh):
    return jax.shard_map(
        body,
        mesh=mesh,
        in_specs=(
            P("col", "row"),
            P("row", "col"),
            P("row", "col"),
            P("row", "col"),
            P("col", None),
            P("col", None),
            P("row", "col"),
        ),
        out_specs=(P("row", "col"), P("row", "col")),
        check_vma=False,
    )
```

profile of v0, /device:TPU:1, one launch (start us, length us, event | category | flops | bytes accessed | tf_op | source)
XLA Modules:
  0.0 317.3 jit_solution(171477621354483594)
XLA Ops:
  7.2 0.0 all-gather.2.cloned.1.call-start
  7.2 0.7 all-gather.2.cloned.1.call-update
  7.9 0.0 reduce-scatter.2.cloned.1.call-start
  7.9 0.7 convert_element_type.37
  8.6 75.4 %all-gather.2.cloned.1.call-done = f32[1024,2048]{1,0:T(8,128)} async-done(((f32[64,2048]{1,0:T(8,128)}), f32[1024,2048]{1,0:T(8,128)}) %all-gather.2.cloned.1.call-update) | async-done | bytes 8388624 | tf_op jit(solution)/shard_map/all_gather | solution.py:43
  84.0 8.2 %mul.30 = f32[16,128,16,128]{3,2,1,0:T(8,128)} broadcast(f32[16,16]{1,0:T(8,128)S(1)} %convert_element_type.37), dimensions={0,2} | broadcast | bytes 16778240 | tf_op jit(solution)/shard_map/mul | solution.py:40
  92.2 112.2 %fusion.2 = f32[1024,2048]{0,1:T(8,128)} fusion(f32[1024,2048]{1,0:T(8,128)S(1)} %copy-done.4, f32[2048,2048]{1,0:T(8,128)} %param.8, f32[256,8,16,128]{3,2,1,0:T(8,128)} %bitcast.26), kind=kOutput, calls=%fused_computation.6 | convolution fusion | flops 51543801856 | bytes 50331648 | tf_op jit(solution)/shard_map/dot_general | solution.py:42
  204.4 0.0 reduce-scatter.2.cloned.1.call-update
  204.4 0.7 copy-done.2
  205.1 0.1 copy.19
  205.2 0.1 reshape.73
  205.3 5.0 %sort.17 = (s32[2048]{0:T(1024)}, s32[2048]{0:T(1024)S(1)}) sort(s32[2048]{0:T(1024)S(1)} %get-tuple-element.10, s32[2048]{0:T(1024)S(1)} %iota.4), dimensions={0}, to_apply=%region_0.0 | sort | flops 22528 | bytes 32768 | tf_op jit(solution)/shard_map/jit(argsort)/sort | solution.py:22
  210.3 11.8 %gather_fusion = s32[2048]{0:T(1024)S(1)} fusion(s32[2048]{0:T(1024)S(1)} %get-tuple-element.11, s32[2048]{0:T(1024)S(1)} %fusion.13), kind=kCustom, calls=%fused_computation | custom fusion | bytes 24576 | tf_op jit(solution)/shard_map/gather | solution.py:25
  222.1 0.0 copy-start.3
  222.1 0.7 convert_element_type.34
  222.9 8.0 %all-to-all-start = ((f32[128,1,16]{2,1,0:T(1,128)}), f32[128,1,16]{2,1,0:T(1,128)S(1)}, u32[]{:S(2)}, u32[]{:S(2)}) async-start(f32[128,1,16]{2,1,0:T(1,128)} %bitcast), calls=%async_computation | async-start | bytes 131072 | tf_op jit(solution)/shard_map/all_to_all | solution.py:28
  230.9 26.0 %reduce-scatter.2.cloned.1.call-done = f32[128,2048]{0,1:T(8,128)} async-done(((f32[1024,2048]{0,1:T(8,128)}), f32[128,2048]{0,1:T(8,128)}) %reduce-scatter.2.cloned.1.call-update) | async-done | bytes 1048592 | tf_op jit(solution)/shard_map/reduce_scatter | solution.py:49
  256.9 1.6 copy.21
  258.4 0.2 reshape.74
  258.6 7.6 %gather_fusion.1 = f32[2048,128]{1,0:T(8,128)} fusion(f32[2048,128]{1,0:T(8,128)S(1)} %reshape.74, s32[2048]{0:T(1024)S(1)} %fusion.13), kind=kCustom, calls=%fused_computation.1 | custom fusion | bytes 2105344 | tf_op jit(solution)/shard_map/gather | solution.py:24
  266.3 8.4 %all-to-all-start.1 = ((f32[128,16,128]{2,1,0:T(8,128)}), f32[128,16,128]{2,1,0:T(8,128)S(1)}, u32[]{:S(2)}, u32[]{:S(2)}) async-start(f32[128,16,128]{2,1,0:T(8,128)} %bitcast.3), calls=%async_computation.2 | async-start | bytes 2097152 | tf_op jit(solution)/shard_map/all_to_all | solution.py:27
  274.7 0.1 copy.22
  274.8 2.5 mul.33
  277.3 5.5 %mul.34 = f32[4,512,512]{2,1,0:T(8,128)} reshape(f32[16,128,4,128]{3,2,1,0:T(4,128)} %mul.33) | data formatting | bytes 8388608 | tf_op jit(solution)/shard_map/mul | solution.py:56
  282.8 0.2 convert_reduce_fusion
  283.0 0.1 convert_element_type.36
  283.1 10.4 %all-to-all-done.1 = f32[128,16,128]{2,1,0:T(8,128)S(1)} async-done(((f32[128,16,128]{2,1,0:T(8,128)}), f32[128,16,128]{2,1,0:T(8,128)S(1)}, u32[]{:S(2)}, u32[]{:S(2)}) %all-to-all-start.1) | async-done | bytes 1048608 | tf_op jit(solution)/shard_map/all_to_all | solution.py:27
  293.5 5.8 %scatter_custom_fusion = f32[2048,128]{1,0:T(8,128)S(1)} fusion(s32[2048]{0:T(1024)S(1)} %bitcast.31, f32[2048,128]{1,0:T(8,128)S(1)} %bitcast.30, f32[]{:T(128)} %constant.60.clone.1), kind=kCustom, calls=%fused_computation.11 | custom fusion | bytes 1048580 | tf_op jit(solution)/shard_map/scatter | solution.py:52
  299.3 0.2 reshape.77
  299.5 0.1 div.47
  299.7 9.5 %fusion.3 = f32[4,512,128]{2,1,0:T(8,128)S(1)} fusion(f32[4,512,512]{2,1,0:T(8,128)} %bitcast.29, f32[4,512,512]{2,1,0:T(8,128)} %mul.34, f32[16,4,8,512]{3,2,1,0:T(8,128)S(1)} %bitcast.27), kind=kOutput, calls=%fused_computation.7 | convolution fusion | flops 1611661312 | bytes 10485760 | tf_op jit(solution)/shard_map/okr,krs->oks/dot_general | solution.py:58
  309.2 1.3 copy.25
  (15 shorter events, 0.1 us)
Async XLA Ops:
  7.2 76.8 %all-gather.2.cloned.1.call-start = ((), (), s32[]{:S(2)}) async-start(), calls=%async_computation.3 | async-start | bytes 8912896 | tf_op jit(solution)/shard_map/all_gather | solution.py:43
  7.9 249.0 %reduce-scatter.2.cloned.1.call-start = ((), (), s32[]{:S(2)}) async-start(), calls=%async_computation.4 | async-start | bytes 9437184 | tf_op jit(solution)/shard_map/reduce_scatter | solution.py:49
  84.0 8.2 %copy-start.4 = (f32[1024,2048]{1,0:T(8,128)S(1)}, f32[1024,2048]{1,0:T(8,128)}, u32[]{:S(2)}) copy-start(f32[1024,2048]{1,0:T(8,128)} %all-gather.2.cloned.1.call-done) | copy-start | bytes 25165828
  204.4 0.7 copy-start.2
  222.1 52.6 %copy-start.3 = (s32[16,4]{0,1:T(4,128)S(1)}, s32[16,4]{0,1:T(4,128)}, u32[]{:S(2)}) copy-start(s32[16,4]{0,1:T(4,128)} %param.12) | copy-start | bytes 772
  222.9 43.4 %all-to-all-start = ((f32[128,1,16]{2,1,0:T(1,128)}), f32[128,1,16]{2,1,0:T(1,128)S(1)}, u32[]{:S(2)}, u32[]{:S(2)}) async-start(f32[128,1,16]{2,1,0:T(1,128)} %bitcast), calls=%async_computation | async-start | bytes 131072 | tf_op jit(solution)/shard_map/all_to_all | solution.py:28
  266.3 27.2 %all-to-all-start.1 = ((f32[128,16,128]{2,1,0:T(8,128)}), f32[128,16,128]{2,1,0:T(8,128)S(1)}, u32[]{:S(2)}, u32[]{:S(2)}) async-start(f32[128,16,128]{2,1,0:T(8,128)} %bitcast.3), calls=%async_computation.2 | async-start | bytes 2097152 | tf_op jit(solution)/shard_map/all_to_all | solution.py:27
  274.7 24.8 %copy-start.1 = (f32[128,2048]{1,0:T(8,128)S(1)}, f32[128,2048]{1,0:T(8,128)}, u32[]{:S(2)}) copy-start(f32[128,2048]{1,0:T(8,128)} %param.10) | copy-start | bytes 3145732
  299.7 10.8 %copy-start = (f32[128,2048]{1,0:T(8,128)}, f32[128,2048]{1,0:T(8,128)S(1)}, u32[]{:S(2)}) copy-start(f32[128,2048]{1,0:T(8,128)S(1)} %div.47) | copy-start | bytes 3145732
Sparse Core Ops, SparseCore 0:
  10.1 73.8 all-gather.1
  204.5 52.3 reduce-scatter.1
where the time goes:
time: 318 us; the launch traced here: 317 us
  matrix products  122 us (38%)
  waiting for transfers between devices  112 us (35%)
  local copies, waits for them, and re-layouts  46.4 us (15%)
  starting transfers between devices  16.5 us (5%)
  between operations  14.2 us (4%)
  other arithmetic  6.13 us (2%)
    dot_general x1, matrix products, body(): jnp.dot(lax.all_gather(amplitudes, 'col', axis=0, tiled=True), masked, pr...  112 us
    all_gather x1, waiting for transfers between devices, body(): lax.all_gather(amplitudes, 'col', axis=0, tiled=True)  75.4 us
    reduce_scatter x1, waiting for transfers between devices, body(): lax.psum_scatter(partial_value, 'row', scatter_dimension=0, tiled=True)  26 us
    gather x1, local copies, waits for them, and re-layouts, deliver(): places = place[order].astype(jnp.float32).reshape(ndev, per_peer)  11.8 us
    all_to_all x1, waiting for transfers between devices, deliver(): lax.all_to_all(sending, ('row', 'col'), split_axis=0, concat_axis=0, tile...  10.4 us
    dot_general x1, matrix products, body(): jnp.einsum('okr,krs->oks', update.reshape(local_rows, cols // RB, RB), cy...  9.5 us
    all_to_all x1, starting transfers between devices, deliver(): lax.all_to_all(sending, ('row', 'col'), split_axis=0, concat_axis=0, tile...  8.42 us
    mul x1, local copies, waits for them, and re-layouts, body(): integrals.reshape(cd_rows // TILE, TILE, cols // TILE, TILE)  8.18 us
  transfers between devices with their start and end apart: 4, of which 3 were waited for; matrix products, arithmetic and copies ran while one was open for 11% of the time, Pallas kernels for 0%

commit v1 on v0

v1 whole, which is shorter than its diff:
```python
import functools

import jax
import jax.numpy as jnp
from jax import lax
from jax.experimental import pallas as pl
from jax.experimental.pallas import tpu as pltpu
from jax.sharding import Mesh, PartitionSpec as P

TILE = 128
RB = 512
VT = 256
ROWS = 128
TPD = 16
CAP = 16
NZ = 4
SPLITS = (32, 32)
NB = 256
MIB = 1 << 20

f32 = jnp.float32
bf16 = jnp.bfloat16


def split(x):
    hi = x.astype(bf16)
    return hi, (x - hi.astype(f32)).astype(bf16)


def call(kernel, out_shape, *, vmem=48, flops=0, nbytes=0, **kw):
    return pl.pallas_call(
        kernel,
        out_shape=out_shape,
        compiler_params=pltpu.CompilerParams(vmem_limit_bytes=vmem * MIB),
        cost_estimate=pl.CostEstimate(flops=flops, bytes_accessed=nbytes, transcendentals=0),
        **kw,
    )


def prep_kernel(mask_ref, x_ref, hi_ref, lo_ref, *, tile_rows, tile_cols, step_axis):
    step = pl.program_id(0)
    for i in range(tile_rows):
        for j in range(tile_cols):
            mi = i + (step * tile_rows if step_axis == 0 else 0)
            mj = j + (step * tile_cols if step_axis == 1 else 0)
            m = mask_ref[mi, mj].astype(f32)
            sl = (slice(i * TILE, (i + 1) * TILE), slice(j * TILE, (j + 1) * TILE))
            hi, lo = split(x_ref[sl] * m)
            hi_ref[sl] = hi
            lo_ref[sl] = lo


def prep(x, mask, block, step_axis):
    rows, cols = x.shape
    grid = (rows // block[0],) if step_axis == 0 else (cols // block[1],)
    imap = (lambda n: (n, 0)) if step_axis == 0 else (lambda n: (0, n))
    spec = pl.BlockSpec(block, imap)
    out = jax.ShapeDtypeStruct((rows, cols), bf16)
    return call(
        functools.partial(prep_kernel, tile_rows=block[0] // TILE, tile_cols=block[1] // TILE, step_axis=step_axis),
        (out, out),
        grid=grid,
        in_specs=[pl.BlockSpec(memory_space=pltpu.SMEM), spec],
        out_specs=(spec, spec),
        nbytes=rows * cols * 8,
        flops=rows * cols * 4,
    )(mask, x)


def mm_kernel(order_ref, a_ref, bh_ref, bl_ref, o_ref, ah, al, *, sub):
    @pl.when(pl.program_id(0) == 0)
    def _():
        for i in range(NZ):
            r = order_ref[i]
            for j in range(2):
                hi, lo = split(a_ref[2 * r + j])
                at = slice((2 * i + j) * sub, (2 * i + j + 1) * sub)
                ah[at, :] = hi
                al[at, :] = lo

    dot = functools.partial(jnp.dot, preferred_element_type=f32)
    acc = dot(ah[...], bh_ref[...]) + dot(ah[...], bl_ref[...]) + dot(al[...], bh_ref[...])
    for i in range(NZ):
        for t in range(NB // TILE):
            o_ref[i, t] = acc[2 * sub * i : 2 * sub * (i + 1), t * TILE : (t + 1) * TILE]


def multiply(a, bh, bl, order, part):
    sub = SPLITS[part]
    assert sum(SPLITS[:part]) % sub == 0
    at = sum(SPLITS[:part]) // sub
    depth, cols = bh.shape
    m = NZ * 2 * sub
    return call(
        functools.partial(mm_kernel, sub=sub),
        jax.ShapeDtypeStruct((NZ, cols // TILE, 2 * sub, TILE), f32),
        grid=(cols // NB,),
        in_specs=[
            pl.BlockSpec(memory_space=pltpu.SMEM),
            pl.BlockSpec((16, sub, depth), lambda n: (0, at, 0)),
            pl.BlockSpec((depth, NB), lambda n: (0, n)),
            pl.BlockSpec((depth, NB), lambda n: (0, n)),
        ],
        out_specs=pl.BlockSpec((NZ, NB // TILE, 2 * sub, TILE), lambda n: (0, n, 0, 0)),
        scratch_shapes=[pltpu.VMEM((m, depth), bf16), pltpu.VMEM((m, depth), bf16)],
        flops=6 * m * depth * cols,
        nbytes=4 * depth * cols + 4 * m * cols,
    )(order, a, bh, bl)


def far_kernel(mine_ref, got_ref, p_ref, m_ref):
    half = TPD // 2
    p_ref[...] = mine_ref[0, :half] + got_ref[0, :half]
    m_ref[...] = mine_ref[0, half:] + got_ref[0, half:]


def far(mine, got):
    block = (1,) + mine.shape[1:]
    shape = jax.ShapeDtypeStruct((TPD // 2,) + mine.shape[2:], f32)
    spec = pl.BlockSpec(block, lambda n: (0, 0, 0, 0))
    whole = pl.BlockSpec(shape.shape, lambda n: (0, 0, 0))
    return call(far_kernel, (shape, shape), grid=(1,), in_specs=[spec, spec], out_specs=(whole, whole), nbytes=3 * 1024 * 512)(mine, got)


def near_kernel(mine_ref, got_ref, gp_ref, gm_ref, p_ref, m_ref):
    half = TPD // 2
    p_ref[:half] = mine_ref[0, :half] + got_ref[0, :half] + gp_ref[...]
    p_ref[half:] = mine_ref[0, half:] + got_ref[0, half:]
    m_ref[:half] = mine_ref[1, :half] + got_ref[1, :half]
    m_ref[half:] = mine_ref[1, half:] + got_ref[1, half:] + gm_ref[...]


def near(mine, got, gp, gm):
    rows = mine.shape[2]
    two = pl.BlockSpec((pl.Element(2), pl.Element(TPD), pl.Element(rows), pl.Element(TILE)), lambda n: (1, 0, 0, 0))
    part = pl.BlockSpec(gp.shape, lambda n: (0, 0, 0))
    shape = jax.ShapeDtypeStruct(mine.shape[1:], f32)
    whole = pl.BlockSpec(shape.shape, lambda n: (0, 0, 0))
    return call(near_kernel, (shape, shape), grid=(1,), in_specs=[two, two, part, part], out_specs=(whole, whole), nbytes=7 * 1024 * 512)(mine, got, gp, gm)


def gather_kernel(idx_ref, *refs):
    ins, (out_ref, scr) = refs[:-2], refs[-2:]
    base = 0
    for c in range(len(SPLITS)):
        mine, got, rp, rm = ins[4 * c : 4 * c + 4]
        rows = 2 * SPLITS[c]
        for t in range(TPD):
            scr[base + t * rows : base + (t + 1) * rows, :] = mine[0, t] + got[0, t] + rp[t] + rm[t]
        base += TPD * rows

    def step(g, carry):
        for k in range(16):
            i = g * 16 + k
            out_ref[pl.ds(i, 1), :] = scr[pl.ds(idx_ref[i], 1), :]
        return carry

    lax.fori_loop(0, ROWS * TPD // 16, step, 0)


def gather(idx, parts):
    units = ROWS * TPD
    specs = [pl.BlockSpec(memory_space=pltpu.SMEM)]
    flat = []
    for mine, got, rp, rm in parts:
        own = pl.BlockSpec((1,) + mine.shape[1:], lambda n: (NZ - 1, 0, 0, 0))
        whole = pl.BlockSpec(rp.shape, lambda n: (0, 0, 0))
        specs += [own, own, whole, whole]
        flat += [mine, got, rp, rm]
    return call(
        gather_kernel,
        jax.ShapeDtypeStruct((units, TILE), f32),
        grid=(1,),
        in_specs=specs,
        out_specs=pl.BlockSpec((units, TILE), lambda n: (0, 0)),
        scratch_shapes=[pltpu.VMEM((units, TILE), f32)],
        nbytes=5 * units * TILE * 4,
    )(idx, *flat)


def finish_kernel(place_ref, got_ref, den_ref, ch_ref, cl_ref, up_ref, ct_ref, scr):
    def step(g, carry):
        for k in range(16):
            i = g * 16 + k
            scr[pl.ds(place_ref[i], 1), :] = got_ref[pl.ds(i, 1), :]
        return carry

    lax.fori_loop(0, ROWS * TPD // 16, step, 0)
    for t in range(TPD):
        at = slice(t * TILE, (t + 1) * TILE)
        up_ref[:, at] = scr[at, :] / den_ref[:, at]
    dot = functools.partial(jnp.dot, preferred_element_type=f32)
    for k in range(TPD * TILE // RB):
        at = slice(k * RB, (k + 1) * RB)
        hi, lo = split(up_ref[:, at])
        ct_ref[:, at] = dot(hi, ch_ref[at, :]) + dot(hi, cl_ref[at, :]) + dot(lo, ch_ref[at, :])


def finish(place, got, den, ch, cl):
    shape = jax.ShapeDtypeStruct(den.shape, f32)
    whole = lambda s: pl.BlockSpec(s, lambda n: (0, 0))
    return call(
        finish_kernel,
        (shape, shape),
        grid=(1,),
        in_specs=[pl.BlockSpec(memory_space=pltpu.SMEM), whole(got.shape), whole(den.shape), whole(ch.shape), whole(cl.shape)],
        out_specs=(whole(den.shape), whole(den.shape)),
        scratch_shapes=[pltpu.VMEM(got.shape, f32)],
        nbytes=8 << 20,
    )(place, got, den, ch, cl)


def plan(destination):
    flat = destination.reshape(-1)
    out_row = flat // VT
    out_tile = flat % VT
    owner = out_row // ROWS * (VT // TPD) + out_tile // TPD
    place = out_tile % TPD * ROWS + out_row % ROWS
    unit = jnp.arange(ROWS * TPD, dtype=jnp.int32)
    row, tile = unit // TPD, unit % TPD
    block, sub = row // 64, row % 64
    at = jnp.zeros_like(unit)
    first, base = 0, 0
    for rows in SPLITS:
        here = base + tile * (2 * rows) + block * rows + (sub - first)
        at = jnp.where(sub >= first, here, at)
        first += rows
        base += TPD * 2 * rows
    key = lax.sort((owner << 22) | (at << 11) | place)
    return (key >> 11) & 2047, key & 2047


def ring(step):
    return [(i, (i + step) % NZ) for i in range(NZ)]


def body(amplitudes, integrals, integral_mask, denominators, cycle_tiles, cycle_mask, destination):
    everyone = ("z", "core", "y", "x")
    z = lax.axis_index("z")
    core = lax.axis_index("core")
    depth = integrals.shape[0]

    gathered = lax.all_gather(amplitudes, ("y", "x"), axis=0, tiled=True).reshape(16, 64, depth)

    bh, bl = prep(integrals, integral_mask, (depth, NB), 1)
    source, place = plan(destination)
    place = place.astype(f32).reshape(128, 1, CAP)
    got_place = lax.all_to_all(place, everyone, split_axis=0, concat_axis=0, tiled=True)
    got_place = got_place.reshape(-1).astype(jnp.int32)
    ch, cl = prep(cycle_tiles, cycle_mask, (512, RB), 0)
    bh, bl, ch, cl, source, got_place = lax.optimization_barrier((bh, bl, ch, cl, source, got_place))

    towards = jnp.array([2, 1, 3, 0], jnp.int32)
    order = 2 * ((z + towards) % NZ)
    own_order, other_order = order + core, order + (1 - core)

    parts = []
    for c in range(len(SPLITS)):
        theirs = multiply(gathered, bh, bl, other_order, c)
        got = lax.ppermute(theirs, "core", [(0, 1), (1, 0)])
        mine = multiply(gathered, bh, bl, own_order, c)
        far_p, far_m = far(mine, got)
        gp = lax.ppermute(far_p, "z", ring(1))
        gm = lax.ppermute(far_m, "z", ring(-1))
        near_p, near_m = near(mine, got, gp, gm)
        rp = lax.ppermute(near_p, "z", ring(1))
        rm = lax.ppermute(near_m, "z", ring(-1))
        parts.append((mine, got, rp, rm))

    sending = gather(source, parts).reshape(128, CAP, TILE)
    units = lax.all_to_all(sending, everyone, split_axis=0, concat_axis=0, tiled=True)
    return finish(got_place, units.reshape(-1, TILE), denominators, ch, cl)


def solution(mesh):
    row, col = ("z", "core"), ("y", "x")
    split_mesh = Mesh(mesh.devices.reshape(4, 2, 4, 4), row + col)
    return jax.shard_map(
        body,
        mesh=split_mesh,
        in_specs=(P(col, row), P(row, col), P(row, col), P(row, col), P(col, None), P(col, None), P(row, col)),
        out_specs=(P(row, col), P(row, col)),
        check_vma=False,
    )
```

time: 318 us -> 218 us (0.69)
  matrix products: 122 us -> 0 us
  Pallas kernels: 0 us -> 81.6 us
  waiting for transfers between devices: 112 us -> 60 us
  local copies, waits for them, and re-layouts: 46.4 us -> 3.84 us
  blocking collectives: 0 us -> 27.6 us
  starting transfers between devices: 16.5 us -> 23.4 us
    dot_general x2 -> x0, matrix products: 122 us -> none  [the longest x1 112 us: body(): jnp.dot(lax.all_gather(amplitudes, 'col', axis=0, tiled=True), masked, pr...]
    pallas_call x0 -> x12, Pallas kernels: none -> 81.6 us  [the longest x4 53.1 us: multiply(): call(functools.partial(mm_kernel, sub=sub), jax.ShapeDtypeStruct((NZ, col...]
    all_gather x1, waiting for transfers between devices: 75.4 us -> 37.3 us  [body(): lax.all_gather(amplitudes, ('y', 'x'), axis=0, tiled=True)]
    all_to_all x0 -> x1, blocking collectives: none -> 27.6 us  [body(): lax.all_to_all(sending, everyone, split_axis=0, concat_axis=0, tiled=True)]
    reduce_scatter x1 -> x0, waiting for transfers between devices: 26 us -> none  [body(): lax.psum_scatter(partial_value, 'row', scatter_dimension=0, tiled=True)]
    ppermute x0 -> x10, waiting for transfers between devices: none -> 22 us  [the longest x2 19.6 us: body(): rp = lax.ppermute(near_p, 'z', ring(1))]
    gather x2 -> x0, local copies, waits for them, and re-layouts: 19.4 us -> none  [the longest x1 11.8 us: deliver(): places = place[order].astype(jnp.float32).reshape(ndev, per_peer)]
    mul x3 -> x0, local copies, waits for them, and re-layouts: 16.2 us -> none  [the longest x1 8.18 us: body(): integrals.reshape(cd_rows // TILE, TILE, cols // TILE, TILE)]
  transfers between devices with their start and end apart: 4 -> 12, of which waited for: 3 -> 4; matrix products, arithmetic and copies ran while one was open for 11% -> 4% of each run, Pallas kernels for 0% -> 27%
where the time goes in v1:
time: 218 us; the launch traced here: 217 us
  Pallas kernels  81.6 us (37%)
  waiting for transfers between devices  60 us (28%)
  blocking collectives  27.6 us (13%)
  starting transfers between devices  23.4 us (11%)
  between operations  14.2 us (7%)
  other arithmetic  5.95 us (3%)
  local copies, waits for them, and re-layouts  3.84 us (2%)
    pallas_call x4, Pallas kernels, multiply(): call(functools.partial(mm_kernel, sub=sub), jax.ShapeDtypeStruct((NZ, col...  53.1 us
    all_gather x1, waiting for transfers between devices, body(): lax.all_gather(amplitudes, ('y', 'x'), axis=0, tiled=True)  37.3 us
    all_to_all x1, blocking collectives, body(): lax.all_to_all(sending, everyone, split_axis=0, concat_axis=0, tiled=True)  27.6 us
    ppermute x2, waiting for transfers between devices, body(): rp = lax.ppermute(near_p, 'z', ring(1))  19.6 us
    pallas_call x2, Pallas kernels, prep(): call(functools.partial(prep_kernel, tile_rows=block[0] // TILE, tile_cols...  18.3 us
    all_to_all x1, starting transfers between devices, body(): lax.all_to_all(place, everyone, split_axis=0, concat_axis=0, tiled=True)  11.5 us
    pallas_call x1, Pallas kernels, finish(): call(finish_kernel, (shape, shape), grid=(1,), in_specs=[pl.BlockSpec(mem...  5.93 us
    ppermute x2, starting transfers between devices, body(): rm = lax.ppermute(near_m, 'z', ring(-1))  5.33 us
  transfers between devices with their start and end apart: 12, of which 4 were waited for; matrix products, arithmetic and copies ran while one was open for 4% of the time, Pallas kernels for 27%

profile of v1, /device:TPU:1, one launch (start us, length us, event | category | flops | bytes accessed | tf_op | source)
XLA Modules:
  0.0 216.7 jit_solution(3329116153687529964)
XLA Ops:
  7.2 0.7 all-gather.2.cloned.1.call-update
  7.9 0.8 copy.14
  8.7 0.1 reshape.21
  8.8 5.0 %sort.14 = (s32[2048]{0:T(1024)S(1)}, s32[2048]{0:T(1024)}) sort(s32[2048]{0:T(1024)S(1)} %fusion.10, s32[2048]{0:T(1024)S(1)} %iota.7), dimensions={0}, to_apply=%region_0.1 | sort | flops 22528 | bytes 32768 | tf_op jit(solution)/shard_map/sort | solution.py:229
  13.9 0.7 reshape.22
  14.6 11.5 %all-to-all-start = ((f32[128,1,16]{2,1,0:T(1,128)}), f32[128,1,16]{2,1,0:T(1,128)S(1)}, u32[]{:S(2)}, u32[]{:S(2)}) async-start(f32[128,1,16]{2,1,0:T(1,128)} %bitcast), calls=%async_computation | async-start | bytes 131072 | tf_op jit(solution)/shard_map/all_to_all | solution.py:248
  26.1 0.7 broadcast_add_fusion
  26.8 0.8 copy.13.mask_ref
  27.5 3.4 %shard_map.96 = (bf16[2048,512]{1,0:T(8,128)(2,1)S(1)}, bf16[2048,512]{1,0:T(8,128)(2,1)S(1)}) custom-call(s32[16,4]{1,0:T(8,128)S(1)} %copy.13.mask_ref, f32[2048,512]{1,0:T(8,128)} %x_ref.3), custom_call_target="tpu_custom_call" | custom-call | flops 4194304 | bytes 8388608 | tf_op jit(solution)/shard_map/pallas_call | solution.py:59
  30.9 1.4 copy-done.3
  32.3 15.0 %shard_map.95 = (bf16[2048,2048]{1,0:T(8,128)(2,1)}, bf16[2048,2048]{1,0:T(8,128)(2,1)}) custom-call(s32[16,16]{1,0:T(8,128)S(1)} %copy-done.5, f32[2048,2048]{1,0:T(8,128)} %x_ref.2), custom_call_target="tpu_custom_call" | custom-call | flops 16777216 | bytes 33554432 | tf_op jit(solution)/shard_map/pallas_call | solution.py:59
  47.3 0.2 convert_reduce_fusion
  47.6 37.3 %all-gather.2.cloned.1.call-done = f32[1024,2048]{1,0:T(8,128)} async-done(((f32[64,2048]{1,0:T(8,128)}), f32[1024,2048]{1,0:T(8,128)}) %all-gather.2.cloned.1.call-update) | async-done | bytes 8388624 | tf_op jit(solution)/shard_map/all_gather | solution.py:243
  84.9 13.3 %shard_map.98 = f32[4,16,64,128]{3,2,1,0:T(8,128)S(1)} custom-call(s32[4]{0:T(128)S(1)} %get-tuple-element.41.order_ref, f32[16,64,2048]{2,1,0:T(8,128)} %bitcast.6, bf16[2048,2048]{1,0:T(8,128)(2,1)} %get-tuple-element.29.bh_ref, bf16[2048,2048]{1,0:T(8,128)(2,1)} %get-tuple-element.30.bl_ref), custom_call_target="tpu_custom_call" | custom-call | flops 6442450944 | bytes 18874368 | tf_op jit(solution)/shard_map/pallas_call | solution.py:94
  98.1 0.8 collective-permute-start
  98.9 13.3 %shard_map.102 = f32[4,16,64,128]{3,2,1,0:T(8,128)S(1)} custom-call(s32[4]{0:T(128)S(1)} %get-tuple-element.41.order_ref, f32[16,64,2048]{2,1,0:T(8,128)} %bitcast.7, bf16[2048,2048]{1,0:T(8,128)(2,1)} %get-tuple-element.29.bh_ref, bf16[2048,2048]{1,0:T(8,128)(2,1)} %get-tuple-element.30.bl_ref), custom_call_target="tpu_custom_call" | custom-call | flops 6442450944 | bytes 18874368 | tf_op jit(solution)/shard_map/pallas_call | solution.py:94
  112.2 0.1 collective-permute-start.5
  112.3 13.3 %shard_map.97.mine_ref.refs_0_ = f32[4,16,64,128]{3,2,1,0:T(8,128)S(1)} custom-call(s32[4]{0:T(128)S(1)} %broadcast_add_fusion.1.order_ref, f32[16,64,2048]{2,1,0:T(8,128)} %bitcast.8, bf16[2048,2048]{1,0:T(8,128)(2,1)} %get-tuple-element.29.bh_ref, bf16[2048,2048]{1,0:T(8,128)(2,1)} %get-tuple-element.30.bl_ref), custom_call_target="tpu_custom_call" | custom-call | flops 6442450944 | bytes 18874368 | tf_op jit(solution)/shard_map/pallas_call | solution.py:94
  125.7 1.3 collective-permute-start.1
  127.0 1.5 collective-permute-start.2
  128.5 13.3 %shard_map.101.mine_ref.refs_4_ = f32[4,16,64,128]{3,2,1,0:T(8,128)S(1)} custom-call(s32[4]{0:T(128)S(1)} %broadcast_add_fusion.1.order_ref, f32[16,64,2048]{2,1,0:T(8,128)} %bitcast.9, bf16[2048,2048]{1,0:T(8,128)(2,1)} %get-tuple-element.29.bh_ref, bf16[2048,2048]{1,0:T(8,128)(2,1)} %get-tuple-element.30.bl_ref), custom_call_target="tpu_custom_call" | custom-call | flops 6442450944 | bytes 18874368 | tf_op jit(solution)/shard_map/pallas_call | solution.py:94
  141.9 2.7 %collective-permute-start.7 = (f32[8,64,128]{2,1,0:T(8,128)S(1)}, f32[8,64,128]{2,1,0:T(8,128)S(1)}, u32[]{:S(2)}, u32[]{:S(2)}) collective-permute-start(f32[8,64,128]{2,1,0:T(8,128)S(1)} %get-tuple-element.36), channel_id=1, source_target_pairs={{0,96},{32,0},{64,32},{96,64},{1,97},{33,1},{65,33},{97,65},{2,98}... | collective-permute-start | bytes 786440 | tf_op jit(solution)/shard_map/ppermute | solution.py:264
  144.6 0.2 shard_map.100
  144.9 2.7 %collective-permute-start.4 = (f32[16,64,128]{2,1,0:T(8,128)S(1)}, f32[16,64,128]{2,1,0:T(8,128)S(1)}, u32[]{:S(2)}, u32[]{:S(2)}) collective-permute-start(f32[16,64,128]{2,1,0:T(8,128)S(1)} %get-tuple-element.34), channel_id=1, source_target_pairs={{0,96},{32,0},{64,32},{96,64},{1,97},{33,1},{65,33},{97,65},{2,98}... | collective-permute-start | bytes 1572872 | tf_op jit(solution)/shard_map/ppermute | solution.py:267
  147.5 2.5 %collective-permute-done.6.gp_ref = f32[8,64,128]{2,1,0:T(8,128)S(1)} collective-permute-done((f32[8,64,128]{2,1,0:T(8,128)S(1)}, f32[8,64,128]{2,1,0:T(8,128)S(1)}, u32[]{:S(2)}, u32[]{:S(2)}) %collective-permute-start.6) | collective-permute-done | bytes 262176 | tf_op jit(solution)/shard_map/ppermute | solution.py:263
  150.0 0.1 shard_map.104
  150.2 2.7 %collective-permute-start.9 = (f32[16,64,128]{2,1,0:T(8,128)S(1)}, f32[16,64,128]{2,1,0:T(8,128)S(1)}, u32[]{:S(2)}, u32[]{:S(2)}) collective-permute-start(f32[16,64,128]{2,1,0:T(8,128)S(1)} %get-tuple-element.38), channel_id=1, source_target_pairs={{0,96},{32,0},{64,32},{96,64},{1,97},{33,1},{65,33},{97,65},{2,98}... | collective-permute-start | bytes 1572872 | tf_op jit(solution)/shard_map/ppermute | solution.py:267
  152.9 8.3 %collective-permute-done.3.refs_2_ = f32[16,64,128]{2,1,0:T(8,128)S(1)} collective-permute-done((f32[16,64,128]{2,1,0:T(8,128)S(1)}, f32[16,64,128]{2,1,0:T(8,128)S(1)}, u32[]{:S(2)}, u32[]{:S(2)}) %collective-permute-start.3) | collective-permute-done | bytes 524320 | tf_op jit(solution)/shard_map/ppermute | solution.py:266
  161.2 11.2 %collective-permute-done.8.refs_6_ = f32[16,64,128]{2,1,0:T(8,128)S(1)} collective-permute-done((f32[16,64,128]{2,1,0:T(8,128)S(1)}, f32[16,64,128]{2,1,0:T(8,128)S(1)}, u32[]{:S(2)}, u32[]{:S(2)}) %collective-permute-start.8) | collective-permute-done | bytes 524320 | tf_op jit(solution)/shard_map/ppermute | solution.py:266
  172.5 3.9 %shard_map.105 = f32[2048,128]{1,0:T(8,128)S(1)} custom-call(s32[2048]{0:T(1024)S(1)} %get-tuple-element.28.idx_ref, f32[4,16,64,128]{3,2,1,0:T(8,128)S(1)} %shard_map.97.mine_ref.refs_0_, f32[4,16,64,128]{3,2,1,0:T(8,128)} %copy-done.1, f32[16,64,128]{2,1,0:T(8,128)S(1)} %collective-permute-done.3.refs_2_, ...), custom_call_target="tpu_custom_call" | custom-call | bytes 5242880 | tf_op jit(solution)/shard_map/pallas_call | solution.py:170
  176.3 27.6 %all_to_all.10 = f32[128,16,128]{2,1,0:T(8,128)S(1)} all-to-all(f32[128,16,128]{2,1,0:T(8,128)S(1)} %bitcast.4), channel_id=1, replica_groups=mesh['z'=4,'core'=2,'y'=4,'x'=4] {'z','core','y','x'}, dimensions={0} | all-to-all | bytes 2097152 | tf_op jit(solution)/shard_map/all_to_all | solution.py:271
  203.9 5.9 %shard_map.106 = (f32[128,2048]{1,0:T(8,128)}, f32[128,2048]{1,0:T(8,128)}) custom-call(s32[2048]{0:T(1024)S(1)} %convert_element_type.11.place_ref, f32[2048,128]{1,0:T(8,128)S(1)} %bitcast.5, f32[128,2048]{1,0:T(8,128)S(1)} %copy-done.4, bf16[2048,512]{1,0:T(8,128)(2,1)S(1)} %get-tuple-element.39.ch_ref, bf16[2048,512]{1,0:T(8,128)(2,1)} %copy-done.3), custom_call_target="tpu_custom_call" | custom-call | bytes 8388608 | tf_op jit(solution)/shard_map/pallas_call | solution.py:202
  (30 shorter events, 0.5 us)
Async XLA Ops:
  7.2 77.7 %all-gather.2.cloned.1.call-start = ((), (), s32[]{:S(2)}) async-start(), calls=%async_computation.2 | async-start | bytes 8912896 | tf_op jit(solution)/shard_map/all_gather | solution.py:243
  14.6 32.7 %all-to-all-start = ((f32[128,1,16]{2,1,0:T(1,128)}), f32[128,1,16]{2,1,0:T(1,128)S(1)}, u32[]{:S(2)}, u32[]{:S(2)}) async-start(f32[128,1,16]{2,1,0:T(1,128)} %bitcast), calls=%async_computation | async-start | bytes 131072 | tf_op jit(solution)/shard_map/all_to_all | solution.py:248
  27.5 4.8 %copy-start.5 = (s32[16,16]{1,0:T(8,128)S(1)}, s32[16,16]{1,0:T(8,128)}, u32[]{:S(2)}) copy-start(s32[16,16]{1,0:T(8,128)} %mask_ref.2) | copy-start | bytes 3076
  30.9 1.4 copy-start.3
  98.1 27.4 %collective-permute-start = (f32[4,16,64,128]{3,2,1,0:T(8,128)S(1)}, f32[4,16,64,128]{3,2,1,0:T(8,128)S(1)}, u32[]{:S(2)}, u32[]{:S(2)}) collective-permute-start(f32[4,16,64,128]{3,2,1,0:T(8,128)S(1)} %shard_map.98), channel_id=1, source_target_pairs={{0,16},{16,0},{1,17},{17,1},{2,18},{18,2},{3,19},{19,3},{4,20},{20... | collective-permute-start | bytes 6291464 | tf_op jit(solution)/shard_map/ppermute | solution.py:260
  112.2 29.6 %collective-permute-start.5 = (f32[4,16,64,128]{3,2,1,0:T(8,128)S(1)}, f32[4,16,64,128]{3,2,1,0:T(8,128)S(1)}, u32[]{:S(2)}, u32[]{:S(2)}) collective-permute-start(f32[4,16,64,128]{3,2,1,0:T(8,128)S(1)} %shard_map.102), channel_id=1, source_target_pairs={{0,16},{16,0},{1,17},{17,1},{2,18},{18,2},{3,19},{19,3},{4,20},{20... | collective-permute-start | bytes 6291464 | tf_op jit(solution)/shard_map/ppermute | solution.py:260
  125.6 19.0 %copy-start.1 = (f32[4,16,64,128]{3,2,1,0:T(8,128)}, f32[4,16,64,128]{3,2,1,0:T(8,128)S(1)}, u32[]{:S(2)}) copy-start(f32[4,16,64,128]{3,2,1,0:T(8,128)S(1)} %collective-permute-done.got_ref.refs_1_) | copy-start | bytes 6291460
  125.7 18.9 %collective-permute-start.1 = (f32[8,64,128]{2,1,0:T(8,128)S(1)}, f32[8,64,128]{2,1,0:T(8,128)S(1)}, u32[]{:S(2)}, u32[]{:S(2)}) collective-permute-start(f32[8,64,128]{2,1,0:T(8,128)S(1)} %get-tuple-element.31), channel_id=1, source_target_pairs={{0,32},{32,64},{64,96},{96,0},{1,33},{33,65},{65,97},{97,1},{2,34}... | collective-permute-start | bytes 786440 | tf_op jit(solution)/shard_map/ppermute | solution.py:263
  127.0 17.6 %collective-permute-start.2 = (f32[8,64,128]{2,1,0:T(8,128)S(1)}, f32[8,64,128]{2,1,0:T(8,128)S(1)}, u32[]{:S(2)}, u32[]{:S(2)}) collective-permute-start(f32[8,64,128]{2,1,0:T(8,128)S(1)} %get-tuple-element.32), channel_id=1, source_target_pairs={{0,96},{32,0},{64,32},{96,64},{1,97},{33,1},{65,33},{97,65},{2,98}... | collective-permute-start | bytes 786440 | tf_op jit(solution)/shard_map/ppermute | solution.py:264
  141.8 8.2 %copy-start = (f32[4,16,64,128]{3,2,1,0:T(8,128)}, f32[4,16,64,128]{3,2,1,0:T(8,128)S(1)}, u32[]{:S(2)}) copy-start(f32[4,16,64,128]{3,2,1,0:T(8,128)S(1)} %shard_map.101.mine_ref.refs_4_) | copy-start | bytes 6291460
  141.8 8.2 %copy-start.2 = (f32[4,16,64,128]{3,2,1,0:T(8,128)}, f32[4,16,64,128]{3,2,1,0:T(8,128)S(1)}, u32[]{:S(2)}) copy-start(f32[4,16,64,128]{3,2,1,0:T(8,128)S(1)} %collective-permute-done.5.got_ref.refs_5_) | copy-start | bytes 6291460
  141.9 8.1 %collective-permute-start.6 = (f32[8,64,128]{2,1,0:T(8,128)S(1)}, f32[8,64,128]{2,1,0:T(8,128)S(1)}, u32[]{:S(2)}, u32[]{:S(2)}) collective-permute-start(f32[8,64,128]{2,1,0:T(8,128)S(1)} %get-tuple-element.35), channel_id=1, source_target_pairs={{0,32},{32,64},{64,96},{96,0},{1,33},{33,65},{65,97},{97,1},{2,34}... | collective-permute-start | bytes 786440 | tf_op jit(solution)/shard_map/ppermute | solution.py:263
  141.9 8.1 %collective-permute-start.7 = (f32[8,64,128]{2,1,0:T(8,128)S(1)}, f32[8,64,128]{2,1,0:T(8,128)S(1)}, u32[]{:S(2)}, u32[]{:S(2)}) collective-permute-start(f32[8,64,128]{2,1,0:T(8,128)S(1)} %get-tuple-element.36), channel_id=1, source_target_pairs={{0,96},{32,0},{64,32},{96,64},{1,97},{33,1},{65,33},{97,65},{2,98}... | collective-permute-start | bytes 786440 | tf_op jit(solution)/shard_map/ppermute | solution.py:264
  144.8 16.5 %collective-permute-start.3 = (f32[16,64,128]{2,1,0:T(8,128)S(1)}, f32[16,64,128]{2,1,0:T(8,128)S(1)}, u32[]{:S(2)}, u32[]{:S(2)}) collective-permute-start(f32[16,64,128]{2,1,0:T(8,128)S(1)} %get-tuple-element.33), channel_id=1, source_target_pairs={{0,32},{32,64},{64,96},{96,0},{1,33},{33,65},{65,97},{97,1},{2,34}... | collective-permute-start | bytes 1572872 | tf_op jit(solution)/shard_map/ppermute | solution.py:266
  144.9 16.4 %collective-permute-start.4 = (f32[16,64,128]{2,1,0:T(8,128)S(1)}, f32[16,64,128]{2,1,0:T(8,128)S(1)}, u32[]{:S(2)}, u32[]{:S(2)}) collective-permute-start(f32[16,64,128]{2,1,0:T(8,128)S(1)} %get-tuple-element.34), channel_id=1, source_target_pairs={{0,96},{32,0},{64,32},{96,64},{1,97},{33,1},{65,33},{97,65},{2,98}... | collective-permute-start | bytes 1572872 | tf_op jit(solution)/shard_map/ppermute | solution.py:267
  150.2 22.3 %collective-permute-start.8 = (f32[16,64,128]{2,1,0:T(8,128)S(1)}, f32[16,64,128]{2,1,0:T(8,128)S(1)}, u32[]{:S(2)}, u32[]{:S(2)}) collective-permute-start(f32[16,64,128]{2,1,0:T(8,128)S(1)} %get-tuple-element.37), channel_id=1, source_target_pairs={{0,32},{32,64},{64,96},{96,0},{1,33},{33,65},{65,97},{97,1},{2,34}... | collective-permute-start | bytes 1572872 | tf_op jit(solution)/shard_map/ppermute | solution.py:266
  150.2 22.2 %collective-permute-start.9 = (f32[16,64,128]{2,1,0:T(8,128)S(1)}, f32[16,64,128]{2,1,0:T(8,128)S(1)}, u32[]{:S(2)}, u32[]{:S(2)}) collective-permute-start(f32[16,64,128]{2,1,0:T(8,128)S(1)} %get-tuple-element.38), channel_id=1, source_target_pairs={{0,96},{32,0},{64,32},{96,64},{1,97},{33,1},{65,33},{97,65},{2,98}... | collective-permute-start | bytes 1572872 | tf_op jit(solution)/shard_map/ppermute | solution.py:267
  176.3 27.6 %copy-start.4 = (f32[128,2048]{1,0:T(8,128)S(1)}, f32[128,2048]{1,0:T(8,128)}, u32[]{:S(2)}) copy-start(f32[128,2048]{1,0:T(8,128)} %den_ref.1) | copy-start | bytes 3145732
Sparse Core Ops, SparseCore 0:
  10.1 74.6 all-gather.1

commit v2 on v1

--- a/solution.py
+++ b/solution.py
@@ -14,7 +14,9 @@
 TPD = 16
 CAP = 16
 NZ = 4
-SPLITS = (32, 32)
+PARTS = 2
+SUB = 32
+COLOURS = 4
 NB = 256
 MIB = 1 << 20
 
@@ -37,75 +39,109 @@
     )
 
 
-def prep_kernel(mask_ref, x_ref, hi_ref, lo_ref, *, tile_rows, tile_cols, step_axis):
-    step = pl.program_id(0)
-    for i in range(tile_rows):
-        for j in range(tile_cols):
-            mi = i + (step * tile_rows if step_axis == 0 else 0)
-            mj = j + (step * tile_cols if step_axis == 1 else 0)
-            m = mask_ref[mi, mj].astype(f32)
-            sl = (slice(i * TILE, (i + 1) * TILE), slice(j * TILE, (j + 1) * TILE))
-            hi, lo = split(x_ref[sl] * m)
-            hi_ref[sl] = hi
-            lo_ref[sl] = lo
-
-
-def prep(x, mask, block, step_axis):
-    rows, cols = x.shape
-    grid = (rows // block[0],) if step_axis == 0 else (cols // block[1],)
-    imap = (lambda n: (n, 0)) if step_axis == 0 else (lambda n: (0, n))
-    spec = pl.BlockSpec(block, imap)
-    out = jax.ShapeDtypeStruct((rows, cols), bf16)
-    return call(
-        functools.partial(prep_kernel, tile_rows=block[0] // TILE, tile_cols=block[1] // TILE, step_axis=step_axis),
+def masked_split(mask_ref, x_ref, mi, mj, i, j):
+    m = mask_ref[mi, mj].astype(f32)
+    return split(x_ref[i * TILE : (i + 1) * TILE, j * TILE : (j + 1) * TILE] * m)
+
+
+def cycle_kernel(mask_ref, x_ref, hi_ref, lo_ref):
+    for i in range(RB // TILE):
+        for j in range(RB // TILE):
+            hi, lo = masked_split(mask_ref, x_ref, pl.program_id(0) * (RB // TILE) + i, j, i, j)
+            at = (slice(i * TILE, (i + 1) * TILE), slice(j * TILE, (j + 1) * TILE))
+            hi_ref[at] = hi
+            lo_ref[at] = lo
+
+
+def prepare_cycle(x, mask):
+    spec = pl.BlockSpec((RB, RB), lambda n: (n, 0))
+    out = jax.ShapeDtypeStruct(x.shape, bf16)
+    return call(
+        cycle_kernel,
         (out, out),
-        grid=grid,
+        grid=(x.shape[0] // RB,),
         in_specs=[pl.BlockSpec(memory_space=pltpu.SMEM), spec],
         out_specs=(spec, spec),
-        nbytes=rows * cols * 8,
-        flops=rows * cols * 4,
+        nbytes=x.size * 8,
+        flops=x.size * 4,
     )(mask, x)
 
 
-def mm_kernel(order_ref, a_ref, bh_ref, bl_ref, o_ref, ah, al, *, sub):
+def integrals_kernel(mask_ref, x_ref, *refs, first):
+    hi_ref, lo_ref = refs[-2:]
+    step = first + pl.program_id(0)
+    for i in range(x_ref.shape[0] // TILE):
+        for j in range(NB // TILE):
+            hi, lo = masked_split(mask_ref, x_ref, i, step * (NB // TILE) + j, i, j)
+            at = (0, slice(i * TILE, (i + 1) * TILE), slice(j * TILE, (j + 1) * TILE))
+            hi_ref[at] = hi
+            lo_ref[at] = lo
+
+
+def prepare_integrals(x, mask, first, count, into=None):
+    depth, cols = x.shape
+    out = jax.ShapeDtypeStruct((cols // NB, depth, NB), bf16)
+    spec = pl.BlockSpec((1, depth, NB), lambda n: (n + first, 0, 0))
+    kw = {}
+    specs = [pl.BlockSpec(memory_space=pltpu.SMEM), pl.BlockSpec((depth, NB), lambda n: (0, n + first))]
+    extra = ()
+    if into is not None:
+        extra = into
+        specs += [pl.BlockSpec(memory_space=pl.ANY)] * 2
+        kw["input_output_aliases"] = {2: 0, 3: 1}
+    return call(
+        functools.partial(integrals_kernel, first=first),
+        (out, out),
+        grid=(count,),
+        in_specs=specs,
+        out_specs=(spec, spec),
+        nbytes=depth * NB * 8 * count,
+        flops=depth * NB * 4 * count,
+        **kw,
+    )(mask, x, *extra)
+
+
+def mm_kernel(where_ref, *refs):
+    held, bh_ref, bl_ref, o_ref, ah, al = refs[:-5], *refs[-5:]
+    near, late = held[:COLOURS], held[COLOURS:]
+
     @pl.when(pl.program_id(0) == 0)
     def _():
-        for i in range(NZ):
-            r = order_ref[i]
-            for j in range(2):
-                hi, lo = split(a_ref[2 * r + j])
-                at = slice((2 * i + j) * sub, (2 * i + j + 1) * sub)
-                ah[at, :] = hi
-                al[at, :] = lo
+        for s in range(2 * NZ):
+            rows = []
+            for c in range(COLOURS):
+                w = where_ref[c, s]
+                mine = near[c][jnp.minimum(w, 7)]
+                rows.append(jnp.where(w < 8, mine, late[c][jnp.maximum(w - 8, 0)]))
+            hi, lo = split(jnp.concatenate(rows, axis=0))
+            at = slice(s * SUB, (s + 1) * SUB)
+            ah[at, :] = hi
+            al[at, :] = lo
 
     dot = functools.partial(jnp.dot, preferred_element_type=f32)
-    acc = dot(ah[...], bh_ref[...]) + dot(ah[...], bl_ref[...]) + dot(al[...], bh_ref[...])
+    acc = dot(ah[...], bh_ref[0]) + dot(ah[...], bl_ref[0]) + dot(al[...], bh_ref[0])
     for i in range(NZ):
         for t in range(NB // TILE):
-            o_ref[i, t] = acc[2 * sub * i : 2 * sub * (i + 1), t * TILE : (t + 1) * TILE]
-
-
-def multiply(a, bh, bl, order, part):
-    sub = SPLITS[part]
-    assert sum(SPLITS[:part]) % sub == 0
-    at = sum(SPLITS[:part]) // sub
-    depth, cols = bh.shape
-    m = NZ * 2 * sub
-    return call(
-        functools.partial(mm_kernel, sub=sub),
-        jax.ShapeDtypeStruct((NZ, cols // TILE, 2 * sub, TILE), f32),
-        grid=(cols // NB,),
-        in_specs=[
-            pl.BlockSpec(memory_space=pltpu.SMEM),
-            pl.BlockSpec((16, sub, depth), lambda n: (0, at, 0)),
-            pl.BlockSpec((depth, NB), lambda n: (0, n)),
-            pl.BlockSpec((depth, NB), lambda n: (0, n)),
-        ],
-        out_specs=pl.BlockSpec((NZ, NB // TILE, 2 * sub, TILE), lambda n: (0, n, 0, 0)),
+            o_ref[i, t] = acc[2 * SUB * i : 2 * SUB * (i + 1), t * TILE : (t + 1) * TILE]
+
+
+def multiply(held, bh, bl, where):
+    blocks, depth, _ = bh.shape
+    m = NZ * 2 * SUB
+    chunk = pl.BlockSpec((1, depth, NB), lambda n: (n, 0, 0))
+    return call(
+        mm_kernel,
+        jax.ShapeDtypeStruct((NZ, blocks * NB // TILE, 2 * SUB, TILE), f32),
+        grid=(blocks,),
+        in_specs=[pl.BlockSpec(memory_space=pltpu.SMEM)]
+        + [pl.BlockSpec(h.shape, lambda n: (0, 0, 0)) for h in held]
+        + [chunk, chunk],
+        out_specs=pl.BlockSpec((NZ, NB // TILE, 2 * SUB, TILE), lambda n: (0, n, 0, 0)),
         scratch_shapes=[pltpu.VMEM((m, depth), bf16), pltpu.VMEM((m, depth), bf16)],
-        flops=6 * m * depth * cols,
-        nbytes=4 * depth * cols + 4 * m * cols,
-    )(order, a, bh, bl)
+        vmem=32,
+        flops=6 * m * depth * blocks * NB,
+        nbytes=4 * depth * blocks * NB,
+    )(where, *held, bh, bl)
 
 
 def far_kernel(mine_ref, got_ref, p_ref, m_ref):
@@ -142,9 +178,9 @@
 def gather_kernel(idx_ref, *refs):
     ins, (out_ref, scr) = refs[:-2], refs[-2:]
     base = 0
-    for c in range(len(SPLITS)):
+    for c in range(PARTS):
         mine, got, rp, rm = ins[4 * c : 4 * c + 4]
-        rows = 2 * SPLITS[c]
+        rows = 2 * SUB
         for t in range(TPD):
             scr[base + t * rows : base + (t + 1) * rows, :] = mine[0, t] + got[0, t] + rp[t] + rm[t]
         base += TPD * rows
@@ -218,20 +254,36 @@
     place = out_tile % TPD * ROWS + out_row % ROWS
     unit = jnp.arange(ROWS * TPD, dtype=jnp.int32)
     row, tile = unit // TPD, unit % TPD
-    block, sub = row // 64, row % 64
-    at = jnp.zeros_like(unit)
-    first, base = 0, 0
-    for rows in SPLITS:
-        here = base + tile * (2 * rows) + block * rows + (sub - first)
-        at = jnp.where(sub >= first, here, at)
-        first += rows
-        base += TPD * 2 * rows
+    block, colour, part, sub = row // 64, row // 16 % COLOURS, row // 8 % PARTS, row % 8
+    at = part * (TPD * 2 * SUB) + tile * (2 * SUB) + block * SUB + colour * 8 + sub
     key = lax.sort((owner << 22) | (at << 11) | place)
     return (key >> 11) & 2047, key & 2047
 
 
 def ring(step):
     return [(i, (i + step) % NZ) for i in range(NZ)]
+
+
+EVEN = [(i, i ^ 1) for i in range(4)]
+ODD = [(i, i ^ 3) for i in range(4)]
+EXCHANGES = {"xe": ("x", EVEN), "xo": ("x", ODD), "ye": ("y", EVEN), "yo": ("y", ODD)}
+ORDERS = [["xe", "xo", "ye", "yo"], ["xo", "ye", "yo", "xe"], ["ye", "yo", "xe", "xo"], ["yo", "xe", "xo", "ye"]]
+
+
+def exchange(value, name):
+    axis, pairs = EXCHANGES[name]
+    return lax.ppermute(value, axis, pairs)
+
+
+def places(ys, xs):
+    dx = lax.axis_index("x") ^ xs
+    dy = lax.axis_index("y") ^ ys
+    bits = {"xe": (dx & 1) ^ (dx >> 1), "xo": dx >> 1, "ye": (dy & 1) ^ (dy >> 1), "yo": dy >> 1}
+    return jnp.stack([sum(bits[name] << k for k, name in enumerate(order)) for order in ORDERS])
+
+
+def after(value, *others):
+    return lax.optimization_barrier((value,) + others)[0]
 
 
 def body(amplitudes, integrals, integral_mask, denominators, cycle_tiles, cycle_mask, destination):
@@ -240,34 +292,51 @@
     core = lax.axis_index("core")
     depth = integrals.shape[0]
 
-    gathered = lax.all_gather(amplitudes, ("y", "x"), axis=0, tiled=True).reshape(16, 64, depth)
-
-    bh, bl = prep(integrals, integral_mask, (depth, NB), 1)
-    source, place = plan(destination)
+    towards = jnp.repeat(jnp.array([2, 1, 3, 0], jnp.int32), 2)
+    shard = jnp.array([0, 1] * NZ, jnp.int32)
+    ys = (z + towards) % NZ
+    own = places(ys, 2 * core + shard)
+    other = places(ys, 2 * (1 - core) + shard)
+
+    rows = amplitudes.reshape(COLOURS, PARTS, 1, 8, depth)
+    bufs = [rows[c] for c in range(COLOURS)]
+    got = [exchange(bufs[c], ORDERS[c][0]) for c in range(COLOURS)]
+    bufs = [jnp.concatenate([b, g], axis=1) for b, g in zip(bufs, got)]
+    got = [exchange(bufs[c], ORDERS[c][1]) for c in range(COLOURS)]
+    halves = [[jnp.concatenate([b[p], g[p]], axis=0) for b, g in zip(bufs, got)] for p in range(PARTS)]
+
+    half = integrals.shape[1] // NB // 2
+    b_first = prepare_integrals(integrals, integral_mask, 0, half)
+    bh, bl = prepare_integrals(integrals, integral_mask, half, half, b_first)
+
+    parts = []
+    last = None
+    for p in range(PARTS):
+        bufs = halves[p]
+        if last is not None:
+            bufs = list(lax.optimization_barrier(tuple(bufs) + tuple(last)))[:COLOURS]
+        got = [exchange(bufs[c], ORDERS[c][2]) for c in range(COLOURS)]
+        last = got
+        bufs = [jnp.concatenate([b, g], axis=0) for b, g in zip(bufs, got)]
+        late = [exchange(bufs[c], ORDERS[c][3]) for c in range(COLOURS)]
+        theirs = multiply(bufs + late, bh, bl, other)
+        from_core = lax.ppermute(theirs, "core", [(0, 1), (1, 0)])
+        mine = multiply(bufs + late, bh, bl, own)
+        far_p, far_m = far(mine, from_core)
+        gp = lax.ppermute(far_p, "z", ring(1))
+        gm = lax.ppermute(far_m, "z", ring(-1))
+        near_p, near_m = near(mine, from_core, gp, gm)
+        rp = lax.ppermute(near_p, "z", ring(1))
+        rm = lax.ppermute(near_m, "z", ring(-1))
+        parts.append((mine, from_core, rp, rm))
+
+    source, place = plan(after(destination, theirs))
     place = place.astype(f32).reshape(128, 1, CAP)
     got_place = lax.all_to_all(place, everyone, split_axis=0, concat_axis=0, tiled=True)
     got_place = got_place.reshape(-1).astype(jnp.int32)
-    ch, cl = prep(cycle_tiles, cycle_mask, (512, RB), 0)
-    bh, bl, ch, cl, source, got_place = lax.optimization_barrier((bh, bl, ch, cl, source, got_place))
-
-    towards = jnp.array([2, 1, 3, 0], jnp.int32)
-    order = 2 * ((z + towards) % NZ)
-    own_order, other_order = order + core, order + (1 - core)
-
-    parts = []
-    for c in range(len(SPLITS)):
-        theirs = multiply(gathered, bh, bl, other_order, c)
-        got = lax.ppermute(theirs, "core", [(0, 1), (1, 0)])
-        mine = multiply(gathered, bh, bl, own_order, c)
-        far_p, far_m = far(mine, got)
-        gp = lax.ppermute(far_p, "z", ring(1))
-        gm = lax.ppermute(far_m, "z", ring(-1))
-        near_p, near_m = near(mine, got, gp, gm)
-        rp = lax.ppermute(near_p, "z", ring(1))
-        rm = lax.ppermute(near_m, "z", ring(-1))
-        parts.append((mine, got, rp, rm))
-
-    sending = gather(source, parts).reshape(128, CAP, TILE)
+    ch, cl = prepare_cycle(after(cycle_tiles, theirs), cycle_mask)
+
+    sending = gather(after(source, got_place, ch, cl), parts).reshape(128, CAP, TILE)
     units = lax.all_to_all(sending, everyone, split_axis=0, concat_axis=0, tiled=True)
     return finish(got_place, units.reshape(-1, TILE), denominators, ch, cl)
 

time: 218 us -> 205 us (0.940)
  waiting for transfers between devices: 60 us -> 21.9 us
  starting transfers between devices: 23.4 us -> 57.9 us
  between operations: 14.2 us -> 1.3 us
  local copies, waits for them, and re-layouts: 3.84 us -> 13 us
  Pallas kernels: 81.6 us -> 76.9 us
  blocking collectives: 27.6 us -> 25.1 us
    ppermute x2 -> x26, starting transfers between devices: 0.87 us -> 38.4 us  [the longest x24 25.2 us: exchange(): return lax.ppermute(value, axis, pairs)]
    all_gather x1 -> x0, waiting for transfers between devices: 37.3 us -> none  [body(): lax.all_gather(amplitudes, ('y', 'x'), axis=0, tiled=True)]
    ppermute x2, waiting for transfers between devices: 19.6 us -> 0.01 us  [body(): rp = lax.ppermute(near_p, 'z', ring(1))]
    ppermute x2 -> x26, waiting for transfers between devices: 0.01 us -> 18.3 us  [the longest x24 18.3 us: exchange(): return lax.ppermute(value, axis, pairs)]
    pallas_call x6 -> x7, Pallas kernels: 71.4 us -> 62 us  [the longest x4 43.3 us: multiply(): call(mm_kernel, jax.ShapeDtypeStruct((NZ, blocks * NB // TILE, 2 * SUB, T...]
    unnamed x14 -> x57, local copies, waits for them, and re-layouts: 2.96 us -> 10.6 us
    all_to_all x1, starting transfers between devices: 11.5 us -> 7.74 us  [body(): lax.all_to_all(place, everyone, split_axis=0, concat_axis=0, tiled=True)]
    all_to_all x1, waiting for transfers between devices: 0.01 us -> 3.27 us  [body(): lax.all_to_all(place, everyone, split_axis=0, concat_axis=0, tiled=True)]
  transfers between devices with their start and end apart: 12 -> 35, of which waited for: 4 -> 11; matrix products, arithmetic and copies ran while one was open for 4% -> 4% of each run, Pallas kernels for 27% -> 33%
where the time goes in v2:
time: 205 us; the launch traced here: 204 us
  Pallas kernels  76.9 us (38%)
  starting transfers between devices  57.9 us (28%)
  blocking collectives  25.1 us (12%)
  waiting for transfers between devices  21.9 us (11%)
  local copies, waits for them, and re-layouts  13 us (6%)
  other arithmetic  7.76 us (4%)
    pallas_call x4, Pallas kernels, multiply(): call(mm_kernel, jax.ShapeDtypeStruct((NZ, blocks * NB // TILE, 2 * SUB, T...  43.3 us
    ppermute x24, starting transfers between devices, exchange(): return lax.ppermute(value, axis, pairs)  25.2 us
    all_to_all x1, blocking collectives, body(): lax.all_to_all(sending, everyone, split_axis=0, concat_axis=0, tiled=True)  25.1 us
    ppermute x24, waiting for transfers between devices, exchange(): return lax.ppermute(value, axis, pairs)  18.3 us
    pallas_call x2, Pallas kernels, prepare_integrals(): call(functools.partial(integrals_kernel, first=first), (out, out), grid=(...  15.3 us
    ppermute x2, starting transfers between devices, body(): from_core = lax.ppermute(theirs, 'core', [(0, 1), (1, 0)])  13.2 us
    unnamed x57, local copies, waits for them, and re-layouts  10.6 us
    all_to_all x1, starting transfers between devices, body(): lax.all_to_all(place, everyone, split_axis=0, concat_axis=0, tiled=True)  7.74 us
  transfers between devices with their start and end apart: 35, of which 11 were waited for; matrix products, arithmetic and copies ran while one was open for 4% of the time, Pallas kernels for 33%

profile of v2, /device:TPU:1, one launch (start us, length us, event | category | flops | bytes accessed | tf_op | source)
XLA Modules:
  0.0 203.9 jit_solution(9778906614398089368)
XLA Ops:
  1.8 2.2 %collective-permute-start.4 = (f32[2,1,8,2048]{3,2,1,0:T(8,128)S(1)}, f32[2,1,8,2048]{3,2,1,0:T(8,128)S(1)}, u32[]{:S(2)}, u32[]{:S(2)}) collective-permute-start(f32[2,1,8,2048]{3,2,1,0:T(8,128)S(1)} %get-tuple-element.52), channel_id=1, source_target_pairs={{0,4},{4,0},{8,12},{12,8},{1,5},{5,1},{9,13},{13,9},{2,6},{6,2},{1... | collective-permute-start | bytes 393224 | tf_op jit(solution)/shard_map/ppermute | solution.py:275
  4.0 1.9 collective-permute-start.6
  5.9 2.5 %collective-permute-start.2 = (f32[2,1,8,2048]{3,2,1,0:T(8,128)S(1)}, f32[2,1,8,2048]{3,2,1,0:T(8,128)S(1)}, u32[]{:S(2)}, u32[]{:S(2)}) collective-permute-start(f32[2,1,8,2048]{3,2,1,0:T(8,128)S(1)} %get-tuple-element.50), channel_id=1, source_target_pairs={{0,3},{1,2},{2,1},{3,0},{4,7},{5,6},{6,5},{7,4},{8,11},{9,10},{10,... | collective-permute-start | bytes 393224 | tf_op jit(solution)/shard_map/ppermute | solution.py:275
  11.2 7.6 %shard_map.104 = (bf16[8,2048,256]{2,1,0:T(8,128)(2,1)}, bf16[8,2048,256]{2,1,0:T(8,128)(2,1)}) custom-call(s32[16,16]{1,0:T(8,128)S(1)} %copy-done.13, f32[2048,2048]{1,0:T(8,128)} %x_ref.3), custom_call_target="tpu_custom_call" | custom-call | flops 8388608 | bytes 16777216 | tf_op jit(solution)/shard_map/pallas_call | solution.py:92
  18.8 7.6 %shard_map.105 = (bf16[8,2048,256]{2,1,0:T(8,128)(2,1)}, bf16[8,2048,256]{2,1,0:T(8,128)(2,1)}) custom-call(s32[16,16]{1,0:T(8,128)S(1)} %copy-done.13, f32[2048,2048]{1,0:T(8,128)} %x_ref.3, bf16[8,2048,256]{2,1,0:T(8,128)(2,1)} %get-tuple-element.29.refs_0_, ...), custom_call_target="tpu_custom_call", output_to_operand_aliasing={{0}: (2, {}), {1}: (3, {})} | custom-call | flops 8388608 | bytes 16777216 | tf_op jit(solution)/shard_map/pallas_call | solution.py:92
  29.5 4.4 %collective-permute-done.5 = f32[2,2,8,2048]{3,2,1,0:T(8,128)S(1)} collective-permute-done((f32[2,2,8,2048]{3,2,1,0:T(8,128)S(1)}, f32[2,2,8,2048]{3,2,1,0:T(8,128)S(1)}, u32[]{:S(2)}, u32[]{:S(2)}) %collective-permute-start.5) | collective-permute-done | bytes 262176 | tf_op jit(solution)/shard_map/ppermute | solution.py:275
  37.3 1.9 collective-permute-done.10
  39.2 2.7 %collective-permute-done.11 = f32[4,8,2048]{2,1,0:T(8,128)S(1)} collective-permute-done((f32[4,8,2048]{2,1,0:T(8,128)S(1)}, f32[4,8,2048]{2,1,0:T(8,128)S(1)}, u32[]{:S(2)}, u32[]{:S(2)}) %collective-permute-start.11) | collective-permute-done | bytes 262176 | tf_op jit(solution)/shard_map/ppermute | solution.py:275
  42.3 2.9 %collective-permute-start.15 = (f32[4,8,2048]{2,1,0:T(8,128)S(1)}, f32[4,8,2048]{2,1,0:T(8,128)S(1)}, u32[]{:S(2)}, u32[]{:S(2)}) collective-permute-start(f32[4,8,2048]{2,1,0:T(8,128)S(1)} %pad_maximum_fusion.11), channel_id=1, source_target_pairs={{0,3},{1,2},{2,1},{3,0},{4,7},{5,6},{6,5},{7,4},{8,11},{9,10},{10,... | collective-permute-start | bytes 786440 | tf_op jit(solution)/shard_map/ppermute | solution.py:275
  45.3 1.7 collective-permute-start.13
  49.0 2.7 %collective-permute-start.22 = (f32[8,8,2048]{2,1,0:T(8,128)S(1)}, f32[8,8,2048]{2,1,0:T(8,128)S(1)}, u32[]{:S(2)}, u32[]{:S(2)}) collective-permute-start(f32[8,8,2048]{2,1,0:T(8,128)S(1)} %pad_maximum_fusion.2.refs_2_), channel_id=1, source_target_pairs={{0,3},{1,2},{2,1},{3,0},{4,7},{5,6},{6,5},{7,4},{8,11},{9,10},{10,... | collective-permute-start | bytes 1572872 | tf_op jit(solution)/shard_map/ppermute | solution.py:275
  54.4 5.6 %collective-permute-done.21.refs_5_ = f32[8,8,2048]{2,1,0:T(8,128)S(1)} collective-permute-done((f32[8,8,2048]{2,1,0:T(8,128)S(1)}, f32[8,8,2048]{2,1,0:T(8,128)S(1)}, u32[]{:S(2)}, u32[]{:S(2)}) %collective-permute-start.21) | collective-permute-done | bytes 524320 | tf_op jit(solution)/shard_map/ppermute | solution.py:275
  61.0 2.6 %collective-permute-done.23.refs_7_ = f32[8,8,2048]{2,1,0:T(8,128)S(1)} collective-permute-done((f32[8,8,2048]{2,1,0:T(8,128)S(1)}, f32[8,8,2048]{2,1,0:T(8,128)S(1)}, u32[]{:S(2)}, u32[]{:S(2)}) %collective-permute-start.23) | collective-permute-done | bytes 524320 | tf_op jit(solution)/shard_map/ppermute | solution.py:275
  64.4 10.9 %shard_map.109 = f32[4,16,64,128]{3,2,1,0:T(8,128)S(1)} custom-call(s32[4,8]{1,0:T(4,128)S(1)} %pad_add_fusion.where_ref, f32[8,8,2048]{2,1,0:T(8,128)S(1)} %pad_maximum_fusion.refs_0_, f32[8,8,2048]{2,1,0:T(8,128)S(1)} %pad_maximum_fusion.1.refs_1_, f32[8,8,2048]{2,1,0:T(8,128)S(1)} %pad_maximum_fusion.2.refs_2_, ...), custom_call_target="tpu_custom_call" | custom-call | flops 6442450944 | bytes 16777216 | tf_op jit(solution)/shard_map/pallas_call | solution.py:132
  75.3 12.8 %collective-permute-start.24 = (f32[4,16,64,128]{3,2,1,0:T(8,128)S(1)}, f32[4,16,64,128]{3,2,1,0:T(8,128)S(1)}, u32[]{:S(2)}, u32[]{:S(2)}) collective-permute-start(f32[4,16,64,128]{3,2,1,0:T(8,128)S(1)} %shard_map.109), channel_id=1, source_target_pairs={{0,16},{16,0},{1,17},{17,1},{2,18},{18,2},{3,19},{19,3},{4,20},{20... | collective-permute-start | bytes 6291464 | tf_op jit(solution)/shard_map/ppermute | solution.py:323
  88.1 11.3 %shard_map.106 = f32[4,16,64,128]{3,2,1,0:T(8,128)S(1)} custom-call(s32[4,8]{1,0:T(4,128)S(1)} %pad_add_fusion.where_ref, f32[8,8,2048]{2,1,0:T(8,128)S(1)} %constant_dynamic-update-slice_fusion.refs_0_, f32[8,8,2048]{2,1,0:T(8,128)S(1)} %constant_dynamic-update-slice_fusion.2.refs_1_, f32[8,8,2048]{2,1,0:T(8,128)S(1)} %constant_dynamic-update-slice_fusion.4.refs_2_, ...), custom_call_target="tpu_custom_call" | custom-call | flops 6442450944 | bytes 16777216 | tf_op jit(solution)/shard_map/pallas_call | solution.py:132
  99.9 10.6 %shard_map.108.mine_ref.refs_0_ = f32[4,16,64,128]{3,2,1,0:T(8,128)S(1)} custom-call(s32[4,8]{1,0:T(4,128)S(1)} %pad_add_fusion.1.where_ref, f32[8,8,2048]{2,1,0:T(8,128)S(1)} %pad_maximum_fusion.refs_0_, f32[8,8,2048]{2,1,0:T(8,128)S(1)} %pad_maximum_fusion.1.refs_1_, f32[8,8,2048]{2,1,0:T(8,128)S(1)} %pad_maximum_fusion.2.refs_2_, ...), custom_call_target="tpu_custom_call" | custom-call | flops 6442450944 | bytes 16777216 | tf_op jit(solution)/shard_map/pallas_call | solution.py:132
  113.6 2.1 %collective-permute-start.26 = (f32[8,64,128]{2,1,0:T(8,128)}, f32[8,64,128]{2,1,0:T(8,128)S(1)}, u32[]{:S(2)}, u32[]{:S(2)}) collective-permute-start(f32[8,64,128]{2,1,0:T(8,128)} %get-tuple-element.40), channel_id=1, source_target_pairs={{0,96},{32,0},{64,32},{96,64},{1,97},{33,1},{65,33},{97,65},{2,98}... | collective-permute-start | bytes 786440 | tf_op jit(solution)/shard_map/ppermute | solution.py:327
  115.7 3.4 %copy-done.8 = bf16[8,2048,256]{2,1,0:T(8,128)(2,1)S(1)} copy-done((bf16[8,2048,256]{2,1,0:T(8,128)(2,1)S(1)}, bf16[8,2048,256]{2,1,0:T(8,128)(2,1)}, u32[]{:S(2)}) %copy-start.8) | copy-done | bytes 8388632
  119.1 10.6 %shard_map.112.mine_ref.refs_4_ = f32[4,16,64,128]{3,2,1,0:T(8,128)S(1)} custom-call(s32[4,8]{1,0:T(4,128)S(1)} %pad_add_fusion.1.where_ref, f32[8,8,2048]{2,1,0:T(8,128)S(1)} %constant_dynamic-update-slice_fusion.refs_0_, f32[8,8,2048]{2,1,0:T(8,128)S(1)} %constant_dynamic-update-slice_fusion.2.refs_1_, ...), custom_call_target="tpu_custom_call" | custom-call | flops 6442450944 | bytes 16777216 | tf_op jit(solution)/shard_map/pallas_call | solution.py:132
  131.9 2.7 %collective-permute-start.31 = (f32[8,64,128]{2,1,0:T(8,128)}, f32[8,64,128]{2,1,0:T(8,128)}, u32[]{:S(2)}, u32[]{:S(2)}) collective-permute-start(f32[8,64,128]{2,1,0:T(8,128)} %get-tuple-element.44), channel_id=1, source_target_pairs={{0,96},{32,0},{64,32},{96,64},{1,97},{33,1},{65,33},{97,65},{2,98}... | collective-permute-start | bytes 786440 | tf_op jit(solution)/shard_map/ppermute | solution.py:327
  134.8 1.7 copy-done.4
  137.6 2.7 %collective-permute-start.28 = (f32[16,64,128]{2,1,0:T(8,128)}, f32[16,64,128]{2,1,0:T(8,128)S(1)}, u32[]{:S(2)}, u32[]{:S(2)}) collective-permute-start(f32[16,64,128]{2,1,0:T(8,128)} %get-tuple-element.42), channel_id=1, source_target_pairs={{0,96},{32,0},{64,32},{96,64},{1,97},{33,1},{65,33},{97,65},{2,98}... | collective-permute-start | bytes 1572872 | tf_op jit(solution)/shard_map/ppermute | solution.py:330
  140.6 2.1 %shard_map.114 = (f32[16,64,128]{2,1,0:T(8,128)}, f32[16,64,128]{2,1,0:T(8,128)}) custom-call(f32[4,16,64,128]{3,2,1,0:T(8,128)S(1)} %copy-done.7, f32[4,16,64,128]{3,2,1,0:T(8,128)S(1)} %copy-done.2, f32[8,64,128]{2,1,0:T(8,128)S(1)} %collective-permute-done.30.gp_ref, f32[8,64,128]{2,1,0:T(8,128)} %collective-permute-done.31.gm_ref), custom_call_target="tpu_custom_call" | custom-call | bytes 3670016 | tf_op jit(solution)/shard_map/pallas_call | solution.py:175
  142.6 2.7 %collective-permute-start.33 = (f32[16,64,128]{2,1,0:T(8,128)}, f32[16,64,128]{2,1,0:T(8,128)}, u32[]{:S(2)}, u32[]{:S(2)}) collective-permute-start(f32[16,64,128]{2,1,0:T(8,128)} %get-tuple-element.46), channel_id=1, source_target_pairs={{0,96},{32,0},{64,32},{96,64},{1,97},{33,1},{65,33},{97,65},{2,98}... | collective-permute-start | bytes 1572872 | tf_op jit(solution)/shard_map/ppermute | solution.py:330
  145.3 5.0 %sort.14 = (s32[2048]{0:T(1024)S(1)}, s32[2048]{0:T(1024)}) sort(s32[2048]{0:T(1024)S(1)} %fusion.26, s32[2048]{0:T(1024)S(1)} %iota.7), dimensions={0}, to_apply=%region_0.1 | sort | flops 22528 | bytes 32768 | tf_op jit(solution)/shard_map/sort | solution.py:259
  151.1 7.7 %all-to-all-start = ((f32[128,1,16]{2,1,0:T(1,128)}), f32[128,1,16]{2,1,0:T(1,128)S(1)}, u32[]{:S(2)}, u32[]{:S(2)}) async-start(f32[128,1,16]{2,1,0:T(1,128)} %bitcast.24), calls=%async_computation | async-start | bytes 131072 | tf_op jit(solution)/shard_map/all_to_all | solution.py:335
  158.9 3.5 %shard_map.107 = (bf16[2048,512]{1,0:T(8,128)(2,1)S(1)}, bf16[2048,512]{1,0:T(8,128)(2,1)S(1)}) custom-call(s32[16,4]{1,0:T(8,128)S(1)} %copy.18.mask_ref, f32[2048,512]{1,0:T(8,128)} %x_ref.4), custom_call_target="tpu_custom_call" | custom-call | flops 4194304 | bytes 8388608 | tf_op jit(solution)/shard_map/pallas_call | solution.py:59
  165.2 3.3 %all-to-all-done = f32[128,1,16]{2,1,0:T(1,128)S(1)} async-done(((f32[128,1,16]{2,1,0:T(1,128)}), f32[128,1,16]{2,1,0:T(1,128)S(1)}, u32[]{:S(2)}, u32[]{:S(2)}) %all-to-all-start) | async-done | bytes 8224 | tf_op jit(solution)/shard_map/all_to_all | solution.py:335
  168.8 4.1 %shard_map.115 = f32[2048,128]{1,0:T(8,128)S(1)} custom-call(s32[2048]{0:T(1024)S(1)} %get-tuple-element.38.idx_ref, f32[4,16,64,128]{3,2,1,0:T(8,128)S(1)} %copy-done.5, f32[4,16,64,128]{3,2,1,0:T(8,128)} %copy-done, f32[16,64,128]{2,1,0:T(8,128)S(1)} %collective-permute-done.27.refs_2_, f32[16,64,128]{2,1,0:T(8,128)S(1)} %collective-permute-done.28.refs_3_, ...), custom_call_target="tpu_custom_call" | custom-call | bytes 5242880 | tf_op jit(solution)/shard_map/pallas_call | solution.py:206
  172.9 25.1 %all_to_all.10 = f32[128,16,128]{2,1,0:T(8,128)S(1)} all-to-all(f32[128,16,128]{2,1,0:T(8,128)S(1)} %bitcast.63), channel_id=1, replica_groups=mesh['z'=4,'core'=2,'y'=4,'x'=4] {'z','core','y','x'}, dimensions={0} | all-to-all | bytes 2097152 | tf_op jit(solution)/shard_map/all_to_all | solution.py:340
  198.0 5.9 %shard_map.116 = (f32[128,2048]{1,0:T(8,128)}, f32[128,2048]{1,0:T(8,128)}) custom-call(s32[2048]{0:T(1024)S(1)} %convert_element_type.10.place_ref, f32[2048,128]{1,0:T(8,128)S(1)} %bitcast.64, f32[128,2048]{1,0:T(8,128)S(1)} %copy-done.12, bf16[2048,512]{1,0:T(8,128)(2,1)S(1)} %copy-done.10, bf16[2048,512]{1,0:T(8,128)(2,1)} %copy-done.11), custom_call_target="tpu_custom_call" | custom-call | bytes 8388608 | tf_op jit(solution)/shard_map/pallas_call | solution.py:238
  (156 shorter events, 28.4 us)
Async XLA Ops:
  1.8 24.7 %collective-permute-start.4 = (f32[2,1,8,2048]{3,2,1,0:T(8,128)S(1)}, f32[2,1,8,2048]{3,2,1,0:T(8,128)S(1)}, u32[]{:S(2)}, u32[]{:S(2)}) collective-permute-start(f32[2,1,8,2048]{3,2,1,0:T(8,128)S(1)} %get-tuple-element.52), channel_id=1, source_target_pairs={{0,4},{4,0},{8,12},{12,8},{1,5},{5,1},{9,13},{13,9},{2,6},{6,2},{1... | collective-permute-start | bytes 393224 | tf_op jit(solution)/shard_map/ppermute | solution.py:275
  4.0 23.4 %collective-permute-start.6 = (f32[2,1,8,2048]{3,2,1,0:T(8,128)S(1)}, f32[2,1,8,2048]{3,2,1,0:T(8,128)S(1)}, u32[]{:S(2)}, u32[]{:S(2)}) collective-permute-start(f32[2,1,8,2048]{3,2,1,0:T(8,128)S(1)} %get-tuple-element.49), channel_id=1, source_target_pairs={{0,12},{4,8},{8,4},{12,0},{1,13},{5,9},{9,5},{13,1},{2,14},{6,10},... | collective-permute-start | bytes 393224 | tf_op jit(solution)/shard_map/ppermute | solution.py:275
  5.9 23.1 %collective-permute-start.2 = (f32[2,1,8,2048]{3,2,1,0:T(8,128)S(1)}, f32[2,1,8,2048]{3,2,1,0:T(8,128)S(1)}, u32[]{:S(2)}, u32[]{:S(2)}) collective-permute-start(f32[2,1,8,2048]{3,2,1,0:T(8,128)S(1)} %get-tuple-element.50), channel_id=1, source_target_pairs={{0,3},{1,2},{2,1},{3,0},{4,7},{5,6},{6,5},{7,4},{8,11},{9,10},{10,... | collective-permute-start | bytes 393224 | tf_op jit(solution)/shard_map/ppermute | solution.py:275
  8.4 20.7 %collective-permute-start = (f32[2,1,8,2048]{3,2,1,0:T(8,128)S(1)}, f32[2,1,8,2048]{3,2,1,0:T(8,128)S(1)}, u32[]{:S(2)}, u32[]{:S(2)}) collective-permute-start(f32[2,1,8,2048]{3,2,1,0:T(8,128)S(1)} %get-tuple-element.51), channel_id=1, source_target_pairs={{0,1},{1,0},{2,3},{3,2},{4,5},{5,4},{6,7},{7,6},{8,9},{9,8},{10,11... | collective-permute-start | bytes 393224 | tf_op jit(solution)/shard_map/ppermute | solution.py:275
  26.5 7.4 %collective-permute-start.5 = (f32[2,2,8,2048]{3,2,1,0:T(8,128)S(1)}, f32[2,2,8,2048]{3,2,1,0:T(8,128)S(1)}, u32[]{:S(2)}, u32[]{:S(2)}) collective-permute-start(f32[2,2,8,2048]{3,2,1,0:T(8,128)S(1)} %pad_maximum_fusion.6), channel_id=1, source_target_pairs={{0,12},{4,8},{8,4},{12,0},{1,13},{5,9},{9,5},{13,1},{2,14},{6,10},... | collective-permute-start | bytes 786440 | tf_op jit(solution)/shard_map/ppermute | solution.py:275
  27.4 8.0 %collective-permute-start.7 = (f32[2,2,8,2048]{3,2,1,0:T(8,128)S(1)}, f32[2,2,8,2048]{3,2,1,0:T(8,128)S(1)}, u32[]{:S(2)}, u32[]{:S(2)}) collective-permute-start(f32[2,2,8,2048]{3,2,1,0:T(8,128)S(1)} %pad_maximum_fusion.7), channel_id=1, source_target_pairs={{0,1},{1,0},{2,3},{3,2},{4,5},{5,4},{6,7},{7,6},{8,9},{9,8},{10,11... | collective-permute-start | bytes 786440 | tf_op jit(solution)/shard_map/ppermute | solution.py:275
  29.0 6.8 %collective-permute-start.3 = (f32[2,2,8,2048]{3,2,1,0:T(8,128)S(1)}, f32[2,2,8,2048]{3,2,1,0:T(8,128)S(1)}, u32[]{:S(2)}, u32[]{:S(2)}) collective-permute-start(f32[2,2,8,2048]{3,2,1,0:T(8,128)S(1)} %pad_maximum_fusion.5), channel_id=1, source_target_pairs={{0,4},{4,0},{8,12},{12,8},{1,5},{5,1},{9,13},{13,9},{2,6},{6,2},{1... | collective-permute-start | bytes 786440 | tf_op jit(solution)/shard_map/ppermute | solution.py:275
  29.1 7.5 %collective-permute-start.1 = (f32[2,2,8,2048]{3,2,1,0:T(8,128)S(1)}, f32[2,2,8,2048]{3,2,1,0:T(8,128)S(1)}, u32[]{:S(2)}, u32[]{:S(2)}) collective-permute-start(f32[2,2,8,2048]{3,2,1,0:T(8,128)S(1)} %pad_maximum_fusion.4), channel_id=1, source_target_pairs={{0,3},{1,2},{2,1},{3,0},{4,7},{5,6},{6,5},{7,4},{8,11},{9,10},{10,... | collective-permute-start | bytes 786440 | tf_op jit(solution)/shard_map/ppermute | solution.py:275
  35.5 6.5 %collective-permute-start.11 = (f32[4,8,2048]{2,1,0:T(8,128)S(1)}, f32[4,8,2048]{2,1,0:T(8,128)S(1)}, u32[]{:S(2)}, u32[]{:S(2)}) collective-permute-start(f32[4,8,2048]{2,1,0:T(8,128)S(1)} %pad_maximum_fusion.15), channel_id=1, source_target_pairs={{0,3},{1,2},{2,1},{3,0},{4,7},{5,6},{6,5},{7,4},{8,11},{9,10},{10,... | collective-permute-start | bytes 786440 | tf_op jit(solution)/shard_map/ppermute | solution.py:275
  35.8 6.5 %collective-permute-start.9 = (f32[4,8,2048]{2,1,0:T(8,128)S(1)}, f32[4,8,2048]{2,1,0:T(8,128)S(1)}, u32[]{:S(2)}, u32[]{:S(2)}) collective-permute-start(f32[4,8,2048]{2,1,0:T(8,128)S(1)} %pad_maximum_fusion.13), channel_id=1, source_target_pairs={{0,12},{4,8},{8,4},{12,0},{1,13},{5,9},{9,5},{13,1},{2,14},{6,10},... | collective-permute-start | bytes 786440 | tf_op jit(solution)/shard_map/ppermute | solution.py:275
  42.3 6.6 %collective-permute-start.15 = (f32[4,8,2048]{2,1,0:T(8,128)S(1)}, f32[4,8,2048]{2,1,0:T(8,128)S(1)}, u32[]{:S(2)}, u32[]{:S(2)}) collective-permute-start(f32[4,8,2048]{2,1,0:T(8,128)S(1)} %pad_maximum_fusion.11), channel_id=1, source_target_pairs={{0,3},{1,2},{2,1},{3,0},{4,7},{5,6},{6,5},{7,4},{8,11},{9,10},{10,... | collective-permute-start | bytes 786440 | tf_op jit(solution)/shard_map/ppermute | solution.py:275
  45.3 6.8 %collective-permute-start.13 = (f32[4,8,2048]{2,1,0:T(8,128)S(1)}, f32[4,8,2048]{2,1,0:T(8,128)S(1)}, u32[]{:S(2)}, u32[]{:S(2)}) collective-permute-start(f32[4,8,2048]{2,1,0:T(8,128)S(1)} %pad_maximum_fusion.9), channel_id=1, source_target_pairs={{0,12},{4,8},{8,4},{12,0},{1,13},{5,9},{9,5},{13,1},{2,14},{6,10},... | collective-permute-start | bytes 786440 | tf_op jit(solution)/shard_map/ppermute | solution.py:275
  47.0 6.5 %collective-permute-start.12 = (f32[4,8,2048]{2,1,0:T(8,128)S(1)}, f32[4,8,2048]{2,1,0:T(8,128)S(1)}, u32[]{:S(2)}, u32[]{:S(2)}) collective-permute-start(f32[4,8,2048]{2,1,0:T(8,128)S(1)} %pad_maximum_fusion.8), channel_id=1, source_target_pairs={{0,4},{4,0},{8,12},{12,8},{1,5},{5,1},{9,13},{13,9},{2,6},{6,2},{1... | collective-permute-start | bytes 786440 | tf_op jit(solution)/shard_map/ppermute | solution.py:275
  47.0 12.9 %collective-permute-start.21 = (f32[8,8,2048]{2,1,0:T(8,128)S(1)}, f32[8,8,2048]{2,1,0:T(8,128)S(1)}, u32[]{:S(2)}, u32[]{:S(2)}) collective-permute-start(f32[8,8,2048]{2,1,0:T(8,128)S(1)} %pad_maximum_fusion.1.refs_1_), channel_id=1, source_target_pairs={{0,1},{1,0},{2,3},{3,2},{4,5},{5,4},{6,7},{7,6},{8,9},{9,8},{10,11... | collective-permute-start | bytes 1572872 | tf_op jit(solution)/shard_map/ppermute | solution.py:275
  49.0 11.1 %collective-permute-start.22 = (f32[8,8,2048]{2,1,0:T(8,128)S(1)}, f32[8,8,2048]{2,1,0:T(8,128)S(1)}, u32[]{:S(2)}, u32[]{:S(2)}) collective-permute-start(f32[8,8,2048]{2,1,0:T(8,128)S(1)} %pad_maximum_fusion.2.refs_2_), channel_id=1, source_target_pairs={{0,3},{1,2},{2,1},{3,0},{4,7},{5,6},{6,5},{7,4},{8,11},{9,10},{10,... | collective-permute-start | bytes 1572872 | tf_op jit(solution)/shard_map/ppermute | solution.py:275
  51.7 11.9 %collective-permute-start.23 = (f32[8,8,2048]{2,1,0:T(8,128)S(1)}, f32[8,8,2048]{2,1,0:T(8,128)S(1)}, u32[]{:S(2)}, u32[]{:S(2)}) collective-permute-start(f32[8,8,2048]{2,1,0:T(8,128)S(1)} %pad_maximum_fusion.3.refs_3_), channel_id=1, source_target_pairs={{0,4},{4,0},{8,12},{12,8},{1,5},{5,1},{9,13},{13,9},{2,6},{6,2},{1... | collective-permute-start | bytes 1572872 | tf_op jit(solution)/shard_map/ppermute | solution.py:275
  52.1 12.2 %collective-permute-start.20 = (f32[8,8,2048]{2,1,0:T(8,128)S(1)}, f32[8,8,2048]{2,1,0:T(8,128)S(1)}, u32[]{:S(2)}, u32[]{:S(2)}) collective-permute-start(f32[8,8,2048]{2,1,0:T(8,128)S(1)} %pad_maximum_fusion.refs_0_), channel_id=1, source_target_pairs={{0,12},{4,8},{8,4},{12,0},{1,13},{5,9},{9,5},{13,1},{2,14},{6,10},... | collective-permute-start | bytes 1572872 | tf_op jit(solution)/shard_map/ppermute | solution.py:275
  53.5 34.6 %collective-permute-start.19 = (f32[8,8,2048]{2,1,0:T(8,128)S(1)}, f32[8,8,2048]{2,1,0:T(8,128)S(1)}, u32[]{:S(2)}, u32[]{:S(2)}) collective-permute-start(f32[8,8,2048]{2,1,0:T(8,128)S(1)} %constant_dynamic-update-slice_fusion.6.refs_3_), channel_id=1, source_target_pairs={{0,4},{4,0},{8,12},{12,8},{1,5},{5,1},{9,13},{13,9},{2,6},{6,2},{1... | collective-permute-start | bytes 1572872 | tf_op jit(solution)/shard_map/ppermute | solution.py:275
  59.9 28.2 %collective-permute-start.18 = (f32[8,8,2048]{2,1,0:T(8,128)S(1)}, f32[8,8,2048]{2,1,0:T(8,128)S(1)}, u32[]{:S(2)}, u32[]{:S(2)}) collective-permute-start(f32[8,8,2048]{2,1,0:T(8,128)S(1)} %constant_dynamic-update-slice_fusion.4.refs_2_), channel_id=1, source_target_pairs={{0,3},{1,2},{2,1},{3,0},{4,7},{5,6},{6,5},{7,4},{8,11},{9,10},{10,... | collective-permute-start | bytes 1572872 | tf_op jit(solution)/shard_map/ppermute | solution.py:275
  60.0 28.1 %collective-permute-start.17 = (f32[8,8,2048]{2,1,0:T(8,128)S(1)}, f32[8,8,2048]{2,1,0:T(8,128)S(1)}, u32[]{:S(2)}, u32[]{:S(2)}) collective-permute-start(f32[8,8,2048]{2,1,0:T(8,128)S(1)} %constant_dynamic-update-slice_fusion.2.refs_1_), channel_id=1, source_target_pairs={{0,1},{1,0},{2,3},{3,2},{4,5},{5,4},{6,7},{7,6},{8,9},{9,8},{10,11... | collective-permute-start | bytes 1572872 | tf_op jit(solution)/shard_map/ppermute | solution.py:275
  63.6 24.6 %collective-permute-start.16 = (f32[8,8,2048]{2,1,0:T(8,128)S(1)}, f32[8,8,2048]{2,1,0:T(8,128)S(1)}, u32[]{:S(2)}, u32[]{:S(2)}) collective-permute-start(f32[8,8,2048]{2,1,0:T(8,128)S(1)} %constant_dynamic-update-slice_fusion.refs_0_), channel_id=1, source_target_pairs={{0,12},{4,8},{8,4},{12,0},{1,13},{5,9},{9,5},{13,1},{2,14},{6,10},... | collective-permute-start | bytes 1572872 | tf_op jit(solution)/shard_map/ppermute | solution.py:275
  75.3 35.2 %collective-permute-start.24 = (f32[4,16,64,128]{3,2,1,0:T(8,128)S(1)}, f32[4,16,64,128]{3,2,1,0:T(8,128)S(1)}, u32[]{:S(2)}, u32[]{:S(2)}) collective-permute-start(f32[4,16,64,128]{3,2,1,0:T(8,128)S(1)} %shard_map.109), channel_id=1, source_target_pairs={{0,16},{16,0},{1,17},{17,1},{2,18},{18,2},{3,19},{19,3},{4,20},{20... | collective-permute-start | bytes 6291464 | tf_op jit(solution)/shard_map/ppermute | solution.py:323
  99.4 30.3 %collective-permute-start.29 = (f32[4,16,64,128]{3,2,1,0:T(8,128)S(1)}, f32[4,16,64,128]{3,2,1,0:T(8,128)S(1)}, u32[]{:S(2)}, u32[]{:S(2)}) collective-permute-start(f32[4,16,64,128]{3,2,1,0:T(8,128)S(1)} %shard_map.106), channel_id=1, source_target_pairs={{0,16},{16,0},{1,17},{17,1},{2,18},{18,2},{3,19},{19,3},{4,20},{20... | collective-permute-start | bytes 6291464 | tf_op jit(solution)/shard_map/ppermute | solution.py:323
  112.0 22.8 %collective-permute-start.25 = (f32[8,64,128]{2,1,0:T(8,128)}, f32[8,64,128]{2,1,0:T(8,128)S(1)}, u32[]{:S(2)}, u32[]{:S(2)}) collective-permute-start(f32[8,64,128]{2,1,0:T(8,128)} %get-tuple-element.39), channel_id=1, source_target_pairs={{0,32},{32,64},{64,96},{96,0},{1,33},{33,65},{65,97},{97,1},{2,34}... | collective-permute-start | bytes 786440 | tf_op jit(solution)/shard_map/ppermute | solution.py:326
  113.6 21.1 %collective-permute-start.26 = (f32[8,64,128]{2,1,0:T(8,128)}, f32[8,64,128]{2,1,0:T(8,128)S(1)}, u32[]{:S(2)}, u32[]{:S(2)}) collective-permute-start(f32[8,64,128]{2,1,0:T(8,128)} %get-tuple-element.40), channel_id=1, source_target_pairs={{0,96},{32,0},{64,32},{96,64},{1,97},{33,1},{65,33},{97,65},{2,98}... | collective-permute-start | bytes 786440 | tf_op jit(solution)/shard_map/ppermute | solution.py:327
  131.9 8.7 %collective-permute-start.30 = (f32[8,64,128]{2,1,0:T(8,128)}, f32[8,64,128]{2,1,0:T(8,128)S(1)}, u32[]{:S(2)}, u32[]{:S(2)}) collective-permute-start(f32[8,64,128]{2,1,0:T(8,128)} %get-tuple-element.43), channel_id=1, source_target_pairs={{0,32},{32,64},{64,96},{96,0},{1,33},{33,65},{65,97},{97,1},{2,34}... | collective-permute-start | bytes 786440 | tf_op jit(solution)/shard_map/ppermute | solution.py:326
  131.9 8.7 %collective-permute-start.31 = (f32[8,64,128]{2,1,0:T(8,128)}, f32[8,64,128]{2,1,0:T(8,128)}, u32[]{:S(2)}, u32[]{:S(2)}) collective-permute-start(f32[8,64,128]{2,1,0:T(8,128)} %get-tuple-element.44), channel_id=1, source_target_pairs={{0,96},{32,0},{64,32},{96,64},{1,97},{33,1},{65,33},{97,65},{2,98}... | collective-permute-start | bytes 786440 | tf_op jit(solution)/shard_map/ppermute | solution.py:327
  137.6 31.1 %collective-permute-start.27 = (f32[16,64,128]{2,1,0:T(8,128)}, f32[16,64,128]{2,1,0:T(8,128)S(1)}, u32[]{:S(2)}, u32[]{:S(2)}) collective-permute-start(f32[16,64,128]{2,1,0:T(8,128)} %get-tuple-element.41), channel_id=1, source_target_pairs={{0,32},{32,64},{64,96},{96,0},{1,33},{33,65},{65,97},{97,1},{2,34}... | collective-permute-start | bytes 1572872 | tf_op jit(solution)/shard_map/ppermute | solution.py:329
  137.6 31.1 %collective-permute-start.28 = (f32[16,64,128]{2,1,0:T(8,128)}, f32[16,64,128]{2,1,0:T(8,128)S(1)}, u32[]{:S(2)}, u32[]{:S(2)}) collective-permute-start(f32[16,64,128]{2,1,0:T(8,128)} %get-tuple-element.42), channel_id=1, source_target_pairs={{0,96},{32,0},{64,32},{96,64},{1,97},{33,1},{65,33},{97,65},{2,98}... | collective-permute-start | bytes 1572872 | tf_op jit(solution)/shard_map/ppermute | solution.py:330
  142.6 26.1 %collective-permute-start.32 = (f32[16,64,128]{2,1,0:T(8,128)}, f32[16,64,128]{2,1,0:T(8,128)}, u32[]{:S(2)}, u32[]{:S(2)}) collective-permute-start(f32[16,64,128]{2,1,0:T(8,128)} %get-tuple-element.45), channel_id=1, source_target_pairs={{0,32},{32,64},{64,96},{96,0},{1,33},{33,65},{65,97},{97,1},{2,34}... | collective-permute-start | bytes 1572872 | tf_op jit(solution)/shard_map/ppermute | solution.py:329
  142.6 26.1 %collective-permute-start.33 = (f32[16,64,128]{2,1,0:T(8,128)}, f32[16,64,128]{2,1,0:T(8,128)}, u32[]{:S(2)}, u32[]{:S(2)}) collective-permute-start(f32[16,64,128]{2,1,0:T(8,128)} %get-tuple-element.46), channel_id=1, source_target_pairs={{0,96},{32,0},{64,32},{96,64},{1,97},{33,1},{65,33},{97,65},{2,98}... | collective-permute-start | bytes 1572872 | tf_op jit(solution)/shard_map/ppermute | solution.py:330
  151.1 17.3 %all-to-all-start = ((f32[128,1,16]{2,1,0:T(1,128)}), f32[128,1,16]{2,1,0:T(1,128)S(1)}, u32[]{:S(2)}, u32[]{:S(2)}) async-start(f32[128,1,16]{2,1,0:T(1,128)} %bitcast.24), calls=%async_computation | async-start | bytes 131072 | tf_op jit(solution)/shard_map/all_to_all | solution.py:335
  (29 other events, 322.0 us)

commit v3 on v2

--- a/solution.py
+++ b/solution.py
@@ -18,6 +18,7 @@
 SUB = 32
 COLOURS = 4
 NB = 256
+SLOTS = 4
 MIB = 1 << 20
 
 f32 = jnp.float32
@@ -29,7 +30,7 @@
     return hi, (x - hi.astype(f32)).astype(bf16)
 
 
-def call(kernel, out_shape, *, vmem=48, flops=0, nbytes=0, **kw):
+def call(kernel, out_shape, *, vmem=16, flops=0, nbytes=0, **kw):
     return pl.pallas_call(
         kernel,
         out_shape=out_shape,
@@ -67,81 +68,73 @@
     )(mask, x)
 
 
-def integrals_kernel(mask_ref, x_ref, *refs, first):
-    hi_ref, lo_ref = refs[-2:]
-    step = first + pl.program_id(0)
-    for i in range(x_ref.shape[0] // TILE):
-        for j in range(NB // TILE):
-            hi, lo = masked_split(mask_ref, x_ref, i, step * (NB // TILE) + j, i, j)
-            at = (0, slice(i * TILE, (i + 1) * TILE), slice(j * TILE, (j + 1) * TILE))
-            hi_ref[at] = hi
-            lo_ref[at] = lo
-
-
-def prepare_integrals(x, mask, first, count, into=None):
-    depth, cols = x.shape
-    out = jax.ShapeDtypeStruct((cols // NB, depth, NB), bf16)
-    spec = pl.BlockSpec((1, depth, NB), lambda n: (n + first, 0, 0))
-    kw = {}
-    specs = [pl.BlockSpec(memory_space=pltpu.SMEM), pl.BlockSpec((depth, NB), lambda n: (0, n + first))]
-    extra = ()
-    if into is not None:
-        extra = into
-        specs += [pl.BlockSpec(memory_space=pl.ANY)] * 2
-        kw["input_output_aliases"] = {2: 0, 3: 1}
-    return call(
-        functools.partial(integrals_kernel, first=first),
-        (out, out),
-        grid=(count,),
-        in_specs=specs,
-        out_specs=(spec, spec),
-        nbytes=depth * NB * 8 * count,
-        flops=depth * NB * 4 * count,
-        **kw,
-    )(mask, x, *extra)
-
-
-def mm_kernel(where_ref, *refs):
-    held, bh_ref, bl_ref, o_ref, ah, al = refs[:-5], *refs[-5:]
+def mm_kernel(where_ref, mask_ref, *refs):
+    held, b_ref, o_ref, ah, al, slots, sems = refs[:-6], *refs[-6:]
     near, late = held[:COLOURS], held[COLOURS:]
-
-    @pl.when(pl.program_id(0) == 0)
-    def _():
-        for s in range(2 * NZ):
-            rows = []
-            for c in range(COLOURS):
-                w = where_ref[c, s]
-                mine = near[c][jnp.minimum(w, 7)]
-                rows.append(jnp.where(w < 8, mine, late[c][jnp.maximum(w - 8, 0)]))
-            hi, lo = split(jnp.concatenate(rows, axis=0))
-            at = slice(s * SUB, (s + 1) * SUB)
-            ah[at, :] = hi
-            al[at, :] = lo
+    blocks = b_ref.shape[1] // NB
+    per = NB // TILE
+
+    def fetch(n):
+        slot = n % SLOTS
+        at = pl.ds(pl.multiple_of(n * NB, NB), NB)
+        return pltpu.make_async_copy(b_ref.at[:, at], slots.at[slot], sems.at[slot])
+
+    for n in range(SLOTS):
+        fetch(n).start()
+
+    for s in range(2 * NZ):
+        rows = []
+        for c in range(COLOURS):
+            w = where_ref[c, s]
+            mine = near[c][jnp.minimum(w, 7)]
+            rows.append(jnp.where(w < 8, mine, late[c][jnp.maximum(w - 8, 0)]))
+        hi, lo = split(jnp.concatenate(rows, axis=0))
+        at = slice(s * SUB, (s + 1) * SUB)
+        ah[at, :] = hi
+        al[at, :] = lo
 
     dot = functools.partial(jnp.dot, preferred_element_type=f32)
-    acc = dot(ah[...], bh_ref[0]) + dot(ah[...], bl_ref[0]) + dot(al[...], bh_ref[0])
-    for i in range(NZ):
-        for t in range(NB // TILE):
-            o_ref[i, t] = acc[2 * SUB * i : 2 * SUB * (i + 1), t * TILE : (t + 1) * TILE]
-
-
-def multiply(held, bh, bl, where):
-    blocks, depth, _ = bh.shape
+    tiles = range(b_ref.shape[0] // TILE)
+
+    def step(n, carry):
+        fetch(n).wait()
+        x = slots.at[n % SLOTS]
+        terms = [[masked_split(mask_ref, x, i, n * per + j, i, j) for j in range(per)] for i in tiles]
+        bh, bl = (jnp.concatenate([jnp.concatenate([t[k] for t in row], axis=1) for row in terms], axis=0) for k in range(2))
+        acc = dot(ah[...], bh) + dot(ah[...], bl) + dot(al[...], bh)
+        for i in range(NZ):
+            for t in range(per):
+                o_ref[i, n * per + t] = acc[2 * SUB * i : 2 * SUB * (i + 1), t * TILE : (t + 1) * TILE]
+
+        @pl.when(n + SLOTS < blocks)
+        def _():
+            fetch(n + SLOTS).start()
+
+        return carry
+
+    lax.fori_loop(0, blocks, step, 0)
+
+
+def multiply(held, integrals, mask, where):
+    depth, cols = integrals.shape
     m = NZ * 2 * SUB
-    chunk = pl.BlockSpec((1, depth, NB), lambda n: (n, 0, 0))
+    smem = pl.BlockSpec(memory_space=pltpu.SMEM)
+    vmem = pl.BlockSpec(memory_space=pltpu.VMEM)
     return call(
         mm_kernel,
-        jax.ShapeDtypeStruct((NZ, blocks * NB // TILE, 2 * SUB, TILE), f32),
-        grid=(blocks,),
-        in_specs=[pl.BlockSpec(memory_space=pltpu.SMEM)]
-        + [pl.BlockSpec(h.shape, lambda n: (0, 0, 0)) for h in held]
-        + [chunk, chunk],
-        out_specs=pl.BlockSpec((NZ, NB // TILE, 2 * SUB, TILE), lambda n: (0, n, 0, 0)),
-        scratch_shapes=[pltpu.VMEM((m, depth), bf16), pltpu.VMEM((m, depth), bf16)],
-        vmem=32,
-        flops=6 * m * depth * blocks * NB,
-        nbytes=4 * depth * blocks * NB,
-    )(where, *held, bh, bl)
+        jax.ShapeDtypeStruct((NZ, cols // TILE, 2 * SUB, TILE), f32),
+        in_specs=[smem, smem] + [vmem] * len(held) + [pl.BlockSpec(memory_space=pltpu.HBM)],
+        out_specs=vmem,
+        scratch_shapes=[
+            pltpu.VMEM((m, depth), bf16),
+            pltpu.VMEM((m, depth), bf16),
+            pltpu.VMEM((SLOTS, depth, NB), f32),
+            pltpu.SemaphoreType.DMA((SLOTS,)),
+        ],
+        vmem=48,
+        flops=6 * m * depth * cols,
+        nbytes=4 * depth * cols,
+    )(where, mask, *held, integrals)
 
 
 def far_kernel(mine_ref, got_ref, p_ref, m_ref):
@@ -301,42 +294,54 @@
     rows = amplitudes.reshape(COLOURS, PARTS, 1, 8, depth)
     bufs = [rows[c] for c in range(COLOURS)]
     got = [exchange(bufs[c], ORDERS[c][0]) for c in range(COLOURS)]
+    source, place = plan(destination)
     bufs = [jnp.concatenate([b, g], axis=1) for b, g in zip(bufs, got)]
+    bufs[-1] = after(bufs[-1], source)
     got = [exchange(bufs[c], ORDERS[c][1]) for c in range(COLOURS)]
     halves = [[jnp.concatenate([b[p], g[p]], axis=0) for b, g in zip(bufs, got)] for p in range(PARTS)]
 
-    half = integrals.shape[1] // NB // 2
-    b_first = prepare_integrals(integrals, integral_mask, 0, half)
-    bh, bl = prepare_integrals(integrals, integral_mask, half, half, b_first)
-
-    parts = []
-    last = None
-    for p in range(PARTS):
-        bufs = halves[p]
-        if last is not None:
-            bufs = list(lax.optimization_barrier(tuple(bufs) + tuple(last)))[:COLOURS]
+    def third(bufs):
         got = [exchange(bufs[c], ORDERS[c][2]) for c in range(COLOURS)]
-        last = got
-        bufs = [jnp.concatenate([b, g], axis=0) for b, g in zip(bufs, got)]
-        late = [exchange(bufs[c], ORDERS[c][3]) for c in range(COLOURS)]
-        theirs = multiply(bufs + late, bh, bl, other)
-        from_core = lax.ppermute(theirs, "core", [(0, 1), (1, 0)])
-        mine = multiply(bufs + late, bh, bl, own)
+        return got, [jnp.concatenate([b, g], axis=0) for b, g in zip(bufs, got)]
+
+    def fourth(bufs):
+        return bufs + [exchange(bufs[c], ORDERS[c][3]) for c in range(COLOURS)]
+
+    def product(held, where):
+        return multiply(held, integrals, integral_mask, where)
+
+    def swap(value):
+        return lax.ppermute(value, "core", [(0, 1), (1, 0)])
+
+    _, bufs = third(halves[0])
+    held0 = fourth(bufs)
+    ready = lax.optimization_barrier(tuple(halves[1]) + tuple(held0[COLOURS:]))
+    got, bufs = third(list(ready[:COLOURS]))
+    theirs0 = product(held0, other)
+    from_core0 = swap(theirs0)
+    held1 = fourth(bufs)
+    mine0 = product(held0, after(own, *got))
+    theirs1 = product(held1, after(other, mine0))
+    from_core1 = swap(theirs1)
+    mine1 = product(held1, own)
+
+    ch, cl = prepare_cycle(after(cycle_tiles, theirs1), cycle_mask)
+    sums = []
+    for p, (mine, from_core) in enumerate([(mine0, from_core0), (mine1, from_core1)]):
         far_p, far_m = far(mine, from_core)
         gp = lax.ppermute(far_p, "z", ring(1))
         gm = lax.ppermute(far_m, "z", ring(-1))
+        if p == PARTS - 1:
+            gp = after(gp, ch, cl)
         near_p, near_m = near(mine, from_core, gp, gm)
         rp = lax.ppermute(near_p, "z", ring(1))
         rm = lax.ppermute(near_m, "z", ring(-1))
-        parts.append((mine, from_core, rp, rm))
-
-    source, place = plan(after(destination, theirs))
-    place = place.astype(f32).reshape(128, 1, CAP)
+        sums.append((mine, from_core, rp, rm))
+
+    place = after(place, theirs1).astype(f32).reshape(128, 1, CAP)
     got_place = lax.all_to_all(place, everyone, split_axis=0, concat_axis=0, tiled=True)
     got_place = got_place.reshape(-1).astype(jnp.int32)
-    ch, cl = prepare_cycle(after(cycle_tiles, theirs), cycle_mask)
-
-    sending = gather(after(source, got_place, ch, cl), parts).reshape(128, CAP, TILE)
+    sending = gather(after(source, got_place, ch, cl), sums).reshape(128, CAP, TILE)
     units = lax.all_to_all(sending, everyone, split_axis=0, concat_axis=0, tiled=True)
     return finish(got_place, units.reshape(-1, TILE), denominators, ch, cl)
 

time: 205 us -> 203 us (level)
  blocking collectives: 25.1 us -> 45.2 us
  Pallas kernels: 76.9 us -> 63.7 us
  starting transfers between devices: 57.9 us -> 51.2 us
  waiting for transfers between devices: 21.9 us -> 19.6 us
    all_to_all x0 -> x1, blocking collectives: none -> 19.8 us  [body(): lax.all_to_all(place, everyone, split_axis=0, concat_axis=0, tiled=True)]
    pallas_call x6 -> x4, Pallas kernels: 58.5 us -> 48.3 us  [multiply(): call(mm_kernel, jax.ShapeDtypeStruct((NZ, cols // TILE, 2 * SUB, TILE), f...]
    all_to_all x1 -> x0, starting transfers between devices: 7.74 us -> none  [body(): lax.all_to_all(place, everyone, split_axis=0, concat_axis=0, tiled=True)]
    ppermute x2, starting transfers between devices: 13.2 us -> 17.2 us  [swap(): return lax.ppermute(value, 'core', [(0, 1), (1, 0)])]
    all_to_all x1 -> x0, waiting for transfers between devices: 3.27 us -> none  [body(): lax.all_to_all(place, everyone, split_axis=0, concat_axis=0, tiled=True)]
    ppermute x24, starting transfers between devices: 25.2 us -> 22.3 us  [exchange(): return lax.ppermute(value, axis, pairs)]
    unnamed x57 -> x40, local copies, waits for them, and re-layouts: 10.6 us -> 12 us
  transfers between devices with their start and end apart: 35 -> 34, of which waited for: 11 -> 7; matrix products, arithmetic and copies ran while one was open for 4% -> 5% of each run, Pallas kernels for 33% -> 27%
where the time goes in v3:
time: 203 us; the launch traced here: 202 us
  Pallas kernels  63.7 us (31%)
  starting transfers between devices  51.2 us (25%)
  blocking collectives  45.2 us (22%)
  waiting for transfers between devices  19.6 us (10%)
  local copies, waits for them, and re-layouts  13.7 us (7%)
  other arithmetic  7.74 us (4%)
    pallas_call x4, Pallas kernels, multiply(): call(mm_kernel, jax.ShapeDtypeStruct((NZ, cols // TILE, 2 * SUB, TILE), f...  48.3 us
    all_to_all x1, blocking collectives, body(): lax.all_to_all(sending, everyone, split_axis=0, concat_axis=0, tiled=True)  25.4 us
    ppermute x24, starting transfers between devices, exchange(): return lax.ppermute(value, axis, pairs)  22.3 us
    all_to_all x1, blocking collectives, body(): lax.all_to_all(place, everyone, split_axis=0, concat_axis=0, tiled=True)  19.8 us
    ppermute x24, waiting for transfers between devices, exchange(): return lax.ppermute(value, axis, pairs)  19.6 us
    ppermute x2, starting transfers between devices, swap(): return lax.ppermute(value, 'core', [(0, 1), (1, 0)])  17.2 us
    unnamed x40, local copies, waits for them, and re-layouts  12 us
    ppermute x2, starting transfers between devices, body(): rm = lax.ppermute(near_m, 'z', ring(-1))  5.35 us
  transfers between devices with their start and end apart: 34, of which 7 were waited for; matrix products, arithmetic and copies ran while one was open for 5% of the time, Pallas kernels for 27%

profile of v3, /device:TPU:1, one launch (start us, length us, event | category | flops | bytes accessed | tf_op | source)
XLA Modules:
  0.0 202.3 jit_solution(7703740430719340569)
XLA Ops:
  1.8 3.6 %collective-permute-start.6 = (f32[2,1,8,2048]{3,2,1,0:T(8,128)S(1)}, f32[2,1,8,2048]{3,2,1,0:T(8,128)S(1)}, u32[]{:S(2)}, u32[]{:S(2)}) collective-permute-start(f32[2,1,8,2048]{3,2,1,0:T(8,128)S(1)} %get-tuple-element.49), channel_id=1, source_target_pairs={{0,12},{4,8},{8,4},{12,0},{1,13},{5,9},{9,5},{13,1},{2,14},{6,10},... | collective-permute-start | bytes 393224 | tf_op jit(solution)/shard_map/ppermute | solution.py:268
  5.4 2.5 %collective-permute-start.2 = (f32[2,1,8,2048]{3,2,1,0:T(8,128)S(1)}, f32[2,1,8,2048]{3,2,1,0:T(8,128)S(1)}, u32[]{:S(2)}, u32[]{:S(2)}) collective-permute-start(f32[2,1,8,2048]{3,2,1,0:T(8,128)S(1)} %get-tuple-element.50), channel_id=1, source_target_pairs={{0,3},{1,2},{2,1},{3,0},{4,7},{5,6},{6,5},{7,4},{8,11},{9,10},{10,... | collective-permute-start | bytes 393224 | tf_op jit(solution)/shard_map/ppermute | solution.py:268
  9.7 5.0 %sort.14 = (s32[2048]{0:T(1024)S(1)}, s32[2048]{0:T(1024)}) sort(s32[2048]{0:T(1024)S(1)} %fusion.22, s32[2048]{0:T(1024)S(1)} %iota.7), dimensions={0}, to_apply=%region_0.1 | sort | flops 22528 | bytes 32768 | tf_op jit(solution)/shard_map/sort | solution.py:252
  19.8 3.8 %collective-permute-done.3 = f32[2,2,8,2048]{3,2,1,0:T(8,128)S(1)} collective-permute-done((f32[2,2,8,2048]{3,2,1,0:T(8,128)S(1)}, f32[2,2,8,2048]{3,2,1,0:T(8,128)S(1)}, u32[]{:S(2)}, u32[]{:S(2)}) %collective-permute-start.3) | collective-permute-done | bytes 262176 | tf_op jit(solution)/shard_map/ppermute | solution.py:268
  24.2 2.1 %collective-permute-done.5 = f32[2,2,8,2048]{3,2,1,0:T(8,128)S(1)} collective-permute-done((f32[2,2,8,2048]{3,2,1,0:T(8,128)S(1)}, f32[2,2,8,2048]{3,2,1,0:T(8,128)S(1)}, u32[]{:S(2)}, u32[]{:S(2)}) %collective-permute-start.5) | collective-permute-done | bytes 262176 | tf_op jit(solution)/shard_map/ppermute | solution.py:268
  26.6 2.6 %collective-permute-start.14 = (f32[4,8,2048]{2,1,0:T(8,128)S(1)}, f32[4,8,2048]{2,1,0:T(8,128)S(1)}, u32[]{:S(2)}, u32[]{:S(2)}) collective-permute-start(f32[4,8,2048]{2,1,0:T(8,128)S(1)} %pad_maximum_fusion.15), channel_id=1, source_target_pairs={{0,3},{1,2},{2,1},{3,0},{4,7},{5,6},{6,5},{7,4},{8,11},{9,10},{10,... | collective-permute-start | bytes 786440 | tf_op jit(solution)/shard_map/ppermute | solution.py:268
  29.3 4.1 %collective-permute-done.14 = f32[4,8,2048]{2,1,0:T(8,128)S(1)} collective-permute-done((f32[4,8,2048]{2,1,0:T(8,128)S(1)}, f32[4,8,2048]{2,1,0:T(8,128)S(1)}, u32[]{:S(2)}, u32[]{:S(2)}) %collective-permute-start.14) | collective-permute-done | bytes 262176 | tf_op jit(solution)/shard_map/ppermute | solution.py:268
  33.6 2.6 %collective-permute-start.13 = (f32[8,8,2048]{2,1,0:T(8,128)S(1)}, f32[8,8,2048]{2,1,0:T(8,128)S(1)}, u32[]{:S(2)}, u32[]{:S(2)}) collective-permute-start(f32[8,8,2048]{2,1,0:T(8,128)S(1)} %pad_maximum_fusion.2.refs_2_), channel_id=1, source_target_pairs={{0,3},{1,2},{2,1},{3,0},{4,7},{5,6},{6,5},{7,4},{8,11},{9,10},{10,... | collective-permute-start | bytes 1572872 | tf_op jit(solution)/shard_map/ppermute | solution.py:268
  36.6 7.8 %collective-permute-done.15.refs_7_ = f32[8,8,2048]{2,1,0:T(8,128)S(1)} collective-permute-done((f32[8,8,2048]{2,1,0:T(8,128)S(1)}, f32[8,8,2048]{2,1,0:T(8,128)S(1)}, u32[]{:S(2)}, u32[]{:S(2)}) %collective-permute-start.15) | collective-permute-done | bytes 524320 | tf_op jit(solution)/shard_map/ppermute | solution.py:268
  46.2 2.1 %collective-permute-start.17 = (f32[4,8,2048]{2,1,0:T(8,128)S(1)}, f32[4,8,2048]{2,1,0:T(8,128)S(1)}, u32[]{:S(2)}, u32[]{:S(2)}) collective-permute-start(f32[4,8,2048]{2,1,0:T(8,128)S(1)} %get-tuple-element.28), channel_id=1, source_target_pairs={{0,12},{4,8},{8,4},{12,0},{1,13},{5,9},{9,5},{13,1},{2,14},{6,10},... | collective-permute-start | bytes 786440 | tf_op jit(solution)/shard_map/ppermute | solution.py:268
  48.7 12.1 %shard_map.107 = f32[4,16,64,128]{3,2,1,0:T(8,128)} custom-call(s32[4,8]{1,0:T(4,128)S(1)} %pad_add_fusion.where_ref, s32[16,16]{1,0:T(8,128)S(1)} %copy-done.15, f32[8,8,2048]{2,1,0:T(8,128)S(1)} %pad_maximum_fusion.refs_0_, f32[8,8,2048]{2,1,0:T(8,128)S(1)} %pad_maximum_fusion.1.refs_1_, f32[8,8,2048]{2,1,0:T(8,128)S(1)} %pad_maximum_fusion.2.refs_2_, ...), custom_call_target="tpu_custom_call" | custom-call | flops 6442450944 | bytes 16777216 | tf_op jit(solution)/shard_map/pallas_call | solution.py:123
  60.8 15.3 %collective-permute-start.24 = (f32[4,16,64,128]{3,2,1,0:T(8,128)}, f32[4,16,64,128]{3,2,1,0:T(8,128)S(1)}, u32[]{:S(2)}, u32[]{:S(2)}) collective-permute-start(f32[4,16,64,128]{3,2,1,0:T(8,128)} %shard_map.107), channel_id=1, source_target_pairs={{0,16},{16,0},{1,17},{17,1},{2,18},{18,2},{3,19},{19,3},{4,20},{20... | collective-permute-start | bytes 6291464 | tf_op jit(solution)/shard_map/ppermute | solution.py:314
  79.6 12.1 %shard_map.104.mine_ref.refs_0_ = f32[4,16,64,128]{3,2,1,0:T(8,128)} custom-call(s32[4,8]{1,0:T(4,128)S(1)} %pad_add_fusion.1.where_ref, s32[16,16]{1,0:T(8,128)S(1)} %copy-done.15, f32[8,8,2048]{2,1,0:T(8,128)S(1)} %pad_maximum_fusion.refs_0_, f32[8,8,2048]{2,1,0:T(8,128)S(1)} %pad_maximum_fusion.1.refs_1_, f32[8,8,2048]{2,1,0:T(8,128)S(1)} %pad_maximum_fusion.2.refs_2_, ...), custom_call_target="tpu_custom_call" | custom-call | flops 6442450944 | bytes 16777216 | tf_op jit(solution)/shard_map/pallas_call | solution.py:123
  92.3 12.1 %shard_map.105 = f32[4,16,64,128]{3,2,1,0:T(8,128)} custom-call(s32[4,8]{1,0:T(4,128)S(1)} %pad_add_fusion.where_ref, s32[16,16]{1,0:T(8,128)S(1)} %copy-done.15, f32[8,8,2048]{2,1,0:T(8,128)S(1)} %constant_dynamic-update-slice_fusion.refs_0_, f32[8,8,2048]{2,1,0:T(8,128)S(1)} %constant_dynamic-update-slice_fusion.2.refs_1_, ...), custom_call_target="tpu_custom_call" | custom-call | flops 6442450944 | bytes 16777216 | tf_op jit(solution)/shard_map/pallas_call | solution.py:123
  104.4 1.8 collective-permute-start.29
  107.0 1.6 collective-permute-start.25
  108.7 2.1 %collective-permute-start.26 = (f32[8,64,128]{2,1,0:T(8,128)S(1)}, f32[8,64,128]{2,1,0:T(8,128)S(1)}, u32[]{:S(2)}, u32[]{:S(2)}) collective-permute-start(f32[8,64,128]{2,1,0:T(8,128)S(1)} %get-tuple-element.39), channel_id=1, source_target_pairs={{0,96},{32,0},{64,32},{96,64},{1,97},{33,1},{65,33},{97,65},{2,98}... | collective-permute-start | bytes 786440 | tf_op jit(solution)/shard_map/ppermute | solution.py:333
  110.8 12.1 %shard_map.110.mine_ref.refs_4_ = f32[4,16,64,128]{3,2,1,0:T(8,128)} custom-call(s32[4,8]{1,0:T(4,128)S(1)} %pad_add_fusion.1.where_ref, s32[16,16]{1,0:T(8,128)S(1)} %copy-done.15, f32[8,8,2048]{2,1,0:T(8,128)S(1)} %constant_dynamic-update-slice_fusion.refs_0_, f32[8,8,2048]{2,1,0:T(8,128)S(1)} %constant_dynamic-update-slice_fusion.2.refs_1_, ...), custom_call_target="tpu_custom_call" | custom-call | flops 6442450944 | bytes 16777216 | tf_op jit(solution)/shard_map/pallas_call | solution.py:123
  122.9 1.6 copy-done.6
  126.0 2.7 %collective-permute-start.31 = (f32[8,64,128]{2,1,0:T(8,128)}, f32[8,64,128]{2,1,0:T(8,128)}, u32[]{:S(2)}, u32[]{:S(2)}) collective-permute-start(f32[8,64,128]{2,1,0:T(8,128)} %get-tuple-element.44), channel_id=1, source_target_pairs={{0,96},{32,0},{64,32},{96,64},{1,97},{33,1},{65,33},{97,65},{2,98}... | collective-permute-start | bytes 786440 | tf_op jit(solution)/shard_map/ppermute | solution.py:333
  128.8 2.2 %copy-done.9 = f32[2048,512]{1,0:T(8,128)S(1)} copy-done((f32[2048,512]{1,0:T(8,128)S(1)}, f32[2048,512]{1,0:T(8,128)}, u32[]{:S(2)}) %copy-start.9) | copy-done | bytes 4194328
  131.0 1.6 shard_map.106
  135.6 2.7 %collective-permute-start.28 = (f32[16,64,128]{2,1,0:T(8,128)}, f32[16,64,128]{2,1,0:T(8,128)S(1)}, u32[]{:S(2)}, u32[]{:S(2)}) collective-permute-start(f32[16,64,128]{2,1,0:T(8,128)} %get-tuple-element.41), channel_id=1, source_target_pairs={{0,96},{32,0},{64,32},{96,64},{1,97},{33,1},{65,33},{97,65},{2,98}... | collective-permute-start | bytes 1572872 | tf_op jit(solution)/shard_map/ppermute | solution.py:338
  138.3 2.1 %shard_map.112 = (f32[16,64,128]{2,1,0:T(8,128)}, f32[16,64,128]{2,1,0:T(8,128)}) custom-call(f32[4,16,64,128]{3,2,1,0:T(8,128)S(1)} %copy-done.7, f32[4,16,64,128]{3,2,1,0:T(8,128)S(1)} %copy-done.4, f32[8,64,128]{2,1,0:T(8,128)S(1)} %collective-permute-done.30.gp_ref, f32[8,64,128]{2,1,0:T(8,128)} %collective-permute-done.31.gm_ref), custom_call_target="tpu_custom_call" | custom-call | bytes 3670016 | tf_op jit(solution)/shard_map/pallas_call | solution.py:168
  140.4 2.7 %collective-permute-start.33 = (f32[16,64,128]{2,1,0:T(8,128)}, f32[16,64,128]{2,1,0:T(8,128)}, u32[]{:S(2)}, u32[]{:S(2)}) collective-permute-start(f32[16,64,128]{2,1,0:T(8,128)} %get-tuple-element.46), channel_id=1, source_target_pairs={{0,96},{32,0},{64,32},{96,64},{1,97},{33,1},{65,33},{97,65},{2,98}... | collective-permute-start | bytes 1572872 | tf_op jit(solution)/shard_map/ppermute | solution.py:338
  143.2 19.8 %all_to_all.10 = f32[128,1,16]{2,1,0:T(1,128)S(1)} all-to-all(f32[128,1,16]{2,1,0:T(1,128)S(1)} %bitcast.61), channel_id=1, replica_groups=mesh['z'=4,'core'=2,'y'=4,'x'=4] {'z','core','y','x'}, dimensions={0} | all-to-all | bytes 16384 | tf_op jit(solution)/shard_map/all_to_all | solution.py:342
  163.3 1.6 copy-done.2
  164.9 1.6 copy-done.5
  166.5 1.6 copy-done.8
  168.1 3.7 %shard_map.113 = f32[2048,128]{1,0:T(8,128)S(1)} custom-call(s32[2048]{0:T(1024)S(1)} %get-tuple-element.37.idx_ref, f32[4,16,64,128]{3,2,1,0:T(8,128)S(1)} %copy-done.2, f32[4,16,64,128]{3,2,1,0:T(8,128)S(1)} %collective-permute-done.24.got_ref.refs_1_, f32[16,64,128]{2,1,0:T(8,128)S(1)} %collective-permute-done.27.refs_2_, ...), custom_call_target="tpu_custom_call" | custom-call | bytes 5242880 | tf_op jit(solution)/shard_map/pallas_call | solution.py:199
  171.8 25.4 %all_to_all.11 = f32[128,16,128]{2,1,0:T(8,128)S(1)} all-to-all(f32[128,16,128]{2,1,0:T(8,128)S(1)} %bitcast.59), channel_id=1, replica_groups=mesh['z'=4,'core'=2,'y'=4,'x'=4] {'z','core','y','x'}, dimensions={0} | all-to-all | bytes 2097152 | tf_op jit(solution)/shard_map/all_to_all | solution.py:345
  197.2 5.1 %shard_map.114 = (f32[128,2048]{1,0:T(8,128)}, f32[128,2048]{1,0:T(8,128)}) custom-call(s32[2048]{0:T(1024)S(1)} %convert_element_type.10.place_ref, f32[2048,128]{1,0:T(8,128)S(1)} %bitcast.60, f32[128,2048]{1,0:T(8,128)S(1)} %copy-done.14, bf16[2048,512]{1,0:T(8,128)(2,1)S(1)} %copy-done.11, bf16[2048,512]{1,0:T(8,128)(2,1)S(1)} %copy-done.13), custom_call_target="tpu_custom_call" | custom-call | bytes 8388608 | tf_op jit(solution)/shard_map/pallas_call | solution.py:231
  (132 shorter events, 21.4 us)
Async XLA Ops:
  1.8 14.3 %collective-permute-start.6 = (f32[2,1,8,2048]{3,2,1,0:T(8,128)S(1)}, f32[2,1,8,2048]{3,2,1,0:T(8,128)S(1)}, u32[]{:S(2)}, u32[]{:S(2)}) collective-permute-start(f32[2,1,8,2048]{3,2,1,0:T(8,128)S(1)} %get-tuple-element.49), channel_id=1, source_target_pairs={{0,12},{4,8},{8,4},{12,0},{1,13},{5,9},{9,5},{13,1},{2,14},{6,10},... | collective-permute-start | bytes 393224 | tf_op jit(solution)/shard_map/ppermute | solution.py:268
  5.4 12.3 %collective-permute-start.2 = (f32[2,1,8,2048]{3,2,1,0:T(8,128)S(1)}, f32[2,1,8,2048]{3,2,1,0:T(8,128)S(1)}, u32[]{:S(2)}, u32[]{:S(2)}) collective-permute-start(f32[2,1,8,2048]{3,2,1,0:T(8,128)S(1)} %get-tuple-element.50), channel_id=1, source_target_pairs={{0,3},{1,2},{2,1},{3,0},{4,7},{5,6},{6,5},{7,4},{8,11},{9,10},{10,... | collective-permute-start | bytes 393224 | tf_op jit(solution)/shard_map/ppermute | solution.py:268
  7.9 11.3 %collective-permute-start = (f32[2,1,8,2048]{3,2,1,0:T(8,128)S(1)}, f32[2,1,8,2048]{3,2,1,0:T(8,128)S(1)}, u32[]{:S(2)}, u32[]{:S(2)}) collective-permute-start(f32[2,1,8,2048]{3,2,1,0:T(8,128)S(1)} %get-tuple-element.51), channel_id=1, source_target_pairs={{0,1},{1,0},{2,3},{3,2},{4,5},{5,4},{6,7},{7,6},{8,9},{9,8},{10,11... | collective-permute-start | bytes 393224 | tf_op jit(solution)/shard_map/ppermute | solution.py:268
  7.9 11.6 %collective-permute-start.4 = (f32[2,1,8,2048]{3,2,1,0:T(8,128)S(1)}, f32[2,1,8,2048]{3,2,1,0:T(8,128)S(1)}, u32[]{:S(2)}, u32[]{:S(2)}) collective-permute-start(f32[2,1,8,2048]{3,2,1,0:T(8,128)S(1)} %get-tuple-element.52), channel_id=1, source_target_pairs={{0,4},{4,0},{8,12},{12,8},{1,5},{5,1},{9,13},{13,9},{2,6},{6,2},{1... | collective-permute-start | bytes 393224 | tf_op jit(solution)/shard_map/ppermute | solution.py:268
  16.1 10.4 %collective-permute-start.7 = (f32[2,2,8,2048]{3,2,1,0:T(8,128)S(1)}, f32[2,2,8,2048]{3,2,1,0:T(8,128)S(1)}, u32[]{:S(2)}, u32[]{:S(2)}) collective-permute-start(f32[2,2,8,2048]{3,2,1,0:T(8,128)S(1)} %pad_maximum_fusion.10), channel_id=1, source_target_pairs={{0,1},{1,0},{2,3},{3,2},{4,5},{5,4},{6,7},{7,6},{8,9},{9,8},{10,11... | collective-permute-start | bytes 786440 | tf_op jit(solution)/shard_map/ppermute | solution.py:268
  19.3 9.9 %collective-permute-start.1 = (f32[2,2,8,2048]{3,2,1,0:T(8,128)S(1)}, f32[2,2,8,2048]{3,2,1,0:T(8,128)S(1)}, u32[]{:S(2)}, u32[]{:S(2)}) collective-permute-start(f32[2,2,8,2048]{3,2,1,0:T(8,128)S(1)} %pad_maximum_fusion.4), channel_id=1, source_target_pairs={{0,3},{1,2},{2,1},{3,0},{4,7},{5,6},{6,5},{7,4},{8,11},{9,10},{10,... | collective-permute-start | bytes 786440 | tf_op jit(solution)/shard_map/ppermute | solution.py:268
  19.6 6.8 %collective-permute-start.5 = (f32[2,2,8,2048]{3,2,1,0:T(8,128)S(1)}, f32[2,2,8,2048]{3,2,1,0:T(8,128)S(1)}, u32[]{:S(2)}, u32[]{:S(2)}) collective-permute-start(f32[2,2,8,2048]{3,2,1,0:T(8,128)S(1)} %pad_maximum_fusion.6), channel_id=1, source_target_pairs={{0,12},{4,8},{8,4},{12,0},{1,13},{5,9},{9,5},{13,1},{2,14},{6,10},... | collective-permute-start | bytes 786440 | tf_op jit(solution)/shard_map/ppermute | solution.py:268
  23.7 12.7 %collective-permute-start.10 = (f32[4,8,2048]{2,1,0:T(8,128)S(1)}, f32[4,8,2048]{2,1,0:T(8,128)S(1)}, u32[]{:S(2)}, u32[]{:S(2)}) collective-permute-start(f32[4,8,2048]{2,1,0:T(8,128)S(1)} %pad_maximum_fusion.13), channel_id=1, source_target_pairs={{0,12},{4,8},{8,4},{12,0},{1,13},{5,9},{9,5},{13,1},{2,14},{6,10},... | collective-permute-start | bytes 786440 | tf_op jit(solution)/shard_map/ppermute | solution.py:268
  26.4 7.1 %collective-permute-start.12 = (f32[4,8,2048]{2,1,0:T(8,128)S(1)}, f32[4,8,2048]{2,1,0:T(8,128)S(1)}, u32[]{:S(2)}, u32[]{:S(2)}) collective-permute-start(f32[4,8,2048]{2,1,0:T(8,128)S(1)} %pad_maximum_fusion.14), channel_id=1, source_target_pairs={{0,1},{1,0},{2,3},{3,2},{4,5},{5,4},{6,7},{7,6},{8,9},{9,8},{10,11... | collective-permute-start | bytes 786440 | tf_op jit(solution)/shard_map/ppermute | solution.py:268
  29.2 6.9 %collective-permute-start.8 = (f32[4,8,2048]{2,1,0:T(8,128)S(1)}, f32[4,8,2048]{2,1,0:T(8,128)S(1)}, u32[]{:S(2)}, u32[]{:S(2)}) collective-permute-start(f32[4,8,2048]{2,1,0:T(8,128)S(1)} %pad_maximum_fusion.12), channel_id=1, source_target_pairs={{0,4},{4,0},{8,12},{12,8},{1,5},{5,1},{9,13},{13,9},{2,6},{6,2},{1... | collective-permute-start | bytes 786440 | tf_op jit(solution)/shard_map/ppermute | solution.py:268
  33.4 11.0 %collective-permute-start.15 = (f32[8,8,2048]{2,1,0:T(8,128)S(1)}, f32[8,8,2048]{2,1,0:T(8,128)S(1)}, u32[]{:S(2)}, u32[]{:S(2)}) collective-permute-start(f32[8,8,2048]{2,1,0:T(8,128)S(1)} %pad_maximum_fusion.3.refs_3_), channel_id=1, source_target_pairs={{0,4},{4,0},{8,12},{12,8},{1,5},{5,1},{9,13},{13,9},{2,6},{6,2},{1... | collective-permute-start | bytes 1572872 | tf_op jit(solution)/shard_map/ppermute | solution.py:268
  33.6 11.1 %collective-permute-start.13 = (f32[8,8,2048]{2,1,0:T(8,128)S(1)}, f32[8,8,2048]{2,1,0:T(8,128)S(1)}, u32[]{:S(2)}, u32[]{:S(2)}) collective-permute-start(f32[8,8,2048]{2,1,0:T(8,128)S(1)} %pad_maximum_fusion.2.refs_2_), channel_id=1, source_target_pairs={{0,3},{1,2},{2,1},{3,0},{4,7},{5,6},{6,5},{7,4},{8,11},{9,10},{10,... | collective-permute-start | bytes 1572872 | tf_op jit(solution)/shard_map/ppermute | solution.py:268
  36.2 9.3 %collective-permute-start.9 = (f32[8,8,2048]{2,1,0:T(8,128)S(1)}, f32[8,8,2048]{2,1,0:T(8,128)S(1)}, u32[]{:S(2)}, u32[]{:S(2)}) collective-permute-start(f32[8,8,2048]{2,1,0:T(8,128)S(1)} %pad_maximum_fusion.refs_0_), channel_id=1, source_target_pairs={{0,12},{4,8},{8,4},{12,0},{1,13},{5,9},{9,5},{13,1},{2,14},{6,10},... | collective-permute-start | bytes 1572872 | tf_op jit(solution)/shard_map/ppermute | solution.py:268
  36.4 9.1 %collective-permute-start.11 = (f32[8,8,2048]{2,1,0:T(8,128)S(1)}, f32[8,8,2048]{2,1,0:T(8,128)S(1)}, u32[]{:S(2)}, u32[]{:S(2)}) collective-permute-start(f32[8,8,2048]{2,1,0:T(8,128)S(1)} %pad_maximum_fusion.1.refs_1_), channel_id=1, source_target_pairs={{0,1},{1,0},{2,3},{3,2},{4,5},{5,4},{6,7},{7,6},{8,9},{9,8},{10,11... | collective-permute-start | bytes 1572872 | tf_op jit(solution)/shard_map/ppermute | solution.py:268
  45.5 30.7 %collective-permute-start.16 = (f32[4,8,2048]{2,1,0:T(8,128)S(1)}, f32[4,8,2048]{2,1,0:T(8,128)S(1)}, u32[]{:S(2)}, u32[]{:S(2)}) collective-permute-start(f32[4,8,2048]{2,1,0:T(8,128)S(1)} %get-tuple-element.27), channel_id=1, source_target_pairs={{0,4},{4,0},{8,12},{12,8},{1,5},{5,1},{9,13},{13,9},{2,6},{6,2},{1... | collective-permute-start | bytes 786440 | tf_op jit(solution)/shard_map/ppermute | solution.py:268
  46.2 30.0 %collective-permute-start.17 = (f32[4,8,2048]{2,1,0:T(8,128)S(1)}, f32[4,8,2048]{2,1,0:T(8,128)S(1)}, u32[]{:S(2)}, u32[]{:S(2)}) collective-permute-start(f32[4,8,2048]{2,1,0:T(8,128)S(1)} %get-tuple-element.28), channel_id=1, source_target_pairs={{0,12},{4,8},{8,4},{12,0},{1,13},{5,9},{9,5},{13,1},{2,14},{6,10},... | collective-permute-start | bytes 786440 | tf_op jit(solution)/shard_map/ppermute | solution.py:268
  48.3 27.9 %collective-permute-start.18 = (f32[4,8,2048]{2,1,0:T(8,128)S(1)}, f32[4,8,2048]{2,1,0:T(8,128)S(1)}, u32[]{:S(2)}, u32[]{:S(2)}) collective-permute-start(f32[4,8,2048]{2,1,0:T(8,128)S(1)} %get-tuple-element.29), channel_id=1, source_target_pairs={{0,1},{1,0},{2,3},{3,2},{4,5},{5,4},{6,7},{7,6},{8,9},{9,8},{10,11... | collective-permute-start | bytes 786440 | tf_op jit(solution)/shard_map/ppermute | solution.py:268
  48.4 27.8 %collective-permute-start.19 = (f32[4,8,2048]{2,1,0:T(8,128)S(1)}, f32[4,8,2048]{2,1,0:T(8,128)S(1)}, u32[]{:S(2)}, u32[]{:S(2)}) collective-permute-start(f32[4,8,2048]{2,1,0:T(8,128)S(1)} %get-tuple-element.30), channel_id=1, source_target_pairs={{0,3},{1,2},{2,1},{3,0},{4,7},{5,6},{6,5},{7,4},{8,11},{9,10},{10,... | collective-permute-start | bytes 786440 | tf_op jit(solution)/shard_map/ppermute | solution.py:268
  60.8 45.4 %collective-permute-start.24 = (f32[4,16,64,128]{3,2,1,0:T(8,128)}, f32[4,16,64,128]{3,2,1,0:T(8,128)S(1)}, u32[]{:S(2)}, u32[]{:S(2)}) collective-permute-start(f32[4,16,64,128]{3,2,1,0:T(8,128)} %shard_map.107), channel_id=1, source_target_pairs={{0,16},{16,0},{1,17},{17,1},{2,18},{18,2},{3,19},{19,3},{4,20},{20... | collective-permute-start | bytes 6291464 | tf_op jit(solution)/shard_map/ppermute | solution.py:314
  76.3 15.4 %collective-permute-start.23 = (f32[8,8,2048]{2,1,0:T(8,128)S(1)}, f32[8,8,2048]{2,1,0:T(8,128)S(1)}, u32[]{:S(2)}, u32[]{:S(2)}) collective-permute-start(f32[8,8,2048]{2,1,0:T(8,128)S(1)} %constant_dynamic-update-slice_fusion.6.refs_3_), channel_id=1, source_target_pairs={{0,4},{4,0},{8,12},{12,8},{1,5},{5,1},{9,13},{13,9},{2,6},{6,2},{1... | collective-permute-start | bytes 1572872 | tf_op jit(solution)/shard_map/ppermute | solution.py:268
  76.4 15.3 %collective-permute-start.22 = (f32[8,8,2048]{2,1,0:T(8,128)S(1)}, f32[8,8,2048]{2,1,0:T(8,128)S(1)}, u32[]{:S(2)}, u32[]{:S(2)}) collective-permute-start(f32[8,8,2048]{2,1,0:T(8,128)S(1)} %constant_dynamic-update-slice_fusion.4.refs_2_), channel_id=1, source_target_pairs={{0,3},{1,2},{2,1},{3,0},{4,7},{5,6},{6,5},{7,4},{8,11},{9,10},{10,... | collective-permute-start | bytes 1572872 | tf_op jit(solution)/shard_map/ppermute | solution.py:268
  77.9 13.8 %collective-permute-start.21 = (f32[8,8,2048]{2,1,0:T(8,128)S(1)}, f32[8,8,2048]{2,1,0:T(8,128)S(1)}, u32[]{:S(2)}, u32[]{:S(2)}) collective-permute-start(f32[8,8,2048]{2,1,0:T(8,128)S(1)} %constant_dynamic-update-slice_fusion.2.refs_1_), channel_id=1, source_target_pairs={{0,1},{1,0},{2,3},{3,2},{4,5},{5,4},{6,7},{7,6},{8,9},{9,8},{10,11... | collective-permute-start | bytes 1572872 | tf_op jit(solution)/shard_map/ppermute | solution.py:268
  78.3 14.0 %collective-permute-start.20 = (f32[8,8,2048]{2,1,0:T(8,128)S(1)}, f32[8,8,2048]{2,1,0:T(8,128)S(1)}, u32[]{:S(2)}, u32[]{:S(2)}) collective-permute-start(f32[8,8,2048]{2,1,0:T(8,128)S(1)} %constant_dynamic-update-slice_fusion.refs_0_), channel_id=1, source_target_pairs={{0,12},{4,8},{8,4},{12,0},{1,13},{5,9},{9,5},{13,1},{2,14},{6,10},... | collective-permute-start | bytes 1572872 | tf_op jit(solution)/shard_map/ppermute | solution.py:268
  104.4 18.5 %collective-permute-start.29 = (f32[4,16,64,128]{3,2,1,0:T(8,128)}, f32[4,16,64,128]{3,2,1,0:T(8,128)S(1)}, u32[]{:S(2)}, u32[]{:S(2)}) collective-permute-start(f32[4,16,64,128]{3,2,1,0:T(8,128)} %shard_map.105), channel_id=1, source_target_pairs={{0,16},{16,0},{1,17},{17,1},{2,18},{18,2},{3,19},{19,3},{4,20},{20... | collective-permute-start | bytes 6291464 | tf_op jit(solution)/shard_map/ppermute | solution.py:314
  107.0 26.9 %collective-permute-start.25 = (f32[8,64,128]{2,1,0:T(8,128)}, f32[8,64,128]{2,1,0:T(8,128)S(1)}, u32[]{:S(2)}, u32[]{:S(2)}) collective-permute-start(f32[8,64,128]{2,1,0:T(8,128)} %get-tuple-element.38), channel_id=1, source_target_pairs={{0,32},{32,64},{64,96},{96,0},{1,33},{33,65},{65,97},{97,1},{2,34}... | collective-permute-start | bytes 786440 | tf_op jit(solution)/shard_map/ppermute | solution.py:332
  108.7 25.3 %collective-permute-start.26 = (f32[8,64,128]{2,1,0:T(8,128)S(1)}, f32[8,64,128]{2,1,0:T(8,128)S(1)}, u32[]{:S(2)}, u32[]{:S(2)}) collective-permute-start(f32[8,64,128]{2,1,0:T(8,128)S(1)} %get-tuple-element.39), channel_id=1, source_target_pairs={{0,96},{32,0},{64,32},{96,64},{1,97},{33,1},{65,33},{97,65},{2,98}... | collective-permute-start | bytes 786440 | tf_op jit(solution)/shard_map/ppermute | solution.py:333
  126.0 12.3 %collective-permute-start.30 = (f32[8,64,128]{2,1,0:T(8,128)}, f32[8,64,128]{2,1,0:T(8,128)S(1)}, u32[]{:S(2)}, u32[]{:S(2)}) collective-permute-start(f32[8,64,128]{2,1,0:T(8,128)} %get-tuple-element.42), channel_id=1, source_target_pairs={{0,32},{32,64},{64,96},{96,0},{1,33},{33,65},{65,97},{97,1},{2,34}... | collective-permute-start | bytes 786440 | tf_op jit(solution)/shard_map/ppermute | solution.py:332
  126.0 12.3 %collective-permute-start.31 = (f32[8,64,128]{2,1,0:T(8,128)}, f32[8,64,128]{2,1,0:T(8,128)}, u32[]{:S(2)}, u32[]{:S(2)}) collective-permute-start(f32[8,64,128]{2,1,0:T(8,128)} %get-tuple-element.44), channel_id=1, source_target_pairs={{0,96},{32,0},{64,32},{96,64},{1,97},{33,1},{65,33},{97,65},{2,98}... | collective-permute-start | bytes 786440 | tf_op jit(solution)/shard_map/ppermute | solution.py:333
  135.6 27.7 %collective-permute-start.27 = (f32[16,64,128]{2,1,0:T(8,128)}, f32[16,64,128]{2,1,0:T(8,128)S(1)}, u32[]{:S(2)}, u32[]{:S(2)}) collective-permute-start(f32[16,64,128]{2,1,0:T(8,128)} %get-tuple-element.40), channel_id=1, source_target_pairs={{0,32},{32,64},{64,96},{96,0},{1,33},{33,65},{65,97},{97,1},{2,34}... | collective-permute-start | bytes 1572872 | tf_op jit(solution)/shard_map/ppermute | solution.py:337
  135.6 27.7 %collective-permute-start.28 = (f32[16,64,128]{2,1,0:T(8,128)}, f32[16,64,128]{2,1,0:T(8,128)S(1)}, u32[]{:S(2)}, u32[]{:S(2)}) collective-permute-start(f32[16,64,128]{2,1,0:T(8,128)} %get-tuple-element.41), channel_id=1, source_target_pairs={{0,96},{32,0},{64,32},{96,64},{1,97},{33,1},{65,33},{97,65},{2,98}... | collective-permute-start | bytes 1572872 | tf_op jit(solution)/shard_map/ppermute | solution.py:338
  140.4 22.8 %collective-permute-start.32 = (f32[16,64,128]{2,1,0:T(8,128)}, f32[16,64,128]{2,1,0:T(8,128)}, u32[]{:S(2)}, u32[]{:S(2)}) collective-permute-start(f32[16,64,128]{2,1,0:T(8,128)} %get-tuple-element.45), channel_id=1, source_target_pairs={{0,32},{32,64},{64,96},{96,0},{1,33},{33,65},{65,97},{97,1},{2,34}... | collective-permute-start | bytes 1572872 | tf_op jit(solution)/shard_map/ppermute | solution.py:337
  140.4 22.9 %collective-permute-start.33 = (f32[16,64,128]{2,1,0:T(8,128)}, f32[16,64,128]{2,1,0:T(8,128)}, u32[]{:S(2)}, u32[]{:S(2)}) collective-permute-start(f32[16,64,128]{2,1,0:T(8,128)} %get-tuple-element.46), channel_id=1, source_target_pairs={{0,96},{32,0},{64,32},{96,64},{1,97},{33,1},{65,33},{97,65},{2,98}... | collective-permute-start | bytes 1572872 | tf_op jit(solution)/shard_map/ppermute | solution.py:338
  (19 other events, 152.5 us)

commit v4 on v3

v4 whole, which is shorter than its diff:
```python
import functools

import jax
import jax.numpy as jnp
from jax import lax
from jax.experimental import pallas as pl
from jax.experimental.pallas import tpu as pltpu
from jax.sharding import Mesh, PartitionSpec as P

TILE = 128
RB = 512
VT = 256
ROWS = 128
TPD = 16
CAP = 16
NZ = 4
PARTS = 2
PART = TPD // PARTS
COLOURS = 4
NB = 256
SLOTS = 3
MIB = 1 << 20

f32 = jnp.float32
bf16 = jnp.bfloat16


def split(x):
    hi = x.astype(bf16)
    return hi, (x - hi.astype(f32)).astype(bf16)


def call(kernel, out_shape, *, vmem=16, flops=0, nbytes=0, **kw):
    return pl.pallas_call(
        kernel,
        out_shape=out_shape,
        compiler_params=pltpu.CompilerParams(vmem_limit_bytes=vmem * MIB),
        cost_estimate=pl.CostEstimate(flops=flops, bytes_accessed=nbytes, transcendentals=0),
        **kw,
    )


def masked_split(mask_ref, x_ref, mi, mj, i, j):
    m = mask_ref[mi, mj].astype(f32)
    return split(x_ref[i * TILE : (i + 1) * TILE, j * TILE : (j + 1) * TILE] * m)


def cycle_kernel(mask_ref, x_ref, hi_ref, lo_ref):
    for i in range(RB // TILE):
        for j in range(RB // TILE):
            hi, lo = masked_split(mask_ref, x_ref, pl.program_id(0) * (RB // TILE) + i, j, i, j)
            at = (slice(i * TILE, (i + 1) * TILE), slice(j * TILE, (j + 1) * TILE))
            hi_ref[at] = hi
            lo_ref[at] = lo


def prepare_cycle(x, mask):
    spec = pl.BlockSpec((RB, RB), lambda n: (n, 0))
    out = jax.ShapeDtypeStruct(x.shape, bf16)
    return call(
        cycle_kernel,
        (out, out),
        grid=(x.shape[0] // RB,),
        in_specs=[pl.BlockSpec(memory_space=pltpu.SMEM), spec],
        out_specs=(spec, spec),
        nbytes=x.size * 8,
        flops=x.size * 4,
    )(mask, x)


def mm_body(first, mask_ref, ah, al, b_ref, o_ref, slots, sems, before):
    per = NB // TILE
    blocks = PART // per

    def fetch(n):
        slot = n % SLOTS
        at = pl.ds(pl.multiple_of((first + n) * NB, NB), NB)
        return pltpu.make_async_copy(b_ref.at[:, at], slots.at[slot], sems.at[slot])

    for n in range(SLOTS):
        fetch(n).start()
    before()
    dot = functools.partial(jnp.dot, preferred_element_type=f32)
    tiles = range(b_ref.shape[0] // TILE)

    def step(n, carry):
        fetch(n).wait()
        x = slots.at[n % SLOTS]
        terms = [[masked_split(mask_ref, x, i, (first + n) * per + j, i, j) for j in range(per)] for i in tiles]
        bh, bl = (jnp.concatenate([jnp.concatenate([t[k] for t in row], axis=1) for row in terms], axis=0) for k in range(2))
        acc = dot(ah[...], bh) + dot(ah[...], bl) + dot(al[...], bh)
        for i in range(NZ):
            for t in range(per):
                o_ref[i, n * per + t] = acc[ROWS * i : ROWS * (i + 1), t * TILE : (t + 1) * TILE]

        @pl.when(n + SLOTS < blocks)
        def _():
            fetch(n + SLOTS).start()

        return carry

    lax.fori_loop(0, blocks, step, 0)


def mm_first_kernel(where_ref, mask_ref, *refs):
    held, b_ref, o_ref, ah, al, slots, sems = refs[:-6], *refs[-6:]
    near, late = held[:COLOURS], held[COLOURS:]
    rows = ROWS // 2 // COLOURS

    def gather_rows():
        for s in range(2 * NZ):
            for c in range(COLOURS):
                w = where_ref[c, s]
                mine = near[c][jnp.minimum(w, 7)]
                hi, lo = split(jnp.where(w < 8, mine, late[c][jnp.maximum(w - 8, 0)]))
                at = slice((s * COLOURS + c) * rows, (s * COLOURS + c + 1) * rows)
                ah[at, :] = hi
                al[at, :] = lo

    mm_body(0, mask_ref, ah, al, b_ref, o_ref, slots, sems, gather_rows)


def mm_next_kernel(mask_ref, ah, al, b_ref, o_ref, slots, sems, *, first):
    mm_body(first, mask_ref, ah, al, b_ref, o_ref, slots, sems, lambda: None)


SMEM = pl.BlockSpec(memory_space=pltpu.SMEM)
VMEM = pl.BlockSpec(memory_space=pltpu.VMEM)


def multiply(kernel, inputs, integrals, keep):
    depth, _ = integrals.shape
    m = NZ * ROWS
    shapes = [jax.ShapeDtypeStruct((NZ, PART, ROWS, TILE), f32)]
    shapes += [jax.ShapeDtypeStruct((m, depth), bf16)] * (2 if keep else 0)
    return call(
        kernel,
        tuple(shapes),
        in_specs=[SMEM if x.dtype == jnp.int32 else VMEM for x in inputs] + [pl.BlockSpec(memory_space=pltpu.HBM)],
        out_specs=(VMEM,) * len(shapes),
        scratch_shapes=[pltpu.VMEM((SLOTS, depth, NB), f32), pltpu.SemaphoreType.DMA((SLOTS,))],
        vmem=40,
        flops=40 * 6 * m * depth * PART * TILE,
        nbytes=4 * depth * PART * TILE,
    )(*inputs, integrals)


def far_kernel(mine_ref, got_ref, p_ref, m_ref, plus_ref, minus_ref, own_ref):
    half = PART // 2
    p_ref[...] = mine_ref[0, :half] + got_ref[0, :half]
    m_ref[...] = mine_ref[0, half:] + got_ref[0, half:]
    plus_ref[...] = mine_ref[1] + got_ref[1]
    minus_ref[...] = mine_ref[2] + got_ref[2]
    own_ref[...] = mine_ref[3] + got_ref[3]


def small(kernel, inputs, shapes, scratch=()):
    shapes = tuple(jax.ShapeDtypeStruct(s, f32) for s in shapes)
    return call(
        kernel,
        shapes,
        in_specs=[SMEM if x.dtype == jnp.int32 else VMEM for x in inputs],
        out_specs=(VMEM,) * len(shapes),
        scratch_shapes=[pltpu.VMEM(s, f32) for s in scratch],
        nbytes=4 * sum(x.size for x in inputs),
    )(*inputs)


def far(mine, got):
    part = (PART, ROWS, TILE)
    half = (PART // 2, ROWS, TILE)
    return small(far_kernel, (mine, got), (half, half, part, part, part))


def near_kernel(plus_ref, minus_ref, gp_ref, gm_ref, p_ref, m_ref):
    half = PART // 2
    p_ref[:half] = plus_ref[:half] + gp_ref[...]
    p_ref[half:] = plus_ref[half:]
    m_ref[:half] = minus_ref[:half]
    m_ref[half:] = minus_ref[half:] + gm_ref[...]


def near(plus, minus, gp, gm):
    return small(near_kernel, (plus, minus, gp, gm), (plus.shape, plus.shape))


def gather_kernel(idx_ref, *refs):
    ins, (out_ref, scr) = refs[:-2], refs[-2:]
    for p in range(PARTS):
        own, rp, rm = ins[3 * p : 3 * p + 3]
        for t in range(PART):
            at = (p * PART + t) * ROWS
            scr[at : at + ROWS, :] = own[t] + rp[t] + rm[t]

    def step(g, carry):
        for k in range(CAP):
            out_ref[pl.ds(g * CAP + k, 1), :] = scr[pl.ds(idx_ref[g * CAP + k], 1), :]
        return carry

    lax.fori_loop(0, ROWS * TPD // CAP, step, 0)


def gather(idx, parts):
    units = ROWS * TPD
    flat = [x for part in parts for x in part]
    return small(gather_kernel, (idx, *flat), ((units, TILE),), ((units, TILE),))[0]


def finish_kernel(place_ref, got_ref, den_ref, ch_ref, cl_ref, up_ref, ct_ref, scr):
    def step(g, carry):
        for k in range(CAP):
            scr[pl.ds(place_ref[g * CAP + k], 1), :] = got_ref[pl.ds(g * CAP + k, 1), :]
        return carry

    lax.fori_loop(0, ROWS * TPD // CAP, step, 0)
    for t in range(TPD):
        at = slice(t * TILE, (t + 1) * TILE)
        up_ref[:, at] = scr[at, :] / den_ref[:, at]
    dot = functools.partial(jnp.dot, preferred_element_type=f32)
    for k in range(TPD * TILE // RB):
        at = slice(k * RB, (k + 1) * RB)
        hi, lo = split(up_ref[:, at])
        ct_ref[:, at] = dot(hi, ch_ref[at, :]) + dot(hi, cl_ref[at, :]) + dot(lo, ch_ref[at, :])


def finish(place, got, den, ch, cl):
    shape = jax.ShapeDtypeStruct(den.shape, f32)
    whole = lambda s: pl.BlockSpec(s, lambda n: (0, 0))
    return call(
        finish_kernel,
        (shape, shape),
        grid=(1,),
        in_specs=[pl.BlockSpec(memory_space=pltpu.SMEM), whole(got.shape), whole(den.shape), whole(ch.shape), whole(cl.shape)],
        out_specs=(whole(den.shape), whole(den.shape)),
        scratch_shapes=[pltpu.VMEM((ROWS * TPD, TILE), f32)],
        nbytes=8 << 20,
    )(place, got, den, ch, cl)


def plan(destination):
    flat = destination.reshape(-1)
    out_row = flat // VT
    out_tile = flat % VT
    owner = out_row // ROWS * (VT // TPD) + out_tile // TPD
    place = out_tile % TPD * ROWS + out_row % ROWS
    unit = jnp.arange(ROWS * TPD, dtype=jnp.int32)
    row, tile = unit // TPD, unit % TPD
    at = tile * ROWS + row
    key = lax.sort((owner << 22) | (at << 11) | place)
    return (key >> 11) & 2047, key & 2047


def ring(step):
    return [(i, (i + step) % NZ) for i in range(NZ)]


EVEN = [(i, i ^ 1) for i in range(4)]
ODD = [(i, i ^ 3) for i in range(4)]
EXCHANGES = {"xe": ("x", EVEN), "xo": ("x", ODD), "ye": ("y", EVEN), "yo": ("y", ODD)}
ORDERS = [["xe", "xo", "ye", "yo"], ["xo", "ye", "yo", "xe"], ["ye", "yo", "xe", "xo"], ["yo", "xe", "xo", "ye"]]


def exchange(value, name):
    axis, pairs = EXCHANGES[name]
    return lax.ppermute(value, axis, pairs)


def places(ys, xs):
    dx = lax.axis_index("x") ^ xs
    dy = lax.axis_index("y") ^ ys
    bits = {"xe": (dx & 1) ^ (dx >> 1), "xo": dx >> 1, "ye": (dy & 1) ^ (dy >> 1), "yo": dy >> 1}
    return jnp.stack([sum(bits[name] << k for k, name in enumerate(order)) for order in ORDERS])


def after(value, *others):
    return lax.optimization_barrier((value,) + others)[0]


def body(amplitudes, integrals, integral_mask, denominators, cycle_tiles, cycle_mask, destination):
    everyone = ("z", "core", "y", "x")
    z = lax.axis_index("z")
    core = lax.axis_index("core")
    depth = integrals.shape[0]

    towards = jnp.repeat(jnp.array([2, 1, 3, 0], jnp.int32), 2)
    shard = jnp.array([0, 1] * NZ, jnp.int32)
    ys = (z + towards) % NZ
    own = places(ys, 2 * core + shard)
    other = places(ys, 2 * (1 - core) + shard)

    rows = amplitudes.reshape(COLOURS, 1, 64 // COLOURS, depth)
    bufs = [rows[c] for c in range(COLOURS)]

    def exchanged(k):
        got = [exchange(bufs[c], ORDERS[c][k]) for c in range(COLOURS)]
        return got, [jnp.concatenate([b, g], axis=0) for b, g in zip(bufs, got)]

    _, bufs = exchanged(0)
    got, bufs = exchanged(1)
    source, place = plan(after(destination, *got))
    _, bufs = exchanged(2)
    bufs[-1], source, place = lax.optimization_barrier((bufs[-1], source, place))
    late = [exchange(bufs[c], ORDERS[c][3]) for c in range(COLOURS)]
    held = (*bufs, *late)

    place = place.astype(f32).reshape(128, 1, CAP)
    got_place = lax.all_to_all(place, everyone, split_axis=0, concat_axis=0, tiled=True)
    got_place = got_place.reshape(-1).astype(jnp.int32)
    ch, cl = prepare_cycle(after(cycle_tiles, *bufs), cycle_mask)
    other, got_place, ch, cl, source = lax.optimization_barrier((other, got_place, ch, cl, source))

    def swap(value):
        return lax.ppermute(value, "core", [(0, 1), (1, 0)])

    def along_z(p, m):
        return lax.ppermute(p, "z", ring(1)), lax.ppermute(m, "z", ring(-1))

    def first_product(where):
        return multiply(mm_first_kernel, (where, integral_mask, *held), integrals, True)

    def next_product(mask, hi, lo):
        kernel = functools.partial(mm_next_kernel, first=PART * TILE // NB)
        return multiply(kernel, (mask, hi, lo), integrals, False)[0]

    theirs0, other_hi, other_lo = first_product(other)
    from_core0 = swap(theirs0)
    mine0, own_hi, own_lo = first_product(after(own, theirs0))
    p0, m0, plus0, minus0, base0 = far(mine0, from_core0)
    gp0, gm0 = along_z(p0, m0)
    theirs1 = next_product(after(integral_mask, base0), other_hi, other_lo)
    from_core1 = swap(theirs1)
    near0 = near(plus0, minus0, gp0, gm0)
    rp0, rm0 = along_z(*near0)
    mine1 = next_product(after(integral_mask, *near0), own_hi, own_lo)
    p1, m1, plus1, minus1, base1 = far(mine1, from_core1)
    gp1, gm1 = along_z(p1, m1)
    rp1, rm1 = along_z(*near(plus1, minus1, after(gp1, rp0, rm0), gm1))

    sending = gather(source, ((base0, rp0, rm0), (base1, rp1, rm1))).reshape(128, CAP, TILE)
    units = lax.all_to_all(sending, everyone, split_axis=0, concat_axis=0, tiled=True)
    return finish(got_place, units.reshape(-1, TILE), denominators, ch, cl)


def solution(mesh):
    row, col = ("z", "core"), ("y", "x")
    split_mesh = Mesh(mesh.devices.reshape(4, 2, 4, 4), row + col)
    return jax.shard_map(
        body,
        mesh=split_mesh,
        in_specs=(P(col, row), P(row, col), P(row, col), P(row, col), P(col, None), P(col, None), P(row, col)),
        out_specs=(P(row, col), P(row, col)),
        check_vma=False,
    )
```

time: 203 us -> 192 us (0.946)
  blocking collectives: 45.2 us -> 27.2 us
  waiting for transfers between devices: 19.6 us -> 34.7 us
  local copies, waits for them, and re-layouts: 13.7 us -> 5.91 us
  starting transfers between devices: 51.2 us -> 44.4 us
  other arithmetic: 7.74 us -> 14.3 us
    all_to_all x1 -> x0, blocking collectives: 19.8 us -> none  [body(): lax.all_to_all(place, everyone, split_axis=0, concat_axis=0, tiled=True)]
    ppermute x8, waiting for transfers between devices: 0.02 us -> 16.3 us  [along_z(): return (lax.ppermute(p, 'z', ring(1)), lax.ppermute(m, 'z', ring(-1)))]
    all_to_all x0 -> x1, starting transfers between devices: none -> 16.3 us  [body(): lax.all_to_all(place, everyone, split_axis=0, concat_axis=0, tiled=True)]
    ppermute x2, starting transfers between devices: 17.2 us -> 1.56 us  [swap(): return lax.ppermute(value, 'core', [(0, 1), (1, 0)])]
    ppermute x24 -> x16, waiting for transfers between devices: 19.6 us -> 9.71 us  [exchange(): return lax.ppermute(value, axis, pairs)]
    all_to_all x0 -> x1, waiting for transfers between devices: none -> 8.65 us  [body(): lax.all_to_all(place, everyone, split_axis=0, concat_axis=0, tiled=True)]
    concatenate x14 -> x12, other arithmetic: 0.38 us -> 8.96 us  [exchanged(): return (got, [jnp.concatenate([b, g], axis=0) for b, g in zip(bufs, got)])]
    unnamed x40 -> x23, local copies, waits for them, and re-layouts: 12 us -> 3.66 us
  transfers between devices with their start and end apart: 34 -> 27, of which waited for: 7 -> 7; matrix products, arithmetic and copies ran while one was open for 5% -> 8% of each run, Pallas kernels for 27% -> 20%
where the time goes in v4:
time: 192 us
  Pallas kernels  64.2 us (33%)
  starting transfers between devices  44.4 us (23%)
  waiting for transfers between devices  34.7 us (18%)
  blocking collectives  27.2 us (14%)
  other arithmetic  14.3 us (7%)
  local copies, waits for them, and re-layouts  5.91 us (3%)
    pallas_call x4, Pallas kernels, multiply(): call(kernel, tuple(shapes), in_specs=[SMEM if x.dtype == jnp.int32 else V...  47.2 us
    all_to_all x1, blocking collectives, body(): lax.all_to_all(sending, everyone, split_axis=0, concat_axis=0, tiled=True)  27.2 us
    ppermute x8, waiting for transfers between devices, along_z(): return (lax.ppermute(p, 'z', ring(1)), lax.ppermute(m, 'z', ring(-1)))  16.3 us
    all_to_all x1, starting transfers between devices, body(): lax.all_to_all(place, everyone, split_axis=0, concat_axis=0, tiled=True)  16.3 us
    ppermute x16, starting transfers between devices, exchange(): return lax.ppermute(value, axis, pairs)  15.7 us
    ppermute x8, starting transfers between devices, along_z(): return (lax.ppermute(p, 'z', ring(1)), lax.ppermute(m, 'z', ring(-1)))  10.8 us
    pallas_call x5, Pallas kernels, small(): call(kernel, shapes, in_specs=[SMEM if x.dtype == jnp.int32 else VMEM for...  10.4 us
    ppermute x16, waiting for transfers between devices, exchange(): return lax.ppermute(value, axis, pairs)  9.71 us
  transfers between devices with their start and end apart: 27, of which 7 were waited for; matrix products, arithmetic and copies ran while one was open for 8% of the time, Pallas kernels for 20%

profile of v4, /device:TPU:1, one launch (start us, length us, event | category | flops | bytes accessed | tf_op | source)
XLA Modules:
  0.0 191.6 jit_solution(14739563287467582933)
XLA Ops:
  1.8 2.2 %collective-permute-start.7 = (f32[1,16,2048]{2,1,0:T(8,128)S(1)}, f32[1,16,2048]{2,1,0:T(8,128)S(1)}, u32[]{:S(2)}, u32[]{:S(2)}) collective-permute-start(f32[1,16,2048]{2,1,0:T(8,128)S(1)} %get-tuple-element.79), channel_id=1, source_target_pairs={{0,4},{4,0},{8,12},{12,8},{1,5},{5,1},{9,13},{13,9},{2,6},{6,2},{1... | collective-permute-start | bytes 393224 | tf_op jit(solution)/shard_map/ppermute | solution.py:265
  5.2 1.9 collective-permute-start
  7.1 1.8 collective-permute-start.5
  9.9 2.6 %collective-permute-start.4 = (f32[2,16,2048]{2,1,0:T(8,128)S(1)}, f32[2,16,2048]{2,1,0:T(8,128)S(1)}, u32[]{:S(2)}, u32[]{:S(2)}) collective-permute-start(f32[2,16,2048]{2,1,0:T(8,128)S(1)} %pad_maximum_fusion.9), channel_id=1, source_target_pairs={{0,3},{1,2},{2,1},{3,0},{4,7},{5,6},{6,5},{7,4},{8,11},{9,10},{10,... | collective-permute-start | bytes 786440 | tf_op jit(solution)/shard_map/ppermute | solution.py:265
  12.7 5.3 %collective-permute-done.4 = f32[2,16,2048]{2,1,0:T(8,128)S(1)} collective-permute-done((f32[2,16,2048]{2,1,0:T(8,128)S(1)}, f32[2,16,2048]{2,1,0:T(8,128)S(1)}, u32[]{:S(2)}, u32[]{:S(2)}) %collective-permute-start.4) | collective-permute-done | bytes 262176 | tf_op jit(solution)/shard_map/ppermute | solution.py:265
  19.9 1.2 collective-permute-start.2
  23.6 5.0 %sort.14 = (s32[2048]{0:T(1024)S(1)}, s32[2048]{0:T(1024)}) sort(s32[2048]{0:T(1024)S(1)} %fusion.10, s32[2048]{0:T(1024)S(1)} %iota.7), dimensions={0}, to_apply=%region_0.1 | sort | flops 22528 | bytes 32768 | tf_op jit(solution)/shard_map/sort | solution.py:249
  28.7 4.1 %collective-permute-done.2 = f32[4,16,2048]{2,1,0:T(8,128)} collective-permute-done((f32[4,16,2048]{2,1,0:T(8,128)S(1)}, f32[4,16,2048]{2,1,0:T(8,128)}, u32[]{:S(2)}, u32[]{:S(2)}) %collective-permute-start.2) | collective-permute-done | bytes 524320 | tf_op jit(solution)/shard_map/ppermute | solution.py:265
  34.0 2.1 %pad_maximum_fusion.2.refs_1_ = f32[8,16,2048]{2,1,0:T(8,128)} fusion(f32[4,16,2048]{2,1,0:T(8,128)} %collective-permute-done.10, f32[2,16,2048]{2,1,0:T(8,128)S(1)} %collective-permute-done.6, f32[1,16,2048]{2,1,0:T(8,128)S(1)} %collective-permute-done.5, f32[1,16,2048]{2,1,0:T(8,128)S(1)} %get-tuple-element.82), kind=kLoop, calls=%fused_computation.2 | loop fusion | flops 786432 | bytes 2097152 | tf_op jit(solution)/shard_map/concatenate | solution.py:296
  36.2 2.1 %pad_maximum_fusion.1.refs_0_ = f32[8,16,2048]{2,1,0:T(8,128)} fusion(f32[4,16,2048]{2,1,0:T(8,128)} %collective-permute-done.9, f32[2,16,2048]{2,1,0:T(8,128)S(1)} %collective-permute-done.4, f32[1,16,2048]{2,1,0:T(8,128)S(1)} %collective-permute-done.3, f32[1,16,2048]{2,1,0:T(8,128)S(1)} %get-tuple-element.80), kind=kLoop, calls=%fused_computation.1 | loop fusion | flops 786432 | bytes 2097152 | tf_op jit(solution)/shard_map/concatenate | solution.py:296
  39.8 1.8 collective-permute-start.14
  42.5 16.3 %all-to-all-start = ((f32[128,1,16]{2,1,0:T(1,128)}), f32[128,1,16]{2,1,0:T(1,128)S(1)}, u32[]{:S(2)}, u32[]{:S(2)}) async-start(f32[128,1,16]{2,1,0:T(1,128)} %bitcast.8), calls=%async_computation | async-start | bytes 131072 | tf_op jit(solution)/shard_map/all_to_all | solution.py:307
  58.9 2.2 %copy-done = f32[2048,512]{1,0:T(8,128)S(1)} copy-done((f32[2048,512]{1,0:T(8,128)S(1)}, f32[2048,512]{1,0:T(8,128)}, u32[]{:S(2)}) %copy-start) | copy-done | bytes 4194328
  61.1 1.6 shard_map.104
  62.7 1.4 copy-done.1
  64.0 8.6 %all-to-all-done = f32[128,1,16]{2,1,0:T(1,128)S(1)} async-done(((f32[128,1,16]{2,1,0:T(1,128)}), f32[128,1,16]{2,1,0:T(1,128)S(1)}, u32[]{:S(2)}, u32[]{:S(2)}) %all-to-all-start) | async-done | bytes 8224 | tf_op jit(solution)/shard_map/all_to_all | solution.py:307
  73.0 14.2 %shard_map.105 = (f32[4,8,128,128]{3,2,1,0:T(8,128)}, bf16[512,2048]{1,0:T(8,128)(2,1)S(1)}, bf16[512,2048]{1,0:T(8,128)(2,1)}) custom-call(s32[4,8]{1,0:T(4,128)S(1)} %pad_add_fusion.where_ref, s32[16,16]{1,0:T(8,128)S(1)} %copy-done.4, f32[8,16,2048]{2,1,0:T(8,128)} %pad_maximum_fusion.1.refs_0_, f32[8,16,2048]{2,1,0:T(8,128)} %pad_maximum_fusion.2.refs_1_, ...), custom_call_target="tpu_custom_call" | custom-call | flops 257698037760 | bytes 8388608 | tf_op jit(solution)/shard_map/pallas_call | solution.py:136
  88.1 12.1 %shard_map.106 = (f32[4,8,128,128]{3,2,1,0:T(8,128)S(1)}, bf16[512,2048]{1,0:T(8,128)(2,1)S(1)}, bf16[512,2048]{1,0:T(8,128)(2,1)}) custom-call(s32[4,8]{1,0:T(4,128)S(1)} %pad_add_fusion.1.where_ref, s32[16,16]{1,0:T(8,128)S(1)} %copy-done.4, f32[8,16,2048]{2,1,0:T(8,128)} %pad_maximum_fusion.1.refs_0_, f32[8,16,2048]{2,1,0:T(8,128)} %pad_maximum_fusion.2.refs_1_, ...), custom_call_target="tpu_custom_call" | custom-call | flops 257698037760 | bytes 8388608 | tf_op jit(solution)/shard_map/pallas_call | solution.py:136
  100.3 2.7 %shard_map.107 = (f32[4,128,128]{2,1,0:T(8,128)}, f32[4,128,128]{2,1,0:T(8,128)}, f32[8,128,128]{2,1,0:T(8,128)S(1)}, f32[8,128,128]{2,1,0:T(8,128)S(1)}, f32[8,128,128]{2,1,0:T(8,128)S(1)}) custom-call(f32[4,8,128,128]{3,2,1,0:T(8,128)S(1)} %get-tuple-element.53.mine_ref, f32[4,8,128,128]{3,2,1,0:T(8,128)} %collective-permute-done.16.got_ref), custom_call_target="tpu_custom_call" | custom-call | bytes 4194304 | tf_op jit(solution)/shard_map/pallas_call | solution.py:159
  103.7 2.0 %collective-permute-start.18 = (f32[4,128,128]{2,1,0:T(8,128)}, f32[4,128,128]{2,1,0:T(8,128)}, u32[]{:S(2)}, u32[]{:S(2)}) collective-permute-start(f32[4,128,128]{2,1,0:T(8,128)} %get-tuple-element.58), channel_id=1, source_target_pairs={{0,96},{32,0},{64,32},{96,64},{1,97},{33,1},{65,33},{97,65},{2,98}... | collective-permute-start | bytes 786440 | tf_op jit(solution)/shard_map/ppermute | solution.py:316
  105.7 11.1 %shard_map.110 = f32[4,8,128,128]{3,2,1,0:T(8,128)} custom-call(s32[16,16]{1,0:T(8,128)S(1)} %copy-done.4, bf16[512,2048]{1,0:T(8,128)(2,1)S(1)} %get-tuple-element.65.ah, bf16[512,2048]{1,0:T(8,128)(2,1)S(1)} %copy-done.6, f32[2048,2048]{1,0:T(8,128)} %b_ref.3), custom_call_target="tpu_custom_call" | custom-call | flops 257698037760 | bytes 8388608 | tf_op jit(solution)/shard_map/pallas_call | solution.py:136
  117.5 2.1 %shard_map.108 = (f32[8,128,128]{2,1,0:T(8,128)}, f32[8,128,128]{2,1,0:T(8,128)}) custom-call(f32[8,128,128]{2,1,0:T(8,128)S(1)} %get-tuple-element.55.plus_ref, f32[8,128,128]{2,1,0:T(8,128)S(1)} %get-tuple-element.56.minus_ref, f32[4,128,128]{2,1,0:T(8,128)} %collective-permute-done.17.gp_ref, f32[4,128,128]{2,1,0:T(8,128)} %collective-permute-done.18.gm_ref), custom_call_target="tpu_custom_call" | custom-call | bytes 1572864 | tf_op jit(solution)/shard_map/pallas_call | solution.py:159
  119.6 2.7 %collective-permute-start.20 = (f32[8,128,128]{2,1,0:T(8,128)}, f32[8,128,128]{2,1,0:T(8,128)}, u32[]{:S(2)}, u32[]{:S(2)}) collective-permute-start(f32[8,128,128]{2,1,0:T(8,128)} %get-tuple-element.60), channel_id=1, source_target_pairs={{0,96},{32,0},{64,32},{96,64},{1,97},{33,1},{65,33},{97,65},{2,98}... | collective-permute-start | bytes 1572872 | tf_op jit(solution)/shard_map/ppermute | solution.py:316
  122.2 9.8 %shard_map.109.mine_ref = f32[4,8,128,128]{3,2,1,0:T(8,128)S(1)} custom-call(s32[16,16]{1,0:T(8,128)S(1)} %copy-done.4, bf16[512,2048]{1,0:T(8,128)(2,1)S(1)} %get-tuple-element.62.ah, bf16[512,2048]{1,0:T(8,128)(2,1)S(1)} %copy-done.5, f32[2048,2048]{1,0:T(8,128)} %b_ref.3), custom_call_target="tpu_custom_call" | custom-call | flops 257698037760 | bytes 8388608 | tf_op jit(solution)/shard_map/pallas_call | solution.py:136
  132.0 1.9 shard_map.111
  134.0 2.7 %collective-permute-start.23 = (f32[4,128,128]{2,1,0:T(8,128)S(1)}, f32[4,128,128]{2,1,0:T(8,128)S(1)}, u32[]{:S(2)}, u32[]{:S(2)}) collective-permute-start(f32[4,128,128]{2,1,0:T(8,128)S(1)} %get-tuple-element.72), channel_id=1, source_target_pairs={{0,96},{32,0},{64,32},{96,64},{1,97},{33,1},{65,33},{97,65},{2,98}... | collective-permute-start | bytes 786440 | tf_op jit(solution)/shard_map/ppermute | solution.py:316
  136.6 5.8 %collective-permute-done.22.gp_ref = f32[4,128,128]{2,1,0:T(8,128)S(1)} collective-permute-done((f32[4,128,128]{2,1,0:T(8,128)S(1)}, f32[4,128,128]{2,1,0:T(8,128)S(1)}, u32[]{:S(2)}, u32[]{:S(2)}) %collective-permute-start.22) | collective-permute-done | bytes 262176 | tf_op jit(solution)/shard_map/ppermute | solution.py:316
  142.6 2.7 %collective-permute-start.25 = (f32[8,128,128]{2,1,0:T(8,128)S(1)}, f32[8,128,128]{2,1,0:T(8,128)S(1)}, u32[]{:S(2)}, u32[]{:S(2)}) collective-permute-start(f32[8,128,128]{2,1,0:T(8,128)S(1)} %get-tuple-element.74), channel_id=1, source_target_pairs={{0,96},{32,0},{64,32},{96,64},{1,97},{33,1},{65,33},{97,65},{2,98}... | collective-permute-start | bytes 1572872 | tf_op jit(solution)/shard_map/ppermute | solution.py:316
  145.3 10.5 %collective-permute-done.24.refs_4_ = f32[8,128,128]{2,1,0:T(8,128)S(1)} collective-permute-done((f32[8,128,128]{2,1,0:T(8,128)S(1)}, f32[8,128,128]{2,1,0:T(8,128)S(1)}, u32[]{:S(2)}, u32[]{:S(2)}) %collective-permute-start.24) | collective-permute-done | bytes 524320 | tf_op jit(solution)/shard_map/ppermute | solution.py:316
  155.8 3.6 %shard_map.113 = f32[2048,128]{1,0:T(8,128)S(1)} custom-call(s32[2048]{0:T(1024)S(1)} %get-tuple-element.49.idx_ref, f32[8,128,128]{2,1,0:T(8,128)S(1)} %get-tuple-element.54.refs_0_, f32[8,128,128]{2,1,0:T(8,128)} %collective-permute-done.19.refs_1_, f32[8,128,128]{2,1,0:T(8,128)} %collective-permute-done.20.refs_2_, ...), custom_call_target="tpu_custom_call" | custom-call | bytes 3153920 | tf_op jit(solution)/shard_map/pallas_call | solution.py:159
  159.4 27.2 %all_to_all.10 = f32[128,16,128]{2,1,0:T(8,128)S(1)} all-to-all(f32[128,16,128]{2,1,0:T(8,128)S(1)} %bitcast.27), channel_id=1, replica_groups=mesh['z'=4,'core'=2,'y'=4,'x'=4] {'z','core','y','x'}, dimensions={0} | all-to-all | bytes 2097152 | tf_op jit(solution)/shard_map/all_to_all | solution.py:340
  186.6 5.0 %shard_map.114 = (f32[128,2048]{1,0:T(8,128)}, f32[128,2048]{1,0:T(8,128)}) custom-call(s32[2048]{0:T(1024)S(1)} %convert_element_type.11.place_ref, f32[2048,128]{1,0:T(8,128)S(1)} %bitcast.28, f32[128,2048]{1,0:T(8,128)S(1)} %copy-done.3, bf16[2048,512]{1,0:T(8,128)(2,1)S(1)} %get-tuple-element.75.ch_ref, bf16[2048,512]{1,0:T(8,128)(2,1)S(1)} %copy-done.2), custom_call_target="tpu_custom_call" | custom-call | bytes 8388608 | tf_op jit(solution)/shard_map/pallas_call | solution.py:229
  (87 shorter events, 14.6 us)
Async XLA Ops:
  1.8 7.1 %collective-permute-start.7 = (f32[1,16,2048]{2,1,0:T(8,128)S(1)}, f32[1,16,2048]{2,1,0:T(8,128)S(1)}, u32[]{:S(2)}, u32[]{:S(2)}) collective-permute-start(f32[1,16,2048]{2,1,0:T(8,128)S(1)} %get-tuple-element.79), channel_id=1, source_target_pairs={{0,4},{4,0},{8,12},{12,8},{1,5},{5,1},{9,13},{13,9},{2,6},{6,2},{1... | collective-permute-start | bytes 393224 | tf_op jit(solution)/shard_map/ppermute | solution.py:265
  4.0 5.9 %collective-permute-start.3 = (f32[1,16,2048]{2,1,0:T(8,128)S(1)}, f32[1,16,2048]{2,1,0:T(8,128)S(1)}, u32[]{:S(2)}, u32[]{:S(2)}) collective-permute-start(f32[1,16,2048]{2,1,0:T(8,128)S(1)} %get-tuple-element.80), channel_id=1, source_target_pairs={{0,1},{1,0},{2,3},{3,2},{4,5},{5,4},{6,7},{7,6},{8,9},{9,8},{10,11... | collective-permute-start | bytes 393224 | tf_op jit(solution)/shard_map/ppermute | solution.py:265
  5.2 7.3 %collective-permute-start = (f32[1,16,2048]{2,1,0:T(8,128)S(1)}, f32[1,16,2048]{2,1,0:T(8,128)S(1)}, u32[]{:S(2)}, u32[]{:S(2)}) collective-permute-start(f32[1,16,2048]{2,1,0:T(8,128)S(1)} %get-tuple-element.81), channel_id=1, source_target_pairs={{0,12},{4,8},{8,4},{12,0},{1,13},{5,9},{9,5},{13,1},{2,14},{6,10},... | collective-permute-start | bytes 393224 | tf_op jit(solution)/shard_map/ppermute | solution.py:265
  7.1 5.5 %collective-permute-start.5 = (f32[1,16,2048]{2,1,0:T(8,128)S(1)}, f32[1,16,2048]{2,1,0:T(8,128)S(1)}, u32[]{:S(2)}, u32[]{:S(2)}) collective-permute-start(f32[1,16,2048]{2,1,0:T(8,128)S(1)} %get-tuple-element.82), channel_id=1, source_target_pairs={{0,3},{1,2},{2,1},{3,0},{4,7},{5,6},{6,5},{7,4},{8,11},{9,10},{10,... | collective-permute-start | bytes 393224 | tf_op jit(solution)/shard_map/ppermute | solution.py:265
  8.9 13.6 %collective-permute-start.8 = (f32[2,16,2048]{2,1,0:T(8,128)S(1)}, f32[2,16,2048]{2,1,0:T(8,128)S(1)}, u32[]{:S(2)}, u32[]{:S(2)}) collective-permute-start(f32[2,16,2048]{2,1,0:T(8,128)S(1)} %pad_maximum_fusion.11), channel_id=1, source_target_pairs={{0,12},{4,8},{8,4},{12,0},{1,13},{5,9},{9,5},{13,1},{2,14},{6,10},... | collective-permute-start | bytes 786440 | tf_op jit(solution)/shard_map/ppermute | solution.py:265
  9.9 8.1 %collective-permute-start.4 = (f32[2,16,2048]{2,1,0:T(8,128)S(1)}, f32[2,16,2048]{2,1,0:T(8,128)S(1)}, u32[]{:S(2)}, u32[]{:S(2)}) collective-permute-start(f32[2,16,2048]{2,1,0:T(8,128)S(1)} %pad_maximum_fusion.9), channel_id=1, source_target_pairs={{0,3},{1,2},{2,1},{3,0},{4,7},{5,6},{6,5},{7,4},{8,11},{9,10},{10,... | collective-permute-start | bytes 786440 | tf_op jit(solution)/shard_map/ppermute | solution.py:265
  12.5 7.4 %collective-permute-start.1 = (f32[2,16,2048]{2,1,0:T(8,128)S(1)}, f32[2,16,2048]{2,1,0:T(8,128)S(1)}, u32[]{:S(2)}, u32[]{:S(2)}) collective-permute-start(f32[2,16,2048]{2,1,0:T(8,128)S(1)} %pad_maximum_fusion.8), channel_id=1, source_target_pairs={{0,1},{1,0},{2,3},{3,2},{4,5},{5,4},{6,7},{7,6},{8,9},{9,8},{10,11... | collective-permute-start | bytes 786440 | tf_op jit(solution)/shard_map/ppermute | solution.py:265
  12.6 8.5 %collective-permute-start.6 = (f32[2,16,2048]{2,1,0:T(8,128)S(1)}, f32[2,16,2048]{2,1,0:T(8,128)S(1)}, u32[]{:S(2)}, u32[]{:S(2)}) collective-permute-start(f32[2,16,2048]{2,1,0:T(8,128)S(1)} %pad_maximum_fusion.10), channel_id=1, source_target_pairs={{0,4},{4,0},{8,12},{12,8},{1,5},{5,1},{9,13},{13,9},{2,6},{6,2},{1... | collective-permute-start | bytes 786440 | tf_op jit(solution)/shard_map/ppermute | solution.py:265
  18.8 17.4 %collective-permute-start.9 = (f32[4,16,2048]{2,1,0:T(8,128)}, f32[4,16,2048]{2,1,0:T(8,128)}, u32[]{:S(2)}, u32[]{:S(2)}) collective-permute-start(f32[4,16,2048]{2,1,0:T(8,128)} %pad_maximum_fusion.5), channel_id=1, source_target_pairs={{0,4},{4,0},{8,12},{12,8},{1,5},{5,1},{9,13},{13,9},{2,6},{6,2},{1... | collective-permute-start | bytes 1572872 | tf_op jit(solution)/shard_map/ppermute | solution.py:265
  19.9 12.8 %collective-permute-start.2 = (f32[4,16,2048]{2,1,0:T(8,128)S(1)}, f32[4,16,2048]{2,1,0:T(8,128)}, u32[]{:S(2)}, u32[]{:S(2)}) collective-permute-start(f32[4,16,2048]{2,1,0:T(8,128)S(1)} %pad_maximum_fusion.4), channel_id=1, source_target_pairs={{0,3},{1,2},{2,1},{3,0},{4,7},{5,6},{6,5},{7,4},{8,11},{9,10},{10,... | collective-permute-start | bytes 1572872 | tf_op jit(solution)/shard_map/ppermute | solution.py:265
  22.0 12.0 %collective-permute-start.10 = (f32[4,16,2048]{2,1,0:T(8,128)}, f32[4,16,2048]{2,1,0:T(8,128)}, u32[]{:S(2)}, u32[]{:S(2)}) collective-permute-start(f32[4,16,2048]{2,1,0:T(8,128)} %pad_maximum_fusion.6), channel_id=1, source_target_pairs={{0,12},{4,8},{8,4},{12,0},{1,13},{5,9},{9,5},{13,1},{2,14},{6,10},... | collective-permute-start | bytes 1572872 | tf_op jit(solution)/shard_map/ppermute | solution.py:265
  28.7 10.1 %collective-permute-start.11 = (f32[4,16,2048]{2,1,0:T(8,128)}, f32[4,16,2048]{2,1,0:T(8,128)S(1)}, u32[]{:S(2)}, u32[]{:S(2)}) collective-permute-start(f32[4,16,2048]{2,1,0:T(8,128)} %pad_maximum_fusion.7), channel_id=1, source_target_pairs={{0,1},{1,0},{2,3},{3,2},{4,5},{5,4},{6,7},{7,6},{8,9},{9,8},{10,11... | collective-permute-start | bytes 1572872 | tf_op jit(solution)/shard_map/ppermute | solution.py:265
  36.1 22.7 %copy-start.8 = (s32[16,4]{0,1:T(4,128)S(1)}, s32[16,4]{0,1:T(4,128)}, u32[]{:S(2)}) copy-start(s32[16,4]{0,1:T(4,128)} %param.14) | copy-start | bytes 772
  36.1 36.9 %collective-permute-start.13 = (f32[8,16,2048]{2,1,0:T(8,128)}, f32[8,16,2048]{2,1,0:T(8,128)}, u32[]{:S(2)}, u32[]{:S(2)}) collective-permute-start(f32[8,16,2048]{2,1,0:T(8,128)} %pad_maximum_fusion.2.refs_1_), channel_id=1, source_target_pairs={{0,1},{1,0},{2,3},{3,2},{4,5},{5,4},{6,7},{7,6},{8,9},{9,8},{10,11... | collective-permute-start | bytes 3145736 | tf_op jit(solution)/shard_map/ppermute | solution.py:265
  36.1 36.9 %collective-permute-start.15 = (f32[8,16,2048]{2,1,0:T(8,128)S(1)}, f32[8,16,2048]{2,1,0:T(8,128)}, u32[]{:S(2)}, u32[]{:S(2)}) collective-permute-start(f32[8,16,2048]{2,1,0:T(8,128)S(1)} %pad_maximum_fusion.refs_3_), channel_id=1, source_target_pairs={{0,4},{4,0},{8,12},{12,8},{1,5},{5,1},{9,13},{13,9},{2,6},{6,2},{1... | collective-permute-start | bytes 3145736 | tf_op jit(solution)/shard_map/ppermute | solution.py:265
  38.3 34.7 %collective-permute-start.12 = (f32[8,16,2048]{2,1,0:T(8,128)}, f32[8,16,2048]{2,1,0:T(8,128)}, u32[]{:S(2)}, u32[]{:S(2)}) collective-permute-start(f32[8,16,2048]{2,1,0:T(8,128)} %pad_maximum_fusion.1.refs_0_), channel_id=1, source_target_pairs={{0,12},{4,8},{8,4},{12,0},{1,13},{5,9},{9,5},{13,1},{2,14},{6,10},... | collective-permute-start | bytes 3145736 | tf_op jit(solution)/shard_map/ppermute | solution.py:265
  39.8 33.2 %collective-permute-start.14 = (f32[8,16,2048]{2,1,0:T(8,128)}, f32[8,16,2048]{2,1,0:T(8,128)}, u32[]{:S(2)}, u32[]{:S(2)}) collective-permute-start(f32[8,16,2048]{2,1,0:T(8,128)} %pad_maximum_fusion.3.refs_2_), channel_id=1, source_target_pairs={{0,3},{1,2},{2,1},{3,0},{4,7},{5,6},{6,5},{7,4},{8,11},{9,10},{10,... | collective-permute-start | bytes 3145736 | tf_op jit(solution)/shard_map/ppermute | solution.py:265
  42.5 30.2 %all-to-all-start = ((f32[128,1,16]{2,1,0:T(1,128)}), f32[128,1,16]{2,1,0:T(1,128)S(1)}, u32[]{:S(2)}, u32[]{:S(2)}) async-start(f32[128,1,16]{2,1,0:T(1,128)} %bitcast.8), calls=%async_computation | async-start | bytes 131072 | tf_op jit(solution)/shard_map/all_to_all | solution.py:307
  61.1 11.9 %copy-start.4 = (s32[16,16]{1,0:T(8,128)S(1)}, s32[16,16]{1,0:T(8,128)}, u32[]{:S(2)}) copy-start(s32[16,16]{1,0:T(8,128)} %mask_ref.6) | copy-start | bytes 3076
  87.2 13.1 %collective-permute-start.16 = (f32[4,8,128,128]{3,2,1,0:T(8,128)}, f32[4,8,128,128]{3,2,1,0:T(8,128)}, u32[]{:S(2)}, u32[]{:S(2)}) collective-permute-start(f32[4,8,128,128]{3,2,1,0:T(8,128)} %get-tuple-element.51), channel_id=1, source_target_pairs={{0,16},{16,0},{1,17},{17,1},{2,18},{18,2},{3,19},{19,3},{4,20},{20... | collective-permute-start | bytes 6291464 | tf_op jit(solution)/shard_map/ppermute | solution.py:313
  103.1 14.4 %collective-permute-start.17 = (f32[4,128,128]{2,1,0:T(8,128)}, f32[4,128,128]{2,1,0:T(8,128)}, u32[]{:S(2)}, u32[]{:S(2)}) collective-permute-start(f32[4,128,128]{2,1,0:T(8,128)} %get-tuple-element.57), channel_id=1, source_target_pairs={{0,32},{32,64},{64,96},{96,0},{1,33},{33,65},{65,97},{97,1},{2,34}... | collective-permute-start | bytes 786440 | tf_op jit(solution)/shard_map/ppermute | solution.py:316
  103.7 13.8 %collective-permute-start.18 = (f32[4,128,128]{2,1,0:T(8,128)}, f32[4,128,128]{2,1,0:T(8,128)}, u32[]{:S(2)}, u32[]{:S(2)}) collective-permute-start(f32[4,128,128]{2,1,0:T(8,128)} %get-tuple-element.58), channel_id=1, source_target_pairs={{0,96},{32,0},{64,32},{96,64},{1,97},{33,1},{65,33},{97,65},{2,98}... | collective-permute-start | bytes 786440 | tf_op jit(solution)/shard_map/ppermute | solution.py:316
  105.7 16.5 %copy-start.5 = (bf16[512,2048]{1,0:T(8,128)(2,1)S(1)}, bf16[512,2048]{1,0:T(8,128)(2,1)}, u32[]{:S(2)}) copy-start(bf16[512,2048]{1,0:T(8,128)(2,1)} %get-tuple-element.63.al) | copy-start | bytes 6291460
  116.8 15.2 %collective-permute-start.21 = (f32[4,8,128,128]{3,2,1,0:T(8,128)}, f32[4,8,128,128]{3,2,1,0:T(8,128)}, u32[]{:S(2)}, u32[]{:S(2)}) collective-permute-start(f32[4,8,128,128]{3,2,1,0:T(8,128)} %shard_map.110), channel_id=1, source_target_pairs={{0,16},{16,0},{1,17},{17,1},{2,18},{18,2},{3,19},{19,3},{4,20},{20... | collective-permute-start | bytes 6291464 | tf_op jit(solution)/shard_map/ppermute | solution.py:313
  119.5 17.1 %collective-permute-start.19 = (f32[8,128,128]{2,1,0:T(8,128)}, f32[8,128,128]{2,1,0:T(8,128)}, u32[]{:S(2)}, u32[]{:S(2)}) collective-permute-start(f32[8,128,128]{2,1,0:T(8,128)} %get-tuple-element.59), channel_id=1, source_target_pairs={{0,32},{32,64},{64,96},{96,0},{1,33},{33,65},{65,97},{97,1},{2,34}... | collective-permute-start | bytes 1572872 | tf_op jit(solution)/shard_map/ppermute | solution.py:316
  119.6 17.1 %collective-permute-start.20 = (f32[8,128,128]{2,1,0:T(8,128)}, f32[8,128,128]{2,1,0:T(8,128)}, u32[]{:S(2)}, u32[]{:S(2)}) collective-permute-start(f32[8,128,128]{2,1,0:T(8,128)} %get-tuple-element.60), channel_id=1, source_target_pairs={{0,96},{32,0},{64,32},{96,64},{1,97},{33,1},{65,33},{97,65},{2,98}... | collective-permute-start | bytes 1572872 | tf_op jit(solution)/shard_map/ppermute | solution.py:316
  133.9 8.5 %collective-permute-start.22 = (f32[4,128,128]{2,1,0:T(8,128)S(1)}, f32[4,128,128]{2,1,0:T(8,128)S(1)}, u32[]{:S(2)}, u32[]{:S(2)}) collective-permute-start(f32[4,128,128]{2,1,0:T(8,128)S(1)} %get-tuple-element.70), channel_id=1, source_target_pairs={{0,32},{32,64},{64,96},{96,0},{1,33},{33,65},{65,97},{97,1},{2,34}... | collective-permute-start | bytes 786440 | tf_op jit(solution)/shard_map/ppermute | solution.py:316
  134.0 8.5 %collective-permute-start.23 = (f32[4,128,128]{2,1,0:T(8,128)S(1)}, f32[4,128,128]{2,1,0:T(8,128)S(1)}, u32[]{:S(2)}, u32[]{:S(2)}) collective-permute-start(f32[4,128,128]{2,1,0:T(8,128)S(1)} %get-tuple-element.72), channel_id=1, source_target_pairs={{0,96},{32,0},{64,32},{96,64},{1,97},{33,1},{65,33},{97,65},{2,98}... | collective-permute-start | bytes 786440 | tf_op jit(solution)/shard_map/ppermute | solution.py:316
  142.5 13.2 %collective-permute-start.24 = (f32[8,128,128]{2,1,0:T(8,128)S(1)}, f32[8,128,128]{2,1,0:T(8,128)S(1)}, u32[]{:S(2)}, u32[]{:S(2)}) collective-permute-start(f32[8,128,128]{2,1,0:T(8,128)S(1)} %get-tuple-element.73), channel_id=1, source_target_pairs={{0,32},{32,64},{64,96},{96,0},{1,33},{33,65},{65,97},{97,1},{2,34}... | collective-permute-start | bytes 1572872 | tf_op jit(solution)/shard_map/ppermute | solution.py:316
  142.6 13.2 %collective-permute-start.25 = (f32[8,128,128]{2,1,0:T(8,128)S(1)}, f32[8,128,128]{2,1,0:T(8,128)S(1)}, u32[]{:S(2)}, u32[]{:S(2)}) collective-permute-start(f32[8,128,128]{2,1,0:T(8,128)S(1)} %get-tuple-element.74), channel_id=1, source_target_pairs={{0,96},{32,0},{64,32},{96,64},{1,97},{33,1},{65,33},{97,65},{2,98}... | collective-permute-start | bytes 1572872 | tf_op jit(solution)/shard_map/ppermute | solution.py:316
  155.8 30.9 %copy-start.3 = (f32[128,2048]{1,0:T(8,128)S(1)}, f32[128,2048]{1,0:T(8,128)}, u32[]{:S(2)}) copy-start(f32[128,2048]{1,0:T(8,128)} %den_ref.1) | copy-start | bytes 3145732
  159.4 27.2 %copy-start.2 = (bf16[2048,512]{1,0:T(8,128)(2,1)S(1)}, bf16[2048,512]{1,0:T(8,128)(2,1)}, u32[]{:S(2)}) copy-start(bf16[2048,512]{1,0:T(8,128)(2,1)} %copy-done.1) | copy-start | bytes 6291460
  (6 other events, 30.9 us)

commit v5 on v4

--- a/solution.py
+++ b/solution.py
@@ -14,8 +14,7 @@
 TPD = 16
 CAP = 16
 NZ = 4
-PARTS = 2
-PART = TPD // PARTS
+PARTS = (10, 6)
 COLOURS = 4
 NB = 256
 SLOTS = 3
@@ -68,9 +67,9 @@
     )(mask, x)
 
 
-def mm_body(first, mask_ref, ah, al, b_ref, o_ref, slots, sems, before):
+def mm_body(first, tiles_out, mask_ref, ah, al, b_ref, o_ref, slots, sems, before):
     per = NB // TILE
-    blocks = PART // per
+    blocks = tiles_out // per
 
     def fetch(n):
         slot = n % SLOTS
@@ -103,50 +102,70 @@
 
 
 def mm_first_kernel(where_ref, mask_ref, *refs):
-    held, b_ref, o_ref, ah, al, slots, sems = refs[:-6], *refs[-6:]
+    held, b_ref, o_ref, ah, al, slots, sems, stage, row_sems = refs[:-8], *refs[-8:]
     near, late = held[:COLOURS], held[COLOURS:]
     rows = ROWS // 2 // COLOURS
-
-    def gather_rows():
-        for s in range(2 * NZ):
-            for c in range(COLOURS):
-                w = where_ref[c, s]
-                mine = near[c][jnp.minimum(w, 7)]
-                hi, lo = split(jnp.where(w < 8, mine, late[c][jnp.maximum(w - 8, 0)]))
-                at = slice((s * COLOURS + c) * rows, (s * COLOURS + c + 1) * rows)
-                ah[at, :] = hi
-                al[at, :] = lo
-
-    mm_body(0, mask_ref, ah, al, b_ref, o_ref, slots, sems, gather_rows)
-
-
-def mm_next_kernel(mask_ref, ah, al, b_ref, o_ref, slots, sems, *, first):
-    mm_body(first, mask_ref, ah, al, b_ref, o_ref, slots, sems, lambda: None)
+    pieces = [(s, c) for s in range(2 * NZ) for c in range(COLOURS)]
+
+    def copy(i, src):
+        return pltpu.make_async_copy(src, stage.at[i], row_sems.at[i])
+
+    for i, (s, c) in enumerate(pieces):
+        w = where_ref[c, s]
+
+        @pl.when(w < 8)
+        def _(i=i, c=c, w=w):
+            copy(i, near[c].at[jnp.minimum(w, 7)]).start()
+
+        @pl.when(w >= 8)
+        def _(i=i, c=c, w=w):
+            copy(i, late[c].at[jnp.maximum(w - 8, 0)]).start()
+
+    def split_rows():
+        for i, (s, c) in enumerate(pieces):
+            copy(i, near[c].at[0]).wait()
+            hi, lo = split(stage[i])
+            at = slice(i * rows, (i + 1) * rows)
+            ah[at, :] = hi
+            al[at, :] = lo
+
+    mm_body(0, PARTS[0], mask_ref, ah, al, b_ref, o_ref, slots, sems, split_rows)
+
+
+def mm_next_kernel(mask_ref, ah, al, b_ref, o_ref, slots, sems):
+    mm_body(PARTS[0] * TILE // NB, PARTS[1], mask_ref, ah, al, b_ref, o_ref, slots, sems, lambda: None)
 
 
 SMEM = pl.BlockSpec(memory_space=pltpu.SMEM)
 VMEM = pl.BlockSpec(memory_space=pltpu.VMEM)
 
 
-def multiply(kernel, inputs, integrals, keep):
+HBM = pl.BlockSpec(memory_space=pltpu.HBM)
+
+
+def multiply(kernel, maps, rows, integrals, part, first):
     depth, _ = integrals.shape
     m = NZ * ROWS
-    shapes = [jax.ShapeDtypeStruct((NZ, PART, ROWS, TILE), f32)]
-    shapes += [jax.ShapeDtypeStruct((m, depth), bf16)] * (2 if keep else 0)
+    shapes = [jax.ShapeDtypeStruct((NZ, part, ROWS, TILE), f32)]
+    scratch = [pltpu.VMEM((SLOTS, depth, NB), f32), pltpu.SemaphoreType.DMA((SLOTS,))]
+    if first:
+        pieces = 2 * NZ * COLOURS
+        shapes += [jax.ShapeDtypeStruct((m, depth), bf16)] * 2
+        scratch += [pltpu.VMEM((pieces, m // pieces, depth), f32), pltpu.SemaphoreType.DMA((pieces,))]
     return call(
         kernel,
         tuple(shapes),
-        in_specs=[SMEM if x.dtype == jnp.int32 else VMEM for x in inputs] + [pl.BlockSpec(memory_space=pltpu.HBM)],
+        in_specs=[SMEM] * len(maps) + [HBM if first else VMEM] * len(rows) + [HBM],
         out_specs=(VMEM,) * len(shapes),
-        scratch_shapes=[pltpu.VMEM((SLOTS, depth, NB), f32), pltpu.SemaphoreType.DMA((SLOTS,))],
+        scratch_shapes=scratch,
         vmem=40,
-        flops=40 * 6 * m * depth * PART * TILE,
-        nbytes=4 * depth * PART * TILE,
-    )(*inputs, integrals)
+        flops=40 * 6 * m * depth * part * TILE,
+        nbytes=4 * depth * part * TILE,
+    )(*maps, *rows, integrals)
 
 
 def far_kernel(mine_ref, got_ref, p_ref, m_ref, plus_ref, minus_ref, own_ref):
-    half = PART // 2
+    half = p_ref.shape[0]
     p_ref[...] = mine_ref[0, :half] + got_ref[0, :half]
     m_ref[...] = mine_ref[0, half:] + got_ref[0, half:]
     plus_ref[...] = mine_ref[1] + got_ref[1]
@@ -167,13 +186,13 @@
 
 
 def far(mine, got):
-    part = (PART, ROWS, TILE)
-    half = (PART // 2, ROWS, TILE)
+    part = mine.shape[1:]
+    half = (part[0] // 2, ROWS, TILE)
     return small(far_kernel, (mine, got), (half, half, part, part, part))
 
 
 def near_kernel(plus_ref, minus_ref, gp_ref, gm_ref, p_ref, m_ref):
-    half = PART // 2
+    half = gp_ref.shape[0]
     p_ref[:half] = plus_ref[:half] + gp_ref[...]
     p_ref[half:] = plus_ref[half:]
     m_ref[:half] = minus_ref[:half]
@@ -186,10 +205,10 @@
 
 def gather_kernel(idx_ref, *refs):
     ins, (out_ref, scr) = refs[:-2], refs[-2:]
-    for p in range(PARTS):
+    for p, part in enumerate(PARTS):
         own, rp, rm = ins[3 * p : 3 * p + 3]
-        for t in range(PART):
-            at = (p * PART + t) * ROWS
+        for t in range(part):
+            at = (sum(PARTS[:p]) + t) * ROWS
             scr[at : at + ROWS, :] = own[t] + rp[t] + rm[t]
 
     def step(g, carry):
@@ -296,18 +315,16 @@
         return got, [jnp.concatenate([b, g], axis=0) for b, g in zip(bufs, got)]
 
     _, bufs = exchanged(0)
-    got, bufs = exchanged(1)
-    source, place = plan(after(destination, *got))
+    _, bufs = exchanged(1)
     _, bufs = exchanged(2)
-    bufs[-1], source, place = lax.optimization_barrier((bufs[-1], source, place))
     late = [exchange(bufs[c], ORDERS[c][3]) for c in range(COLOURS)]
     held = (*bufs, *late)
 
+    source, place = plan(after(destination, *bufs))
     place = place.astype(f32).reshape(128, 1, CAP)
     got_place = lax.all_to_all(place, everyone, split_axis=0, concat_axis=0, tiled=True)
     got_place = got_place.reshape(-1).astype(jnp.int32)
-    ch, cl = prepare_cycle(after(cycle_tiles, *bufs), cycle_mask)
-    other, got_place, ch, cl, source = lax.optimization_barrier((other, got_place, ch, cl, source))
+    other, got_place, source = lax.optimization_barrier((other, got_place, source))
 
     def swap(value):
         return lax.ppermute(value, "core", [(0, 1), (1, 0)])
@@ -316,11 +333,10 @@
         return lax.ppermute(p, "z", ring(1)), lax.ppermute(m, "z", ring(-1))
 
     def first_product(where):
-        return multiply(mm_first_kernel, (where, integral_mask, *held), integrals, True)
+        return multiply(mm_first_kernel, (where, integral_mask), held, integrals, PARTS[0], True)
 
     def next_product(mask, hi, lo):
-        kernel = functools.partial(mm_next_kernel, first=PART * TILE // NB)
-        return multiply(kernel, (mask, hi, lo), integrals, False)[0]
+        return multiply(mm_next_kernel, (mask,), (hi, lo), integrals, PARTS[1], False)[0]
 
     theirs0, other_hi, other_lo = first_product(other)
     from_core0 = swap(theirs0)
@@ -334,7 +350,8 @@
     mine1 = next_product(after(integral_mask, *near0), own_hi, own_lo)
     p1, m1, plus1, minus1, base1 = far(mine1, from_core1)
     gp1, gm1 = along_z(p1, m1)
-    rp1, rm1 = along_z(*near(plus1, minus1, after(gp1, rp0, rm0), gm1))
+    ch, cl = prepare_cycle(after(cycle_tiles, base1), cycle_mask)
+    rp1, rm1 = along_z(*near(plus1, minus1, after(gp1, rp0, rm0, ch, cl), gm1))
 
     sending = gather(source, ((base0, rp0, rm0), (base1, rp1, rm1))).reshape(128, CAP, TILE)
     units = lax.all_to_all(sending, everyone, split_axis=0, concat_axis=0, tiled=True)

time: 192 us -> 185 us (0.964)
  other arithmetic: 14.3 us -> 7.51 us
  Pallas kernels: 64.2 us -> 66.8 us
    concatenate x12, other arithmetic: 8.96 us -> 1.52 us  [exchanged(): return (got, [jnp.concatenate([b, g], axis=0) for b, g in zip(bufs, got)])]
    ppermute x8, waiting for transfers between devices: 16.3 us -> 11.4 us  [along_z(): return (lax.ppermute(p, 'z', ring(1)), lax.ppermute(m, 'z', ring(-1)))]
    all_to_all x1, starting transfers between devices: 16.3 us -> 13.3 us  [body(): lax.all_to_all(place, everyone, split_axis=0, concat_axis=0, tiled=True)]
    pallas_call x4, Pallas kernels: 47.2 us -> 50 us  [multiply(): call(kernel, tuple(shapes), in_specs=[SMEM] * len(maps) + [HBM if first e...]
    all_to_all x1, waiting for transfers between devices: 8.65 us -> 10.9 us  [body(): lax.all_to_all(place, everyone, split_axis=0, concat_axis=0, tiled=True)]
  transfers between devices with their start and end apart: 27 -> 27, of which waited for: 7 -> 6; matrix products, arithmetic and copies ran while one was open for 8% -> 5% of each run, Pallas kernels for 20% -> 21%
where the time goes in v5:
time: 185 us
  Pallas kernels  66.8 us (36%)
  starting transfers between devices  43.8 us (24%)
  waiting for transfers between devices  33.5 us (18%)
  blocking collectives  25.6 us (14%)
  other arithmetic  7.51 us (4%)
  local copies, waits for them, and re-layouts  6.32 us (3%)
    pallas_call x4, Pallas kernels, multiply(): call(kernel, tuple(shapes), in_specs=[SMEM] * len(maps) + [HBM if first e...  50 us
    all_to_all x1, blocking collectives, body(): lax.all_to_all(sending, everyone, split_axis=0, concat_axis=0, tiled=True)  25.6 us
    ppermute x16, starting transfers between devices, exchange(): return lax.ppermute(value, axis, pairs)  17.2 us
    all_to_all x1, starting transfers between devices, body(): lax.all_to_all(place, everyone, split_axis=0, concat_axis=0, tiled=True)  13.3 us
    ppermute x8, waiting for transfers between devices, along_z(): return (lax.ppermute(p, 'z', ring(1)), lax.ppermute(m, 'z', ring(-1)))  11.4 us
    ppermute x16, waiting for transfers between devices, exchange(): return lax.ppermute(value, axis, pairs)  11.2 us
    all_to_all x1, waiting for transfers between devices, body(): lax.all_to_all(place, everyone, split_axis=0, concat_axis=0, tiled=True)  10.9 us
    ppermute x8, starting transfers between devices, along_z(): return (lax.ppermute(p, 'z', ring(1)), lax.ppermute(m, 'z', ring(-1)))  10.8 us
  transfers between devices with their start and end apart: 27, of which 6 were waited for; matrix products, arithmetic and copies ran while one was open for 5% of the time, Pallas kernels for 21%

profile of v5, /device:TPU:1, one launch (start us, length us, event | category | flops | bytes accessed | tf_op | source)
XLA Modules:
  0.0 184.6 jit_solution(17638592599660016845)
XLA Ops:
  1.8 2.1 %collective-permute-start = (f32[1,16,2048]{2,1,0:T(8,128)S(1)}, f32[1,16,2048]{2,1,0:T(8,128)S(1)}, u32[]{:S(2)}, u32[]{:S(2)}) collective-permute-start(f32[1,16,2048]{2,1,0:T(8,128)S(1)} %get-tuple-element.71), channel_id=1, source_target_pairs={{0,1},{1,0},{2,3},{3,2},{4,5},{5,4},{6,7},{7,6},{8,9},{9,8},{10,11... | collective-permute-start | bytes 393224 | tf_op jit(solution)/shard_map/ppermute | solution.py:284
  3.9 1.8 collective-permute-start.3
  5.7 1.3 collective-permute-start.6
  7.0 1.9 %collective-permute-start.9 = (f32[1,16,2048]{2,1,0:T(8,128)S(1)}, f32[1,16,2048]{2,1,0:T(8,128)S(1)}, u32[]{:S(2)}, u32[]{:S(2)}) collective-permute-start(f32[1,16,2048]{2,1,0:T(8,128)S(1)} %get-tuple-element.69), channel_id=1, source_target_pairs={{0,12},{4,8},{8,4},{12,0},{1,13},{5,9},{9,5},{13,1},{2,14},{6,10},... | collective-permute-start | bytes 393224 | tf_op jit(solution)/shard_map/ppermute | solution.py:284
  11.2 1.8 collective-permute-start.7
  13.2 3.9 %collective-permute-done.1 = f32[2,16,2048]{2,1,0:T(8,128)S(1)} collective-permute-done((f32[2,16,2048]{2,1,0:T(8,128)S(1)}, f32[2,16,2048]{2,1,0:T(8,128)S(1)}, u32[]{:S(2)}, u32[]{:S(2)}) %collective-permute-start.1) | collective-permute-done | bytes 262176 | tf_op jit(solution)/shard_map/ppermute | solution.py:284
  18.8 2.0 %collective-permute-start.11 = (f32[4,16,2048]{2,1,0:T(8,128)S(1)}, f32[4,16,2048]{2,1,0:T(8,128)S(1)}, u32[]{:S(2)}, u32[]{:S(2)}) collective-permute-start(f32[4,16,2048]{2,1,0:T(8,128)S(1)} %pad_maximum_fusion.7), channel_id=1, source_target_pairs={{0,3},{1,2},{2,1},{3,0},{4,7},{5,6},{6,5},{7,4},{8,11},{9,10},{10,... | collective-permute-start | bytes 1572872 | tf_op jit(solution)/shard_map/ppermute | solution.py:284
  20.8 7.0 %collective-permute-done.2 = f32[4,16,2048]{2,1,0:T(8,128)S(1)} collective-permute-done((f32[4,16,2048]{2,1,0:T(8,128)S(1)}, f32[4,16,2048]{2,1,0:T(8,128)S(1)}, u32[]{:S(2)}, u32[]{:S(2)}) %collective-permute-start.2) | collective-permute-done | bytes 524320 | tf_op jit(solution)/shard_map/ppermute | solution.py:284
  30.0 1.5 collective-permute-start.14
  33.0 5.0 %sort.14 = (s32[2048]{0:T(1024)S(1)}, s32[2048]{0:T(1024)}) sort(s32[2048]{0:T(1024)S(1)} %fusion.10, s32[2048]{0:T(1024)S(1)} %iota.7), dimensions={0}, to_apply=%region_0.1 | sort | flops 22528 | bytes 32768 | tf_op jit(solution)/shard_map/sort | solution.py:268
  38.7 13.3 %all-to-all-start = ((f32[128,1,16]{2,1,0:T(1,128)}), f32[128,1,16]{2,1,0:T(1,128)S(1)}, u32[]{:S(2)}, u32[]{:S(2)}) async-start(f32[128,1,16]{2,1,0:T(1,128)} %bitcast.8), calls=%async_computation | async-start | bytes 131072 | tf_op jit(solution)/shard_map/all_to_all | solution.py:325
  52.1 10.9 %all-to-all-done = f32[128,1,16]{2,1,0:T(1,128)S(1)} async-done(((f32[128,1,16]{2,1,0:T(1,128)}), f32[128,1,16]{2,1,0:T(1,128)S(1)}, u32[]{:S(2)}, u32[]{:S(2)}) %all-to-all-start) | async-done | bytes 8224 | tf_op jit(solution)/shard_map/all_to_all | solution.py:325
  63.3 17.0 %shard_map.104 = (f32[4,10,128,128]{3,2,1,0:T(8,128)}, bf16[512,2048]{1,0:T(8,128)(2,1)S(1)}, bf16[512,2048]{1,0:T(8,128)(2,1)S(1)}) custom-call(s32[4,8]{1,0:T(4,128)S(1)} %pad_add_fusion.where_ref, s32[16,16]{1,0:T(8,128)S(1)} %copy-done.3, f32[8,16,2048]{2,1,0:T(8,128)S(1)} %pad_maximum_fusion.refs_0_, f32[8,16,2048]{2,1,0:T(8,128)S(1)} %pad_maximum_fusion.1.refs_1_, ...), custom_call_target="tpu_custom_call" | custom-call | flops 322122547200 | bytes 10485760 | tf_op jit(solution)/shard_map/pallas_call | solution.py:155
  80.4 16.0 %shard_map.105 = (f32[4,10,128,128]{3,2,1,0:T(8,128)}, bf16[512,2048]{1,0:T(8,128)(2,1)S(1)}, bf16[512,2048]{1,0:T(8,128)(2,1)S(1)}) custom-call(s32[4,8]{1,0:T(4,128)S(1)} %pad_add_fusion.1.where_ref, s32[16,16]{1,0:T(8,128)S(1)} %copy-done.3, f32[8,16,2048]{2,1,0:T(8,128)S(1)} %pad_maximum_fusion.refs_0_, f32[8,16,2048]{2,1,0:T(8,128)S(1)} %pad_maximum_fusion.1.refs_1_, ...), custom_call_target="tpu_custom_call" | custom-call | flops 322122547200 | bytes 10485760 | tf_op jit(solution)/shard_map/pallas_call | solution.py:155
  96.4 1.7 copy-done.1
  98.2 2.7 %shard_map.106 = (f32[5,128,128]{2,1,0:T(8,128)}, f32[5,128,128]{2,1,0:T(8,128)}, f32[10,128,128]{2,1,0:T(8,128)S(1)}, f32[10,128,128]{2,1,0:T(8,128)S(1)}, f32[10,128,128]{2,1,0:T(8,128)S(1)}) custom-call(f32[4,10,128,128]{3,2,1,0:T(8,128)S(1)} %copy-done.1, f32[4,10,128,128]{3,2,1,0:T(8,128)} %collective-permute-done.16.got_ref), custom_call_target="tpu_custom_call" | custom-call | bytes 5242880 | tf_op jit(solution)/shard_map/pallas_call | solution.py:178
  101.4 2.2 %collective-permute-start.18 = (f32[5,128,128]{2,1,0:T(8,128)}, f32[5,128,128]{2,1,0:T(8,128)}, u32[]{:S(2)}, u32[]{:S(2)}) collective-permute-start(f32[5,128,128]{2,1,0:T(8,128)} %get-tuple-element.47), channel_id=1, source_target_pairs={{0,96},{32,0},{64,32},{96,64},{1,97},{33,1},{65,33},{97,65},{2,98}... | collective-permute-start | bytes 983048 | tf_op jit(solution)/shard_map/ppermute | solution.py:333
  103.6 9.0 %shard_map.109 = f32[4,6,128,128]{3,2,1,0:T(8,128)} custom-call(s32[16,16]{1,0:T(8,128)S(1)} %copy-done.3, bf16[512,2048]{1,0:T(8,128)(2,1)S(1)} %get-tuple-element.54.ah, bf16[512,2048]{1,0:T(8,128)(2,1)S(1)} %get-tuple-element.55.al, f32[2048,2048]{1,0:T(8,128)} %b_ref.3), custom_call_target="tpu_custom_call" | custom-call | flops 193273528320 | bytes 6291456 | tf_op jit(solution)/shard_map/pallas_call | solution.py:155
  112.6 2.4 %collective-permute-start.21 = (f32[4,6,128,128]{3,2,1,0:T(8,128)}, f32[4,6,128,128]{3,2,1,0:T(8,128)}, u32[]{:S(2)}, u32[]{:S(2)}) collective-permute-start(f32[4,6,128,128]{3,2,1,0:T(8,128)} %shard_map.109), channel_id=1, source_target_pairs={{0,16},{16,0},{1,17},{17,1},{2,18},{18,2},{3,19},{19,3},{4,20},{20... | collective-permute-start | bytes 4718600 | tf_op jit(solution)/shard_map/ppermute | solution.py:330
  115.0 2.2 %shard_map.107 = (f32[10,128,128]{2,1,0:T(8,128)}, f32[10,128,128]{2,1,0:T(8,128)}) custom-call(f32[10,128,128]{2,1,0:T(8,128)S(1)} %get-tuple-element.44.plus_ref, f32[10,128,128]{2,1,0:T(8,128)S(1)} %get-tuple-element.45.minus_ref, f32[5,128,128]{2,1,0:T(8,128)} %collective-permute-done.17.gp_ref, f32[5,128,128]{2,1,0:T(8,128)} %collective-permute-done.18.gm_ref), custom_call_target="tpu_custom_call" | custom-call | bytes 1966080 | tf_op jit(solution)/shard_map/pallas_call | solution.py:178
  117.2 2.7 %collective-permute-start.20 = (f32[10,128,128]{2,1,0:T(8,128)}, f32[10,128,128]{2,1,0:T(8,128)}, u32[]{:S(2)}, u32[]{:S(2)}) collective-permute-start(f32[10,128,128]{2,1,0:T(8,128)} %get-tuple-element.49), channel_id=1, source_target_pairs={{0,96},{32,0},{64,32},{96,64},{1,97},{33,1},{65,33},{97,65},{2,98}... | collective-permute-start | bytes 1966088 | tf_op jit(solution)/shard_map/ppermute | solution.py:333
  119.9 7.9 %shard_map.108.mine_ref = f32[4,6,128,128]{3,2,1,0:T(8,128)S(1)} custom-call(s32[16,16]{1,0:T(8,128)S(1)} %copy-done.3, bf16[512,2048]{1,0:T(8,128)(2,1)S(1)} %get-tuple-element.51.ah, bf16[512,2048]{1,0:T(8,128)(2,1)S(1)} %get-tuple-element.52.al, f32[2048,2048]{1,0:T(8,128)} %b_ref.3), custom_call_target="tpu_custom_call" | custom-call | flops 193273528320 | bytes 6291456 | tf_op jit(solution)/shard_map/pallas_call | solution.py:155
  127.8 1.6 shard_map.110
  129.5 2.7 %collective-permute-start.23 = (f32[3,128,128]{2,1,0:T(8,128)S(1)}, f32[3,128,128]{2,1,0:T(8,128)S(1)}, u32[]{:S(2)}, u32[]{:S(2)}) collective-permute-start(f32[3,128,128]{2,1,0:T(8,128)S(1)} %get-tuple-element.64), channel_id=1, source_target_pairs={{0,96},{32,0},{64,32},{96,64},{1,97},{33,1},{65,33},{97,65},{2,98}... | collective-permute-start | bytes 589832 | tf_op jit(solution)/shard_map/ppermute | solution.py:333
  132.2 2.2 %copy-done = f32[2048,512]{1,0:T(8,128)S(1)} copy-done((f32[2048,512]{1,0:T(8,128)S(1)}, f32[2048,512]{1,0:T(8,128)}, u32[]{:S(2)}) %copy-start) | copy-done | bytes 4194328
  134.4 1.6 shard_map.111
  136.1 3.1 %collective-permute-done.22.gp_ref = f32[3,128,128]{2,1,0:T(8,128)S(1)} collective-permute-done((f32[3,128,128]{2,1,0:T(8,128)S(1)}, f32[3,128,128]{2,1,0:T(8,128)S(1)}, u32[]{:S(2)}, u32[]{:S(2)}) %collective-permute-start.22) | collective-permute-done | bytes 196640 | tf_op jit(solution)/shard_map/ppermute | solution.py:333
  139.3 2.7 %collective-permute-start.25 = (f32[6,128,128]{2,1,0:T(8,128)S(1)}, f32[6,128,128]{2,1,0:T(8,128)S(1)}, u32[]{:S(2)}, u32[]{:S(2)}) collective-permute-start(f32[6,128,128]{2,1,0:T(8,128)S(1)} %get-tuple-element.66), channel_id=1, source_target_pairs={{0,96},{32,0},{64,32},{96,64},{1,97},{33,1},{65,33},{97,65},{2,98}... | collective-permute-start | bytes 1179656 | tf_op jit(solution)/shard_map/ppermute | solution.py:333
  142.0 8.4 %collective-permute-done.24.refs_4_ = f32[6,128,128]{2,1,0:T(8,128)S(1)} collective-permute-done((f32[6,128,128]{2,1,0:T(8,128)S(1)}, f32[6,128,128]{2,1,0:T(8,128)S(1)}, u32[]{:S(2)}, u32[]{:S(2)}) %collective-permute-start.24) | collective-permute-done | bytes 393248 | tf_op jit(solution)/shard_map/ppermute | solution.py:333
  150.3 3.6 %shard_map.113 = f32[2048,128]{1,0:T(8,128)S(1)} custom-call(s32[2048]{0:T(1024)S(1)} %get-tuple-element.38.idx_ref, f32[10,128,128]{2,1,0:T(8,128)S(1)} %get-tuple-element.43.refs_0_, f32[10,128,128]{2,1,0:T(8,128)} %collective-permute-done.19.refs_1_, f32[10,128,128]{2,1,0:T(8,128)} %collective-permute-done.20.refs_2_, ...), custom_call_target="tpu_custom_call" | custom-call | bytes 3153920 | tf_op jit(solution)/shard_map/pallas_call | solution.py:178
  154.0 25.6 %all_to_all.10 = f32[128,16,128]{2,1,0:T(8,128)S(1)} all-to-all(f32[128,16,128]{2,1,0:T(8,128)S(1)} %bitcast.27), channel_id=1, replica_groups=mesh['z'=4,'core'=2,'y'=4,'x'=4] {'z','core','y','x'}, dimensions={0} | all-to-all | bytes 2097152 | tf_op jit(solution)/shard_map/all_to_all | solution.py:357
  179.6 5.0 %shard_map.114 = (f32[128,2048]{1,0:T(8,128)}, f32[128,2048]{1,0:T(8,128)}) custom-call(s32[2048]{0:T(1024)S(1)} %convert_element_type.11.place_ref, f32[2048,128]{1,0:T(8,128)S(1)} %bitcast.28, f32[128,2048]{1,0:T(8,128)S(1)} %copy-done.2, bf16[2048,512]{1,0:T(8,128)(2,1)S(1)} %get-tuple-element.61.ch_ref, bf16[2048,512]{1,0:T(8,128)(2,1)S(1)} %get-tuple-element.62.cl_ref), custom_call_target="tpu_custom_call" | custom-call | bytes 8388608 | tf_op jit(solution)/shard_map/pallas_call | solution.py:248
  (86 shorter events, 10.7 us)
Async XLA Ops:
  1.8 8.0 %collective-permute-start = (f32[1,16,2048]{2,1,0:T(8,128)S(1)}, f32[1,16,2048]{2,1,0:T(8,128)S(1)}, u32[]{:S(2)}, u32[]{:S(2)}) collective-permute-start(f32[1,16,2048]{2,1,0:T(8,128)S(1)} %get-tuple-element.71), channel_id=1, source_target_pairs={{0,1},{1,0},{2,3},{3,2},{4,5},{5,4},{6,7},{7,6},{8,9},{9,8},{10,11... | collective-permute-start | bytes 393224 | tf_op jit(solution)/shard_map/ppermute | solution.py:284
  3.9 6.8 %collective-permute-start.3 = (f32[1,16,2048]{2,1,0:T(8,128)S(1)}, f32[1,16,2048]{2,1,0:T(8,128)S(1)}, u32[]{:S(2)}, u32[]{:S(2)}) collective-permute-start(f32[1,16,2048]{2,1,0:T(8,128)S(1)} %get-tuple-element.70), channel_id=1, source_target_pairs={{0,3},{1,2},{2,1},{3,0},{4,7},{5,6},{6,5},{7,4},{8,11},{9,10},{10,... | collective-permute-start | bytes 393224 | tf_op jit(solution)/shard_map/ppermute | solution.py:284
  5.7 5.5 %collective-permute-start.6 = (f32[1,16,2048]{2,1,0:T(8,128)S(1)}, f32[1,16,2048]{2,1,0:T(8,128)S(1)}, u32[]{:S(2)}, u32[]{:S(2)}) collective-permute-start(f32[1,16,2048]{2,1,0:T(8,128)S(1)} %get-tuple-element.72), channel_id=1, source_target_pairs={{0,4},{4,0},{8,12},{12,8},{1,5},{5,1},{9,13},{13,9},{2,6},{6,2},{1... | collective-permute-start | bytes 393224 | tf_op jit(solution)/shard_map/ppermute | solution.py:284
  7.0 6.0 %collective-permute-start.9 = (f32[1,16,2048]{2,1,0:T(8,128)S(1)}, f32[1,16,2048]{2,1,0:T(8,128)S(1)}, u32[]{:S(2)}, u32[]{:S(2)}) collective-permute-start(f32[1,16,2048]{2,1,0:T(8,128)S(1)} %get-tuple-element.69), channel_id=1, source_target_pairs={{0,12},{4,8},{8,4},{12,0},{1,13},{5,9},{9,5},{13,1},{2,14},{6,10},... | collective-permute-start | bytes 393224 | tf_op jit(solution)/shard_map/ppermute | solution.py:284
  9.7 7.3 %collective-permute-start.1 = (f32[2,16,2048]{2,1,0:T(8,128)S(1)}, f32[2,16,2048]{2,1,0:T(8,128)S(1)}, u32[]{:S(2)}, u32[]{:S(2)}) collective-permute-start(f32[2,16,2048]{2,1,0:T(8,128)S(1)} %pad_maximum_fusion.8), channel_id=1, source_target_pairs={{0,3},{1,2},{2,1},{3,0},{4,7},{5,6},{6,5},{7,4},{8,11},{9,10},{10,... | collective-permute-start | bytes 786440 | tf_op jit(solution)/shard_map/ppermute | solution.py:284
  10.7 6.8 %collective-permute-start.4 = (f32[2,16,2048]{2,1,0:T(8,128)S(1)}, f32[2,16,2048]{2,1,0:T(8,128)S(1)}, u32[]{:S(2)}, u32[]{:S(2)}) collective-permute-start(f32[2,16,2048]{2,1,0:T(8,128)S(1)} %pad_maximum_fusion.9), channel_id=1, source_target_pairs={{0,4},{4,0},{8,12},{12,8},{1,5},{5,1},{9,13},{13,9},{2,6},{6,2},{1... | collective-permute-start | bytes 786440 | tf_op jit(solution)/shard_map/ppermute | solution.py:284
  11.2 7.6 %copy-start.6 = (f32[1,16,2048]{2,1,0:T(8,128)}, f32[1,16,2048]{2,1,0:T(8,128)S(1)}, u32[]{:S(2)}) copy-start(f32[1,16,2048]{2,1,0:T(8,128)S(1)} %collective-permute-done.6) | copy-start | bytes 393220
  11.2 7.4 %collective-permute-start.7 = (f32[2,16,2048]{2,1,0:T(8,128)S(1)}, f32[2,16,2048]{2,1,0:T(8,128)S(1)}, u32[]{:S(2)}, u32[]{:S(2)}) collective-permute-start(f32[2,16,2048]{2,1,0:T(8,128)S(1)} %pad_maximum_fusion.10), channel_id=1, source_target_pairs={{0,12},{4,8},{8,4},{12,0},{1,13},{5,9},{9,5},{13,1},{2,14},{6,10},... | collective-permute-start | bytes 786440 | tf_op jit(solution)/shard_map/ppermute | solution.py:284
  13.0 5.7 %copy-start.4 = (f32[1,16,2048]{2,1,0:T(8,128)}, f32[1,16,2048]{2,1,0:T(8,128)S(1)}, u32[]{:S(2)}) copy-start(f32[1,16,2048]{2,1,0:T(8,128)S(1)} %collective-permute-done.9) | copy-start | bytes 393220
  13.1 5.6 %collective-permute-start.10 = (f32[2,16,2048]{2,1,0:T(8,128)S(1)}, f32[2,16,2048]{2,1,0:T(8,128)S(1)}, u32[]{:S(2)}, u32[]{:S(2)}) collective-permute-start(f32[2,16,2048]{2,1,0:T(8,128)S(1)} %pad_maximum_fusion.11), channel_id=1, source_target_pairs={{0,1},{1,0},{2,3},{3,2},{4,5},{5,4},{6,7},{7,6},{8,9},{9,8},{10,11... | collective-permute-start | bytes 786440 | tf_op jit(solution)/shard_map/ppermute | solution.py:284
  17.1 10.8 %collective-permute-start.2 = (f32[4,16,2048]{2,1,0:T(8,128)S(1)}, f32[4,16,2048]{2,1,0:T(8,128)S(1)}, u32[]{:S(2)}, u32[]{:S(2)}) collective-permute-start(f32[4,16,2048]{2,1,0:T(8,128)S(1)} %pad_maximum_fusion.4), channel_id=1, source_target_pairs={{0,4},{4,0},{8,12},{12,8},{1,5},{5,1},{9,13},{13,9},{2,6},{6,2},{1... | collective-permute-start | bytes 1572872 | tf_op jit(solution)/shard_map/ppermute | solution.py:284
  17.6 11.7 %collective-permute-start.5 = (f32[4,16,2048]{2,1,0:T(8,128)S(1)}, f32[4,16,2048]{2,1,0:T(8,128)S(1)}, u32[]{:S(2)}, u32[]{:S(2)}) collective-permute-start(f32[4,16,2048]{2,1,0:T(8,128)S(1)} %pad_maximum_fusion.5), channel_id=1, source_target_pairs={{0,12},{4,8},{8,4},{12,0},{1,13},{5,9},{9,5},{13,1},{2,14},{6,10},... | collective-permute-start | bytes 1572872 | tf_op jit(solution)/shard_map/ppermute | solution.py:284
  18.6 11.3 %collective-permute-start.8 = (f32[4,16,2048]{2,1,0:T(8,128)S(1)}, f32[4,16,2048]{2,1,0:T(8,128)S(1)}, u32[]{:S(2)}, u32[]{:S(2)}) collective-permute-start(f32[4,16,2048]{2,1,0:T(8,128)S(1)} %pad_maximum_fusion.6), channel_id=1, source_target_pairs={{0,1},{1,0},{2,3},{3,2},{4,5},{5,4},{6,7},{7,6},{8,9},{9,8},{10,11... | collective-permute-start | bytes 1572872 | tf_op jit(solution)/shard_map/ppermute | solution.py:284
  18.8 12.7 %collective-permute-start.11 = (f32[4,16,2048]{2,1,0:T(8,128)S(1)}, f32[4,16,2048]{2,1,0:T(8,128)S(1)}, u32[]{:S(2)}, u32[]{:S(2)}) collective-permute-start(f32[4,16,2048]{2,1,0:T(8,128)S(1)} %pad_maximum_fusion.7), channel_id=1, source_target_pairs={{0,3},{1,2},{2,1},{3,0},{4,7},{5,6},{6,5},{7,4},{8,11},{9,10},{10,... | collective-permute-start | bytes 1572872 | tf_op jit(solution)/shard_map/ppermute | solution.py:284
  20.8 9.1 %copy-start.7 = (f32[1,16,2048]{2,1,0:T(8,128)S(1)}, f32[1,16,2048]{2,1,0:T(8,128)}, u32[]{:S(2)}) copy-start(f32[1,16,2048]{2,1,0:T(8,128)} %copy-done.6) | copy-start | bytes 393220
  28.0 35.3 %collective-permute-start.12 = (f32[8,16,2048]{2,1,0:T(8,128)S(1)}, f32[8,16,2048]{2,1,0:T(8,128)}, u32[]{:S(2)}, u32[]{:S(2)}) collective-permute-start(f32[8,16,2048]{2,1,0:T(8,128)S(1)} %pad_maximum_fusion.refs_0_), channel_id=1, source_target_pairs={{0,12},{4,8},{8,4},{12,0},{1,13},{5,9},{9,5},{13,1},{2,14},{6,10},... | collective-permute-start | bytes 3145736 | tf_op jit(solution)/shard_map/ppermute | solution.py:284
  29.4 33.8 %copy-start.3 = (s32[16,16]{1,0:T(8,128)S(1)}, s32[16,16]{1,0:T(8,128)}, u32[]{:S(2)}) copy-start(s32[16,16]{1,0:T(8,128)} %mask_ref.6) | copy-start | bytes 3076
  29.4 33.8 %collective-permute-start.13 = (f32[8,16,2048]{2,1,0:T(8,128)S(1)}, f32[8,16,2048]{2,1,0:T(8,128)}, u32[]{:S(2)}, u32[]{:S(2)}) collective-permute-start(f32[8,16,2048]{2,1,0:T(8,128)S(1)} %pad_maximum_fusion.1.refs_1_), channel_id=1, source_target_pairs={{0,1},{1,0},{2,3},{3,2},{4,5},{5,4},{6,7},{7,6},{8,9},{9,8},{10,11... | collective-permute-start | bytes 3145736 | tf_op jit(solution)/shard_map/ppermute | solution.py:284
  30.0 33.2 %collective-permute-start.14 = (f32[8,16,2048]{2,1,0:T(8,128)S(1)}, f32[8,16,2048]{2,1,0:T(8,128)}, u32[]{:S(2)}, u32[]{:S(2)}) collective-permute-start(f32[8,16,2048]{2,1,0:T(8,128)S(1)} %pad_maximum_fusion.2.refs_2_), channel_id=1, source_target_pairs={{0,3},{1,2},{2,1},{3,0},{4,7},{5,6},{6,5},{7,4},{8,11},{9,10},{10,... | collective-permute-start | bytes 3145736 | tf_op jit(solution)/shard_map/ppermute | solution.py:284
  32.6 30.7 %collective-permute-start.15 = (f32[8,16,2048]{2,1,0:T(8,128)}, f32[8,16,2048]{2,1,0:T(8,128)}, u32[]{:S(2)}, u32[]{:S(2)}) collective-permute-start(f32[8,16,2048]{2,1,0:T(8,128)} %pad_maximum_fusion.3.refs_3_), channel_id=1, source_target_pairs={{0,4},{4,0},{8,12},{12,8},{1,5},{5,1},{9,13},{13,9},{2,6},{6,2},{1... | collective-permute-start | bytes 3145736 | tf_op jit(solution)/shard_map/ppermute | solution.py:284
  38.7 24.2 %all-to-all-start = ((f32[128,1,16]{2,1,0:T(1,128)}), f32[128,1,16]{2,1,0:T(1,128)S(1)}, u32[]{:S(2)}, u32[]{:S(2)}) async-start(f32[128,1,16]{2,1,0:T(1,128)} %bitcast.8), calls=%async_computation | async-start | bytes 131072 | tf_op jit(solution)/shard_map/all_to_all | solution.py:325
  80.3 16.1 %collective-permute-start.16 = (f32[4,10,128,128]{3,2,1,0:T(8,128)}, f32[4,10,128,128]{3,2,1,0:T(8,128)}, u32[]{:S(2)}, u32[]{:S(2)}) collective-permute-start(f32[4,10,128,128]{3,2,1,0:T(8,128)} %get-tuple-element.40), channel_id=1, source_target_pairs={{0,16},{16,0},{1,17},{17,1},{2,18},{18,2},{3,19},{19,3},{4,20},{20... | collective-permute-start | bytes 7864328 | tf_op jit(solution)/shard_map/ppermute | solution.py:330
  100.9 14.1 %collective-permute-start.17 = (f32[5,128,128]{2,1,0:T(8,128)}, f32[5,128,128]{2,1,0:T(8,128)}, u32[]{:S(2)}, u32[]{:S(2)}) collective-permute-start(f32[5,128,128]{2,1,0:T(8,128)} %get-tuple-element.46), channel_id=1, source_target_pairs={{0,32},{32,64},{64,96},{96,0},{1,33},{33,65},{65,97},{97,1},{2,34}... | collective-permute-start | bytes 983048 | tf_op jit(solution)/shard_map/ppermute | solution.py:333
  101.4 13.6 %collective-permute-start.18 = (f32[5,128,128]{2,1,0:T(8,128)}, f32[5,128,128]{2,1,0:T(8,128)}, u32[]{:S(2)}, u32[]{:S(2)}) collective-permute-start(f32[5,128,128]{2,1,0:T(8,128)} %get-tuple-element.47), channel_id=1, source_target_pairs={{0,96},{32,0},{64,32},{96,64},{1,97},{33,1},{65,33},{97,65},{2,98}... | collective-permute-start | bytes 983048 | tf_op jit(solution)/shard_map/ppermute | solution.py:333
  112.6 15.2 %collective-permute-start.21 = (f32[4,6,128,128]{3,2,1,0:T(8,128)}, f32[4,6,128,128]{3,2,1,0:T(8,128)}, u32[]{:S(2)}, u32[]{:S(2)}) collective-permute-start(f32[4,6,128,128]{3,2,1,0:T(8,128)} %shard_map.109), channel_id=1, source_target_pairs={{0,16},{16,0},{1,17},{17,1},{2,18},{18,2},{3,19},{19,3},{4,20},{20... | collective-permute-start | bytes 4718600 | tf_op jit(solution)/shard_map/ppermute | solution.py:330
  117.2 18.9 %collective-permute-start.19 = (f32[10,128,128]{2,1,0:T(8,128)}, f32[10,128,128]{2,1,0:T(8,128)}, u32[]{:S(2)}, u32[]{:S(2)}) collective-permute-start(f32[10,128,128]{2,1,0:T(8,128)} %get-tuple-element.48), channel_id=1, source_target_pairs={{0,32},{32,64},{64,96},{96,0},{1,33},{33,65},{65,97},{97,1},{2,34}... | collective-permute-start | bytes 1966088 | tf_op jit(solution)/shard_map/ppermute | solution.py:333
  117.2 18.9 %collective-permute-start.20 = (f32[10,128,128]{2,1,0:T(8,128)}, f32[10,128,128]{2,1,0:T(8,128)}, u32[]{:S(2)}, u32[]{:S(2)}) collective-permute-start(f32[10,128,128]{2,1,0:T(8,128)} %get-tuple-element.49), channel_id=1, source_target_pairs={{0,96},{32,0},{64,32},{96,64},{1,97},{33,1},{65,33},{97,65},{2,98}... | collective-permute-start | bytes 1966088 | tf_op jit(solution)/shard_map/ppermute | solution.py:333
  129.4 9.7 %collective-permute-start.22 = (f32[3,128,128]{2,1,0:T(8,128)S(1)}, f32[3,128,128]{2,1,0:T(8,128)S(1)}, u32[]{:S(2)}, u32[]{:S(2)}) collective-permute-start(f32[3,128,128]{2,1,0:T(8,128)S(1)} %get-tuple-element.59), channel_id=1, source_target_pairs={{0,32},{32,64},{64,96},{96,0},{1,33},{33,65},{65,97},{97,1},{2,34}... | collective-permute-start | bytes 589832 | tf_op jit(solution)/shard_map/ppermute | solution.py:333
  129.5 9.7 %collective-permute-start.23 = (f32[3,128,128]{2,1,0:T(8,128)S(1)}, f32[3,128,128]{2,1,0:T(8,128)S(1)}, u32[]{:S(2)}, u32[]{:S(2)}) collective-permute-start(f32[3,128,128]{2,1,0:T(8,128)S(1)} %get-tuple-element.64), channel_id=1, source_target_pairs={{0,96},{32,0},{64,32},{96,64},{1,97},{33,1},{65,33},{97,65},{2,98}... | collective-permute-start | bytes 589832 | tf_op jit(solution)/shard_map/ppermute | solution.py:333
  139.2 11.1 %collective-permute-start.24 = (f32[6,128,128]{2,1,0:T(8,128)S(1)}, f32[6,128,128]{2,1,0:T(8,128)S(1)}, u32[]{:S(2)}, u32[]{:S(2)}) collective-permute-start(f32[6,128,128]{2,1,0:T(8,128)S(1)} %get-tuple-element.65), channel_id=1, source_target_pairs={{0,32},{32,64},{64,96},{96,0},{1,33},{33,65},{65,97},{97,1},{2,34}... | collective-permute-start | bytes 1179656 | tf_op jit(solution)/shard_map/ppermute | solution.py:333
  139.3 11.0 %collective-permute-start.25 = (f32[6,128,128]{2,1,0:T(8,128)S(1)}, f32[6,128,128]{2,1,0:T(8,128)S(1)}, u32[]{:S(2)}, u32[]{:S(2)}) collective-permute-start(f32[6,128,128]{2,1,0:T(8,128)S(1)} %get-tuple-element.66), channel_id=1, source_target_pairs={{0,96},{32,0},{64,32},{96,64},{1,97},{33,1},{65,33},{97,65},{2,98}... | collective-permute-start | bytes 1179656 | tf_op jit(solution)/shard_map/ppermute | solution.py:333
  153.9 25.6 %copy-start.2 = (f32[128,2048]{1,0:T(8,128)S(1)}, f32[128,2048]{1,0:T(8,128)}, u32[]{:S(2)}) copy-start(f32[128,2048]{1,0:T(8,128)} %den_ref.1) | copy-start | bytes 3145732
  (6 other events, 18.5 us)

commit v6 on v5

--- a/solution.py
+++ b/solution.py
@@ -67,26 +67,45 @@
     )(mask, x)
 
 
-def mm_body(first, tiles_out, mask_ref, ah, al, b_ref, o_ref, slots, sems, before):
+def integrals_kernel(mask_ref, x_ref, out_ref):
+    for i in range(x_ref.shape[0] // TILE):
+        for j in range(NB // TILE):
+            terms = masked_split(mask_ref, x_ref, i, pl.program_id(0) * (NB // TILE) + j, i, j)
+            for k in range(2):
+                out_ref[0, k, i * TILE : (i + 1) * TILE, j * TILE : (j + 1) * TILE] = terms[k]
+
+
+def prepare_integrals(x, mask):
+    depth, cols = x.shape
+    return call(
+        integrals_kernel,
+        jax.ShapeDtypeStruct((cols // NB, 2, depth, NB), bf16),
+        grid=(cols // NB,),
+        in_specs=[pl.BlockSpec(memory_space=pltpu.SMEM), pl.BlockSpec((depth, NB), lambda n: (0, n))],
+        out_specs=pl.BlockSpec((1, 2, depth, NB), lambda n: (n, 0, 0, 0)),
+        vmem=49,
+        nbytes=x.size * 8,
+        flops=x.size * 4,
+    )(mask, x)
+
+
+def mm_body(first, tiles_out, ah, al, b_ref, o_ref, slots, sems, before):
     per = NB // TILE
     blocks = tiles_out // per
 
     def fetch(n):
         slot = n % SLOTS
-        at = pl.ds(pl.multiple_of((first + n) * NB, NB), NB)
-        return pltpu.make_async_copy(b_ref.at[:, at], slots.at[slot], sems.at[slot])
+        return pltpu.make_async_copy(b_ref.at[first + n], slots.at[slot], sems.at[slot])
 
     for n in range(SLOTS):
         fetch(n).start()
     before()
     dot = functools.partial(jnp.dot, preferred_element_type=f32)
-    tiles = range(b_ref.shape[0] // TILE)
 
     def step(n, carry):
         fetch(n).wait()
-        x = slots.at[n % SLOTS]
-        terms = [[masked_split(mask_ref, x, i, (first + n) * per + j, i, j) for j in range(per)] for i in tiles]
-        bh, bl = (jnp.concatenate([jnp.concatenate([t[k] for t in row], axis=1) for row in terms], axis=0) for k in range(2))
+        slot = n % SLOTS
+        bh, bl = slots[slot, 0], slots[slot, 1]
         acc = dot(ah[...], bh) + dot(ah[...], bl) + dot(al[...], bh)
         for i in range(NZ):
             for t in range(per):
@@ -101,7 +120,7 @@
     lax.fori_loop(0, blocks, step, 0)
 
 
-def mm_first_kernel(where_ref, mask_ref, *refs):
+def mm_first_kernel(where_ref, *refs):
     held, b_ref, o_ref, ah, al, slots, sems, stage, row_sems = refs[:-8], *refs[-8:]
     near, late = held[:COLOURS], held[COLOURS:]
     rows = ROWS // 2 // COLOURS
@@ -129,11 +148,11 @@
             ah[at, :] = hi
             al[at, :] = lo
 
-    mm_body(0, PARTS[0], mask_ref, ah, al, b_ref, o_ref, slots, sems, split_rows)
-
-
-def mm_next_kernel(mask_ref, ah, al, b_ref, o_ref, slots, sems):
-    mm_body(PARTS[0] * TILE // NB, PARTS[1], mask_ref, ah, al, b_ref, o_ref, slots, sems, lambda: None)
+    mm_body(0, PARTS[0], ah, al, b_ref, o_ref, slots, sems, split_rows)
+
+
+def mm_next_kernel(ready_ref, ah, al, b_ref, o_ref, slots, sems):
+    mm_body(PARTS[0] * TILE // NB, PARTS[1], ah, al, b_ref, o_ref, slots, sems, lambda: None)
 
 
 SMEM = pl.BlockSpec(memory_space=pltpu.SMEM)
@@ -144,10 +163,10 @@
 
 
 def multiply(kernel, maps, rows, integrals, part, first):
-    depth, _ = integrals.shape
+    depth = integrals.shape[2]
     m = NZ * ROWS
     shapes = [jax.ShapeDtypeStruct((NZ, part, ROWS, TILE), f32)]
-    scratch = [pltpu.VMEM((SLOTS, depth, NB), f32), pltpu.SemaphoreType.DMA((SLOTS,))]
+    scratch = [pltpu.VMEM((SLOTS, 2, depth, NB), bf16), pltpu.SemaphoreType.DMA((SLOTS,))]
     if first:
         pieces = 2 * NZ * COLOURS
         shapes += [jax.ShapeDtypeStruct((m, depth), bf16)] * 2
@@ -158,7 +177,7 @@
         in_specs=[SMEM] * len(maps) + [HBM if first else VMEM] * len(rows) + [HBM],
         out_specs=(VMEM,) * len(shapes),
         scratch_shapes=scratch,
-        vmem=40,
+        vmem=49,
         flops=40 * 6 * m * depth * part * TILE,
         nbytes=4 * depth * part * TILE,
     )(*maps, *rows, integrals)
@@ -203,7 +222,10 @@
     return small(near_kernel, (plus, minus, gp, gm), (plus.shape, plus.shape))
 
 
-def gather_kernel(idx_ref, *refs):
+SLAB = CAP + 1
+
+
+def gather_kernel(idx_ref, place_ref, *refs):
     ins, (out_ref, scr) = refs[:-2], refs[-2:]
     for p, part in enumerate(PARTS):
         own, rp, rm = ins[3 * p : 3 * p + 3]
@@ -213,25 +235,32 @@
 
     def step(g, carry):
         for k in range(CAP):
-            out_ref[pl.ds(g * CAP + k, 1), :] = scr[pl.ds(idx_ref[g * CAP + k], 1), :]
+            out_ref[pl.ds(g * SLAB + k, 1), :] = scr[pl.ds(idx_ref[g * CAP + k], 1), :]
+        out_ref[pl.ds(g * SLAB + CAP, 1), :] = place_ref[pl.ds(g, 1), :]
         return carry
 
     lax.fori_loop(0, ROWS * TPD // CAP, step, 0)
 
 
-def gather(idx, parts):
+def gather(idx, place, parts):
     units = ROWS * TPD
     flat = [x for part in parts for x in part]
-    return small(gather_kernel, (idx, *flat), ((units, TILE),), ((units, TILE),))[0]
-
-
-def finish_kernel(place_ref, got_ref, den_ref, ch_ref, cl_ref, up_ref, ct_ref, scr):
+    return small(gather_kernel, (idx, place, *flat), ((units // CAP * SLAB, TILE),), ((units, TILE),))[0]
+
+
+def finish_kernel(got_ref, den_ref, ch_ref, cl_ref, up_ref, ct_ref, scr, place_vec, place_ref, sem):
+    peers = ROWS * TPD // CAP
+    place_vec[...] = got_ref[pl.ds(CAP, peers, stride=SLAB), :].astype(jnp.int32)
+    copy = pltpu.make_async_copy(place_vec, place_ref, sem)
+    copy.start()
+    copy.wait()
+
     def step(g, carry):
         for k in range(CAP):
-            scr[pl.ds(place_ref[g * CAP + k], 1), :] = got_ref[pl.ds(g * CAP + k, 1), :]
+            scr[pl.ds(place_ref[g, k], 1), :] = got_ref[pl.ds(g * SLAB + k, 1), :]
         return carry
 
-    lax.fori_loop(0, ROWS * TPD // CAP, step, 0)
+    lax.fori_loop(0, peers, step, 0)
     for t in range(TPD):
         at = slice(t * TILE, (t + 1) * TILE)
         up_ref[:, at] = scr[at, :] / den_ref[:, at]
@@ -242,18 +271,22 @@
         ct_ref[:, at] = dot(hi, ch_ref[at, :]) + dot(hi, cl_ref[at, :]) + dot(lo, ch_ref[at, :])
 
 
-def finish(place, got, den, ch, cl):
+def finish(got, den, ch, cl):
     shape = jax.ShapeDtypeStruct(den.shape, f32)
-    whole = lambda s: pl.BlockSpec(s, lambda n: (0, 0))
+    peers = ROWS * TPD // CAP
     return call(
         finish_kernel,
         (shape, shape),
-        grid=(1,),
-        in_specs=[pl.BlockSpec(memory_space=pltpu.SMEM), whole(got.shape), whole(den.shape), whole(ch.shape), whole(cl.shape)],
-        out_specs=(whole(den.shape), whole(den.shape)),
-        scratch_shapes=[pltpu.VMEM((ROWS * TPD, TILE), f32)],
+        in_specs=[VMEM] * 4,
+        out_specs=(VMEM, VMEM),
+        scratch_shapes=[
+            pltpu.VMEM((ROWS * TPD, TILE), f32),
+            pltpu.VMEM((peers, TILE), jnp.int32),
+            pltpu.SMEM((peers, TILE), jnp.int32),
+            pltpu.SemaphoreType.DMA,
+        ],
         nbytes=8 << 20,
-    )(place, got, den, ch, cl)
+    )(got, den, ch, cl)
 
 
 def plan(destination):
@@ -321,10 +354,9 @@
     held = (*bufs, *late)
 
     source, place = plan(after(destination, *bufs))
-    place = place.astype(f32).reshape(128, 1, CAP)
-    got_place = lax.all_to_all(place, everyone, split_axis=0, concat_axis=0, tiled=True)
-    got_place = got_place.reshape(-1).astype(jnp.int32)
-    other, got_place, source = lax.optimization_barrier((other, got_place, source))
+    place = jnp.pad(place.astype(f32).reshape(128, CAP), ((0, 0), (0, TILE - CAP)))
+    terms = prepare_integrals(after(integrals, *bufs), integral_mask)
+    other, source, place = lax.optimization_barrier((other, source, place))
 
     def swap(value):
         return lax.ppermute(value, "core", [(0, 1), (1, 0)])
@@ -333,29 +365,29 @@
         return lax.ppermute(p, "z", ring(1)), lax.ppermute(m, "z", ring(-1))
 
     def first_product(where):
-        return multiply(mm_first_kernel, (where, integral_mask), held, integrals, PARTS[0], True)
-
-    def next_product(mask, hi, lo):
-        return multiply(mm_next_kernel, (mask,), (hi, lo), integrals, PARTS[1], False)[0]
+        return multiply(mm_first_kernel, (where,), held, terms, PARTS[0], True)
+
+    def next_product(ready, hi, lo):
+        return multiply(mm_next_kernel, (ready,), (hi, lo), terms, PARTS[1], False)[0]
 
     theirs0, other_hi, other_lo = first_product(other)
     from_core0 = swap(theirs0)
     mine0, own_hi, own_lo = first_product(after(own, theirs0))
     p0, m0, plus0, minus0, base0 = far(mine0, from_core0)
     gp0, gm0 = along_z(p0, m0)
-    theirs1 = next_product(after(integral_mask, base0), other_hi, other_lo)
+    theirs1 = next_product(after(other, base0), other_hi, other_lo)
     from_core1 = swap(theirs1)
     near0 = near(plus0, minus0, gp0, gm0)
     rp0, rm0 = along_z(*near0)
-    mine1 = next_product(after(integral_mask, *near0), own_hi, own_lo)
+    mine1 = next_product(after(own, *near0), own_hi, own_lo)
     p1, m1, plus1, minus1, base1 = far(mine1, from_core1)
     gp1, gm1 = along_z(p1, m1)
     ch, cl = prepare_cycle(after(cycle_tiles, base1), cycle_mask)
     rp1, rm1 = along_z(*near(plus1, minus1, after(gp1, rp0, rm0, ch, cl), gm1))
 
-    sending = gather(source, ((base0, rp0, rm0), (base1, rp1, rm1))).reshape(128, CAP, TILE)
+    sending = gather(source, place, ((base0, rp0, rm0), (base1, rp1, rm1))).reshape(128, 1, SLAB * TILE)
     units = lax.all_to_all(sending, everyone, split_axis=0, concat_axis=0, tiled=True)
-    return finish(got_place, units.reshape(-1, TILE), denominators, ch, cl)
+    return finish(units.reshape(-1, TILE), denominators, ch, cl)
 
 
 def solution(mesh):

time: 185 us -> 183 us (0.989)
  Pallas kernels: 66.8 us -> 82 us
  waiting for transfers between devices: 33.5 us -> 22.1 us
  starting transfers between devices: 43.8 us -> 35.2 us
  blocking collectives: 25.6 us -> 29.1 us
    pallas_call x1 -> x2, Pallas kernels: 5 us -> 20.7 us  [the longest x1 14.8 us: prepare_integrals(): call(integrals_kernel, jax.ShapeDtypeStruct((cols // NB, 2, depth, NB), b...]
    all_to_all x1 -> x0, starting transfers between devices: 13.3 us -> none  [body(): lax.all_to_all(place, everyone, split_axis=0, concat_axis=0, tiled=True)]
    all_to_all x1 -> x0, waiting for transfers between devices: 10.9 us -> none  [body(): lax.all_to_all(place, everyone, split_axis=0, concat_axis=0, tiled=True)]
    all_to_all x1, blocking collectives: 25.6 us -> 29.1 us  [body(): lax.all_to_all(sending, everyone, split_axis=0, concat_axis=0, tiled=True)]
    ppermute x2, starting transfers between devices: 2.44 us -> 5.91 us  [swap(): return lax.ppermute(value, 'core', [(0, 1), (1, 0)])]
    unnamed x23 -> x27, local copies, waits for them, and re-layouts: 4.05 us -> 4.06 us
  transfers between devices with their start and end apart: 27 -> 26, of which waited for: 6 -> 6; matrix products, arithmetic and copies ran while one was open for 5% -> 4% of each run, Pallas kernels for 21% -> 29%
where the time goes in v6:
time: 183 us; the launch traced here: 182 us
  Pallas kernels  82 us (45%)
  starting transfers between devices  35.2 us (19%)
  blocking collectives  29.1 us (16%)
  waiting for transfers between devices  22.1 us (12%)
  other arithmetic  7.31 us (4%)
  local copies, waits for them, and re-layouts  5.62 us (3%)
    pallas_call x4, Pallas kernels, multiply(): call(kernel, tuple(shapes), in_specs=[SMEM] * len(maps) + [HBM if first e...  49.3 us
    all_to_all x1, blocking collectives, body(): lax.all_to_all(sending, everyone, split_axis=0, concat_axis=0, tiled=True)  29.1 us
    ppermute x16, starting transfers between devices, exchange(): return lax.ppermute(value, axis, pairs)  17.2 us
    pallas_call x1, Pallas kernels, prepare_integrals(): call(integrals_kernel, jax.ShapeDtypeStruct((cols // NB, 2, depth, NB), b...  14.8 us
    ppermute x8, starting transfers between devices, along_z(): return (lax.ppermute(p, 'z', ring(1)), lax.ppermute(m, 'z', ring(-1)))  12.1 us
    ppermute x16, waiting for transfers between devices, exchange(): return lax.ppermute(value, axis, pairs)  11.3 us
    ppermute x8, waiting for transfers between devices, along_z(): return (lax.ppermute(p, 'z', ring(1)), lax.ppermute(m, 'z', ring(-1)))  10.8 us
    pallas_call x5, Pallas kernels, small(): call(kernel, shapes, in_specs=[SMEM if x.dtype == jnp.int32 else VMEM for...  10.4 us
  transfers between devices with their start and end apart: 26, of which 6 were waited for; matrix products, arithmetic and copies ran while one was open for 4% of the time, Pallas kernels for 29%

profile of v6, /device:TPU:1, one launch (start us, length us, event | category | flops | bytes accessed | tf_op | source)
XLA Modules:
  0.0 182.5 jit_solution(16160544407815126589)
XLA Ops:
  1.8 2.1 %collective-permute-start = (f32[1,16,2048]{2,1,0:T(8,128)S(1)}, f32[1,16,2048]{2,1,0:T(8,128)S(1)}, u32[]{:S(2)}, u32[]{:S(2)}) collective-permute-start(f32[1,16,2048]{2,1,0:T(8,128)S(1)} %get-tuple-element.73), channel_id=1, source_target_pairs={{0,1},{1,0},{2,3},{3,2},{4,5},{5,4},{6,7},{7,6},{8,9},{9,8},{10,11... | collective-permute-start | bytes 393224 | tf_op jit(solution)/shard_map/ppermute | solution.py:317
  3.9 1.8 collective-permute-start.3
  5.7 1.3 collective-permute-start.6
  7.0 1.9 %collective-permute-start.9 = (f32[1,16,2048]{2,1,0:T(8,128)S(1)}, f32[1,16,2048]{2,1,0:T(8,128)S(1)}, u32[]{:S(2)}, u32[]{:S(2)}) collective-permute-start(f32[1,16,2048]{2,1,0:T(8,128)S(1)} %get-tuple-element.71), channel_id=1, source_target_pairs={{0,12},{4,8},{8,4},{12,0},{1,13},{5,9},{9,5},{13,1},{2,14},{6,10},... | collective-permute-start | bytes 393224 | tf_op jit(solution)/shard_map/ppermute | solution.py:317
  11.2 1.8 collective-permute-start.7
  13.2 3.9 %collective-permute-done.1 = f32[2,16,2048]{2,1,0:T(8,128)S(1)} collective-permute-done((f32[2,16,2048]{2,1,0:T(8,128)S(1)}, f32[2,16,2048]{2,1,0:T(8,128)S(1)}, u32[]{:S(2)}, u32[]{:S(2)}) %collective-permute-start.1) | collective-permute-done | bytes 262176 | tf_op jit(solution)/shard_map/ppermute | solution.py:317
  18.8 2.0 %collective-permute-start.11 = (f32[4,16,2048]{2,1,0:T(8,128)S(1)}, f32[4,16,2048]{2,1,0:T(8,128)S(1)}, u32[]{:S(2)}, u32[]{:S(2)}) collective-permute-start(f32[4,16,2048]{2,1,0:T(8,128)S(1)} %pad_maximum_fusion.7), channel_id=1, source_target_pairs={{0,3},{1,2},{2,1},{3,0},{4,7},{5,6},{6,5},{7,4},{8,11},{9,10},{10,... | collective-permute-start | bytes 1572872 | tf_op jit(solution)/shard_map/ppermute | solution.py:317
  20.8 7.0 %collective-permute-done.2 = f32[4,16,2048]{2,1,0:T(8,128)S(1)} collective-permute-done((f32[4,16,2048]{2,1,0:T(8,128)S(1)}, f32[4,16,2048]{2,1,0:T(8,128)S(1)}, u32[]{:S(2)}, u32[]{:S(2)}) %collective-permute-start.2) | collective-permute-done | bytes 524320 | tf_op jit(solution)/shard_map/ppermute | solution.py:317
  30.0 1.5 collective-permute-start.14
  33.0 5.0 %sort.14 = (s32[2048]{0:T(1024)S(1)}, s32[2048]{0:T(1024)}) sort(s32[2048]{0:T(1024)S(1)} %fusion.10, s32[2048]{0:T(1024)S(1)} %iota.7), dimensions={0}, to_apply=%region_0.1 | sort | flops 22528 | bytes 32768 | tf_op jit(solution)/shard_map/sort | solution.py:301
  38.1 14.8 %shard_map.104.refs_8_.b_ref = bf16[8,2,2048,256]{3,2,1,0:T(8,128)(2,1)} custom-call(s32[16,16]{1,0:T(8,128)S(1)} %copy-done.3, f32[2048,2048]{1,0:T(8,128)} %x_ref), custom_call_target="tpu_custom_call" | custom-call | flops 16777216 | bytes 33554432 | tf_op jit(solution)/shard_map/pallas_call | solution.py:80
  53.1 15.9 %shard_map.105 = (f32[4,10,128,128]{3,2,1,0:T(8,128)}, bf16[512,2048]{1,0:T(8,128)(2,1)}, bf16[512,2048]{1,0:T(8,128)(2,1)}) custom-call(s32[4,8]{1,0:T(4,128)S(1)} %pad_add_fusion.where_ref.ready_ref, f32[8,16,2048]{2,1,0:T(8,128)S(1)} %pad_maximum_fusion.refs_0_, f32[8,16,2048]{2,1,0:T(8,128)S(1)} %pad_maximum_fusion.1.refs_1_, ...), custom_call_target="tpu_custom_call" | custom-call | flops 322122547200 | bytes 10485760 | tf_op jit(solution)/shard_map/pallas_call | solution.py:174
  69.0 4.3 %collective-permute-start.16 = (f32[4,10,128,128]{3,2,1,0:T(8,128)}, f32[4,10,128,128]{3,2,1,0:T(8,128)}, u32[]{:S(2)}, u32[]{:S(2)}) collective-permute-start(f32[4,10,128,128]{3,2,1,0:T(8,128)} %get-tuple-element.42), channel_id=1, source_target_pairs={{0,16},{16,0},{1,17},{17,1},{2,18},{18,2},{3,19},{19,3},{4,20},{20... | collective-permute-start | bytes 7864328 | tf_op jit(solution)/shard_map/ppermute | solution.py:362
  73.3 14.9 %shard_map.106 = (f32[4,10,128,128]{3,2,1,0:T(8,128)}, bf16[512,2048]{1,0:T(8,128)(2,1)}, bf16[512,2048]{1,0:T(8,128)(2,1)}) custom-call(s32[4,8]{1,0:T(4,128)S(1)} %pad_add_fusion.1.where_ref.ready_ref, f32[8,16,2048]{2,1,0:T(8,128)S(1)} %pad_maximum_fusion.refs_0_, f32[8,16,2048]{2,1,0:T(8,128)S(1)} %pad_maximum_fusion.1.refs_1_, ...), custom_call_target="tpu_custom_call" | custom-call | flops 322122547200 | bytes 10485760 | tf_op jit(solution)/shard_map/pallas_call | solution.py:174
  88.2 1.7 copy-done.1
  89.9 2.9 %shard_map.107 = (f32[5,128,128]{2,1,0:T(8,128)}, f32[5,128,128]{2,1,0:T(8,128)}, f32[10,128,128]{2,1,0:T(8,128)S(1)}, f32[10,128,128]{2,1,0:T(8,128)S(1)}, f32[10,128,128]{2,1,0:T(8,128)S(1)}) custom-call(f32[4,10,128,128]{3,2,1,0:T(8,128)S(1)} %copy-done.1, f32[4,10,128,128]{3,2,1,0:T(8,128)} %collective-permute-done.16.got_ref), custom_call_target="tpu_custom_call" | custom-call | bytes 5242880 | tf_op jit(solution)/shard_map/pallas_call | solution.py:197
  92.8 2.7 %collective-permute-start.17 = (f32[5,128,128]{2,1,0:T(8,128)}, f32[5,128,128]{2,1,0:T(8,128)}, u32[]{:S(2)}, u32[]{:S(2)}) collective-permute-start(f32[5,128,128]{2,1,0:T(8,128)} %get-tuple-element.48), channel_id=1, source_target_pairs={{0,32},{32,64},{64,96},{96,0},{1,33},{33,65},{65,97},{97,1},{2,34}... | collective-permute-start | bytes 983048 | tf_op jit(solution)/shard_map/ppermute | solution.py:365
  96.7 9.9 %shard_map.110 = f32[4,6,128,128]{3,2,1,0:T(8,128)} custom-call(s32[4,8]{1,0:T(4,128)S(1)} %pad_add_fusion.where_ref.ready_ref, bf16[512,2048]{1,0:T(8,128)(2,1)S(1)} %copy-done.5, bf16[512,2048]{1,0:T(8,128)(2,1)} %get-tuple-element.57.al, bf16[8,2,2048,256]{3,2,1,0:T(8,128)(2,1)} %shard_map.104.refs_8_.b_ref), custom_call_target="tpu_custom_call" | custom-call | flops 193273528320 | bytes 6291456 | tf_op jit(solution)/shard_map/pallas_call | solution.py:174
  106.6 1.6 collective-permute-start.21
  108.2 2.2 %shard_map.108 = (f32[10,128,128]{2,1,0:T(8,128)}, f32[10,128,128]{2,1,0:T(8,128)}) custom-call(f32[10,128,128]{2,1,0:T(8,128)S(1)} %get-tuple-element.46.plus_ref, f32[10,128,128]{2,1,0:T(8,128)S(1)} %get-tuple-element.47.minus_ref, f32[5,128,128]{2,1,0:T(8,128)} %collective-permute-done.17.gp_ref, f32[5,128,128]{2,1,0:T(8,128)} %collective-permute-done.18.gm_ref), custom_call_target="tpu_custom_call" | custom-call | bytes 1966080 | tf_op jit(solution)/shard_map/pallas_call | solution.py:197
  111.1 2.1 %collective-permute-start.20 = (f32[10,128,128]{2,1,0:T(8,128)}, f32[10,128,128]{2,1,0:T(8,128)}, u32[]{:S(2)}, u32[]{:S(2)}) collective-permute-start(f32[10,128,128]{2,1,0:T(8,128)} %get-tuple-element.51), channel_id=1, source_target_pairs={{0,96},{32,0},{64,32},{96,64},{1,97},{33,1},{65,33},{97,65},{2,98}... | collective-permute-start | bytes 1966088 | tf_op jit(solution)/shard_map/ppermute | solution.py:365
  113.1 8.6 %shard_map.109.mine_ref = f32[4,6,128,128]{3,2,1,0:T(8,128)S(1)} custom-call(s32[4,8]{1,0:T(4,128)S(1)} %pad_add_fusion.1.where_ref.ready_ref, bf16[512,2048]{1,0:T(8,128)(2,1)S(1)} %copy-done.4, bf16[512,2048]{1,0:T(8,128)(2,1)} %get-tuple-element.54.al, bf16[8,2,2048,256]{3,2,1,0:T(8,128)(2,1)} %shard_map.104.refs_8_.b_ref), custom_call_target="tpu_custom_call" | custom-call | flops 193273528320 | bytes 6291456 | tf_op jit(solution)/shard_map/pallas_call | solution.py:174
  121.7 1.6 shard_map.111
  123.4 2.7 %collective-permute-start.23 = (f32[3,128,128]{2,1,0:T(8,128)S(1)}, f32[3,128,128]{2,1,0:T(8,128)S(1)}, u32[]{:S(2)}, u32[]{:S(2)}) collective-permute-start(f32[3,128,128]{2,1,0:T(8,128)S(1)} %get-tuple-element.66), channel_id=1, source_target_pairs={{0,96},{32,0},{64,32},{96,64},{1,97},{33,1},{65,33},{97,65},{2,98}... | collective-permute-start | bytes 589832 | tf_op jit(solution)/shard_map/ppermute | solution.py:365
  126.1 2.2 %copy-done = f32[2048,512]{1,0:T(8,128)S(1)} copy-done((f32[2048,512]{1,0:T(8,128)S(1)}, f32[2048,512]{1,0:T(8,128)}, u32[]{:S(2)}) %copy-start) | copy-done | bytes 4194328
  128.3 1.6 shard_map.112
  130.0 2.4 %collective-permute-done.22.gp_ref = f32[3,128,128]{2,1,0:T(8,128)S(1)} collective-permute-done((f32[3,128,128]{2,1,0:T(8,128)S(1)}, f32[3,128,128]{2,1,0:T(8,128)S(1)}, u32[]{:S(2)}, u32[]{:S(2)}) %collective-permute-start.22) | collective-permute-done | bytes 196640 | tf_op jit(solution)/shard_map/ppermute | solution.py:365
  133.4 1.9 %collective-permute-start.25 = (f32[6,128,128]{2,1,0:T(8,128)S(1)}, f32[6,128,128]{2,1,0:T(8,128)S(1)}, u32[]{:S(2)}, u32[]{:S(2)}) collective-permute-start(f32[6,128,128]{2,1,0:T(8,128)S(1)} %get-tuple-element.68), channel_id=1, source_target_pairs={{0,96},{32,0},{64,32},{96,64},{1,97},{33,1},{65,33},{97,65},{2,98}... | collective-permute-start | bytes 1179656 | tf_op jit(solution)/shard_map/ppermute | solution.py:365
  135.2 8.4 %collective-permute-done.24.refs_4_ = f32[6,128,128]{2,1,0:T(8,128)S(1)} collective-permute-done((f32[6,128,128]{2,1,0:T(8,128)S(1)}, f32[6,128,128]{2,1,0:T(8,128)S(1)}, u32[]{:S(2)}, u32[]{:S(2)}) %collective-permute-start.24) | collective-permute-done | bytes 393248 | tf_op jit(solution)/shard_map/ppermute | solution.py:365
  143.6 3.7 %shard_map.114 = f32[2176,128]{1,0:T(8,128)S(1)} custom-call(s32[2048]{0:T(1024)S(1)} %get-tuple-element.38.idx_ref, f32[128,128]{1,0:T(8,128)S(1)} %pad.4.place_ref, f32[10,128,128]{2,1,0:T(8,128)S(1)} %get-tuple-element.45.refs_0_, f32[10,128,128]{2,1,0:T(8,128)} %collective-permute-done.19.refs_1_, f32[10,128,128]{2,1,0:T(8,128)} %collective-permute-done.20.refs_2_, ...), custom_call_target="tpu_custom_call" | custom-call | bytes 3219456 | tf_op jit(solution)/shard_map/pallas_call | solution.py:197
  147.3 29.1 %all_to_all.5 = f32[128,1,2176]{2,1,0:T(1,128)S(1)} all-to-all(f32[128,1,2176]{2,1,0:T(1,128)S(1)} %bitcast.26), channel_id=1, replica_groups=mesh['z'=4,'core'=2,'y'=4,'x'=4] {'z','core','y','x'}, dimensions={0} | all-to-all | bytes 2228224 | tf_op jit(solution)/shard_map/all_to_all | solution.py:389
  176.4 6.0 %shard_map.115 = (f32[128,2048]{1,0:T(8,128)}, f32[128,2048]{1,0:T(8,128)}) custom-call(f32[2176,128]{1,0:T(8,128)S(1)} %bitcast.27, f32[128,2048]{1,0:T(8,128)S(1)} %copy-done.2, bf16[2048,512]{1,0:T(8,128)(2,1)S(1)} %get-tuple-element.63.ch_ref, bf16[2048,512]{1,0:T(8,128)(2,1)S(1)} %get-tuple-element.64.cl_ref), custom_call_target="tpu_custom_call" | custom-call | bytes 8388608 | tf_op jit(solution)/shard_map/pallas_call | solution.py:277
  (88 shorter events, 12.0 us)
Async XLA Ops:
  1.8 8.0 %collective-permute-start = (f32[1,16,2048]{2,1,0:T(8,128)S(1)}, f32[1,16,2048]{2,1,0:T(8,128)S(1)}, u32[]{:S(2)}, u32[]{:S(2)}) collective-permute-start(f32[1,16,2048]{2,1,0:T(8,128)S(1)} %get-tuple-element.73), channel_id=1, source_target_pairs={{0,1},{1,0},{2,3},{3,2},{4,5},{5,4},{6,7},{7,6},{8,9},{9,8},{10,11... | collective-permute-start | bytes 393224 | tf_op jit(solution)/shard_map/ppermute | solution.py:317
  3.9 6.8 %collective-permute-start.3 = (f32[1,16,2048]{2,1,0:T(8,128)S(1)}, f32[1,16,2048]{2,1,0:T(8,128)S(1)}, u32[]{:S(2)}, u32[]{:S(2)}) collective-permute-start(f32[1,16,2048]{2,1,0:T(8,128)S(1)} %get-tuple-element.72), channel_id=1, source_target_pairs={{0,3},{1,2},{2,1},{3,0},{4,7},{5,6},{6,5},{7,4},{8,11},{9,10},{10,... | collective-permute-start | bytes 393224 | tf_op jit(solution)/shard_map/ppermute | solution.py:317
  5.7 5.5 %collective-permute-start.6 = (f32[1,16,2048]{2,1,0:T(8,128)S(1)}, f32[1,16,2048]{2,1,0:T(8,128)S(1)}, u32[]{:S(2)}, u32[]{:S(2)}) collective-permute-start(f32[1,16,2048]{2,1,0:T(8,128)S(1)} %get-tuple-element.74), channel_id=1, source_target_pairs={{0,4},{4,0},{8,12},{12,8},{1,5},{5,1},{9,13},{13,9},{2,6},{6,2},{1... | collective-permute-start | bytes 393224 | tf_op jit(solution)/shard_map/ppermute | solution.py:317
  7.0 6.0 %collective-permute-start.9 = (f32[1,16,2048]{2,1,0:T(8,128)S(1)}, f32[1,16,2048]{2,1,0:T(8,128)S(1)}, u32[]{:S(2)}, u32[]{:S(2)}) collective-permute-start(f32[1,16,2048]{2,1,0:T(8,128)S(1)} %get-tuple-element.71), channel_id=1, source_target_pairs={{0,12},{4,8},{8,4},{12,0},{1,13},{5,9},{9,5},{13,1},{2,14},{6,10},... | collective-permute-start | bytes 393224 | tf_op jit(solution)/shard_map/ppermute | solution.py:317
  9.7 7.3 %collective-permute-start.1 = (f32[2,16,2048]{2,1,0:T(8,128)S(1)}, f32[2,16,2048]{2,1,0:T(8,128)S(1)}, u32[]{:S(2)}, u32[]{:S(2)}) collective-permute-start(f32[2,16,2048]{2,1,0:T(8,128)S(1)} %pad_maximum_fusion.8), channel_id=1, source_target_pairs={{0,3},{1,2},{2,1},{3,0},{4,7},{5,6},{6,5},{7,4},{8,11},{9,10},{10,... | collective-permute-start | bytes 786440 | tf_op jit(solution)/shard_map/ppermute | solution.py:317
  10.7 6.8 %collective-permute-start.4 = (f32[2,16,2048]{2,1,0:T(8,128)S(1)}, f32[2,16,2048]{2,1,0:T(8,128)S(1)}, u32[]{:S(2)}, u32[]{:S(2)}) collective-permute-start(f32[2,16,2048]{2,1,0:T(8,128)S(1)} %pad_maximum_fusion.9), channel_id=1, source_target_pairs={{0,4},{4,0},{8,12},{12,8},{1,5},{5,1},{9,13},{13,9},{2,6},{6,2},{1... | collective-permute-start | bytes 786440 | tf_op jit(solution)/shard_map/ppermute | solution.py:317
  11.2 7.6 %copy-start.8 = (f32[1,16,2048]{2,1,0:T(8,128)}, f32[1,16,2048]{2,1,0:T(8,128)S(1)}, u32[]{:S(2)}) copy-start(f32[1,16,2048]{2,1,0:T(8,128)S(1)} %collective-permute-done.6) | copy-start | bytes 393220
  11.2 7.4 %collective-permute-start.7 = (f32[2,16,2048]{2,1,0:T(8,128)S(1)}, f32[2,16,2048]{2,1,0:T(8,128)S(1)}, u32[]{:S(2)}, u32[]{:S(2)}) collective-permute-start(f32[2,16,2048]{2,1,0:T(8,128)S(1)} %pad_maximum_fusion.10), channel_id=1, source_target_pairs={{0,12},{4,8},{8,4},{12,0},{1,13},{5,9},{9,5},{13,1},{2,14},{6,10},... | collective-permute-start | bytes 786440 | tf_op jit(solution)/shard_map/ppermute | solution.py:317
  13.1 5.6 %collective-permute-start.10 = (f32[2,16,2048]{2,1,0:T(8,128)S(1)}, f32[2,16,2048]{2,1,0:T(8,128)S(1)}, u32[]{:S(2)}, u32[]{:S(2)}) collective-permute-start(f32[2,16,2048]{2,1,0:T(8,128)S(1)} %pad_maximum_fusion.11), channel_id=1, source_target_pairs={{0,1},{1,0},{2,3},{3,2},{4,5},{5,4},{6,7},{7,6},{8,9},{9,8},{10,11... | collective-permute-start | bytes 786440 | tf_op jit(solution)/shard_map/ppermute | solution.py:317
  17.1 10.8 %collective-permute-start.2 = (f32[4,16,2048]{2,1,0:T(8,128)S(1)}, f32[4,16,2048]{2,1,0:T(8,128)S(1)}, u32[]{:S(2)}, u32[]{:S(2)}) collective-permute-start(f32[4,16,2048]{2,1,0:T(8,128)S(1)} %pad_maximum_fusion.4), channel_id=1, source_target_pairs={{0,4},{4,0},{8,12},{12,8},{1,5},{5,1},{9,13},{13,9},{2,6},{6,2},{1... | collective-permute-start | bytes 1572872 | tf_op jit(solution)/shard_map/ppermute | solution.py:317
  17.6 11.7 %collective-permute-start.5 = (f32[4,16,2048]{2,1,0:T(8,128)S(1)}, f32[4,16,2048]{2,1,0:T(8,128)S(1)}, u32[]{:S(2)}, u32[]{:S(2)}) collective-permute-start(f32[4,16,2048]{2,1,0:T(8,128)S(1)} %pad_maximum_fusion.5), channel_id=1, source_target_pairs={{0,12},{4,8},{8,4},{12,0},{1,13},{5,9},{9,5},{13,1},{2,14},{6,10},... | collective-permute-start | bytes 1572872 | tf_op jit(solution)/shard_map/ppermute | solution.py:317
  18.6 11.3 %collective-permute-start.8 = (f32[4,16,2048]{2,1,0:T(8,128)S(1)}, f32[4,16,2048]{2,1,0:T(8,128)S(1)}, u32[]{:S(2)}, u32[]{:S(2)}) collective-permute-start(f32[4,16,2048]{2,1,0:T(8,128)S(1)} %pad_maximum_fusion.6), channel_id=1, source_target_pairs={{0,1},{1,0},{2,3},{3,2},{4,5},{5,4},{6,7},{7,6},{8,9},{9,8},{10,11... | collective-permute-start | bytes 1572872 | tf_op jit(solution)/shard_map/ppermute | solution.py:317
  18.8 12.7 %collective-permute-start.11 = (f32[4,16,2048]{2,1,0:T(8,128)S(1)}, f32[4,16,2048]{2,1,0:T(8,128)S(1)}, u32[]{:S(2)}, u32[]{:S(2)}) collective-permute-start(f32[4,16,2048]{2,1,0:T(8,128)S(1)} %pad_maximum_fusion.7), channel_id=1, source_target_pairs={{0,3},{1,2},{2,1},{3,0},{4,7},{5,6},{6,5},{7,4},{8,11},{9,10},{10,... | collective-permute-start | bytes 1572872 | tf_op jit(solution)/shard_map/ppermute | solution.py:317
  20.8 9.1 %copy-start.9 = (f32[1,16,2048]{2,1,0:T(8,128)S(1)}, f32[1,16,2048]{2,1,0:T(8,128)}, u32[]{:S(2)}) copy-start(f32[1,16,2048]{2,1,0:T(8,128)} %copy-done.8) | copy-start | bytes 393220
  28.0 24.9 %collective-permute-start.12 = (f32[8,16,2048]{2,1,0:T(8,128)S(1)}, f32[8,16,2048]{2,1,0:T(8,128)}, u32[]{:S(2)}, u32[]{:S(2)}) collective-permute-start(f32[8,16,2048]{2,1,0:T(8,128)S(1)} %pad_maximum_fusion.refs_0_), channel_id=1, source_target_pairs={{0,12},{4,8},{8,4},{12,0},{1,13},{5,9},{9,5},{13,1},{2,14},{6,10},... | collective-permute-start | bytes 3145736 | tf_op jit(solution)/shard_map/ppermute | solution.py:317
  29.4 8.7 %copy-start.3 = (s32[16,16]{1,0:T(8,128)S(1)}, s32[16,16]{1,0:T(8,128)}, u32[]{:S(2)}) copy-start(s32[16,16]{1,0:T(8,128)} %mask_ref.2) | copy-start | bytes 3076
  29.4 23.5 %collective-permute-start.13 = (f32[8,16,2048]{2,1,0:T(8,128)S(1)}, f32[8,16,2048]{2,1,0:T(8,128)}, u32[]{:S(2)}, u32[]{:S(2)}) collective-permute-start(f32[8,16,2048]{2,1,0:T(8,128)S(1)} %pad_maximum_fusion.1.refs_1_), channel_id=1, source_target_pairs={{0,1},{1,0},{2,3},{3,2},{4,5},{5,4},{6,7},{7,6},{8,9},{9,8},{10,11... | collective-permute-start | bytes 3145736 | tf_op jit(solution)/shard_map/ppermute | solution.py:317
  30.0 22.9 %collective-permute-start.14 = (f32[8,16,2048]{2,1,0:T(8,128)S(1)}, f32[8,16,2048]{2,1,0:T(8,128)}, u32[]{:S(2)}, u32[]{:S(2)}) collective-permute-start(f32[8,16,2048]{2,1,0:T(8,128)S(1)} %pad_maximum_fusion.2.refs_2_), channel_id=1, source_target_pairs={{0,3},{1,2},{2,1},{3,0},{4,7},{5,6},{6,5},{7,4},{8,11},{9,10},{10,... | collective-permute-start | bytes 3145736 | tf_op jit(solution)/shard_map/ppermute | solution.py:317
  32.6 20.5 %collective-permute-start.15 = (f32[8,16,2048]{2,1,0:T(8,128)}, f32[8,16,2048]{2,1,0:T(8,128)}, u32[]{:S(2)}, u32[]{:S(2)}) collective-permute-start(f32[8,16,2048]{2,1,0:T(8,128)} %pad_maximum_fusion.3.refs_3_), channel_id=1, source_target_pairs={{0,4},{4,0},{8,12},{12,8},{1,5},{5,1},{9,13},{13,9},{2,6},{6,2},{1... | collective-permute-start | bytes 3145736 | tf_op jit(solution)/shard_map/ppermute | solution.py:317
  69.0 19.2 %collective-permute-start.16 = (f32[4,10,128,128]{3,2,1,0:T(8,128)}, f32[4,10,128,128]{3,2,1,0:T(8,128)}, u32[]{:S(2)}, u32[]{:S(2)}) collective-permute-start(f32[4,10,128,128]{3,2,1,0:T(8,128)} %get-tuple-element.42), channel_id=1, source_target_pairs={{0,16},{16,0},{1,17},{17,1},{2,18},{18,2},{3,19},{19,3},{4,20},{20... | collective-permute-start | bytes 7864328 | tf_op jit(solution)/shard_map/ppermute | solution.py:362
  89.9 6.8 %copy-start.5 = (bf16[512,2048]{1,0:T(8,128)(2,1)S(1)}, bf16[512,2048]{1,0:T(8,128)(2,1)}, u32[]{:S(2)}) copy-start(bf16[512,2048]{1,0:T(8,128)(2,1)} %get-tuple-element.56.ah) | copy-start | bytes 6291460
  92.8 15.4 %collective-permute-start.17 = (f32[5,128,128]{2,1,0:T(8,128)}, f32[5,128,128]{2,1,0:T(8,128)}, u32[]{:S(2)}, u32[]{:S(2)}) collective-permute-start(f32[5,128,128]{2,1,0:T(8,128)} %get-tuple-element.48), channel_id=1, source_target_pairs={{0,32},{32,64},{64,96},{96,0},{1,33},{33,65},{65,97},{97,1},{2,34}... | collective-permute-start | bytes 983048 | tf_op jit(solution)/shard_map/ppermute | solution.py:365
  95.5 12.7 %collective-permute-start.18 = (f32[5,128,128]{2,1,0:T(8,128)}, f32[5,128,128]{2,1,0:T(8,128)}, u32[]{:S(2)}, u32[]{:S(2)}) collective-permute-start(f32[5,128,128]{2,1,0:T(8,128)} %get-tuple-element.49), channel_id=1, source_target_pairs={{0,96},{32,0},{64,32},{96,64},{1,97},{33,1},{65,33},{97,65},{2,98}... | collective-permute-start | bytes 983048 | tf_op jit(solution)/shard_map/ppermute | solution.py:365
  96.7 16.4 %copy-start.4 = (bf16[512,2048]{1,0:T(8,128)(2,1)S(1)}, bf16[512,2048]{1,0:T(8,128)(2,1)}, u32[]{:S(2)}) copy-start(bf16[512,2048]{1,0:T(8,128)(2,1)} %get-tuple-element.53.ah) | copy-start | bytes 6291460
  106.6 15.1 %collective-permute-start.21 = (f32[4,6,128,128]{3,2,1,0:T(8,128)}, f32[4,6,128,128]{3,2,1,0:T(8,128)}, u32[]{:S(2)}, u32[]{:S(2)}) collective-permute-start(f32[4,6,128,128]{3,2,1,0:T(8,128)} %shard_map.110), channel_id=1, source_target_pairs={{0,16},{16,0},{1,17},{17,1},{2,18},{18,2},{3,19},{19,3},{4,20},{20... | collective-permute-start | bytes 4718600 | tf_op jit(solution)/shard_map/ppermute | solution.py:362
  110.4 19.5 %collective-permute-start.19 = (f32[10,128,128]{2,1,0:T(8,128)}, f32[10,128,128]{2,1,0:T(8,128)}, u32[]{:S(2)}, u32[]{:S(2)}) collective-permute-start(f32[10,128,128]{2,1,0:T(8,128)} %get-tuple-element.50), channel_id=1, source_target_pairs={{0,32},{32,64},{64,96},{96,0},{1,33},{33,65},{65,97},{97,1},{2,34}... | collective-permute-start | bytes 1966088 | tf_op jit(solution)/shard_map/ppermute | solution.py:365
  111.1 18.9 %collective-permute-start.20 = (f32[10,128,128]{2,1,0:T(8,128)}, f32[10,128,128]{2,1,0:T(8,128)}, u32[]{:S(2)}, u32[]{:S(2)}) collective-permute-start(f32[10,128,128]{2,1,0:T(8,128)} %get-tuple-element.51), channel_id=1, source_target_pairs={{0,96},{32,0},{64,32},{96,64},{1,97},{33,1},{65,33},{97,65},{2,98}... | collective-permute-start | bytes 1966088 | tf_op jit(solution)/shard_map/ppermute | solution.py:365
  123.3 9.1 %collective-permute-start.22 = (f32[3,128,128]{2,1,0:T(8,128)S(1)}, f32[3,128,128]{2,1,0:T(8,128)S(1)}, u32[]{:S(2)}, u32[]{:S(2)}) collective-permute-start(f32[3,128,128]{2,1,0:T(8,128)S(1)} %get-tuple-element.61), channel_id=1, source_target_pairs={{0,32},{32,64},{64,96},{96,0},{1,33},{33,65},{65,97},{97,1},{2,34}... | collective-permute-start | bytes 589832 | tf_op jit(solution)/shard_map/ppermute | solution.py:365
  123.4 9.0 %collective-permute-start.23 = (f32[3,128,128]{2,1,0:T(8,128)S(1)}, f32[3,128,128]{2,1,0:T(8,128)S(1)}, u32[]{:S(2)}, u32[]{:S(2)}) collective-permute-start(f32[3,128,128]{2,1,0:T(8,128)S(1)} %get-tuple-element.66), channel_id=1, source_target_pairs={{0,96},{32,0},{64,32},{96,64},{1,97},{33,1},{65,33},{97,65},{2,98}... | collective-permute-start | bytes 589832 | tf_op jit(solution)/shard_map/ppermute | solution.py:365
  132.5 11.1 %collective-permute-start.24 = (f32[6,128,128]{2,1,0:T(8,128)S(1)}, f32[6,128,128]{2,1,0:T(8,128)S(1)}, u32[]{:S(2)}, u32[]{:S(2)}) collective-permute-start(f32[6,128,128]{2,1,0:T(8,128)S(1)} %get-tuple-element.67), channel_id=1, source_target_pairs={{0,32},{32,64},{64,96},{96,0},{1,33},{33,65},{65,97},{97,1},{2,34}... | collective-permute-start | bytes 1179656 | tf_op jit(solution)/shard_map/ppermute | solution.py:365
  133.4 10.2 %collective-permute-start.25 = (f32[6,128,128]{2,1,0:T(8,128)S(1)}, f32[6,128,128]{2,1,0:T(8,128)S(1)}, u32[]{:S(2)}, u32[]{:S(2)}) collective-permute-start(f32[6,128,128]{2,1,0:T(8,128)S(1)} %get-tuple-element.68), channel_id=1, source_target_pairs={{0,96},{32,0},{64,32},{96,64},{1,97},{33,1},{65,33},{97,65},{2,98}... | collective-permute-start | bytes 1179656 | tf_op jit(solution)/shard_map/ppermute | solution.py:365
  147.3 29.1 %copy-start.2 = (f32[128,2048]{1,0:T(8,128)S(1)}, f32[128,2048]{1,0:T(8,128)}, u32[]{:S(2)}) copy-start(f32[128,2048]{1,0:T(8,128)} %den_ref.1) | copy-start | bytes 3145732
  (7 other events, 24.2 us)

commit v7 on v6

--- a/solution.py
+++ b/solution.py
@@ -177,7 +177,7 @@
         in_specs=[SMEM] * len(maps) + [HBM if first else VMEM] * len(rows) + [HBM],
         out_specs=(VMEM,) * len(shapes),
         scratch_shapes=scratch,
-        vmem=49,
+        vmem=38,
         flops=40 * 6 * m * depth * part * TILE,
         nbytes=4 * depth * part * TILE,
     )(*maps, *rows, integrals)
@@ -353,10 +353,7 @@
     late = [exchange(bufs[c], ORDERS[c][3]) for c in range(COLOURS)]
     held = (*bufs, *late)
 
-    source, place = plan(after(destination, *bufs))
-    place = jnp.pad(place.astype(f32).reshape(128, CAP), ((0, 0), (0, TILE - CAP)))
     terms = prepare_integrals(after(integrals, *bufs), integral_mask)
-    other, source, place = lax.optimization_barrier((other, source, place))
 
     def swap(value):
         return lax.ppermute(value, "core", [(0, 1), (1, 0)])
@@ -383,7 +380,11 @@
     p1, m1, plus1, minus1, base1 = far(mine1, from_core1)
     gp1, gm1 = along_z(p1, m1)
     ch, cl = prepare_cycle(after(cycle_tiles, base1), cycle_mask)
-    rp1, rm1 = along_z(*near(plus1, minus1, after(gp1, rp0, rm0, ch, cl), gm1))
+    near1 = near(plus1, minus1, after(gp1, rp0, rm0, ch, cl), gm1)
+    rp1, rm1 = along_z(*near1)
+
+    source, place = plan(after(destination, *near1))
+    place = jnp.pad(place.astype(f32).reshape(128, CAP), ((0, 0), (0, TILE - CAP)))
 
     sending = gather(source, place, ((base0, rp0, rm0), (base1, rp1, rm1))).reshape(128, 1, SLAB * TILE)
     units = lax.all_to_all(sending, everyone, split_axis=0, concat_axis=0, tiled=True)

time: 183 us -> 182 us (level)
  local copies, waits for them, and re-layouts: 5.62 us -> 8.93 us
    ppermute x8, waiting for transfers between devices: 10.8 us -> 0.87 us  [along_z(): return (lax.ppermute(p, 'z', ring(1)), lax.ppermute(m, 'z', ring(-1)))]
    ppermute x16, waiting for transfers between devices: 11.3 us -> 20 us  [exchange(): return lax.ppermute(value, axis, pairs)]
    pallas_call x4, Pallas kernels: 49.3 us -> 45.3 us  [multiply(): call(kernel, tuple(shapes), in_specs=[SMEM] * len(maps) + [HBM if first e...]
    pallas_call x5, Pallas kernels: 10.4 us -> 13.1 us  [small(): call(kernel, shapes, in_specs=[SMEM if x.dtype == jnp.int32 else VMEM for...]
    unnamed x27 -> x23, local copies, waits for them, and re-layouts: 4.06 us -> 4.43 us
  transfers between devices with their start and end apart: 26 -> 26, of which waited for: 6 -> 7; matrix products, arithmetic and copies ran while one was open for 4% -> 6% of each run, Pallas kernels for 29% -> 28%
where the time goes in v7:
time: 182 us
  Pallas kernels  80.6 us (44%)
  starting transfers between devices  34.8 us (19%)
  blocking collectives  28.2 us (15%)
  waiting for transfers between devices  20.9 us (11%)
  local copies, waits for them, and re-layouts  8.93 us (5%)
  other arithmetic  7.36 us (4%)
    pallas_call x4, Pallas kernels, multiply(): call(kernel, tuple(shapes), in_specs=[SMEM] * len(maps) + [HBM if first e...  45.3 us
    all_to_all x1, blocking collectives, body(): lax.all_to_all(sending, everyone, split_axis=0, concat_axis=0, tiled=True)  28.2 us
    ppermute x16, waiting for transfers between devices, exchange(): return lax.ppermute(value, axis, pairs)  20 us
    ppermute x16, starting transfers between devices, exchange(): return lax.ppermute(value, axis, pairs)  17.2 us
    pallas_call x1, Pallas kernels, prepare_integrals(): call(integrals_kernel, jax.ShapeDtypeStruct((cols // NB, 2, depth, NB), b...  14.8 us
    pallas_call x5, Pallas kernels, small(): call(kernel, shapes, in_specs=[SMEM if x.dtype == jnp.int32 else VMEM for...  13.1 us
    ppermute x8, starting transfers between devices, along_z(): return (lax.ppermute(p, 'z', ring(1)), lax.ppermute(m, 'z', ring(-1)))  11.8 us
    pallas_call x1, Pallas kernels, finish(): call(finish_kernel, (shape, shape), in_specs=[VMEM] * 4, out_specs=(VMEM,...  5.93 us
  transfers between devices with their start and end apart: 26, of which 7 were waited for; matrix products, arithmetic and copies ran while one was open for 6% of the time, Pallas kernels for 28%

profile of v7, /device:TPU:1, one launch (start us, length us, event | category | flops | bytes accessed | tf_op | source)
XLA Modules:
  0.0 181.9 jit_solution(6241194263745947095)
XLA Ops:
  1.8 2.2 %collective-permute-start.6 = (f32[1,16,2048]{2,1,0:T(8,128)S(1)}, f32[1,16,2048]{2,1,0:T(8,128)S(1)}, u32[]{:S(2)}, u32[]{:S(2)}) collective-permute-start(f32[1,16,2048]{2,1,0:T(8,128)S(1)} %get-tuple-element.68), channel_id=1, source_target_pairs={{0,4},{4,0},{8,12},{12,8},{1,5},{5,1},{9,13},{13,9},{2,6},{6,2},{1... | collective-permute-start | bytes 393224 | tf_op jit(solution)/shard_map/ppermute | solution.py:317
  4.0 1.9 %collective-permute-start.9 = (f32[1,16,2048]{2,1,0:T(8,128)S(1)}, f32[1,16,2048]{2,1,0:T(8,128)S(1)}, u32[]{:S(2)}, u32[]{:S(2)}) collective-permute-start(f32[1,16,2048]{2,1,0:T(8,128)S(1)} %get-tuple-element.65), channel_id=1, source_target_pairs={{0,12},{4,8},{8,4},{12,0},{1,13},{5,9},{9,5},{13,1},{2,14},{6,10},... | collective-permute-start | bytes 393224 | tf_op jit(solution)/shard_map/ppermute | solution.py:317
  5.9 2.5 %collective-permute-start.3 = (f32[1,16,2048]{2,1,0:T(8,128)S(1)}, f32[1,16,2048]{2,1,0:T(8,128)S(1)}, u32[]{:S(2)}, u32[]{:S(2)}) collective-permute-start(f32[1,16,2048]{2,1,0:T(8,128)S(1)} %get-tuple-element.66), channel_id=1, source_target_pairs={{0,3},{1,2},{2,1},{3,0},{4,7},{5,6},{6,5},{7,4},{8,11},{9,10},{10,... | collective-permute-start | bytes 393224 | tf_op jit(solution)/shard_map/ppermute | solution.py:317
  8.4 1.5 collective-permute-start.7
  12.5 1.5 collective-permute-start.1
  14.0 1.7 collective-permute-done.7
  15.8 1.5 collective-permute-start.8
  18.6 2.1 %collective-permute-start.5 = (f32[4,16,2048]{2,1,0:T(8,128)S(1)}, f32[4,16,2048]{2,1,0:T(8,128)S(1)}, u32[]{:S(2)}, u32[]{:S(2)}) collective-permute-start(f32[4,16,2048]{2,1,0:T(8,128)S(1)} %pad_maximum_fusion.5), channel_id=1, source_target_pairs={{0,12},{4,8},{8,4},{12,0},{1,13},{5,9},{9,5},{13,1},{2,14},{6,10},... | collective-permute-start | bytes 1572872 | tf_op jit(solution)/shard_map/ppermute | solution.py:317
  20.9 8.0 %collective-permute-done.8 = f32[4,16,2048]{2,1,0:T(8,128)S(1)} collective-permute-done((f32[4,16,2048]{2,1,0:T(8,128)S(1)}, f32[4,16,2048]{2,1,0:T(8,128)S(1)}, u32[]{:S(2)}, u32[]{:S(2)}) %collective-permute-start.8) | collective-permute-done | bytes 524320 | tf_op jit(solution)/shard_map/ppermute | solution.py:317
  30.0 2.3 %collective-permute-done.11 = f32[4,16,2048]{2,1,0:T(8,128)S(1)} collective-permute-done((f32[4,16,2048]{2,1,0:T(8,128)S(1)}, f32[4,16,2048]{2,1,0:T(8,128)S(1)}, u32[]{:S(2)}, u32[]{:S(2)}) %collective-permute-start.11) | collective-permute-done | bytes 524320 | tf_op jit(solution)/shard_map/ppermute | solution.py:317
  34.9 14.8 %shard_map.104.refs_8_.b_ref = bf16[8,2,2048,256]{3,2,1,0:T(8,128)(2,1)} custom-call(s32[16,16]{1,0:T(8,128)S(1)} %copy-done.6, f32[2048,2048]{1,0:T(8,128)} %x_ref), custom_call_target="tpu_custom_call" | custom-call | flops 16777216 | bytes 33554432 | tf_op jit(solution)/shard_map/pallas_call | solution.py:80
  49.7 6.0 %collective-permute-done.14.refs_6_ = f32[8,16,2048]{2,1,0:T(8,128)} collective-permute-done((f32[8,16,2048]{2,1,0:T(8,128)S(1)}, f32[8,16,2048]{2,1,0:T(8,128)}, u32[]{:S(2)}, u32[]{:S(2)}) %collective-permute-start.14) | collective-permute-done | bytes 1048608 | tf_op jit(solution)/shard_map/ppermute | solution.py:317
  55.7 15.9 %shard_map.105 = (f32[4,10,128,128]{3,2,1,0:T(8,128)}, bf16[512,2048]{1,0:T(8,128)(2,1)S(1)}, bf16[512,2048]{1,0:T(8,128)(2,1)S(1)}) custom-call(s32[4,8]{1,0:T(4,128)S(1)} %pad_add_fusion.1.where_ref.ready_ref, f32[8,16,2048]{2,1,0:T(8,128)} %pad_maximum_fusion.refs_0_, f32[8,16,2048]{2,1,0:T(8,128)S(1)} %pad_maximum_fusion.1.refs_1_, ...), custom_call_target="tpu_custom_call" | custom-call | flops 322122547200 | bytes 10485760 | tf_op jit(solution)/shard_map/pallas_call | solution.py:174
  71.6 4.1 %collective-permute-start.16 = (f32[4,10,128,128]{3,2,1,0:T(8,128)}, f32[4,10,128,128]{3,2,1,0:T(8,128)}, u32[]{:S(2)}, u32[]{:S(2)}) collective-permute-start(f32[4,10,128,128]{3,2,1,0:T(8,128)} %get-tuple-element.34), channel_id=1, source_target_pairs={{0,16},{16,0},{1,17},{17,1},{2,18},{18,2},{3,19},{19,3},{4,20},{20... | collective-permute-start | bytes 7864328 | tf_op jit(solution)/shard_map/ppermute | solution.py:359
  75.7 13.1 %shard_map.106 = (f32[4,10,128,128]{3,2,1,0:T(8,128)S(1)}, bf16[512,2048]{1,0:T(8,128)(2,1)S(1)}, bf16[512,2048]{1,0:T(8,128)(2,1)S(1)}) custom-call(s32[4,8]{1,0:T(4,128)S(1)} %pad_add_fusion.where_ref.ready_ref, f32[8,16,2048]{2,1,0:T(8,128)} %pad_maximum_fusion.refs_0_, f32[8,16,2048]{2,1,0:T(8,128)S(1)} %pad_maximum_fusion.1.refs_1_, ...), custom_call_target="tpu_custom_call" | custom-call | flops 322122547200 | bytes 10485760 | tf_op jit(solution)/shard_map/pallas_call | solution.py:174
  88.8 2.8 %shard_map.107 = (f32[5,128,128]{2,1,0:T(8,128)}, f32[5,128,128]{2,1,0:T(8,128)}, f32[10,128,128]{2,1,0:T(8,128)S(1)}, f32[10,128,128]{2,1,0:T(8,128)S(1)}, f32[10,128,128]{2,1,0:T(8,128)S(1)}) custom-call(f32[4,10,128,128]{3,2,1,0:T(8,128)S(1)} %get-tuple-element.36.mine_ref, f32[4,10,128,128]{3,2,1,0:T(8,128)} %collective-permute-done.16.got_ref), custom_call_target="tpu_custom_call" | custom-call | bytes 5242880 | tf_op jit(solution)/shard_map/pallas_call | solution.py:197
  91.7 2.9 %collective-permute-start.17 = (f32[5,128,128]{2,1,0:T(8,128)}, f32[5,128,128]{2,1,0:T(8,128)}, u32[]{:S(2)}, u32[]{:S(2)}) collective-permute-start(f32[5,128,128]{2,1,0:T(8,128)} %get-tuple-element.39), channel_id=1, source_target_pairs={{0,32},{32,64},{64,96},{96,0},{1,33},{33,65},{65,97},{97,1},{2,34}... | collective-permute-start | bytes 983048 | tf_op jit(solution)/shard_map/ppermute | solution.py:362
  95.5 8.7 %shard_map.110 = f32[4,6,128,128]{3,2,1,0:T(8,128)} custom-call(s32[4,8]{1,0:T(4,128)S(1)} %pad_add_fusion.1.where_ref.ready_ref, bf16[512,2048]{1,0:T(8,128)(2,1)S(1)} %get-tuple-element.48.ah, bf16[512,2048]{1,0:T(8,128)(2,1)S(1)} %get-tuple-element.49.al, bf16[8,2,2048,256]{3,2,1,0:T(8,128)(2,1)} %shard_map.104.refs_8_.b_ref), custom_call_target="tpu_custom_call" | custom-call | flops 193273528320 | bytes 6291456 | tf_op jit(solution)/shard_map/pallas_call | solution.py:174
  104.2 1.6 collective-permute-start.19
  105.8 2.2 %shard_map.108 = (f32[10,128,128]{2,1,0:T(8,128)}, f32[10,128,128]{2,1,0:T(8,128)}) custom-call(f32[10,128,128]{2,1,0:T(8,128)S(1)} %get-tuple-element.37.plus_ref, f32[10,128,128]{2,1,0:T(8,128)S(1)} %get-tuple-element.38.minus_ref, f32[5,128,128]{2,1,0:T(8,128)} %collective-permute-done.17.gp_ref, f32[5,128,128]{2,1,0:T(8,128)} %collective-permute-done.18.gm_ref), custom_call_target="tpu_custom_call" | custom-call | bytes 1966080 | tf_op jit(solution)/shard_map/pallas_call | solution.py:197
  108.9 1.8 collective-permute-start.22
  110.7 7.6 %shard_map.109.mine_ref = f32[4,6,128,128]{3,2,1,0:T(8,128)S(1)} custom-call(s32[4,8]{1,0:T(4,128)S(1)} %pad_add_fusion.where_ref.ready_ref, bf16[512,2048]{1,0:T(8,128)(2,1)S(1)} %get-tuple-element.44.ah, bf16[512,2048]{1,0:T(8,128)(2,1)S(1)} %get-tuple-element.45.al, bf16[8,2,2048,256]{3,2,1,0:T(8,128)(2,1)} %shard_map.104.refs_8_.b_ref), custom_call_target="tpu_custom_call" | custom-call | flops 193273528320 | bytes 6291456 | tf_op jit(solution)/shard_map/pallas_call | solution.py:174
  118.3 2.3 %shard_map.111 = (f32[3,128,128]{2,1,0:T(8,128)}, f32[3,128,128]{2,1,0:T(8,128)}, f32[6,128,128]{2,1,0:T(8,128)S(1)}, f32[6,128,128]{2,1,0:T(8,128)S(1)}, f32[6,128,128]{2,1,0:T(8,128)S(1)}) custom-call(f32[4,6,128,128]{3,2,1,0:T(8,128)S(1)} %shard_map.109.mine_ref, f32[4,6,128,128]{3,2,1,0:T(8,128)} %collective-permute-done.19.got_ref), custom_call_target="tpu_custom_call" | custom-call | bytes 3145728 | tf_op jit(solution)/shard_map/pallas_call | solution.py:197
  121.3 2.7 %collective-permute-start.23 = (f32[3,128,128]{2,1,0:T(8,128)}, f32[3,128,128]{2,1,0:T(8,128)}, u32[]{:S(2)}, u32[]{:S(2)}) collective-permute-start(f32[3,128,128]{2,1,0:T(8,128)} %get-tuple-element.58), channel_id=1, source_target_pairs={{0,96},{32,0},{64,32},{96,64},{1,97},{33,1},{65,33},{97,65},{2,98}... | collective-permute-start | bytes 589832 | tf_op jit(solution)/shard_map/ppermute | solution.py:362
  124.1 2.2 %copy-done = f32[2048,512]{1,0:T(8,128)S(1)} copy-done((f32[2048,512]{1,0:T(8,128)S(1)}, f32[2048,512]{1,0:T(8,128)}, u32[]{:S(2)}) %copy-start) | copy-done | bytes 4194328
  126.2 1.6 shard_map.112
  130.1 1.9 %shard_map.113 = (f32[6,128,128]{2,1,0:T(8,128)}, f32[6,128,128]{2,1,0:T(8,128)}) custom-call(f32[6,128,128]{2,1,0:T(8,128)S(1)} %get-tuple-element.50.plus_ref, f32[6,128,128]{2,1,0:T(8,128)S(1)} %copy-done.5, f32[3,128,128]{2,1,0:T(8,128)} %collective-permute-done.20.gp_ref, f32[3,128,128]{2,1,0:T(8,128)} %collective-permute-done.23.gm_ref), custom_call_target="tpu_custom_call" | custom-call | bytes 1179648 | tf_op jit(solution)/shard_map/pallas_call | solution.py:197
  133.1 1.6 collective-permute-start.25
  136.4 5.0 %sort.14 = (s32[2048]{0:T(1024)}, s32[2048]{0:T(1024)}) sort(s32[2048]{0:T(1024)S(1)} %fusion.10, s32[2048]{0:T(1024)S(1)} %iota.7), dimensions={0}, to_apply=%region_0.1 | sort | flops 22528 | bytes 32768 | tf_op jit(solution)/shard_map/sort | solution.py:301
  143.7 3.9 %shard_map.114 = f32[2176,128]{1,0:T(8,128)S(1)} custom-call(s32[2048]{0:T(1024)S(1)} %get-tuple-element.70.idx_ref, f32[128,128]{1,0:T(8,128)S(1)} %pad.4.place_ref, f32[10,128,128]{2,1,0:T(8,128)S(1)} %get-tuple-element.46.refs_0_, f32[10,128,128]{2,1,0:T(8,128)} %collective-permute-done.21.refs_1_, f32[10,128,128]{2,1,0:T(8,128)} %collective-permute-done.22.refs_2_, ...), custom_call_target="tpu_custom_call" | custom-call | bytes 3219456 | tf_op jit(solution)/shard_map/pallas_call | solution.py:197
  147.6 28.2 %all_to_all.5 = f32[128,1,2176]{2,1,0:T(1,128)S(1)} all-to-all(f32[128,1,2176]{2,1,0:T(1,128)S(1)} %bitcast.26), channel_id=1, replica_groups=mesh['z'=4,'core'=2,'y'=4,'x'=4] {'z','core','y','x'}, dimensions={0} | all-to-all | bytes 2228224 | tf_op jit(solution)/shard_map/all_to_all | solution.py:390
  175.8 5.9 %shard_map.115 = (f32[128,2048]{1,0:T(8,128)}, f32[128,2048]{1,0:T(8,128)}) custom-call(f32[2176,128]{1,0:T(8,128)S(1)} %bitcast.27, f32[128,2048]{1,0:T(8,128)S(1)} %copy-done.3, bf16[2048,512]{1,0:T(8,128)(2,1)S(1)} %get-tuple-element.55.ch_ref, bf16[2048,512]{1,0:T(8,128)(2,1)S(1)} %copy-done.2), custom_call_target="tpu_custom_call" | custom-call | bytes 8388608 | tf_op jit(solution)/shard_map/pallas_call | solution.py:277
  (84 shorter events, 18.8 us)
Async XLA Ops:
  1.8 6.6 %collective-permute-start.6 = (f32[1,16,2048]{2,1,0:T(8,128)S(1)}, f32[1,16,2048]{2,1,0:T(8,128)S(1)}, u32[]{:S(2)}, u32[]{:S(2)}) collective-permute-start(f32[1,16,2048]{2,1,0:T(8,128)S(1)} %get-tuple-element.68), channel_id=1, source_target_pairs={{0,4},{4,0},{8,12},{12,8},{1,5},{5,1},{9,13},{13,9},{2,6},{6,2},{1... | collective-permute-start | bytes 393224 | tf_op jit(solution)/shard_map/ppermute | solution.py:317
  4.0 5.9 %collective-permute-start.9 = (f32[1,16,2048]{2,1,0:T(8,128)S(1)}, f32[1,16,2048]{2,1,0:T(8,128)S(1)}, u32[]{:S(2)}, u32[]{:S(2)}) collective-permute-start(f32[1,16,2048]{2,1,0:T(8,128)S(1)} %get-tuple-element.65), channel_id=1, source_target_pairs={{0,12},{4,8},{8,4},{12,0},{1,13},{5,9},{9,5},{13,1},{2,14},{6,10},... | collective-permute-start | bytes 393224 | tf_op jit(solution)/shard_map/ppermute | solution.py:317
  5.9 5.3 %collective-permute-start.3 = (f32[1,16,2048]{2,1,0:T(8,128)S(1)}, f32[1,16,2048]{2,1,0:T(8,128)S(1)}, u32[]{:S(2)}, u32[]{:S(2)}) collective-permute-start(f32[1,16,2048]{2,1,0:T(8,128)S(1)} %get-tuple-element.66), channel_id=1, source_target_pairs={{0,3},{1,2},{2,1},{3,0},{4,7},{5,6},{6,5},{7,4},{8,11},{9,10},{10,... | collective-permute-start | bytes 393224 | tf_op jit(solution)/shard_map/ppermute | solution.py:317
  8.4 4.1 %collective-permute-start = (f32[1,16,2048]{2,1,0:T(8,128)S(1)}, f32[1,16,2048]{2,1,0:T(8,128)S(1)}, u32[]{:S(2)}, u32[]{:S(2)}) collective-permute-start(f32[1,16,2048]{2,1,0:T(8,128)S(1)} %get-tuple-element.67), channel_id=1, source_target_pairs={{0,1},{1,0},{2,3},{3,2},{4,5},{5,4},{6,7},{7,6},{8,9},{9,8},{10,11... | collective-permute-start | bytes 393224 | tf_op jit(solution)/shard_map/ppermute | solution.py:317
  8.4 7.4 %collective-permute-start.7 = (f32[2,16,2048]{2,1,0:T(8,128)S(1)}, f32[2,16,2048]{2,1,0:T(8,128)S(1)}, u32[]{:S(2)}, u32[]{:S(2)}) collective-permute-start(f32[2,16,2048]{2,1,0:T(8,128)S(1)} %pad_maximum_fusion.10), channel_id=1, source_target_pairs={{0,12},{4,8},{8,4},{12,0},{1,13},{5,9},{9,5},{13,1},{2,14},{6,10},... | collective-permute-start | bytes 786440 | tf_op jit(solution)/shard_map/ppermute | solution.py:317
  9.9 8.1 %collective-permute-start.10 = (f32[2,16,2048]{2,1,0:T(8,128)S(1)}, f32[2,16,2048]{2,1,0:T(8,128)S(1)}, u32[]{:S(2)}, u32[]{:S(2)}) collective-permute-start(f32[2,16,2048]{2,1,0:T(8,128)S(1)} %pad_maximum_fusion.11), channel_id=1, source_target_pairs={{0,1},{1,0},{2,3},{3,2},{4,5},{5,4},{6,7},{7,6},{8,9},{9,8},{10,11... | collective-permute-start | bytes 786440 | tf_op jit(solution)/shard_map/ppermute | solution.py:317
  11.2 7.3 %collective-permute-start.4 = (f32[2,16,2048]{2,1,0:T(8,128)S(1)}, f32[2,16,2048]{2,1,0:T(8,128)S(1)}, u32[]{:S(2)}, u32[]{:S(2)}) collective-permute-start(f32[2,16,2048]{2,1,0:T(8,128)S(1)} %pad_maximum_fusion.9), channel_id=1, source_target_pairs={{0,4},{4,0},{8,12},{12,8},{1,5},{5,1},{9,13},{13,9},{2,6},{6,2},{1... | collective-permute-start | bytes 786440 | tf_op jit(solution)/shard_map/ppermute | solution.py:317
  12.5 8.2 %collective-permute-start.1 = (f32[2,16,2048]{2,1,0:T(8,128)S(1)}, f32[2,16,2048]{2,1,0:T(8,128)S(1)}, u32[]{:S(2)}, u32[]{:S(2)}) collective-permute-start(f32[2,16,2048]{2,1,0:T(8,128)S(1)} %pad_maximum_fusion.8), channel_id=1, source_target_pairs={{0,3},{1,2},{2,1},{3,0},{4,7},{5,6},{6,5},{7,4},{8,11},{9,10},{10,... | collective-permute-start | bytes 786440 | tf_op jit(solution)/shard_map/ppermute | solution.py:317
  15.8 13.1 %collective-permute-start.8 = (f32[4,16,2048]{2,1,0:T(8,128)S(1)}, f32[4,16,2048]{2,1,0:T(8,128)S(1)}, u32[]{:S(2)}, u32[]{:S(2)}) collective-permute-start(f32[4,16,2048]{2,1,0:T(8,128)S(1)} %pad_maximum_fusion.6), channel_id=1, source_target_pairs={{0,1},{1,0},{2,3},{3,2},{4,5},{5,4},{6,7},{7,6},{8,9},{9,8},{10,11... | collective-permute-start | bytes 1572872 | tf_op jit(solution)/shard_map/ppermute | solution.py:317
  18.1 14.3 %collective-permute-start.11 = (f32[4,16,2048]{2,1,0:T(8,128)S(1)}, f32[4,16,2048]{2,1,0:T(8,128)S(1)}, u32[]{:S(2)}, u32[]{:S(2)}) collective-permute-start(f32[4,16,2048]{2,1,0:T(8,128)S(1)} %pad_maximum_fusion.7), channel_id=1, source_target_pairs={{0,3},{1,2},{2,1},{3,0},{4,7},{5,6},{6,5},{7,4},{8,11},{9,10},{10,... | collective-permute-start | bytes 1572872 | tf_op jit(solution)/shard_map/ppermute | solution.py:317
  18.6 14.1 %collective-permute-start.5 = (f32[4,16,2048]{2,1,0:T(8,128)S(1)}, f32[4,16,2048]{2,1,0:T(8,128)S(1)}, u32[]{:S(2)}, u32[]{:S(2)}) collective-permute-start(f32[4,16,2048]{2,1,0:T(8,128)S(1)} %pad_maximum_fusion.5), channel_id=1, source_target_pairs={{0,12},{4,8},{8,4},{12,0},{1,13},{5,9},{9,5},{13,1},{2,14},{6,10},... | collective-permute-start | bytes 1572872 | tf_op jit(solution)/shard_map/ppermute | solution.py:317
  20.8 12.1 %collective-permute-start.2 = (f32[4,16,2048]{2,1,0:T(8,128)S(1)}, f32[4,16,2048]{2,1,0:T(8,128)S(1)}, u32[]{:S(2)}, u32[]{:S(2)}) collective-permute-start(f32[4,16,2048]{2,1,0:T(8,128)S(1)} %pad_maximum_fusion.4), channel_id=1, source_target_pairs={{0,4},{4,0},{8,12},{12,8},{1,5},{5,1},{9,13},{13,9},{2,6},{6,2},{1... | collective-permute-start | bytes 1572872 | tf_op jit(solution)/shard_map/ppermute | solution.py:317
  29.0 26.6 %collective-permute-start.14 = (f32[8,16,2048]{2,1,0:T(8,128)S(1)}, f32[8,16,2048]{2,1,0:T(8,128)}, u32[]{:S(2)}, u32[]{:S(2)}) collective-permute-start(f32[8,16,2048]{2,1,0:T(8,128)S(1)} %pad_maximum_fusion.2.refs_2_), channel_id=1, source_target_pairs={{0,3},{1,2},{2,1},{3,0},{4,7},{5,6},{6,5},{7,4},{8,11},{9,10},{10,... | collective-permute-start | bytes 3145736 | tf_op jit(solution)/shard_map/ppermute | solution.py:317
  32.5 2.4 %copy-start.6 = (s32[16,16]{1,0:T(8,128)S(1)}, s32[16,16]{1,0:T(8,128)}, u32[]{:S(2)}) copy-start(s32[16,16]{1,0:T(8,128)} %mask_ref.2) | copy-start | bytes 3076
  32.5 23.2 %collective-permute-start.15 = (f32[8,16,2048]{2,1,0:T(8,128)S(1)}, f32[8,16,2048]{2,1,0:T(8,128)}, u32[]{:S(2)}, u32[]{:S(2)}) collective-permute-start(f32[8,16,2048]{2,1,0:T(8,128)S(1)} %pad_maximum_fusion.3.refs_3_), channel_id=1, source_target_pairs={{0,4},{4,0},{8,12},{12,8},{1,5},{5,1},{9,13},{13,9},{2,6},{6,2},{1... | collective-permute-start | bytes 3145736 | tf_op jit(solution)/shard_map/ppermute | solution.py:317
  32.8 22.9 %collective-permute-start.13 = (f32[8,16,2048]{2,1,0:T(8,128)S(1)}, f32[8,16,2048]{2,1,0:T(8,128)}, u32[]{:S(2)}, u32[]{:S(2)}) collective-permute-start(f32[8,16,2048]{2,1,0:T(8,128)S(1)} %pad_maximum_fusion.1.refs_1_), channel_id=1, source_target_pairs={{0,1},{1,0},{2,3},{3,2},{4,5},{5,4},{6,7},{7,6},{8,9},{9,8},{10,11... | collective-permute-start | bytes 3145736 | tf_op jit(solution)/shard_map/ppermute | solution.py:317
  33.9 21.7 %collective-permute-start.12 = (f32[8,16,2048]{2,1,0:T(8,128)}, f32[8,16,2048]{2,1,0:T(8,128)}, u32[]{:S(2)}, u32[]{:S(2)}) collective-permute-start(f32[8,16,2048]{2,1,0:T(8,128)} %pad_maximum_fusion.refs_0_), channel_id=1, source_target_pairs={{0,12},{4,8},{8,4},{12,0},{1,13},{5,9},{9,5},{13,1},{2,14},{6,10},... | collective-permute-start | bytes 3145736 | tf_op jit(solution)/shard_map/ppermute | solution.py:317
  71.6 17.3 %collective-permute-start.16 = (f32[4,10,128,128]{3,2,1,0:T(8,128)}, f32[4,10,128,128]{3,2,1,0:T(8,128)}, u32[]{:S(2)}, u32[]{:S(2)}) collective-permute-start(f32[4,10,128,128]{3,2,1,0:T(8,128)} %get-tuple-element.34), channel_id=1, source_target_pairs={{0,16},{16,0},{1,17},{17,1},{2,18},{18,2},{3,19},{19,3},{4,20},{20... | collective-permute-start | bytes 7864328 | tf_op jit(solution)/shard_map/ppermute | solution.py:359
  91.7 14.2 %collective-permute-start.17 = (f32[5,128,128]{2,1,0:T(8,128)}, f32[5,128,128]{2,1,0:T(8,128)}, u32[]{:S(2)}, u32[]{:S(2)}) collective-permute-start(f32[5,128,128]{2,1,0:T(8,128)} %get-tuple-element.39), channel_id=1, source_target_pairs={{0,32},{32,64},{64,96},{96,0},{1,33},{33,65},{65,97},{97,1},{2,34}... | collective-permute-start | bytes 983048 | tf_op jit(solution)/shard_map/ppermute | solution.py:362
  94.5 11.3 %collective-permute-start.18 = (f32[5,128,128]{2,1,0:T(8,128)}, f32[5,128,128]{2,1,0:T(8,128)}, u32[]{:S(2)}, u32[]{:S(2)}) collective-permute-start(f32[5,128,128]{2,1,0:T(8,128)} %get-tuple-element.40), channel_id=1, source_target_pairs={{0,96},{32,0},{64,32},{96,64},{1,97},{33,1},{65,33},{97,65},{2,98}... | collective-permute-start | bytes 983048 | tf_op jit(solution)/shard_map/ppermute | solution.py:362
  104.2 14.1 %collective-permute-start.19 = (f32[4,6,128,128]{3,2,1,0:T(8,128)}, f32[4,6,128,128]{3,2,1,0:T(8,128)}, u32[]{:S(2)}, u32[]{:S(2)}) collective-permute-start(f32[4,6,128,128]{3,2,1,0:T(8,128)} %shard_map.110), channel_id=1, source_target_pairs={{0,16},{16,0},{1,17},{17,1},{2,18},{18,2},{3,19},{19,3},{4,20},{20... | collective-permute-start | bytes 4718600 | tf_op jit(solution)/shard_map/ppermute | solution.py:359
  108.0 21.2 %collective-permute-start.21 = (f32[10,128,128]{2,1,0:T(8,128)}, f32[10,128,128]{2,1,0:T(8,128)}, u32[]{:S(2)}, u32[]{:S(2)}) collective-permute-start(f32[10,128,128]{2,1,0:T(8,128)} %get-tuple-element.41), channel_id=1, source_target_pairs={{0,32},{32,64},{64,96},{96,0},{1,33},{33,65},{65,97},{97,1},{2,34}... | collective-permute-start | bytes 1966088 | tf_op jit(solution)/shard_map/ppermute | solution.py:362
  108.9 20.3 %collective-permute-start.22 = (f32[10,128,128]{2,1,0:T(8,128)}, f32[10,128,128]{2,1,0:T(8,128)}, u32[]{:S(2)}, u32[]{:S(2)}) collective-permute-start(f32[10,128,128]{2,1,0:T(8,128)} %get-tuple-element.42), channel_id=1, source_target_pairs={{0,96},{32,0},{64,32},{96,64},{1,97},{33,1},{65,33},{97,65},{2,98}... | collective-permute-start | bytes 1966088 | tf_op jit(solution)/shard_map/ppermute | solution.py:362
  118.2 5.7 %copy-start.8 = (s32[16,4]{0,1:T(4,128)S(1)}, s32[16,4]{0,1:T(4,128)}, u32[]{:S(2)}) copy-start(s32[16,4]{0,1:T(4,128)} %param.14) | copy-start | bytes 772
  121.3 8.8 %collective-permute-start.20 = (f32[3,128,128]{2,1,0:T(8,128)}, f32[3,128,128]{2,1,0:T(8,128)}, u32[]{:S(2)}, u32[]{:S(2)}) collective-permute-start(f32[3,128,128]{2,1,0:T(8,128)} %get-tuple-element.52), channel_id=1, source_target_pairs={{0,32},{32,64},{64,96},{96,0},{1,33},{33,65},{65,97},{97,1},{2,34}... | collective-permute-start | bytes 589832 | tf_op jit(solution)/shard_map/ppermute | solution.py:362
  121.3 8.8 %collective-permute-start.23 = (f32[3,128,128]{2,1,0:T(8,128)}, f32[3,128,128]{2,1,0:T(8,128)}, u32[]{:S(2)}, u32[]{:S(2)}) collective-permute-start(f32[3,128,128]{2,1,0:T(8,128)} %get-tuple-element.58), channel_id=1, source_target_pairs={{0,96},{32,0},{64,32},{96,64},{1,97},{33,1},{65,33},{97,65},{2,98}... | collective-permute-start | bytes 589832 | tf_op jit(solution)/shard_map/ppermute | solution.py:362
  126.2 3.8 %copy-start.5 = (f32[6,128,128]{2,1,0:T(8,128)S(1)}, f32[6,128,128]{2,1,0:T(8,128)}, u32[]{:S(2)}) copy-start(f32[6,128,128]{2,1,0:T(8,128)} %copy-done.4) | copy-start | bytes 1179652
  126.2 8.5 %copy-start.7 = (s32[128,16]{0,1:T(8,128)S(1)}, s32[128,16]{0,1:T(8,128)}, u32[]{:S(2)}) copy-start(s32[128,16]{0,1:T(8,128)} %param.15) | copy-start | bytes 24580
  132.0 11.7 %collective-permute-start.24 = (f32[6,128,128]{2,1,0:T(8,128)}, f32[6,128,128]{2,1,0:T(8,128)S(1)}, u32[]{:S(2)}, u32[]{:S(2)}) collective-permute-start(f32[6,128,128]{2,1,0:T(8,128)} %get-tuple-element.59), channel_id=1, source_target_pairs={{0,32},{32,64},{64,96},{96,0},{1,33},{33,65},{65,97},{97,1},{2,34}... | collective-permute-start | bytes 1179656 | tf_op jit(solution)/shard_map/ppermute | solution.py:362
  133.1 10.6 %collective-permute-start.25 = (f32[6,128,128]{2,1,0:T(8,128)}, f32[6,128,128]{2,1,0:T(8,128)}, u32[]{:S(2)}, u32[]{:S(2)}) collective-permute-start(f32[6,128,128]{2,1,0:T(8,128)} %get-tuple-element.60), channel_id=1, source_target_pairs={{0,96},{32,0},{64,32},{96,64},{1,97},{33,1},{65,33},{97,65},{2,98}... | collective-permute-start | bytes 1179656 | tf_op jit(solution)/shard_map/ppermute | solution.py:362
  143.7 32.1 %copy-start.3 = (f32[128,2048]{1,0:T(8,128)S(1)}, f32[128,2048]{1,0:T(8,128)}, u32[]{:S(2)}) copy-start(f32[128,2048]{1,0:T(8,128)} %den_ref.1) | copy-start | bytes 3145732
  147.6 28.2 %copy-start.2 = (bf16[2048,512]{1,0:T(8,128)(2,1)S(1)}, bf16[2048,512]{1,0:T(8,128)(2,1)}, u32[]{:S(2)}) copy-start(bf16[2048,512]{1,0:T(8,128)(2,1)} %copy-done.1) | copy-start | bytes 6291460
  (5 other events, 8.9 us)

commit v8 on v6

--- a/solution.py
+++ b/solution.py
@@ -177,7 +177,7 @@
         in_specs=[SMEM] * len(maps) + [HBM if first else VMEM] * len(rows) + [HBM],
         out_specs=(VMEM,) * len(shapes),
         scratch_shapes=scratch,
-        vmem=49,
+        vmem=38,
         flops=40 * 6 * m * depth * part * TILE,
         nbytes=4 * depth * part * TILE,
     )(*maps, *rows, integrals)

time: 183 us -> 179 us (0.978)
  Pallas kernels: 82 us -> 78.5 us
    pallas_call x4, Pallas kernels: 49.3 us -> 45.9 us  [multiply(): call(kernel, tuple(shapes), in_specs=[SMEM] * len(maps) + [HBM if first e...]
    unnamed x27 -> x21, local copies, waits for them, and re-layouts: 4.06 us -> 2.32 us
  transfers between devices with their start and end apart: 26 -> 26, of which waited for: 6 -> 6; matrix products, arithmetic and copies ran while one was open for 4% -> 4% of each run, Pallas kernels for 29% -> 28%
where the time goes in v8:
time: 179 us; the launch traced here: 178 us
  Pallas kernels  78.5 us (44%)
  starting transfers between devices  35.2 us (20%)
  blocking collectives  29.1 us (16%)
  waiting for transfers between devices  23.1 us (13%)
  other arithmetic  7.31 us (4%)
  local copies, waits for them, and re-layouts  3.88 us (2%)
    pallas_call x4, Pallas kernels, multiply(): call(kernel, tuple(shapes), in_specs=[SMEM] * len(maps) + [HBM if first e...  45.9 us
    all_to_all x1, blocking collectives, body(): lax.all_to_all(sending, everyone, split_axis=0, concat_axis=0, tiled=True)  29.1 us
    ppermute x16, starting transfers between devices, exchange(): return lax.ppermute(value, axis, pairs)  17.2 us
    pallas_call x1, Pallas kernels, prepare_integrals(): call(integrals_kernel, jax.ShapeDtypeStruct((cols // NB, 2, depth, NB), b...  14.8 us
    ppermute x8, starting transfers between devices, along_z(): return (lax.ppermute(p, 'z', ring(1)), lax.ppermute(m, 'z', ring(-1)))  12.1 us
    ppermute x8, waiting for transfers between devices, along_z(): return (lax.ppermute(p, 'z', ring(1)), lax.ppermute(m, 'z', ring(-1)))  11.8 us
    ppermute x16, waiting for transfers between devices, exchange(): return lax.ppermute(value, axis, pairs)  11.3 us
    pallas_call x5, Pallas kernels, small(): call(kernel, shapes, in_specs=[SMEM if x.dtype == jnp.int32 else VMEM for...  10.2 us
  transfers between devices with their start and end apart: 26, of which 6 were waited for; matrix products, arithmetic and copies ran while one was open for 4% of the time, Pallas kernels for 28%

profile of v8, /device:TPU:1, one launch (start us, length us, event | category | flops | bytes accessed | tf_op | source)
XLA Modules:
  0.0 178.2 jit_solution(12280888800247754449)
XLA Ops:
  1.8 2.1 %collective-permute-start = (f32[1,16,2048]{2,1,0:T(8,128)S(1)}, f32[1,16,2048]{2,1,0:T(8,128)S(1)}, u32[]{:S(2)}, u32[]{:S(2)}) collective-permute-start(f32[1,16,2048]{2,1,0:T(8,128)S(1)} %get-tuple-element.73), channel_id=1, source_target_pairs={{0,1},{1,0},{2,3},{3,2},{4,5},{5,4},{6,7},{7,6},{8,9},{9,8},{10,11... | collective-permute-start | bytes 393224 | tf_op jit(solution)/shard_map/ppermute | solution.py:317
  3.9 1.8 %collective-permute-start.3 = (f32[1,16,2048]{2,1,0:T(8,128)S(1)}, f32[1,16,2048]{2,1,0:T(8,128)S(1)}, u32[]{:S(2)}, u32[]{:S(2)}) collective-permute-start(f32[1,16,2048]{2,1,0:T(8,128)S(1)} %get-tuple-element.72), channel_id=1, source_target_pairs={{0,3},{1,2},{2,1},{3,0},{4,7},{5,6},{6,5},{7,4},{8,11},{9,10},{10,... | collective-permute-start | bytes 393224 | tf_op jit(solution)/shard_map/ppermute | solution.py:317
  5.7 1.3 collective-permute-start.6
  7.0 1.9 %collective-permute-start.9 = (f32[1,16,2048]{2,1,0:T(8,128)S(1)}, f32[1,16,2048]{2,1,0:T(8,128)S(1)}, u32[]{:S(2)}, u32[]{:S(2)}) collective-permute-start(f32[1,16,2048]{2,1,0:T(8,128)S(1)} %get-tuple-element.71), channel_id=1, source_target_pairs={{0,12},{4,8},{8,4},{12,0},{1,13},{5,9},{9,5},{13,1},{2,14},{6,10},... | collective-permute-start | bytes 393224 | tf_op jit(solution)/shard_map/ppermute | solution.py:317
  11.2 1.8 %collective-permute-start.7 = (f32[2,16,2048]{2,1,0:T(8,128)S(1)}, f32[2,16,2048]{2,1,0:T(8,128)S(1)}, u32[]{:S(2)}, u32[]{:S(2)}) collective-permute-start(f32[2,16,2048]{2,1,0:T(8,128)S(1)} %pad_maximum_fusion.10), channel_id=1, source_target_pairs={{0,12},{4,8},{8,4},{12,0},{1,13},{5,9},{9,5},{13,1},{2,14},{6,10},... | collective-permute-start | bytes 786440 | tf_op jit(solution)/shard_map/ppermute | solution.py:317
  13.2 3.9 %collective-permute-done.1 = f32[2,16,2048]{2,1,0:T(8,128)S(1)} collective-permute-done((f32[2,16,2048]{2,1,0:T(8,128)S(1)}, f32[2,16,2048]{2,1,0:T(8,128)S(1)}, u32[]{:S(2)}, u32[]{:S(2)}) %collective-permute-start.1) | collective-permute-done | bytes 262176 | tf_op jit(solution)/shard_map/ppermute | solution.py:317
  18.8 2.0 %collective-permute-start.11 = (f32[4,16,2048]{2,1,0:T(8,128)S(1)}, f32[4,16,2048]{2,1,0:T(8,128)S(1)}, u32[]{:S(2)}, u32[]{:S(2)}) collective-permute-start(f32[4,16,2048]{2,1,0:T(8,128)S(1)} %pad_maximum_fusion.7), channel_id=1, source_target_pairs={{0,3},{1,2},{2,1},{3,0},{4,7},{5,6},{6,5},{7,4},{8,11},{9,10},{10,... | collective-permute-start | bytes 1572872 | tf_op jit(solution)/shard_map/ppermute | solution.py:317
  20.8 7.0 %collective-permute-done.2 = f32[4,16,2048]{2,1,0:T(8,128)S(1)} collective-permute-done((f32[4,16,2048]{2,1,0:T(8,128)S(1)}, f32[4,16,2048]{2,1,0:T(8,128)S(1)}, u32[]{:S(2)}, u32[]{:S(2)}) %collective-permute-start.2) | collective-permute-done | bytes 524320 | tf_op jit(solution)/shard_map/ppermute | solution.py:317
  30.0 1.5 collective-permute-start.14
  33.0 5.0 %sort.14 = (s32[2048]{0:T(1024)S(1)}, s32[2048]{0:T(1024)}) sort(s32[2048]{0:T(1024)S(1)} %fusion.10, s32[2048]{0:T(1024)S(1)} %iota.7), dimensions={0}, to_apply=%region_0.1 | sort | flops 22528 | bytes 32768 | tf_op jit(solution)/shard_map/sort | solution.py:301
  38.1 14.8 %shard_map.104.refs_8_.b_ref = bf16[8,2,2048,256]{3,2,1,0:T(8,128)(2,1)} custom-call(s32[16,16]{1,0:T(8,128)S(1)} %copy-done.2, f32[2048,2048]{1,0:T(8,128)} %x_ref), custom_call_target="tpu_custom_call" | custom-call | flops 16777216 | bytes 33554432 | tf_op jit(solution)/shard_map/pallas_call | solution.py:80
  53.1 16.0 %shard_map.105 = (f32[4,10,128,128]{3,2,1,0:T(8,128)}, bf16[512,2048]{1,0:T(8,128)(2,1)S(1)}, bf16[512,2048]{1,0:T(8,128)(2,1)S(1)}) custom-call(s32[4,8]{1,0:T(4,128)S(1)} %pad_add_fusion.where_ref.ready_ref, f32[8,16,2048]{2,1,0:T(8,128)S(1)} %pad_maximum_fusion.refs_0_, f32[8,16,2048]{2,1,0:T(8,128)S(1)} %pad_maximum_fusion.1.refs_1_, ...), custom_call_target="tpu_custom_call" | custom-call | flops 322122547200 | bytes 10485760 | tf_op jit(solution)/shard_map/pallas_call | solution.py:174
  69.0 4.3 %collective-permute-start.16 = (f32[4,10,128,128]{3,2,1,0:T(8,128)}, f32[4,10,128,128]{3,2,1,0:T(8,128)}, u32[]{:S(2)}, u32[]{:S(2)}) collective-permute-start(f32[4,10,128,128]{3,2,1,0:T(8,128)} %get-tuple-element.42), channel_id=1, source_target_pairs={{0,16},{16,0},{1,17},{17,1},{2,18},{18,2},{3,19},{19,3},{4,20},{20... | collective-permute-start | bytes 7864328 | tf_op jit(solution)/shard_map/ppermute | solution.py:362
  73.3 13.5 %shard_map.106 = (f32[4,10,128,128]{3,2,1,0:T(8,128)S(1)}, bf16[512,2048]{1,0:T(8,128)(2,1)S(1)}, bf16[512,2048]{1,0:T(8,128)(2,1)S(1)}) custom-call(s32[4,8]{1,0:T(4,128)S(1)} %pad_add_fusion.1.where_ref.ready_ref, f32[8,16,2048]{2,1,0:T(8,128)S(1)} %pad_maximum_fusion.refs_0_, f32[8,16,2048]{2,1,0:T(8,128)S(1)} %pad_maximum_fusion.1.refs_1_, ...), custom_call_target="tpu_custom_call" | custom-call | flops 322122547200 | bytes 10485760 | tf_op jit(solution)/shard_map/pallas_call | solution.py:174
  86.9 2.7 %shard_map.107 = (f32[5,128,128]{2,1,0:T(8,128)}, f32[5,128,128]{2,1,0:T(8,128)}, f32[10,128,128]{2,1,0:T(8,128)S(1)}, f32[10,128,128]{2,1,0:T(8,128)S(1)}, f32[10,128,128]{2,1,0:T(8,128)S(1)}) custom-call(f32[4,10,128,128]{3,2,1,0:T(8,128)S(1)} %get-tuple-element.44.mine_ref, f32[4,10,128,128]{3,2,1,0:T(8,128)} %collective-permute-done.16.got_ref), custom_call_target="tpu_custom_call" | custom-call | bytes 5242880 | tf_op jit(solution)/shard_map/pallas_call | solution.py:197
  89.6 2.7 %collective-permute-start.17 = (f32[5,128,128]{2,1,0:T(8,128)}, f32[5,128,128]{2,1,0:T(8,128)}, u32[]{:S(2)}, u32[]{:S(2)}) collective-permute-start(f32[5,128,128]{2,1,0:T(8,128)} %get-tuple-element.48), channel_id=1, source_target_pairs={{0,32},{32,64},{64,96},{96,0},{1,33},{33,65},{65,97},{97,1},{2,34}... | collective-permute-start | bytes 983048 | tf_op jit(solution)/shard_map/ppermute | solution.py:365
  92.3 1.2 collective-permute-start.18
  93.5 8.8 %shard_map.110 = f32[4,6,128,128]{3,2,1,0:T(8,128)} custom-call(s32[4,8]{1,0:T(4,128)S(1)} %pad_add_fusion.where_ref.ready_ref, bf16[512,2048]{1,0:T(8,128)(2,1)S(1)} %get-tuple-element.56.ah, bf16[512,2048]{1,0:T(8,128)(2,1)S(1)} %get-tuple-element.57.al, bf16[8,2,2048,256]{3,2,1,0:T(8,128)(2,1)} %shard_map.104.refs_8_.b_ref), custom_call_target="tpu_custom_call" | custom-call | flops 193273528320 | bytes 6291456 | tf_op jit(solution)/shard_map/pallas_call | solution.py:174
  102.3 1.6 collective-permute-start.21
  103.9 2.2 %shard_map.108 = (f32[10,128,128]{2,1,0:T(8,128)}, f32[10,128,128]{2,1,0:T(8,128)}) custom-call(f32[10,128,128]{2,1,0:T(8,128)S(1)} %get-tuple-element.46.plus_ref, f32[10,128,128]{2,1,0:T(8,128)S(1)} %get-tuple-element.47.minus_ref, f32[5,128,128]{2,1,0:T(8,128)} %collective-permute-done.17.gp_ref, f32[5,128,128]{2,1,0:T(8,128)} %collective-permute-done.18.gm_ref), custom_call_target="tpu_custom_call" | custom-call | bytes 1966080 | tf_op jit(solution)/shard_map/pallas_call | solution.py:197
  106.7 2.0 %collective-permute-start.20 = (f32[10,128,128]{2,1,0:T(8,128)}, f32[10,128,128]{2,1,0:T(8,128)}, u32[]{:S(2)}, u32[]{:S(2)}) collective-permute-start(f32[10,128,128]{2,1,0:T(8,128)} %get-tuple-element.51), channel_id=1, source_target_pairs={{0,96},{32,0},{64,32},{96,64},{1,97},{33,1},{65,33},{97,65},{2,98}... | collective-permute-start | bytes 1966088 | tf_op jit(solution)/shard_map/ppermute | solution.py:365
  108.8 7.6 %shard_map.109.mine_ref = f32[4,6,128,128]{3,2,1,0:T(8,128)S(1)} custom-call(s32[4,8]{1,0:T(4,128)S(1)} %pad_add_fusion.1.where_ref.ready_ref, bf16[512,2048]{1,0:T(8,128)(2,1)S(1)} %get-tuple-element.53.ah, bf16[512,2048]{1,0:T(8,128)(2,1)S(1)} %get-tuple-element.54.al, bf16[8,2,2048,256]{3,2,1,0:T(8,128)(2,1)} %shard_map.104.refs_8_.b_ref), custom_call_target="tpu_custom_call" | custom-call | flops 193273528320 | bytes 6291456 | tf_op jit(solution)/shard_map/pallas_call | solution.py:174
  116.5 1.6 shard_map.111
  118.1 2.7 %collective-permute-start.23 = (f32[3,128,128]{2,1,0:T(8,128)S(1)}, f32[3,128,128]{2,1,0:T(8,128)S(1)}, u32[]{:S(2)}, u32[]{:S(2)}) collective-permute-start(f32[3,128,128]{2,1,0:T(8,128)S(1)} %get-tuple-element.66), channel_id=1, source_target_pairs={{0,96},{32,0},{64,32},{96,64},{1,97},{33,1},{65,33},{97,65},{2,98}... | collective-permute-start | bytes 589832 | tf_op jit(solution)/shard_map/ppermute | solution.py:365
  120.9 2.2 %copy-done = f32[2048,512]{1,0:T(8,128)S(1)} copy-done((f32[2048,512]{1,0:T(8,128)S(1)}, f32[2048,512]{1,0:T(8,128)}, u32[]{:S(2)}) %copy-start) | copy-done | bytes 4194328
  123.0 1.6 shard_map.112
  124.7 3.4 %collective-permute-done.22.gp_ref = f32[3,128,128]{2,1,0:T(8,128)S(1)} collective-permute-done((f32[3,128,128]{2,1,0:T(8,128)S(1)}, f32[3,128,128]{2,1,0:T(8,128)S(1)}, u32[]{:S(2)}, u32[]{:S(2)}) %collective-permute-start.22) | collective-permute-done | bytes 196640 | tf_op jit(solution)/shard_map/ppermute | solution.py:365
  129.0 1.8 %collective-permute-start.25 = (f32[6,128,128]{2,1,0:T(8,128)S(1)}, f32[6,128,128]{2,1,0:T(8,128)S(1)}, u32[]{:S(2)}, u32[]{:S(2)}) collective-permute-start(f32[6,128,128]{2,1,0:T(8,128)S(1)} %get-tuple-element.68), channel_id=1, source_target_pairs={{0,96},{32,0},{64,32},{96,64},{1,97},{33,1},{65,33},{97,65},{2,98}... | collective-permute-start | bytes 1179656 | tf_op jit(solution)/shard_map/ppermute | solution.py:365
  130.9 8.4 %collective-permute-done.24.refs_4_ = f32[6,128,128]{2,1,0:T(8,128)S(1)} collective-permute-done((f32[6,128,128]{2,1,0:T(8,128)S(1)}, f32[6,128,128]{2,1,0:T(8,128)S(1)}, u32[]{:S(2)}, u32[]{:S(2)}) %collective-permute-start.24) | collective-permute-done | bytes 393248 | tf_op jit(solution)/shard_map/ppermute | solution.py:365
  139.2 3.7 %shard_map.114 = f32[2176,128]{1,0:T(8,128)S(1)} custom-call(s32[2048]{0:T(1024)S(1)} %get-tuple-element.38.idx_ref, f32[128,128]{1,0:T(8,128)S(1)} %pad.4.place_ref, f32[10,128,128]{2,1,0:T(8,128)S(1)} %get-tuple-element.45.refs_0_, f32[10,128,128]{2,1,0:T(8,128)} %collective-permute-done.19.refs_1_, f32[10,128,128]{2,1,0:T(8,128)} %collective-permute-done.20.refs_2_, ...), custom_call_target="tpu_custom_call" | custom-call | bytes 3219456 | tf_op jit(solution)/shard_map/pallas_call | solution.py:197
  142.9 29.1 %all_to_all.5 = f32[128,1,2176]{2,1,0:T(1,128)S(1)} all-to-all(f32[128,1,2176]{2,1,0:T(1,128)S(1)} %bitcast.26), channel_id=1, replica_groups=mesh['z'=4,'core'=2,'y'=4,'x'=4] {'z','core','y','x'}, dimensions={0} | all-to-all | bytes 2228224 | tf_op jit(solution)/shard_map/all_to_all | solution.py:389
  172.1 6.0 %shard_map.115 = (f32[128,2048]{1,0:T(8,128)}, f32[128,2048]{1,0:T(8,128)}) custom-call(f32[2176,128]{1,0:T(8,128)S(1)} %bitcast.27, f32[128,2048]{1,0:T(8,128)S(1)} %copy-done.1, bf16[2048,512]{1,0:T(8,128)(2,1)S(1)} %get-tuple-element.63.ch_ref, bf16[2048,512]{1,0:T(8,128)(2,1)S(1)} %get-tuple-element.64.cl_ref), custom_call_target="tpu_custom_call" | custom-call | bytes 8388608 | tf_op jit(solution)/shard_map/pallas_call | solution.py:277
  (82 shorter events, 10.8 us)
Async XLA Ops:
  1.8 8.0 %collective-permute-start = (f32[1,16,2048]{2,1,0:T(8,128)S(1)}, f32[1,16,2048]{2,1,0:T(8,128)S(1)}, u32[]{:S(2)}, u32[]{:S(2)}) collective-permute-start(f32[1,16,2048]{2,1,0:T(8,128)S(1)} %get-tuple-element.73), channel_id=1, source_target_pairs={{0,1},{1,0},{2,3},{3,2},{4,5},{5,4},{6,7},{7,6},{8,9},{9,8},{10,11... | collective-permute-start | bytes 393224 | tf_op jit(solution)/shard_map/ppermute | solution.py:317
  3.9 6.8 %collective-permute-start.3 = (f32[1,16,2048]{2,1,0:T(8,128)S(1)}, f32[1,16,2048]{2,1,0:T(8,128)S(1)}, u32[]{:S(2)}, u32[]{:S(2)}) collective-permute-start(f32[1,16,2048]{2,1,0:T(8,128)S(1)} %get-tuple-element.72), channel_id=1, source_target_pairs={{0,3},{1,2},{2,1},{3,0},{4,7},{5,6},{6,5},{7,4},{8,11},{9,10},{10,... | collective-permute-start | bytes 393224 | tf_op jit(solution)/shard_map/ppermute | solution.py:317
  5.7 5.5 %collective-permute-start.6 = (f32[1,16,2048]{2,1,0:T(8,128)S(1)}, f32[1,16,2048]{2,1,0:T(8,128)S(1)}, u32[]{:S(2)}, u32[]{:S(2)}) collective-permute-start(f32[1,16,2048]{2,1,0:T(8,128)S(1)} %get-tuple-element.74), channel_id=1, source_target_pairs={{0,4},{4,0},{8,12},{12,8},{1,5},{5,1},{9,13},{13,9},{2,6},{6,2},{1... | collective-permute-start | bytes 393224 | tf_op jit(solution)/shard_map/ppermute | solution.py:317
  7.0 6.0 %collective-permute-start.9 = (f32[1,16,2048]{2,1,0:T(8,128)S(1)}, f32[1,16,2048]{2,1,0:T(8,128)S(1)}, u32[]{:S(2)}, u32[]{:S(2)}) collective-permute-start(f32[1,16,2048]{2,1,0:T(8,128)S(1)} %get-tuple-element.71), channel_id=1, source_target_pairs={{0,12},{4,8},{8,4},{12,0},{1,13},{5,9},{9,5},{13,1},{2,14},{6,10},... | collective-permute-start | bytes 393224 | tf_op jit(solution)/shard_map/ppermute | solution.py:317
  9.7 7.3 %collective-permute-start.1 = (f32[2,16,2048]{2,1,0:T(8,128)S(1)}, f32[2,16,2048]{2,1,0:T(8,128)S(1)}, u32[]{:S(2)}, u32[]{:S(2)}) collective-permute-start(f32[2,16,2048]{2,1,0:T(8,128)S(1)} %pad_maximum_fusion.8), channel_id=1, source_target_pairs={{0,3},{1,2},{2,1},{3,0},{4,7},{5,6},{6,5},{7,4},{8,11},{9,10},{10,... | collective-permute-start | bytes 786440 | tf_op jit(solution)/shard_map/ppermute | solution.py:317
  10.7 6.8 %collective-permute-start.4 = (f32[2,16,2048]{2,1,0:T(8,128)S(1)}, f32[2,16,2048]{2,1,0:T(8,128)S(1)}, u32[]{:S(2)}, u32[]{:S(2)}) collective-permute-start(f32[2,16,2048]{2,1,0:T(8,128)S(1)} %pad_maximum_fusion.9), channel_id=1, source_target_pairs={{0,4},{4,0},{8,12},{12,8},{1,5},{5,1},{9,13},{13,9},{2,6},{6,2},{1... | collective-permute-start | bytes 786440 | tf_op jit(solution)/shard_map/ppermute | solution.py:317
  11.2 7.6 %copy-start.5 = (f32[1,16,2048]{2,1,0:T(8,128)}, f32[1,16,2048]{2,1,0:T(8,128)S(1)}, u32[]{:S(2)}) copy-start(f32[1,16,2048]{2,1,0:T(8,128)S(1)} %collective-permute-done.6) | copy-start | bytes 393220
  11.2 7.4 %collective-permute-start.7 = (f32[2,16,2048]{2,1,0:T(8,128)S(1)}, f32[2,16,2048]{2,1,0:T(8,128)S(1)}, u32[]{:S(2)}, u32[]{:S(2)}) collective-permute-start(f32[2,16,2048]{2,1,0:T(8,128)S(1)} %pad_maximum_fusion.10), channel_id=1, source_target_pairs={{0,12},{4,8},{8,4},{12,0},{1,13},{5,9},{9,5},{13,1},{2,14},{6,10},... | collective-permute-start | bytes 786440 | tf_op jit(solution)/shard_map/ppermute | solution.py:317
  13.0 5.7 %copy-start.3 = (f32[1,16,2048]{2,1,0:T(8,128)}, f32[1,16,2048]{2,1,0:T(8,128)S(1)}, u32[]{:S(2)}) copy-start(f32[1,16,2048]{2,1,0:T(8,128)S(1)} %collective-permute-done.9) | copy-start | bytes 393220
  13.1 5.6 %collective-permute-start.10 = (f32[2,16,2048]{2,1,0:T(8,128)S(1)}, f32[2,16,2048]{2,1,0:T(8,128)S(1)}, u32[]{:S(2)}, u32[]{:S(2)}) collective-permute-start(f32[2,16,2048]{2,1,0:T(8,128)S(1)} %pad_maximum_fusion.11), channel_id=1, source_target_pairs={{0,1},{1,0},{2,3},{3,2},{4,5},{5,4},{6,7},{7,6},{8,9},{9,8},{10,11... | collective-permute-start | bytes 786440 | tf_op jit(solution)/shard_map/ppermute | solution.py:317
  17.1 10.8 %collective-permute-start.2 = (f32[4,16,2048]{2,1,0:T(8,128)S(1)}, f32[4,16,2048]{2,1,0:T(8,128)S(1)}, u32[]{:S(2)}, u32[]{:S(2)}) collective-permute-start(f32[4,16,2048]{2,1,0:T(8,128)S(1)} %pad_maximum_fusion.4), channel_id=1, source_target_pairs={{0,4},{4,0},{8,12},{12,8},{1,5},{5,1},{9,13},{13,9},{2,6},{6,2},{1... | collective-permute-start | bytes 1572872 | tf_op jit(solution)/shard_map/ppermute | solution.py:317
  17.6 11.7 %collective-permute-start.5 = (f32[4,16,2048]{2,1,0:T(8,128)S(1)}, f32[4,16,2048]{2,1,0:T(8,128)S(1)}, u32[]{:S(2)}, u32[]{:S(2)}) collective-permute-start(f32[4,16,2048]{2,1,0:T(8,128)S(1)} %pad_maximum_fusion.5), channel_id=1, source_target_pairs={{0,12},{4,8},{8,4},{12,0},{1,13},{5,9},{9,5},{13,1},{2,14},{6,10},... | collective-permute-start | bytes 1572872 | tf_op jit(solution)/shard_map/ppermute | solution.py:317
  18.6 11.3 %collective-permute-start.8 = (f32[4,16,2048]{2,1,0:T(8,128)S(1)}, f32[4,16,2048]{2,1,0:T(8,128)S(1)}, u32[]{:S(2)}, u32[]{:S(2)}) collective-permute-start(f32[4,16,2048]{2,1,0:T(8,128)S(1)} %pad_maximum_fusion.6), channel_id=1, source_target_pairs={{0,1},{1,0},{2,3},{3,2},{4,5},{5,4},{6,7},{7,6},{8,9},{9,8},{10,11... | collective-permute-start | bytes 1572872 | tf_op jit(solution)/shard_map/ppermute | solution.py:317
  18.8 12.7 %collective-permute-start.11 = (f32[4,16,2048]{2,1,0:T(8,128)S(1)}, f32[4,16,2048]{2,1,0:T(8,128)S(1)}, u32[]{:S(2)}, u32[]{:S(2)}) collective-permute-start(f32[4,16,2048]{2,1,0:T(8,128)S(1)} %pad_maximum_fusion.7), channel_id=1, source_target_pairs={{0,3},{1,2},{2,1},{3,0},{4,7},{5,6},{6,5},{7,4},{8,11},{9,10},{10,... | collective-permute-start | bytes 1572872 | tf_op jit(solution)/shard_map/ppermute | solution.py:317
  20.8 9.1 %copy-start.6 = (f32[1,16,2048]{2,1,0:T(8,128)S(1)}, f32[1,16,2048]{2,1,0:T(8,128)}, u32[]{:S(2)}) copy-start(f32[1,16,2048]{2,1,0:T(8,128)} %copy-done.5) | copy-start | bytes 393220
  28.0 24.9 %collective-permute-start.12 = (f32[8,16,2048]{2,1,0:T(8,128)S(1)}, f32[8,16,2048]{2,1,0:T(8,128)}, u32[]{:S(2)}, u32[]{:S(2)}) collective-permute-start(f32[8,16,2048]{2,1,0:T(8,128)S(1)} %pad_maximum_fusion.refs_0_), channel_id=1, source_target_pairs={{0,12},{4,8},{8,4},{12,0},{1,13},{5,9},{9,5},{13,1},{2,14},{6,10},... | collective-permute-start | bytes 3145736 | tf_op jit(solution)/shard_map/ppermute | solution.py:317
  29.4 8.7 %copy-start.2 = (s32[16,16]{1,0:T(8,128)S(1)}, s32[16,16]{1,0:T(8,128)}, u32[]{:S(2)}) copy-start(s32[16,16]{1,0:T(8,128)} %mask_ref.2) | copy-start | bytes 3076
  29.4 23.5 %collective-permute-start.13 = (f32[8,16,2048]{2,1,0:T(8,128)S(1)}, f32[8,16,2048]{2,1,0:T(8,128)}, u32[]{:S(2)}, u32[]{:S(2)}) collective-permute-start(f32[8,16,2048]{2,1,0:T(8,128)S(1)} %pad_maximum_fusion.1.refs_1_), channel_id=1, source_target_pairs={{0,1},{1,0},{2,3},{3,2},{4,5},{5,4},{6,7},{7,6},{8,9},{9,8},{10,11... | collective-permute-start | bytes 3145736 | tf_op jit(solution)/shard_map/ppermute | solution.py:317
  30.0 22.9 %collective-permute-start.14 = (f32[8,16,2048]{2,1,0:T(8,128)S(1)}, f32[8,16,2048]{2,1,0:T(8,128)}, u32[]{:S(2)}, u32[]{:S(2)}) collective-permute-start(f32[8,16,2048]{2,1,0:T(8,128)S(1)} %pad_maximum_fusion.2.refs_2_), channel_id=1, source_target_pairs={{0,3},{1,2},{2,1},{3,0},{4,7},{5,6},{6,5},{7,4},{8,11},{9,10},{10,... | collective-permute-start | bytes 3145736 | tf_op jit(solution)/shard_map/ppermute | solution.py:317
  32.6 20.5 %collective-permute-start.15 = (f32[8,16,2048]{2,1,0:T(8,128)}, f32[8,16,2048]{2,1,0:T(8,128)}, u32[]{:S(2)}, u32[]{:S(2)}) collective-permute-start(f32[8,16,2048]{2,1,0:T(8,128)} %pad_maximum_fusion.3.refs_3_), channel_id=1, source_target_pairs={{0,4},{4,0},{8,12},{12,8},{1,5},{5,1},{9,13},{13,9},{2,6},{6,2},{1... | collective-permute-start | bytes 3145736 | tf_op jit(solution)/shard_map/ppermute | solution.py:317
  69.0 17.8 %collective-permute-start.16 = (f32[4,10,128,128]{3,2,1,0:T(8,128)}, f32[4,10,128,128]{3,2,1,0:T(8,128)}, u32[]{:S(2)}, u32[]{:S(2)}) collective-permute-start(f32[4,10,128,128]{3,2,1,0:T(8,128)} %get-tuple-element.42), channel_id=1, source_target_pairs={{0,16},{16,0},{1,17},{17,1},{2,18},{18,2},{3,19},{19,3},{4,20},{20... | collective-permute-start | bytes 7864328 | tf_op jit(solution)/shard_map/ppermute | solution.py:362
  89.6 14.3 %collective-permute-start.17 = (f32[5,128,128]{2,1,0:T(8,128)}, f32[5,128,128]{2,1,0:T(8,128)}, u32[]{:S(2)}, u32[]{:S(2)}) collective-permute-start(f32[5,128,128]{2,1,0:T(8,128)} %get-tuple-element.48), channel_id=1, source_target_pairs={{0,32},{32,64},{64,96},{96,0},{1,33},{33,65},{65,97},{97,1},{2,34}... | collective-permute-start | bytes 983048 | tf_op jit(solution)/shard_map/ppermute | solution.py:365
  92.3 11.6 %collective-permute-start.18 = (f32[5,128,128]{2,1,0:T(8,128)}, f32[5,128,128]{2,1,0:T(8,128)}, u32[]{:S(2)}, u32[]{:S(2)}) collective-permute-start(f32[5,128,128]{2,1,0:T(8,128)} %get-tuple-element.49), channel_id=1, source_target_pairs={{0,96},{32,0},{64,32},{96,64},{1,97},{33,1},{65,33},{97,65},{2,98}... | collective-permute-start | bytes 983048 | tf_op jit(solution)/shard_map/ppermute | solution.py:365
  102.3 14.1 %collective-permute-start.21 = (f32[4,6,128,128]{3,2,1,0:T(8,128)}, f32[4,6,128,128]{3,2,1,0:T(8,128)}, u32[]{:S(2)}, u32[]{:S(2)}) collective-permute-start(f32[4,6,128,128]{3,2,1,0:T(8,128)} %shard_map.110), channel_id=1, source_target_pairs={{0,16},{16,0},{1,17},{17,1},{2,18},{18,2},{3,19},{19,3},{4,20},{20... | collective-permute-start | bytes 4718600 | tf_op jit(solution)/shard_map/ppermute | solution.py:362
  106.1 18.6 %collective-permute-start.19 = (f32[10,128,128]{2,1,0:T(8,128)}, f32[10,128,128]{2,1,0:T(8,128)}, u32[]{:S(2)}, u32[]{:S(2)}) collective-permute-start(f32[10,128,128]{2,1,0:T(8,128)} %get-tuple-element.50), channel_id=1, source_target_pairs={{0,32},{32,64},{64,96},{96,0},{1,33},{33,65},{65,97},{97,1},{2,34}... | collective-permute-start | bytes 1966088 | tf_op jit(solution)/shard_map/ppermute | solution.py:365
  106.7 17.9 %collective-permute-start.20 = (f32[10,128,128]{2,1,0:T(8,128)}, f32[10,128,128]{2,1,0:T(8,128)}, u32[]{:S(2)}, u32[]{:S(2)}) collective-permute-start(f32[10,128,128]{2,1,0:T(8,128)} %get-tuple-element.51), channel_id=1, source_target_pairs={{0,96},{32,0},{64,32},{96,64},{1,97},{33,1},{65,33},{97,65},{2,98}... | collective-permute-start | bytes 1966088 | tf_op jit(solution)/shard_map/ppermute | solution.py:365
  116.4 4.3 %copy-start.8 = (s32[16,4]{0,1:T(4,128)S(1)}, s32[16,4]{0,1:T(4,128)}, u32[]{:S(2)}) copy-start(s32[16,4]{0,1:T(4,128)} %param.14) | copy-start | bytes 772
  118.0 10.0 %collective-permute-start.22 = (f32[3,128,128]{2,1,0:T(8,128)S(1)}, f32[3,128,128]{2,1,0:T(8,128)S(1)}, u32[]{:S(2)}, u32[]{:S(2)}) collective-permute-start(f32[3,128,128]{2,1,0:T(8,128)S(1)} %get-tuple-element.61), channel_id=1, source_target_pairs={{0,32},{32,64},{64,96},{96,0},{1,33},{33,65},{65,97},{97,1},{2,34}... | collective-permute-start | bytes 589832 | tf_op jit(solution)/shard_map/ppermute | solution.py:365
  118.1 10.0 %collective-permute-start.23 = (f32[3,128,128]{2,1,0:T(8,128)S(1)}, f32[3,128,128]{2,1,0:T(8,128)S(1)}, u32[]{:S(2)}, u32[]{:S(2)}) collective-permute-start(f32[3,128,128]{2,1,0:T(8,128)S(1)} %get-tuple-element.66), channel_id=1, source_target_pairs={{0,96},{32,0},{64,32},{96,64},{1,97},{33,1},{65,33},{97,65},{2,98}... | collective-permute-start | bytes 589832 | tf_op jit(solution)/shard_map/ppermute | solution.py:365
  128.1 11.1 %collective-permute-start.24 = (f32[6,128,128]{2,1,0:T(8,128)S(1)}, f32[6,128,128]{2,1,0:T(8,128)S(1)}, u32[]{:S(2)}, u32[]{:S(2)}) collective-permute-start(f32[6,128,128]{2,1,0:T(8,128)S(1)} %get-tuple-element.67), channel_id=1, source_target_pairs={{0,32},{32,64},{64,96},{96,0},{1,33},{33,65},{65,97},{97,1},{2,34}... | collective-permute-start | bytes 1179656 | tf_op jit(solution)/shard_map/ppermute | solution.py:365
  129.0 10.2 %collective-permute-start.25 = (f32[6,128,128]{2,1,0:T(8,128)S(1)}, f32[6,128,128]{2,1,0:T(8,128)S(1)}, u32[]{:S(2)}, u32[]{:S(2)}) collective-permute-start(f32[6,128,128]{2,1,0:T(8,128)S(1)} %get-tuple-element.68), channel_id=1, source_target_pairs={{0,96},{32,0},{64,32},{96,64},{1,97},{33,1},{65,33},{97,65},{2,98}... | collective-permute-start | bytes 1179656 | tf_op jit(solution)/shard_map/ppermute | solution.py:365
  142.9 29.1 %copy-start.1 = (f32[128,2048]{1,0:T(8,128)S(1)}, f32[128,2048]{1,0:T(8,128)}, u32[]{:S(2)}) copy-start(f32[128,2048]{1,0:T(8,128)} %den_ref.1) | copy-start | bytes 3145732
  (4 other events, 12.3 us)

commit v9 on v8

--- a/solution.py
+++ b/solution.py
@@ -17,7 +17,7 @@
 PARTS = (10, 6)
 COLOURS = 4
 NB = 256
-SLOTS = 3
+SLOTS = 2
 MIB = 1 << 20
 
 f32 = jnp.float32
@@ -83,7 +83,7 @@
         grid=(cols // NB,),
         in_specs=[pl.BlockSpec(memory_space=pltpu.SMEM), pl.BlockSpec((depth, NB), lambda n: (0, n))],
         out_specs=pl.BlockSpec((1, 2, depth, NB), lambda n: (n, 0, 0, 0)),
-        vmem=49,
+        vmem=56,
         nbytes=x.size * 8,
         flops=x.size * 4,
     )(mask, x)
@@ -97,24 +97,23 @@
         slot = n % SLOTS
         return pltpu.make_async_copy(b_ref.at[first + n], slots.at[slot], sems.at[slot])
 
-    for n in range(SLOTS):
-        fetch(n).start()
+    fetch(0).start()
     before()
     dot = functools.partial(jnp.dot, preferred_element_type=f32)
 
     def step(n, carry):
         fetch(n).wait()
+
+        @pl.when(n + 1 < blocks)
+        def _():
+            fetch(n + 1).start()
+
         slot = n % SLOTS
         bh, bl = slots[slot, 0], slots[slot, 1]
         acc = dot(ah[...], bh) + dot(ah[...], bl) + dot(al[...], bh)
         for i in range(NZ):
             for t in range(per):
                 o_ref[i, n * per + t] = acc[ROWS * i : ROWS * (i + 1), t * TILE : (t + 1) * TILE]
-
-        @pl.when(n + SLOTS < blocks)
-        def _():
-            fetch(n + SLOTS).start()
-
         return carry
 
     lax.fori_loop(0, blocks, step, 0)
@@ -234,8 +233,9 @@
             scr[at : at + ROWS, :] = own[t] + rp[t] + rm[t]
 
     def step(g, carry):
+        rows = [scr[pl.ds(idx_ref[g * CAP + k], 1), :] for k in range(CAP)]
         for k in range(CAP):
-            out_ref[pl.ds(g * SLAB + k, 1), :] = scr[pl.ds(idx_ref[g * CAP + k], 1), :]
+            out_ref[pl.ds(g * SLAB + k, 1), :] = rows[k]
         out_ref[pl.ds(g * SLAB + CAP, 1), :] = place_ref[pl.ds(g, 1), :]
         return carry
 
@@ -256,8 +256,9 @@
     copy.wait()
 
     def step(g, carry):
+        rows = [got_ref[pl.ds(g * SLAB + k, 1), :] for k in range(CAP)]
         for k in range(CAP):
-            scr[pl.ds(place_ref[g, k], 1), :] = got_ref[pl.ds(g * SLAB + k, 1), :]
+            scr[pl.ds(place_ref[g, k], 1), :] = rows[k]
         return carry
 
     lax.fori_loop(0, peers, step, 0)

time: 179 us -> 177 us (0.989)
  no operation moved by 1% of the time
where the time goes in v9:
time: 177 us
  Pallas kernels  78.4 us (44%)
  starting transfers between devices  35.3 us (20%)
  blocking collectives  27.9 us (16%)
  waiting for transfers between devices  23 us (13%)
  other arithmetic  7.31 us (4%)
  local copies, waits for them, and re-layouts  3.86 us (2%)
    pallas_call x4, Pallas kernels, multiply(): call(kernel, tuple(shapes), in_specs=[SMEM] * len(maps) + [HBM if first e...  45.8 us
    all_to_all x1, blocking collectives, body(): lax.all_to_all(sending, everyone, split_axis=0, concat_axis=0, tiled=True)  27.9 us
    ppermute x16, starting transfers between devices, exchange(): return lax.ppermute(value, axis, pairs)  17.2 us
    pallas_call x1, Pallas kernels, prepare_integrals(): call(integrals_kernel, jax.ShapeDtypeStruct((cols // NB, 2, depth, NB), b...  14.8 us
    ppermute x8, starting transfers between devices, along_z(): return (lax.ppermute(p, 'z', ring(1)), lax.ppermute(m, 'z', ring(-1)))  12 us
    ppermute x8, waiting for transfers between devices, along_z(): return (lax.ppermute(p, 'z', ring(1)), lax.ppermute(m, 'z', ring(-1)))  11.8 us
    ppermute x16, waiting for transfers between devices, exchange(): return lax.ppermute(value, axis, pairs)  11.3 us
    pallas_call x5, Pallas kernels, small(): call(kernel, shapes, in_specs=[SMEM if x.dtype == jnp.int32 else VMEM for...  10.2 us
  transfers between devices with their start and end apart: 26, of which 6 were waited for; matrix products, arithmetic and copies ran while one was open for 4% of the time, Pallas kernels for 28%

profile of v9, /device:TPU:1, one launch (start us, length us, event | category | flops | bytes accessed | tf_op | source)
XLA Modules:
  0.0 176.9 jit_solution(1488574802277957997)
XLA Ops:
  1.8 2.1 %collective-permute-start = (f32[1,16,2048]{2,1,0:T(8,128)S(1)}, f32[1,16,2048]{2,1,0:T(8,128)S(1)}, u32[]{:S(2)}, u32[]{:S(2)}) collective-permute-start(f32[1,16,2048]{2,1,0:T(8,128)S(1)} %get-tuple-element.73), channel_id=1, source_target_pairs={{0,1},{1,0},{2,3},{3,2},{4,5},{5,4},{6,7},{7,6},{8,9},{9,8},{10,11... | collective-permute-start | bytes 393224 | tf_op jit(solution)/shard_map/ppermute | solution.py:318
  3.9 1.8 %collective-permute-start.3 = (f32[1,16,2048]{2,1,0:T(8,128)S(1)}, f32[1,16,2048]{2,1,0:T(8,128)S(1)}, u32[]{:S(2)}, u32[]{:S(2)}) collective-permute-start(f32[1,16,2048]{2,1,0:T(8,128)S(1)} %get-tuple-element.72), channel_id=1, source_target_pairs={{0,3},{1,2},{2,1},{3,0},{4,7},{5,6},{6,5},{7,4},{8,11},{9,10},{10,... | collective-permute-start | bytes 393224 | tf_op jit(solution)/shard_map/ppermute | solution.py:318
  5.7 1.3 collective-permute-start.6
  7.0 1.9 %collective-permute-start.9 = (f32[1,16,2048]{2,1,0:T(8,128)S(1)}, f32[1,16,2048]{2,1,0:T(8,128)S(1)}, u32[]{:S(2)}, u32[]{:S(2)}) collective-permute-start(f32[1,16,2048]{2,1,0:T(8,128)S(1)} %get-tuple-element.71), channel_id=1, source_target_pairs={{0,12},{4,8},{8,4},{12,0},{1,13},{5,9},{9,5},{13,1},{2,14},{6,10},... | collective-permute-start | bytes 393224 | tf_op jit(solution)/shard_map/ppermute | solution.py:318
  11.2 1.8 %collective-permute-start.7 = (f32[2,16,2048]{2,1,0:T(8,128)S(1)}, f32[2,16,2048]{2,1,0:T(8,128)S(1)}, u32[]{:S(2)}, u32[]{:S(2)}) collective-permute-start(f32[2,16,2048]{2,1,0:T(8,128)S(1)} %pad_maximum_fusion.10), channel_id=1, source_target_pairs={{0,12},{4,8},{8,4},{12,0},{1,13},{5,9},{9,5},{13,1},{2,14},{6,10},... | collective-permute-start | bytes 786440 | tf_op jit(solution)/shard_map/ppermute | solution.py:318
  13.1 3.9 %collective-permute-done.1 = f32[2,16,2048]{2,1,0:T(8,128)S(1)} collective-permute-done((f32[2,16,2048]{2,1,0:T(8,128)S(1)}, f32[2,16,2048]{2,1,0:T(8,128)S(1)}, u32[]{:S(2)}, u32[]{:S(2)}) %collective-permute-start.1) | collective-permute-done | bytes 262176 | tf_op jit(solution)/shard_map/ppermute | solution.py:318
  18.8 2.0 %collective-permute-start.11 = (f32[4,16,2048]{2,1,0:T(8,128)S(1)}, f32[4,16,2048]{2,1,0:T(8,128)S(1)}, u32[]{:S(2)}, u32[]{:S(2)}) collective-permute-start(f32[4,16,2048]{2,1,0:T(8,128)S(1)} %pad_maximum_fusion.7), channel_id=1, source_target_pairs={{0,3},{1,2},{2,1},{3,0},{4,7},{5,6},{6,5},{7,4},{8,11},{9,10},{10,... | collective-permute-start | bytes 1572872 | tf_op jit(solution)/shard_map/ppermute | solution.py:318
  20.8 7.0 %collective-permute-done.2 = f32[4,16,2048]{2,1,0:T(8,128)S(1)} collective-permute-done((f32[4,16,2048]{2,1,0:T(8,128)S(1)}, f32[4,16,2048]{2,1,0:T(8,128)S(1)}, u32[]{:S(2)}, u32[]{:S(2)}) %collective-permute-start.2) | collective-permute-done | bytes 524320 | tf_op jit(solution)/shard_map/ppermute | solution.py:318
  30.0 1.5 collective-permute-start.14
  33.0 5.0 %sort.14 = (s32[2048]{0:T(1024)S(1)}, s32[2048]{0:T(1024)}) sort(s32[2048]{0:T(1024)S(1)} %fusion.10, s32[2048]{0:T(1024)S(1)} %iota.7), dimensions={0}, to_apply=%region_0.1 | sort | flops 22528 | bytes 32768 | tf_op jit(solution)/shard_map/sort | solution.py:302
  38.1 14.8 %shard_map.104.refs_8_.b_ref = bf16[8,2,2048,256]{3,2,1,0:T(8,128)(2,1)} custom-call(s32[16,16]{1,0:T(8,128)} %mask_ref.2, f32[2048,2048]{1,0:T(8,128)} %x_ref), custom_call_target="tpu_custom_call" | custom-call | flops 16777216 | bytes 33554432 | tf_op jit(solution)/shard_map/pallas_call | solution.py:80
  53.0 16.0 %shard_map.105 = (f32[4,10,128,128]{3,2,1,0:T(8,128)}, bf16[512,2048]{1,0:T(8,128)(2,1)S(1)}, bf16[512,2048]{1,0:T(8,128)(2,1)S(1)}) custom-call(s32[4,8]{1,0:T(4,128)S(1)} %pad_add_fusion.where_ref.ready_ref, f32[8,16,2048]{2,1,0:T(8,128)S(1)} %pad_maximum_fusion.refs_0_, f32[8,16,2048]{2,1,0:T(8,128)S(1)} %pad_maximum_fusion.1.refs_1_, ...), custom_call_target="tpu_custom_call" | custom-call | flops 322122547200 | bytes 10485760 | tf_op jit(solution)/shard_map/pallas_call | solution.py:173
  69.0 4.4 %collective-permute-start.16 = (f32[4,10,128,128]{3,2,1,0:T(8,128)}, f32[4,10,128,128]{3,2,1,0:T(8,128)}, u32[]{:S(2)}, u32[]{:S(2)}) collective-permute-start(f32[4,10,128,128]{3,2,1,0:T(8,128)} %get-tuple-element.42), channel_id=1, source_target_pairs={{0,16},{16,0},{1,17},{17,1},{2,18},{18,2},{3,19},{19,3},{4,20},{20... | collective-permute-start | bytes 7864328 | tf_op jit(solution)/shard_map/ppermute | solution.py:363
  73.3 13.5 %shard_map.106 = (f32[4,10,128,128]{3,2,1,0:T(8,128)S(1)}, bf16[512,2048]{1,0:T(8,128)(2,1)S(1)}, bf16[512,2048]{1,0:T(8,128)(2,1)S(1)}) custom-call(s32[4,8]{1,0:T(4,128)S(1)} %pad_add_fusion.1.where_ref.ready_ref, f32[8,16,2048]{2,1,0:T(8,128)S(1)} %pad_maximum_fusion.refs_0_, f32[8,16,2048]{2,1,0:T(8,128)S(1)} %pad_maximum_fusion.1.refs_1_, ...), custom_call_target="tpu_custom_call" | custom-call | flops 322122547200 | bytes 10485760 | tf_op jit(solution)/shard_map/pallas_call | solution.py:173
  86.8 2.7 %shard_map.107 = (f32[5,128,128]{2,1,0:T(8,128)}, f32[5,128,128]{2,1,0:T(8,128)}, f32[10,128,128]{2,1,0:T(8,128)S(1)}, f32[10,128,128]{2,1,0:T(8,128)S(1)}, f32[10,128,128]{2,1,0:T(8,128)S(1)}) custom-call(f32[4,10,128,128]{3,2,1,0:T(8,128)S(1)} %get-tuple-element.44.mine_ref, f32[4,10,128,128]{3,2,1,0:T(8,128)} %collective-permute-done.16.got_ref), custom_call_target="tpu_custom_call" | custom-call | bytes 5242880 | tf_op jit(solution)/shard_map/pallas_call | solution.py:196
  89.6 1.5 collective-permute-start.17
  91.1 2.4 %collective-permute-start.18 = (f32[5,128,128]{2,1,0:T(8,128)}, f32[5,128,128]{2,1,0:T(8,128)}, u32[]{:S(2)}, u32[]{:S(2)}) collective-permute-start(f32[5,128,128]{2,1,0:T(8,128)} %get-tuple-element.49), channel_id=1, source_target_pairs={{0,96},{32,0},{64,32},{96,64},{1,97},{33,1},{65,33},{97,65},{2,98}... | collective-permute-start | bytes 983048 | tf_op jit(solution)/shard_map/ppermute | solution.py:366
  93.5 8.8 %shard_map.110 = f32[4,6,128,128]{3,2,1,0:T(8,128)} custom-call(s32[4,8]{1,0:T(4,128)S(1)} %pad_add_fusion.where_ref.ready_ref, bf16[512,2048]{1,0:T(8,128)(2,1)S(1)} %get-tuple-element.56.ah, bf16[512,2048]{1,0:T(8,128)(2,1)S(1)} %get-tuple-element.57.al, bf16[8,2,2048,256]{3,2,1,0:T(8,128)(2,1)} %shard_map.104.refs_8_.b_ref), custom_call_target="tpu_custom_call" | custom-call | flops 193273528320 | bytes 6291456 | tf_op jit(solution)/shard_map/pallas_call | solution.py:173
  102.2 1.6 collective-permute-start.21
  103.9 2.2 %shard_map.108 = (f32[10,128,128]{2,1,0:T(8,128)}, f32[10,128,128]{2,1,0:T(8,128)}) custom-call(f32[10,128,128]{2,1,0:T(8,128)S(1)} %get-tuple-element.46.plus_ref, f32[10,128,128]{2,1,0:T(8,128)S(1)} %get-tuple-element.47.minus_ref, f32[5,128,128]{2,1,0:T(8,128)} %collective-permute-done.17.gp_ref, f32[5,128,128]{2,1,0:T(8,128)} %collective-permute-done.18.gm_ref), custom_call_target="tpu_custom_call" | custom-call | bytes 1966080 | tf_op jit(solution)/shard_map/pallas_call | solution.py:196
  106.1 2.7 %collective-permute-start.20 = (f32[10,128,128]{2,1,0:T(8,128)}, f32[10,128,128]{2,1,0:T(8,128)}, u32[]{:S(2)}, u32[]{:S(2)}) collective-permute-start(f32[10,128,128]{2,1,0:T(8,128)} %get-tuple-element.51), channel_id=1, source_target_pairs={{0,96},{32,0},{64,32},{96,64},{1,97},{33,1},{65,33},{97,65},{2,98}... | collective-permute-start | bytes 1966088 | tf_op jit(solution)/shard_map/ppermute | solution.py:366
  108.8 7.6 %shard_map.109.mine_ref = f32[4,6,128,128]{3,2,1,0:T(8,128)S(1)} custom-call(s32[4,8]{1,0:T(4,128)S(1)} %pad_add_fusion.1.where_ref.ready_ref, bf16[512,2048]{1,0:T(8,128)(2,1)S(1)} %get-tuple-element.53.ah, bf16[512,2048]{1,0:T(8,128)(2,1)S(1)} %get-tuple-element.54.al, bf16[8,2,2048,256]{3,2,1,0:T(8,128)(2,1)} %shard_map.104.refs_8_.b_ref), custom_call_target="tpu_custom_call" | custom-call | flops 193273528320 | bytes 6291456 | tf_op jit(solution)/shard_map/pallas_call | solution.py:173
  116.4 1.6 shard_map.111
  118.1 2.7 %collective-permute-start.23 = (f32[3,128,128]{2,1,0:T(8,128)S(1)}, f32[3,128,128]{2,1,0:T(8,128)S(1)}, u32[]{:S(2)}, u32[]{:S(2)}) collective-permute-start(f32[3,128,128]{2,1,0:T(8,128)S(1)} %get-tuple-element.66), channel_id=1, source_target_pairs={{0,96},{32,0},{64,32},{96,64},{1,97},{33,1},{65,33},{97,65},{2,98}... | collective-permute-start | bytes 589832 | tf_op jit(solution)/shard_map/ppermute | solution.py:366
  120.8 2.2 %copy-done = f32[2048,512]{1,0:T(8,128)S(1)} copy-done((f32[2048,512]{1,0:T(8,128)S(1)}, f32[2048,512]{1,0:T(8,128)}, u32[]{:S(2)}) %copy-start) | copy-done | bytes 4194328
  123.0 1.6 shard_map.112
  124.6 3.4 %collective-permute-done.22.gp_ref = f32[3,128,128]{2,1,0:T(8,128)S(1)} collective-permute-done((f32[3,128,128]{2,1,0:T(8,128)S(1)}, f32[3,128,128]{2,1,0:T(8,128)S(1)}, u32[]{:S(2)}, u32[]{:S(2)}) %collective-permute-start.22) | collective-permute-done | bytes 196640 | tf_op jit(solution)/shard_map/ppermute | solution.py:366
  128.2 2.7 %collective-permute-start.25 = (f32[6,128,128]{2,1,0:T(8,128)S(1)}, f32[6,128,128]{2,1,0:T(8,128)S(1)}, u32[]{:S(2)}, u32[]{:S(2)}) collective-permute-start(f32[6,128,128]{2,1,0:T(8,128)S(1)} %get-tuple-element.68), channel_id=1, source_target_pairs={{0,96},{32,0},{64,32},{96,64},{1,97},{33,1},{65,33},{97,65},{2,98}... | collective-permute-start | bytes 1179656 | tf_op jit(solution)/shard_map/ppermute | solution.py:366
  130.9 8.4 %collective-permute-done.24.refs_4_ = f32[6,128,128]{2,1,0:T(8,128)S(1)} collective-permute-done((f32[6,128,128]{2,1,0:T(8,128)S(1)}, f32[6,128,128]{2,1,0:T(8,128)S(1)}, u32[]{:S(2)}, u32[]{:S(2)}) %collective-permute-start.24) | collective-permute-done | bytes 393248 | tf_op jit(solution)/shard_map/ppermute | solution.py:366
  139.2 3.7 %shard_map.114 = f32[2176,128]{1,0:T(8,128)S(1)} custom-call(s32[2048]{0:T(1024)S(1)} %get-tuple-element.38.idx_ref, f32[128,128]{1,0:T(8,128)S(1)} %pad.4.place_ref, f32[10,128,128]{2,1,0:T(8,128)S(1)} %get-tuple-element.45.refs_0_, f32[10,128,128]{2,1,0:T(8,128)} %collective-permute-done.19.refs_1_, f32[10,128,128]{2,1,0:T(8,128)} %collective-permute-done.20.refs_2_, ...), custom_call_target="tpu_custom_call" | custom-call | bytes 3219456 | tf_op jit(solution)/shard_map/pallas_call | solution.py:196
  142.9 27.9 %all_to_all.5 = f32[128,1,2176]{2,1,0:T(1,128)S(1)} all-to-all(f32[128,1,2176]{2,1,0:T(1,128)S(1)} %bitcast.26), channel_id=1, replica_groups=mesh['z'=4,'core'=2,'y'=4,'x'=4] {'z','core','y','x'}, dimensions={0} | all-to-all | bytes 2228224 | tf_op jit(solution)/shard_map/all_to_all | solution.py:390
  170.8 6.0 %shard_map.115 = (f32[128,2048]{1,0:T(8,128)}, f32[128,2048]{1,0:T(8,128)}) custom-call(f32[2176,128]{1,0:T(8,128)S(1)} %bitcast.27, f32[128,2048]{1,0:T(8,128)S(1)} %copy-done.1, bf16[2048,512]{1,0:T(8,128)(2,1)S(1)} %get-tuple-element.63.ch_ref, bf16[2048,512]{1,0:T(8,128)(2,1)S(1)} %get-tuple-element.64.cl_ref), custom_call_target="tpu_custom_call" | custom-call | bytes 8388608 | tf_op jit(solution)/shard_map/pallas_call | solution.py:278
  (76 shorter events, 9.3 us)
Async XLA Ops:
  1.8 8.0 %collective-permute-start = (f32[1,16,2048]{2,1,0:T(8,128)S(1)}, f32[1,16,2048]{2,1,0:T(8,128)S(1)}, u32[]{:S(2)}, u32[]{:S(2)}) collective-permute-start(f32[1,16,2048]{2,1,0:T(8,128)S(1)} %get-tuple-element.73), channel_id=1, source_target_pairs={{0,1},{1,0},{2,3},{3,2},{4,5},{5,4},{6,7},{7,6},{8,9},{9,8},{10,11... | collective-permute-start | bytes 393224 | tf_op jit(solution)/shard_map/ppermute | solution.py:318
  3.9 6.8 %collective-permute-start.3 = (f32[1,16,2048]{2,1,0:T(8,128)S(1)}, f32[1,16,2048]{2,1,0:T(8,128)S(1)}, u32[]{:S(2)}, u32[]{:S(2)}) collective-permute-start(f32[1,16,2048]{2,1,0:T(8,128)S(1)} %get-tuple-element.72), channel_id=1, source_target_pairs={{0,3},{1,2},{2,1},{3,0},{4,7},{5,6},{6,5},{7,4},{8,11},{9,10},{10,... | collective-permute-start | bytes 393224 | tf_op jit(solution)/shard_map/ppermute | solution.py:318
  5.7 5.5 %collective-permute-start.6 = (f32[1,16,2048]{2,1,0:T(8,128)S(1)}, f32[1,16,2048]{2,1,0:T(8,128)S(1)}, u32[]{:S(2)}, u32[]{:S(2)}) collective-permute-start(f32[1,16,2048]{2,1,0:T(8,128)S(1)} %get-tuple-element.74), channel_id=1, source_target_pairs={{0,4},{4,0},{8,12},{12,8},{1,5},{5,1},{9,13},{13,9},{2,6},{6,2},{1... | collective-permute-start | bytes 393224 | tf_op jit(solution)/shard_map/ppermute | solution.py:318
  7.0 6.0 %collective-permute-start.9 = (f32[1,16,2048]{2,1,0:T(8,128)S(1)}, f32[1,16,2048]{2,1,0:T(8,128)S(1)}, u32[]{:S(2)}, u32[]{:S(2)}) collective-permute-start(f32[1,16,2048]{2,1,0:T(8,128)S(1)} %get-tuple-element.71), channel_id=1, source_target_pairs={{0,12},{4,8},{8,4},{12,0},{1,13},{5,9},{9,5},{13,1},{2,14},{6,10},... | collective-permute-start | bytes 393224 | tf_op jit(solution)/shard_map/ppermute | solution.py:318
  9.7 7.3 %collective-permute-start.1 = (f32[2,16,2048]{2,1,0:T(8,128)S(1)}, f32[2,16,2048]{2,1,0:T(8,128)S(1)}, u32[]{:S(2)}, u32[]{:S(2)}) collective-permute-start(f32[2,16,2048]{2,1,0:T(8,128)S(1)} %pad_maximum_fusion.8), channel_id=1, source_target_pairs={{0,3},{1,2},{2,1},{3,0},{4,7},{5,6},{6,5},{7,4},{8,11},{9,10},{10,... | collective-permute-start | bytes 786440 | tf_op jit(solution)/shard_map/ppermute | solution.py:318
  10.7 6.8 %collective-permute-start.4 = (f32[2,16,2048]{2,1,0:T(8,128)S(1)}, f32[2,16,2048]{2,1,0:T(8,128)S(1)}, u32[]{:S(2)}, u32[]{:S(2)}) collective-permute-start(f32[2,16,2048]{2,1,0:T(8,128)S(1)} %pad_maximum_fusion.9), channel_id=1, source_target_pairs={{0,4},{4,0},{8,12},{12,8},{1,5},{5,1},{9,13},{13,9},{2,6},{6,2},{1... | collective-permute-start | bytes 786440 | tf_op jit(solution)/shard_map/ppermute | solution.py:318
  11.2 7.6 %copy-start.2 = (f32[1,16,2048]{2,1,0:T(8,128)}, f32[1,16,2048]{2,1,0:T(8,128)S(1)}, u32[]{:S(2)}) copy-start(f32[1,16,2048]{2,1,0:T(8,128)S(1)} %collective-permute-done.6) | copy-start | bytes 393220
  11.2 7.4 %collective-permute-start.7 = (f32[2,16,2048]{2,1,0:T(8,128)S(1)}, f32[2,16,2048]{2,1,0:T(8,128)S(1)}, u32[]{:S(2)}, u32[]{:S(2)}) collective-permute-start(f32[2,16,2048]{2,1,0:T(8,128)S(1)} %pad_maximum_fusion.10), channel_id=1, source_target_pairs={{0,12},{4,8},{8,4},{12,0},{1,13},{5,9},{9,5},{13,1},{2,14},{6,10},... | collective-permute-start | bytes 786440 | tf_op jit(solution)/shard_map/ppermute | solution.py:318
  13.1 5.6 %collective-permute-start.10 = (f32[2,16,2048]{2,1,0:T(8,128)S(1)}, f32[2,16,2048]{2,1,0:T(8,128)S(1)}, u32[]{:S(2)}, u32[]{:S(2)}) collective-permute-start(f32[2,16,2048]{2,1,0:T(8,128)S(1)} %pad_maximum_fusion.11), channel_id=1, source_target_pairs={{0,1},{1,0},{2,3},{3,2},{4,5},{5,4},{6,7},{7,6},{8,9},{9,8},{10,11... | collective-permute-start | bytes 786440 | tf_op jit(solution)/shard_map/ppermute | solution.py:318
  17.1 10.8 %collective-permute-start.2 = (f32[4,16,2048]{2,1,0:T(8,128)S(1)}, f32[4,16,2048]{2,1,0:T(8,128)S(1)}, u32[]{:S(2)}, u32[]{:S(2)}) collective-permute-start(f32[4,16,2048]{2,1,0:T(8,128)S(1)} %pad_maximum_fusion.4), channel_id=1, source_target_pairs={{0,4},{4,0},{8,12},{12,8},{1,5},{5,1},{9,13},{13,9},{2,6},{6,2},{1... | collective-permute-start | bytes 1572872 | tf_op jit(solution)/shard_map/ppermute | solution.py:318
  17.6 11.7 %collective-permute-start.5 = (f32[4,16,2048]{2,1,0:T(8,128)S(1)}, f32[4,16,2048]{2,1,0:T(8,128)S(1)}, u32[]{:S(2)}, u32[]{:S(2)}) collective-permute-start(f32[4,16,2048]{2,1,0:T(8,128)S(1)} %pad_maximum_fusion.5), channel_id=1, source_target_pairs={{0,12},{4,8},{8,4},{12,0},{1,13},{5,9},{9,5},{13,1},{2,14},{6,10},... | collective-permute-start | bytes 1572872 | tf_op jit(solution)/shard_map/ppermute | solution.py:318
  18.6 11.3 %collective-permute-start.8 = (f32[4,16,2048]{2,1,0:T(8,128)S(1)}, f32[4,16,2048]{2,1,0:T(8,128)S(1)}, u32[]{:S(2)}, u32[]{:S(2)}) collective-permute-start(f32[4,16,2048]{2,1,0:T(8,128)S(1)} %pad_maximum_fusion.6), channel_id=1, source_target_pairs={{0,1},{1,0},{2,3},{3,2},{4,5},{5,4},{6,7},{7,6},{8,9},{9,8},{10,11... | collective-permute-start | bytes 1572872 | tf_op jit(solution)/shard_map/ppermute | solution.py:318
  18.8 12.7 %collective-permute-start.11 = (f32[4,16,2048]{2,1,0:T(8,128)S(1)}, f32[4,16,2048]{2,1,0:T(8,128)S(1)}, u32[]{:S(2)}, u32[]{:S(2)}) collective-permute-start(f32[4,16,2048]{2,1,0:T(8,128)S(1)} %pad_maximum_fusion.7), channel_id=1, source_target_pairs={{0,3},{1,2},{2,1},{3,0},{4,7},{5,6},{6,5},{7,4},{8,11},{9,10},{10,... | collective-permute-start | bytes 1572872 | tf_op jit(solution)/shard_map/ppermute | solution.py:318
  20.8 9.1 %copy-start.3 = (f32[1,16,2048]{2,1,0:T(8,128)S(1)}, f32[1,16,2048]{2,1,0:T(8,128)}, u32[]{:S(2)}) copy-start(f32[1,16,2048]{2,1,0:T(8,128)} %copy-done.2) | copy-start | bytes 393220
  27.9 24.9 %collective-permute-start.12 = (f32[8,16,2048]{2,1,0:T(8,128)S(1)}, f32[8,16,2048]{2,1,0:T(8,128)}, u32[]{:S(2)}, u32[]{:S(2)}) collective-permute-start(f32[8,16,2048]{2,1,0:T(8,128)S(1)} %pad_maximum_fusion.refs_0_), channel_id=1, source_target_pairs={{0,12},{4,8},{8,4},{12,0},{1,13},{5,9},{9,5},{13,1},{2,14},{6,10},... | collective-permute-start | bytes 3145736 | tf_op jit(solution)/shard_map/ppermute | solution.py:318
  29.4 3.3 %copy-start.6 = (s32[8]{0:T(128)S(1)}, s32[8]{0:T(128)}, u32[]{:S(2)}) copy-start(s32[8]{0:T(128)} %constant.136.clone) | copy-start | bytes 100
  29.4 3.3 %copy-start.4 = (s32[128,16]{0,1:T(8,128)S(1)}, s32[128,16]{0,1:T(8,128)}, u32[]{:S(2)}) copy-start(s32[128,16]{0,1:T(8,128)} %param.15) | copy-start | bytes 24580
  29.4 23.5 %collective-permute-start.13 = (f32[8,16,2048]{2,1,0:T(8,128)S(1)}, f32[8,16,2048]{2,1,0:T(8,128)}, u32[]{:S(2)}, u32[]{:S(2)}) collective-permute-start(f32[8,16,2048]{2,1,0:T(8,128)S(1)} %pad_maximum_fusion.1.refs_1_), channel_id=1, source_target_pairs={{0,1},{1,0},{2,3},{3,2},{4,5},{5,4},{6,7},{7,6},{8,9},{9,8},{10,11... | collective-permute-start | bytes 3145736 | tf_op jit(solution)/shard_map/ppermute | solution.py:318
  30.0 22.9 %collective-permute-start.14 = (f32[8,16,2048]{2,1,0:T(8,128)S(1)}, f32[8,16,2048]{2,1,0:T(8,128)}, u32[]{:S(2)}, u32[]{:S(2)}) collective-permute-start(f32[8,16,2048]{2,1,0:T(8,128)S(1)} %pad_maximum_fusion.2.refs_2_), channel_id=1, source_target_pairs={{0,3},{1,2},{2,1},{3,0},{4,7},{5,6},{6,5},{7,4},{8,11},{9,10},{10,... | collective-permute-start | bytes 3145736 | tf_op jit(solution)/shard_map/ppermute | solution.py:318
  32.5 20.5 %collective-permute-start.15 = (f32[8,16,2048]{2,1,0:T(8,128)}, f32[8,16,2048]{2,1,0:T(8,128)}, u32[]{:S(2)}, u32[]{:S(2)}) collective-permute-start(f32[8,16,2048]{2,1,0:T(8,128)} %pad_maximum_fusion.3.refs_3_), channel_id=1, source_target_pairs={{0,4},{4,0},{8,12},{12,8},{1,5},{5,1},{9,13},{13,9},{2,6},{6,2},{1... | collective-permute-start | bytes 3145736 | tf_op jit(solution)/shard_map/ppermute | solution.py:318
  69.0 17.9 %collective-permute-start.16 = (f32[4,10,128,128]{3,2,1,0:T(8,128)}, f32[4,10,128,128]{3,2,1,0:T(8,128)}, u32[]{:S(2)}, u32[]{:S(2)}) collective-permute-start(f32[4,10,128,128]{3,2,1,0:T(8,128)} %get-tuple-element.42), channel_id=1, source_target_pairs={{0,16},{16,0},{1,17},{17,1},{2,18},{18,2},{3,19},{19,3},{4,20},{20... | collective-permute-start | bytes 7864328 | tf_op jit(solution)/shard_map/ppermute | solution.py:363
  89.6 14.3 %collective-permute-start.17 = (f32[5,128,128]{2,1,0:T(8,128)}, f32[5,128,128]{2,1,0:T(8,128)}, u32[]{:S(2)}, u32[]{:S(2)}) collective-permute-start(f32[5,128,128]{2,1,0:T(8,128)} %get-tuple-element.48), channel_id=1, source_target_pairs={{0,32},{32,64},{64,96},{96,0},{1,33},{33,65},{65,97},{97,1},{2,34}... | collective-permute-start | bytes 983048 | tf_op jit(solution)/shard_map/ppermute | solution.py:366
  91.1 12.8 %collective-permute-start.18 = (f32[5,128,128]{2,1,0:T(8,128)}, f32[5,128,128]{2,1,0:T(8,128)}, u32[]{:S(2)}, u32[]{:S(2)}) collective-permute-start(f32[5,128,128]{2,1,0:T(8,128)} %get-tuple-element.49), channel_id=1, source_target_pairs={{0,96},{32,0},{64,32},{96,64},{1,97},{33,1},{65,33},{97,65},{2,98}... | collective-permute-start | bytes 983048 | tf_op jit(solution)/shard_map/ppermute | solution.py:366
  102.2 14.2 %collective-permute-start.21 = (f32[4,6,128,128]{3,2,1,0:T(8,128)}, f32[4,6,128,128]{3,2,1,0:T(8,128)}, u32[]{:S(2)}, u32[]{:S(2)}) collective-permute-start(f32[4,6,128,128]{3,2,1,0:T(8,128)} %shard_map.110), channel_id=1, source_target_pairs={{0,16},{16,0},{1,17},{17,1},{2,18},{18,2},{3,19},{19,3},{4,20},{20... | collective-permute-start | bytes 4718600 | tf_op jit(solution)/shard_map/ppermute | solution.py:363
  106.1 18.5 %collective-permute-start.19 = (f32[10,128,128]{2,1,0:T(8,128)}, f32[10,128,128]{2,1,0:T(8,128)}, u32[]{:S(2)}, u32[]{:S(2)}) collective-permute-start(f32[10,128,128]{2,1,0:T(8,128)} %get-tuple-element.50), channel_id=1, source_target_pairs={{0,32},{32,64},{64,96},{96,0},{1,33},{33,65},{65,97},{97,1},{2,34}... | collective-permute-start | bytes 1966088 | tf_op jit(solution)/shard_map/ppermute | solution.py:366
  106.1 18.6 %collective-permute-start.20 = (f32[10,128,128]{2,1,0:T(8,128)}, f32[10,128,128]{2,1,0:T(8,128)}, u32[]{:S(2)}, u32[]{:S(2)}) collective-permute-start(f32[10,128,128]{2,1,0:T(8,128)} %get-tuple-element.51), channel_id=1, source_target_pairs={{0,96},{32,0},{64,32},{96,64},{1,97},{33,1},{65,33},{97,65},{2,98}... | collective-permute-start | bytes 1966088 | tf_op jit(solution)/shard_map/ppermute | solution.py:366
  116.4 4.3 %copy-start.5 = (s32[16,4]{0,1:T(4,128)S(1)}, s32[16,4]{0,1:T(4,128)}, u32[]{:S(2)}) copy-start(s32[16,4]{0,1:T(4,128)} %param.14) | copy-start | bytes 772
  118.0 10.1 %collective-permute-start.22 = (f32[3,128,128]{2,1,0:T(8,128)S(1)}, f32[3,128,128]{2,1,0:T(8,128)S(1)}, u32[]{:S(2)}, u32[]{:S(2)}) collective-permute-start(f32[3,128,128]{2,1,0:T(8,128)S(1)} %get-tuple-element.61), channel_id=1, source_target_pairs={{0,32},{32,64},{64,96},{96,0},{1,33},{33,65},{65,97},{97,1},{2,34}... | collective-permute-start | bytes 589832 | tf_op jit(solution)/shard_map/ppermute | solution.py:366
  118.1 10.0 %collective-permute-start.23 = (f32[3,128,128]{2,1,0:T(8,128)S(1)}, f32[3,128,128]{2,1,0:T(8,128)S(1)}, u32[]{:S(2)}, u32[]{:S(2)}) collective-permute-start(f32[3,128,128]{2,1,0:T(8,128)S(1)} %get-tuple-element.66), channel_id=1, source_target_pairs={{0,96},{32,0},{64,32},{96,64},{1,97},{33,1},{65,33},{97,65},{2,98}... | collective-permute-start | bytes 589832 | tf_op jit(solution)/shard_map/ppermute | solution.py:366
  128.1 11.1 %collective-permute-start.24 = (f32[6,128,128]{2,1,0:T(8,128)S(1)}, f32[6,128,128]{2,1,0:T(8,128)S(1)}, u32[]{:S(2)}, u32[]{:S(2)}) collective-permute-start(f32[6,128,128]{2,1,0:T(8,128)S(1)} %get-tuple-element.67), channel_id=1, source_target_pairs={{0,32},{32,64},{64,96},{96,0},{1,33},{33,65},{65,97},{97,1},{2,34}... | collective-permute-start | bytes 1179656 | tf_op jit(solution)/shard_map/ppermute | solution.py:366
  128.2 11.0 %collective-permute-start.25 = (f32[6,128,128]{2,1,0:T(8,128)S(1)}, f32[6,128,128]{2,1,0:T(8,128)S(1)}, u32[]{:S(2)}, u32[]{:S(2)}) collective-permute-start(f32[6,128,128]{2,1,0:T(8,128)S(1)} %get-tuple-element.68), channel_id=1, source_target_pairs={{0,96},{32,0},{64,32},{96,64},{1,97},{33,1},{65,33},{97,65},{2,98}... | collective-permute-start | bytes 1179656 | tf_op jit(solution)/shard_map/ppermute | solution.py:366
  142.9 27.9 %copy-start.1 = (f32[128,2048]{1,0:T(8,128)S(1)}, f32[128,2048]{1,0:T(8,128)}, u32[]{:S(2)}) copy-start(f32[128,2048]{1,0:T(8,128)} %den_ref.1) | copy-start | bytes 3145732
  (1 other events, 2.2 us)

commit v10 on v9

--- a/solution.py
+++ b/solution.py
@@ -182,13 +182,10 @@
     )(*maps, *rows, integrals)
 
 
-def far_kernel(mine_ref, got_ref, p_ref, m_ref, plus_ref, minus_ref, own_ref):
+def far_kernel(mine_ref, got_ref, p_ref, m_ref):
     half = p_ref.shape[0]
     p_ref[...] = mine_ref[0, :half] + got_ref[0, :half]
     m_ref[...] = mine_ref[0, half:] + got_ref[0, half:]
-    plus_ref[...] = mine_ref[1] + got_ref[1]
-    minus_ref[...] = mine_ref[2] + got_ref[2]
-    own_ref[...] = mine_ref[3] + got_ref[3]
 
 
 def small(kernel, inputs, shapes, scratch=()):
@@ -203,22 +200,46 @@
     )(*inputs)
 
 
+def blocks_of(x, first, count):
+    sizes = (count,) + x.shape[1:]
+    return pl.BlockSpec(tuple(pl.Element(n) for n in sizes), lambda n: (first, 0, 0, 0))
+
+
+def whole_of(x):
+    return pl.BlockSpec(x.shape, lambda n: (0, 0, 0))
+
+
 def far(mine, got):
-    part = mine.shape[1:]
-    half = (part[0] // 2, ROWS, TILE)
-    return small(far_kernel, (mine, got), (half, half, part, part, part))
-
-
-def near_kernel(plus_ref, minus_ref, gp_ref, gm_ref, p_ref, m_ref):
+    half = jax.ShapeDtypeStruct((mine.shape[1] // 2, ROWS, TILE), f32)
+    return call(
+        far_kernel,
+        (half, half),
+        grid=(1,),
+        in_specs=[blocks_of(mine, 0, 1), blocks_of(got, 0, 1)],
+        out_specs=(whole_of(half), whole_of(half)),
+        nbytes=mine.size * 2,
+    )(mine, got)
+
+
+def near_kernel(mine_ref, got_ref, gp_ref, gm_ref, p_ref, m_ref, own_ref):
     half = gp_ref.shape[0]
-    p_ref[:half] = plus_ref[:half] + gp_ref[...]
-    p_ref[half:] = plus_ref[half:]
-    m_ref[:half] = minus_ref[:half]
-    m_ref[half:] = minus_ref[half:] + gm_ref[...]
-
-
-def near(plus, minus, gp, gm):
-    return small(near_kernel, (plus, minus, gp, gm), (plus.shape, plus.shape))
+    p_ref[:half] = mine_ref[0, :half] + got_ref[0, :half] + gp_ref[...]
+    p_ref[half:] = mine_ref[0, half:] + got_ref[0, half:]
+    m_ref[:half] = mine_ref[1, :half] + got_ref[1, :half]
+    m_ref[half:] = mine_ref[1, half:] + got_ref[1, half:] + gm_ref[...]
+    own_ref[...] = mine_ref[2] + got_ref[2]
+
+
+def near(mine, got, gp, gm):
+    part = jax.ShapeDtypeStruct(mine.shape[1:], f32)
+    return call(
+        near_kernel,
+        (part, part, part),
+        grid=(1,),
+        in_specs=[blocks_of(mine, 1, 3), blocks_of(got, 1, 3), whole_of(gp), whole_of(gm)],
+        out_specs=(whole_of(part),) * 3,
+        nbytes=mine.size * 8,
+    )(mine, got, gp, gm)
 
 
 SLAB = CAP + 1
@@ -374,17 +395,18 @@
     theirs0, other_hi, other_lo = first_product(other)
     from_core0 = swap(theirs0)
     mine0, own_hi, own_lo = first_product(after(own, theirs0))
-    p0, m0, plus0, minus0, base0 = far(mine0, from_core0)
+    p0, m0 = far(mine0, from_core0)
     gp0, gm0 = along_z(p0, m0)
-    theirs1 = next_product(after(other, base0), other_hi, other_lo)
+    theirs1 = next_product(after(other, p0), other_hi, other_lo)
     from_core1 = swap(theirs1)
-    near0 = near(plus0, minus0, gp0, gm0)
-    rp0, rm0 = along_z(*near0)
-    mine1 = next_product(after(own, *near0), own_hi, own_lo)
-    p1, m1, plus1, minus1, base1 = far(mine1, from_core1)
+    near0_p, near0_m, base0 = near(mine0, from_core0, gp0, gm0)
+    rp0, rm0 = along_z(near0_p, near0_m)
+    mine1 = next_product(after(own, near0_p), own_hi, own_lo)
+    p1, m1 = far(mine1, from_core1)
     gp1, gm1 = along_z(p1, m1)
-    ch, cl = prepare_cycle(after(cycle_tiles, base1), cycle_mask)
-    rp1, rm1 = along_z(*near(plus1, minus1, after(gp1, rp0, rm0, ch, cl), gm1))
+    ch, cl = prepare_cycle(after(cycle_tiles, p1), cycle_mask)
+    near1_p, near1_m, base1 = near(mine1, from_core1, after(gp1, rp0, rm0, ch, cl), gm1)
+    rp1, rm1 = along_z(near1_p, near1_m)
 
     sending = gather(source, place, ((base0, rp0, rm0), (base1, rp1, rm1))).reshape(128, 1, SLAB * TILE)
     units = lax.all_to_all(sending, everyone, split_axis=0, concat_axis=0, tiled=True)

time: 177 us -> 179 us (1.011)
    pallas_call x0 -> x4, Pallas kernels: none -> 7.2 us  [the longest x2 4.21 us: near(): call(near_kernel, (part, part, part), grid=(1,), in_specs=[blocks_of(mine...]
    pallas_call x5 -> x1, Pallas kernels: 10.2 us -> 3.68 us  [small(): call(kernel, shapes, in_specs=[SMEM if x.dtype == jnp.int32 else VMEM for...]
where the time goes in v10:
time: 179 us; the launch traced here: 178 us
  Pallas kernels  78.9 us (44%)
  starting transfers between devices  35.3 us (20%)
  blocking collectives  27.9 us (16%)
  waiting for transfers between devices  23.6 us (13%)
  other arithmetic  7.31 us (4%)
  local copies, waits for them, and re-layouts  3.86 us (2%)
    pallas_call x4, Pallas kernels, multiply(): call(kernel, tuple(shapes), in_specs=[SMEM] * len(maps) + [HBM if first e...  45.7 us
    all_to_all x1, blocking collectives, body(): lax.all_to_all(sending, everyone, split_axis=0, concat_axis=0, tiled=True)  27.9 us
    ppermute x16, starting transfers between devices, exchange(): return lax.ppermute(value, axis, pairs)  17.2 us
    pallas_call x1, Pallas kernels, prepare_integrals(): call(integrals_kernel, jax.ShapeDtypeStruct((cols // NB, 2, depth, NB), b...  14.8 us
    ppermute x8, waiting for transfers between devices, along_z(): return (lax.ppermute(p, 'z', ring(1)), lax.ppermute(m, 'z', ring(-1)))  12.3 us
    ppermute x8, starting transfers between devices, along_z(): return (lax.ppermute(p, 'z', ring(1)), lax.ppermute(m, 'z', ring(-1)))  12.1 us
    ppermute x16, waiting for transfers between devices, exchange(): return lax.ppermute(value, axis, pairs)  11.3 us
    pallas_call x1, Pallas kernels, finish(): call(finish_kernel, (shape, shape), in_specs=[VMEM] * 4, out_specs=(VMEM,...  5.95 us
  transfers between devices with their start and end apart: 26, of which 6 were waited for; matrix products, arithmetic and copies ran while one was open for 4% of the time, Pallas kernels for 28%

profile of v10, /device:TPU:1, one launch (start us, length us, event | category | flops | bytes accessed | tf_op | source)
XLA Modules:
  0.0 177.9 jit_solution(11878758240077406502)
XLA Ops:
  1.8 2.1 %collective-permute-start = (f32[1,16,2048]{2,1,0:T(8,128)S(1)}, f32[1,16,2048]{2,1,0:T(8,128)S(1)}, u32[]{:S(2)}, u32[]{:S(2)}) collective-permute-start(f32[1,16,2048]{2,1,0:T(8,128)S(1)} %get-tuple-element.65), channel_id=1, source_target_pairs={{0,1},{1,0},{2,3},{3,2},{4,5},{5,4},{6,7},{7,6},{8,9},{9,8},{10,11... | collective-permute-start | bytes 393224 | tf_op jit(solution)/shard_map/ppermute | solution.py:339
  3.9 1.8 %collective-permute-start.3 = (f32[1,16,2048]{2,1,0:T(8,128)S(1)}, f32[1,16,2048]{2,1,0:T(8,128)S(1)}, u32[]{:S(2)}, u32[]{:S(2)}) collective-permute-start(f32[1,16,2048]{2,1,0:T(8,128)S(1)} %get-tuple-element.64), channel_id=1, source_target_pairs={{0,3},{1,2},{2,1},{3,0},{4,7},{5,6},{6,5},{7,4},{8,11},{9,10},{10,... | collective-permute-start | bytes 393224 | tf_op jit(solution)/shard_map/ppermute | solution.py:339
  5.7 1.3 collective-permute-start.6
  7.0 1.9 %collective-permute-start.9 = (f32[1,16,2048]{2,1,0:T(8,128)S(1)}, f32[1,16,2048]{2,1,0:T(8,128)S(1)}, u32[]{:S(2)}, u32[]{:S(2)}) collective-permute-start(f32[1,16,2048]{2,1,0:T(8,128)S(1)} %get-tuple-element.63), channel_id=1, source_target_pairs={{0,12},{4,8},{8,4},{12,0},{1,13},{5,9},{9,5},{13,1},{2,14},{6,10},... | collective-permute-start | bytes 393224 | tf_op jit(solution)/shard_map/ppermute | solution.py:339
  11.2 1.8 %collective-permute-start.7 = (f32[2,16,2048]{2,1,0:T(8,128)S(1)}, f32[2,16,2048]{2,1,0:T(8,128)S(1)}, u32[]{:S(2)}, u32[]{:S(2)}) collective-permute-start(f32[2,16,2048]{2,1,0:T(8,128)S(1)} %pad_maximum_fusion.10), channel_id=1, source_target_pairs={{0,12},{4,8},{8,4},{12,0},{1,13},{5,9},{9,5},{13,1},{2,14},{6,10},... | collective-permute-start | bytes 786440 | tf_op jit(solution)/shard_map/ppermute | solution.py:339
  13.1 3.9 %collective-permute-done.1 = f32[2,16,2048]{2,1,0:T(8,128)S(1)} collective-permute-done((f32[2,16,2048]{2,1,0:T(8,128)S(1)}, f32[2,16,2048]{2,1,0:T(8,128)S(1)}, u32[]{:S(2)}, u32[]{:S(2)}) %collective-permute-start.1) | collective-permute-done | bytes 262176 | tf_op jit(solution)/shard_map/ppermute | solution.py:339
  18.8 2.0 %collective-permute-start.11 = (f32[4,16,2048]{2,1,0:T(8,128)S(1)}, f32[4,16,2048]{2,1,0:T(8,128)S(1)}, u32[]{:S(2)}, u32[]{:S(2)}) collective-permute-start(f32[4,16,2048]{2,1,0:T(8,128)S(1)} %pad_maximum_fusion.7), channel_id=1, source_target_pairs={{0,3},{1,2},{2,1},{3,0},{4,7},{5,6},{6,5},{7,4},{8,11},{9,10},{10,... | collective-permute-start | bytes 1572872 | tf_op jit(solution)/shard_map/ppermute | solution.py:339
  20.8 7.0 %collective-permute-done.2 = f32[4,16,2048]{2,1,0:T(8,128)S(1)} collective-permute-done((f32[4,16,2048]{2,1,0:T(8,128)S(1)}, f32[4,16,2048]{2,1,0:T(8,128)S(1)}, u32[]{:S(2)}, u32[]{:S(2)}) %collective-permute-start.2) | collective-permute-done | bytes 524320 | tf_op jit(solution)/shard_map/ppermute | solution.py:339
  30.0 1.5 collective-permute-start.14
  33.0 5.0 %sort.14 = (s32[2048]{0:T(1024)S(1)}, s32[2048]{0:T(1024)}) sort(s32[2048]{0:T(1024)S(1)} %fusion.10, s32[2048]{0:T(1024)S(1)} %iota.7), dimensions={0}, to_apply=%region_0.1 | sort | flops 22528 | bytes 32768 | tf_op jit(solution)/shard_map/sort | solution.py:323
  38.1 14.8 %shard_map.104.refs_8_.b_ref = bf16[8,2,2048,256]{3,2,1,0:T(8,128)(2,1)} custom-call(s32[16,16]{1,0:T(8,128)} %mask_ref.2, f32[2048,2048]{1,0:T(8,128)} %x_ref), custom_call_target="tpu_custom_call" | custom-call | flops 16777216 | bytes 33554432 | tf_op jit(solution)/shard_map/pallas_call | solution.py:80
  53.0 16.0 %shard_map.105 = (f32[4,10,128,128]{3,2,1,0:T(8,128)}, bf16[512,2048]{1,0:T(8,128)(2,1)S(1)}, bf16[512,2048]{1,0:T(8,128)(2,1)S(1)}) custom-call(s32[4,8]{1,0:T(4,128)S(1)} %pad_add_fusion.where_ref.ready_ref, f32[8,16,2048]{2,1,0:T(8,128)S(1)} %pad_maximum_fusion.refs_0_, f32[8,16,2048]{2,1,0:T(8,128)S(1)} %pad_maximum_fusion.1.refs_1_, ...), custom_call_target="tpu_custom_call" | custom-call | flops 322122547200 | bytes 10485760 | tf_op jit(solution)/shard_map/pallas_call | solution.py:173
  69.0 4.4 %collective-permute-start.16 = (f32[4,10,128,128]{3,2,1,0:T(8,128)}, f32[4,10,128,128]{3,2,1,0:T(8,128)}, u32[]{:S(2)}, u32[]{:S(2)}) collective-permute-start(f32[4,10,128,128]{3,2,1,0:T(8,128)} %get-tuple-element.38), channel_id=1, source_target_pairs={{0,16},{16,0},{1,17},{17,1},{2,18},{18,2},{3,19},{19,3},{4,20},{20... | collective-permute-start | bytes 7864328 | tf_op jit(solution)/shard_map/ppermute | solution.py:384
  73.4 13.3 %shard_map.106 = (f32[4,10,128,128]{3,2,1,0:T(8,128)S(1)}, bf16[512,2048]{1,0:T(8,128)(2,1)S(1)}, bf16[512,2048]{1,0:T(8,128)(2,1)S(1)}) custom-call(s32[4,8]{1,0:T(4,128)S(1)} %pad_add_fusion.1.where_ref.ready_ref, f32[8,16,2048]{2,1,0:T(8,128)S(1)} %pad_maximum_fusion.refs_0_, f32[8,16,2048]{2,1,0:T(8,128)S(1)} %pad_maximum_fusion.1.refs_1_, ...), custom_call_target="tpu_custom_call" | custom-call | flops 322122547200 | bytes 10485760 | tf_op jit(solution)/shard_map/pallas_call | solution.py:173
  86.7 2.0 %shard_map.107 = (f32[5,128,128]{2,1,0:T(8,128)}, f32[5,128,128]{2,1,0:T(8,128)}) custom-call(f32[4,10,128,128]{3,2,1,0:T(8,128)S(1)} %get-tuple-element.40.mine_ref, f32[4,10,128,128]{3,2,1,0:T(8,128)} %collective-permute-done.16.got_ref), custom_call_target="tpu_custom_call" | custom-call | bytes 1310720 | tf_op jit(solution)/shard_map/pallas_call | solution.py:214
  88.7 1.6 collective-permute-start.17
  90.3 2.4 %collective-permute-start.18 = (f32[5,128,128]{2,1,0:T(8,128)}, f32[5,128,128]{2,1,0:T(8,128)}, u32[]{:S(2)}, u32[]{:S(2)}) collective-permute-start(f32[5,128,128]{2,1,0:T(8,128)} %get-tuple-element.42), channel_id=1, source_target_pairs={{0,96},{32,0},{64,32},{96,64},{1,97},{33,1},{65,33},{97,65},{2,98}... | collective-permute-start | bytes 983048 | tf_op jit(solution)/shard_map/ppermute | solution.py:387
  92.7 8.7 %shard_map.110 = f32[4,6,128,128]{3,2,1,0:T(8,128)} custom-call(s32[4,8]{1,0:T(4,128)S(1)} %pad_add_fusion.where_ref.ready_ref, bf16[512,2048]{1,0:T(8,128)(2,1)S(1)} %get-tuple-element.50.ah, bf16[512,2048]{1,0:T(8,128)(2,1)S(1)} %get-tuple-element.51.al, bf16[8,2,2048,256]{3,2,1,0:T(8,128)(2,1)} %shard_map.104.refs_8_.b_ref), custom_call_target="tpu_custom_call" | custom-call | flops 193273528320 | bytes 6291456 | tf_op jit(solution)/shard_map/pallas_call | solution.py:173
  101.4 1.5 collective-permute-start.21
  103.0 2.8 %shard_map.108 = (f32[10,128,128]{2,1,0:T(8,128)}, f32[10,128,128]{2,1,0:T(8,128)}, f32[10,128,128]{2,1,0:T(8,128)S(1)}) custom-call(f32[4,10,128,128]{3,2,1,0:T(8,128)S(1)} %get-tuple-element.40.mine_ref, f32[4,10,128,128]{3,2,1,0:T(8,128)} %collective-permute-done.16.got_ref, f32[5,128,128]{2,1,0:T(8,128)} %collective-permute-done.17.gp_ref, ...), custom_call_target="tpu_custom_call" | custom-call | bytes 5242880 | tf_op jit(solution)/shard_map/pallas_call | solution.py:235
  105.8 2.7 %collective-permute-start.20 = (f32[10,128,128]{2,1,0:T(8,128)}, f32[10,128,128]{2,1,0:T(8,128)}, u32[]{:S(2)}, u32[]{:S(2)}) collective-permute-start(f32[10,128,128]{2,1,0:T(8,128)} %get-tuple-element.45), channel_id=1, source_target_pairs={{0,96},{32,0},{64,32},{96,64},{1,97},{33,1},{65,33},{97,65},{2,98}... | collective-permute-start | bytes 1966088 | tf_op jit(solution)/shard_map/ppermute | solution.py:387
  108.4 7.6 %shard_map.109.mine_ref = f32[4,6,128,128]{3,2,1,0:T(8,128)S(1)} custom-call(s32[4,8]{1,0:T(4,128)S(1)} %pad_add_fusion.1.where_ref.ready_ref, bf16[512,2048]{1,0:T(8,128)(2,1)S(1)} %get-tuple-element.47.ah, bf16[512,2048]{1,0:T(8,128)(2,1)S(1)} %get-tuple-element.48.al, bf16[8,2,2048,256]{3,2,1,0:T(8,128)(2,1)} %shard_map.104.refs_8_.b_ref), custom_call_target="tpu_custom_call" | custom-call | flops 193273528320 | bytes 6291456 | tf_op jit(solution)/shard_map/pallas_call | solution.py:173
  117.2 2.7 %collective-permute-start.23 = (f32[3,128,128]{2,1,0:T(8,128)S(1)}, f32[3,128,128]{2,1,0:T(8,128)S(1)}, u32[]{:S(2)}, u32[]{:S(2)}) collective-permute-start(f32[3,128,128]{2,1,0:T(8,128)S(1)} %get-tuple-element.57), channel_id=1, source_target_pairs={{0,96},{32,0},{64,32},{96,64},{1,97},{33,1},{65,33},{97,65},{2,98}... | collective-permute-start | bytes 589832 | tf_op jit(solution)/shard_map/ppermute | solution.py:387
  120.0 2.2 %copy-done = f32[2048,512]{1,0:T(8,128)S(1)} copy-done((f32[2048,512]{1,0:T(8,128)S(1)}, f32[2048,512]{1,0:T(8,128)}, u32[]{:S(2)}) %copy-start) | copy-done | bytes 4194328
  122.2 1.6 shard_map.112
  123.8 3.9 %collective-permute-done.22.gp_ref = f32[3,128,128]{2,1,0:T(8,128)S(1)} collective-permute-done((f32[3,128,128]{2,1,0:T(8,128)S(1)}, f32[3,128,128]{2,1,0:T(8,128)S(1)}, u32[]{:S(2)}, u32[]{:S(2)}) %collective-permute-start.22) | collective-permute-done | bytes 196640 | tf_op jit(solution)/shard_map/ppermute | solution.py:387
  127.7 1.4 shard_map.113
  129.2 2.7 %collective-permute-start.25 = (f32[6,128,128]{2,1,0:T(8,128)S(1)}, f32[6,128,128]{2,1,0:T(8,128)S(1)}, u32[]{:S(2)}, u32[]{:S(2)}) collective-permute-start(f32[6,128,128]{2,1,0:T(8,128)S(1)} %get-tuple-element.60), channel_id=1, source_target_pairs={{0,96},{32,0},{64,32},{96,64},{1,97},{33,1},{65,33},{97,65},{2,98}... | collective-permute-start | bytes 1179656 | tf_op jit(solution)/shard_map/ppermute | solution.py:387
  131.9 8.4 %collective-permute-done.24.refs_4_ = f32[6,128,128]{2,1,0:T(8,128)S(1)} collective-permute-done((f32[6,128,128]{2,1,0:T(8,128)S(1)}, f32[6,128,128]{2,1,0:T(8,128)S(1)}, u32[]{:S(2)}, u32[]{:S(2)}) %collective-permute-start.24) | collective-permute-done | bytes 393248 | tf_op jit(solution)/shard_map/ppermute | solution.py:387
  140.2 3.7 %shard_map.114 = f32[2176,128]{1,0:T(8,128)S(1)} custom-call(s32[2048]{0:T(1024)S(1)} %get-tuple-element.34.idx_ref, f32[128,128]{1,0:T(8,128)S(1)} %pad.4.place_ref, f32[10,128,128]{2,1,0:T(8,128)S(1)} %get-tuple-element.43.refs_0_, f32[10,128,128]{2,1,0:T(8,128)} %collective-permute-done.19.refs_1_, f32[10,128,128]{2,1,0:T(8,128)} %collective-permute-done.20.refs_2_, ...), custom_call_target="tpu_custom_call" | custom-call | bytes 3219456 | tf_op jit(solution)/shard_map/pallas_call | solution.py:193
  143.9 27.9 %all_to_all.5 = f32[128,1,2176]{2,1,0:T(1,128)S(1)} all-to-all(f32[128,1,2176]{2,1,0:T(1,128)S(1)} %bitcast.26), channel_id=1, replica_groups=mesh['z'=4,'core'=2,'y'=4,'x'=4] {'z','core','y','x'}, dimensions={0} | all-to-all | bytes 2228224 | tf_op jit(solution)/shard_map/all_to_all | solution.py:412
  171.8 6.0 %shard_map.115 = (f32[128,2048]{1,0:T(8,128)}, f32[128,2048]{1,0:T(8,128)}) custom-call(f32[2176,128]{1,0:T(8,128)S(1)} %bitcast.27, f32[128,2048]{1,0:T(8,128)S(1)} %copy-done.1, bf16[2048,512]{1,0:T(8,128)(2,1)S(1)} %get-tuple-element.54.ch_ref, bf16[2048,512]{1,0:T(8,128)(2,1)S(1)} %get-tuple-element.55.cl_ref), custom_call_target="tpu_custom_call" | custom-call | bytes 8388608 | tf_op jit(solution)/shard_map/pallas_call | solution.py:299
  (76 shorter events, 10.3 us)
Async XLA Ops:
  1.8 8.0 %collective-permute-start = (f32[1,16,2048]{2,1,0:T(8,128)S(1)}, f32[1,16,2048]{2,1,0:T(8,128)S(1)}, u32[]{:S(2)}, u32[]{:S(2)}) collective-permute-start(f32[1,16,2048]{2,1,0:T(8,128)S(1)} %get-tuple-element.65), channel_id=1, source_target_pairs={{0,1},{1,0},{2,3},{3,2},{4,5},{5,4},{6,7},{7,6},{8,9},{9,8},{10,11... | collective-permute-start | bytes 393224 | tf_op jit(solution)/shard_map/ppermute | solution.py:339
  3.9 6.8 %collective-permute-start.3 = (f32[1,16,2048]{2,1,0:T(8,128)S(1)}, f32[1,16,2048]{2,1,0:T(8,128)S(1)}, u32[]{:S(2)}, u32[]{:S(2)}) collective-permute-start(f32[1,16,2048]{2,1,0:T(8,128)S(1)} %get-tuple-element.64), channel_id=1, source_target_pairs={{0,3},{1,2},{2,1},{3,0},{4,7},{5,6},{6,5},{7,4},{8,11},{9,10},{10,... | collective-permute-start | bytes 393224 | tf_op jit(solution)/shard_map/ppermute | solution.py:339
  5.7 5.5 %collective-permute-start.6 = (f32[1,16,2048]{2,1,0:T(8,128)S(1)}, f32[1,16,2048]{2,1,0:T(8,128)S(1)}, u32[]{:S(2)}, u32[]{:S(2)}) collective-permute-start(f32[1,16,2048]{2,1,0:T(8,128)S(1)} %get-tuple-element.66), channel_id=1, source_target_pairs={{0,4},{4,0},{8,12},{12,8},{1,5},{5,1},{9,13},{13,9},{2,6},{6,2},{1... | collective-permute-start | bytes 393224 | tf_op jit(solution)/shard_map/ppermute | solution.py:339
  7.0 6.0 %collective-permute-start.9 = (f32[1,16,2048]{2,1,0:T(8,128)S(1)}, f32[1,16,2048]{2,1,0:T(8,128)S(1)}, u32[]{:S(2)}, u32[]{:S(2)}) collective-permute-start(f32[1,16,2048]{2,1,0:T(8,128)S(1)} %get-tuple-element.63), channel_id=1, source_target_pairs={{0,12},{4,8},{8,4},{12,0},{1,13},{5,9},{9,5},{13,1},{2,14},{6,10},... | collective-permute-start | bytes 393224 | tf_op jit(solution)/shard_map/ppermute | solution.py:339
  9.7 7.3 %collective-permute-start.1 = (f32[2,16,2048]{2,1,0:T(8,128)S(1)}, f32[2,16,2048]{2,1,0:T(8,128)S(1)}, u32[]{:S(2)}, u32[]{:S(2)}) collective-permute-start(f32[2,16,2048]{2,1,0:T(8,128)S(1)} %pad_maximum_fusion.8), channel_id=1, source_target_pairs={{0,3},{1,2},{2,1},{3,0},{4,7},{5,6},{6,5},{7,4},{8,11},{9,10},{10,... | collective-permute-start | bytes 786440 | tf_op jit(solution)/shard_map/ppermute | solution.py:339
  10.7 6.8 %collective-permute-start.4 = (f32[2,16,2048]{2,1,0:T(8,128)S(1)}, f32[2,16,2048]{2,1,0:T(8,128)S(1)}, u32[]{:S(2)}, u32[]{:S(2)}) collective-permute-start(f32[2,16,2048]{2,1,0:T(8,128)S(1)} %pad_maximum_fusion.9), channel_id=1, source_target_pairs={{0,4},{4,0},{8,12},{12,8},{1,5},{5,1},{9,13},{13,9},{2,6},{6,2},{1... | collective-permute-start | bytes 786440 | tf_op jit(solution)/shard_map/ppermute | solution.py:339
  11.2 7.6 %copy-start.2 = (f32[1,16,2048]{2,1,0:T(8,128)}, f32[1,16,2048]{2,1,0:T(8,128)S(1)}, u32[]{:S(2)}) copy-start(f32[1,16,2048]{2,1,0:T(8,128)S(1)} %collective-permute-done.6) | copy-start | bytes 393220
  11.2 7.4 %collective-permute-start.7 = (f32[2,16,2048]{2,1,0:T(8,128)S(1)}, f32[2,16,2048]{2,1,0:T(8,128)S(1)}, u32[]{:S(2)}, u32[]{:S(2)}) collective-permute-start(f32[2,16,2048]{2,1,0:T(8,128)S(1)} %pad_maximum_fusion.10), channel_id=1, source_target_pairs={{0,12},{4,8},{8,4},{12,0},{1,13},{5,9},{9,5},{13,1},{2,14},{6,10},... | collective-permute-start | bytes 786440 | tf_op jit(solution)/shard_map/ppermute | solution.py:339
  13.1 5.6 %collective-permute-start.10 = (f32[2,16,2048]{2,1,0:T(8,128)S(1)}, f32[2,16,2048]{2,1,0:T(8,128)S(1)}, u32[]{:S(2)}, u32[]{:S(2)}) collective-permute-start(f32[2,16,2048]{2,1,0:T(8,128)S(1)} %pad_maximum_fusion.11), channel_id=1, source_target_pairs={{0,1},{1,0},{2,3},{3,2},{4,5},{5,4},{6,7},{7,6},{8,9},{9,8},{10,11... | collective-permute-start | bytes 786440 | tf_op jit(solution)/shard_map/ppermute | solution.py:339
  17.1 10.8 %collective-permute-start.2 = (f32[4,16,2048]{2,1,0:T(8,128)S(1)}, f32[4,16,2048]{2,1,0:T(8,128)S(1)}, u32[]{:S(2)}, u32[]{:S(2)}) collective-permute-start(f32[4,16,2048]{2,1,0:T(8,128)S(1)} %pad_maximum_fusion.4), channel_id=1, source_target_pairs={{0,4},{4,0},{8,12},{12,8},{1,5},{5,1},{9,13},{13,9},{2,6},{6,2},{1... | collective-permute-start | bytes 1572872 | tf_op jit(solution)/shard_map/ppermute | solution.py:339
  17.6 11.7 %collective-permute-start.5 = (f32[4,16,2048]{2,1,0:T(8,128)S(1)}, f32[4,16,2048]{2,1,0:T(8,128)S(1)}, u32[]{:S(2)}, u32[]{:S(2)}) collective-permute-start(f32[4,16,2048]{2,1,0:T(8,128)S(1)} %pad_maximum_fusion.5), channel_id=1, source_target_pairs={{0,12},{4,8},{8,4},{12,0},{1,13},{5,9},{9,5},{13,1},{2,14},{6,10},... | collective-permute-start | bytes 1572872 | tf_op jit(solution)/shard_map/ppermute | solution.py:339
  18.6 11.3 %collective-permute-start.8 = (f32[4,16,2048]{2,1,0:T(8,128)S(1)}, f32[4,16,2048]{2,1,0:T(8,128)S(1)}, u32[]{:S(2)}, u32[]{:S(2)}) collective-permute-start(f32[4,16,2048]{2,1,0:T(8,128)S(1)} %pad_maximum_fusion.6), channel_id=1, source_target_pairs={{0,1},{1,0},{2,3},{3,2},{4,5},{5,4},{6,7},{7,6},{8,9},{9,8},{10,11... | collective-permute-start | bytes 1572872 | tf_op jit(solution)/shard_map/ppermute | solution.py:339
  18.8 12.7 %collective-permute-start.11 = (f32[4,16,2048]{2,1,0:T(8,128)S(1)}, f32[4,16,2048]{2,1,0:T(8,128)S(1)}, u32[]{:S(2)}, u32[]{:S(2)}) collective-permute-start(f32[4,16,2048]{2,1,0:T(8,128)S(1)} %pad_maximum_fusion.7), channel_id=1, source_target_pairs={{0,3},{1,2},{2,1},{3,0},{4,7},{5,6},{6,5},{7,4},{8,11},{9,10},{10,... | collective-permute-start | bytes 1572872 | tf_op jit(solution)/shard_map/ppermute | solution.py:339
  20.8 9.1 %copy-start.3 = (f32[1,16,2048]{2,1,0:T(8,128)S(1)}, f32[1,16,2048]{2,1,0:T(8,128)}, u32[]{:S(2)}) copy-start(f32[1,16,2048]{2,1,0:T(8,128)} %copy-done.2) | copy-start | bytes 393220
  27.9 24.9 %collective-permute-start.12 = (f32[8,16,2048]{2,1,0:T(8,128)S(1)}, f32[8,16,2048]{2,1,0:T(8,128)}, u32[]{:S(2)}, u32[]{:S(2)}) collective-permute-start(f32[8,16,2048]{2,1,0:T(8,128)S(1)} %pad_maximum_fusion.refs_0_), channel_id=1, source_target_pairs={{0,12},{4,8},{8,4},{12,0},{1,13},{5,9},{9,5},{13,1},{2,14},{6,10},... | collective-permute-start | bytes 3145736 | tf_op jit(solution)/shard_map/ppermute | solution.py:339
  29.4 3.3 %copy-start.6 = (s32[8]{0:T(128)S(1)}, s32[8]{0:T(128)}, u32[]{:S(2)}) copy-start(s32[8]{0:T(128)} %constant.136.clone) | copy-start | bytes 100
  29.4 3.3 %copy-start.4 = (s32[128,16]{0,1:T(8,128)S(1)}, s32[128,16]{0,1:T(8,128)}, u32[]{:S(2)}) copy-start(s32[128,16]{0,1:T(8,128)} %param.15) | copy-start | bytes 24580
  29.4 23.5 %collective-permute-start.13 = (f32[8,16,2048]{2,1,0:T(8,128)S(1)}, f32[8,16,2048]{2,1,0:T(8,128)}, u32[]{:S(2)}, u32[]{:S(2)}) collective-permute-start(f32[8,16,2048]{2,1,0:T(8,128)S(1)} %pad_maximum_fusion.1.refs_1_), channel_id=1, source_target_pairs={{0,1},{1,0},{2,3},{3,2},{4,5},{5,4},{6,7},{7,6},{8,9},{9,8},{10,11... | collective-permute-start | bytes 3145736 | tf_op jit(solution)/shard_map/ppermute | solution.py:339
  30.0 22.9 %collective-permute-start.14 = (f32[8,16,2048]{2,1,0:T(8,128)S(1)}, f32[8,16,2048]{2,1,0:T(8,128)}, u32[]{:S(2)}, u32[]{:S(2)}) collective-permute-start(f32[8,16,2048]{2,1,0:T(8,128)S(1)} %pad_maximum_fusion.2.refs_2_), channel_id=1, source_target_pairs={{0,3},{1,2},{2,1},{3,0},{4,7},{5,6},{6,5},{7,4},{8,11},{9,10},{10,... | collective-permute-start | bytes 3145736 | tf_op jit(solution)/shard_map/ppermute | solution.py:339
  32.5 20.5 %collective-permute-start.15 = (f32[8,16,2048]{2,1,0:T(8,128)}, f32[8,16,2048]{2,1,0:T(8,128)}, u32[]{:S(2)}, u32[]{:S(2)}) collective-permute-start(f32[8,16,2048]{2,1,0:T(8,128)} %pad_maximum_fusion.3.refs_3_), channel_id=1, source_target_pairs={{0,4},{4,0},{8,12},{12,8},{1,5},{5,1},{9,13},{13,9},{2,6},{6,2},{1... | collective-permute-start | bytes 3145736 | tf_op jit(solution)/shard_map/ppermute | solution.py:339
  69.0 17.7 %collective-permute-start.16 = (f32[4,10,128,128]{3,2,1,0:T(8,128)}, f32[4,10,128,128]{3,2,1,0:T(8,128)}, u32[]{:S(2)}, u32[]{:S(2)}) collective-permute-start(f32[4,10,128,128]{3,2,1,0:T(8,128)} %get-tuple-element.38), channel_id=1, source_target_pairs={{0,16},{16,0},{1,17},{17,1},{2,18},{18,2},{3,19},{19,3},{4,20},{20... | collective-permute-start | bytes 7864328 | tf_op jit(solution)/shard_map/ppermute | solution.py:384
  88.7 14.3 %collective-permute-start.17 = (f32[5,128,128]{2,1,0:T(8,128)}, f32[5,128,128]{2,1,0:T(8,128)}, u32[]{:S(2)}, u32[]{:S(2)}) collective-permute-start(f32[5,128,128]{2,1,0:T(8,128)} %get-tuple-element.41), channel_id=1, source_target_pairs={{0,32},{32,64},{64,96},{96,0},{1,33},{33,65},{65,97},{97,1},{2,34}... | collective-permute-start | bytes 983048 | tf_op jit(solution)/shard_map/ppermute | solution.py:387
  90.3 12.7 %collective-permute-start.18 = (f32[5,128,128]{2,1,0:T(8,128)}, f32[5,128,128]{2,1,0:T(8,128)}, u32[]{:S(2)}, u32[]{:S(2)}) collective-permute-start(f32[5,128,128]{2,1,0:T(8,128)} %get-tuple-element.42), channel_id=1, source_target_pairs={{0,96},{32,0},{64,32},{96,64},{1,97},{33,1},{65,33},{97,65},{2,98}... | collective-permute-start | bytes 983048 | tf_op jit(solution)/shard_map/ppermute | solution.py:387
  101.4 14.7 %collective-permute-start.21 = (f32[4,6,128,128]{3,2,1,0:T(8,128)}, f32[4,6,128,128]{3,2,1,0:T(8,128)}, u32[]{:S(2)}, u32[]{:S(2)}) collective-permute-start(f32[4,6,128,128]{3,2,1,0:T(8,128)} %shard_map.110), channel_id=1, source_target_pairs={{0,16},{16,0},{1,17},{17,1},{2,18},{18,2},{3,19},{19,3},{4,20},{20... | collective-permute-start | bytes 4718600 | tf_op jit(solution)/shard_map/ppermute | solution.py:384
  105.8 18.0 %collective-permute-start.19 = (f32[10,128,128]{2,1,0:T(8,128)}, f32[10,128,128]{2,1,0:T(8,128)}, u32[]{:S(2)}, u32[]{:S(2)}) collective-permute-start(f32[10,128,128]{2,1,0:T(8,128)} %get-tuple-element.44), channel_id=1, source_target_pairs={{0,32},{32,64},{64,96},{96,0},{1,33},{33,65},{65,97},{97,1},{2,34}... | collective-permute-start | bytes 1966088 | tf_op jit(solution)/shard_map/ppermute | solution.py:387
  105.8 18.0 %collective-permute-start.20 = (f32[10,128,128]{2,1,0:T(8,128)}, f32[10,128,128]{2,1,0:T(8,128)}, u32[]{:S(2)}, u32[]{:S(2)}) collective-permute-start(f32[10,128,128]{2,1,0:T(8,128)} %get-tuple-element.45), channel_id=1, source_target_pairs={{0,96},{32,0},{64,32},{96,64},{1,97},{33,1},{65,33},{97,65},{2,98}... | collective-permute-start | bytes 1966088 | tf_op jit(solution)/shard_map/ppermute | solution.py:387
  116.1 3.8 %copy-start.5 = (s32[16,4]{0,1:T(4,128)S(1)}, s32[16,4]{0,1:T(4,128)}, u32[]{:S(2)}) copy-start(s32[16,4]{0,1:T(4,128)} %param.14) | copy-start | bytes 772
  117.1 10.6 %collective-permute-start.22 = (f32[3,128,128]{2,1,0:T(8,128)S(1)}, f32[3,128,128]{2,1,0:T(8,128)S(1)}, u32[]{:S(2)}, u32[]{:S(2)}) collective-permute-start(f32[3,128,128]{2,1,0:T(8,128)S(1)} %get-tuple-element.52), channel_id=1, source_target_pairs={{0,32},{32,64},{64,96},{96,0},{1,33},{33,65},{65,97},{97,1},{2,34}... | collective-permute-start | bytes 589832 | tf_op jit(solution)/shard_map/ppermute | solution.py:387
  117.2 10.5 %collective-permute-start.23 = (f32[3,128,128]{2,1,0:T(8,128)S(1)}, f32[3,128,128]{2,1,0:T(8,128)S(1)}, u32[]{:S(2)}, u32[]{:S(2)}) collective-permute-start(f32[3,128,128]{2,1,0:T(8,128)S(1)} %get-tuple-element.57), channel_id=1, source_target_pairs={{0,96},{32,0},{64,32},{96,64},{1,97},{33,1},{65,33},{97,65},{2,98}... | collective-permute-start | bytes 589832 | tf_op jit(solution)/shard_map/ppermute | solution.py:387
  129.1 11.1 %collective-permute-start.24 = (f32[6,128,128]{2,1,0:T(8,128)S(1)}, f32[6,128,128]{2,1,0:T(8,128)S(1)}, u32[]{:S(2)}, u32[]{:S(2)}) collective-permute-start(f32[6,128,128]{2,1,0:T(8,128)S(1)} %get-tuple-element.59), channel_id=1, source_target_pairs={{0,32},{32,64},{64,96},{96,0},{1,33},{33,65},{65,97},{97,1},{2,34}... | collective-permute-start | bytes 1179656 | tf_op jit(solution)/shard_map/ppermute | solution.py:387
  129.2 11.0 %collective-permute-start.25 = (f32[6,128,128]{2,1,0:T(8,128)S(1)}, f32[6,128,128]{2,1,0:T(8,128)S(1)}, u32[]{:S(2)}, u32[]{:S(2)}) collective-permute-start(f32[6,128,128]{2,1,0:T(8,128)S(1)} %get-tuple-element.60), channel_id=1, source_target_pairs={{0,96},{32,0},{64,32},{96,64},{1,97},{33,1},{65,33},{97,65},{2,98}... | collective-permute-start | bytes 1179656 | tf_op jit(solution)/shard_map/ppermute | solution.py:387
  143.9 27.9 %copy-start.1 = (f32[128,2048]{1,0:T(8,128)S(1)}, f32[128,2048]{1,0:T(8,128)}, u32[]{:S(2)}) copy-start(f32[128,2048]{1,0:T(8,128)} %den_ref.1) | copy-start | bytes 3145732
  (1 other events, 2.2 us)
